TPU v7x, 32 devices: a whole 2x2x4 slice. The times are simulated.
32 devices in a mesh: dom: 8 (over z, y), rep: 4 (over x, core).
Axes of the slice: x: 2, y: 2, z: 4, core: 2. Of those that a mesh axis runs over, the one named last changes fastest.
Arguments:
- entities: bfloat16 [2048, 400], P('dom'), may hold values from -2.5 to 2.5, as said below
- relation: float32 [1000, 400], replicated, may hold values from 0.25 to 1.75
- serve_ids: int32 [8, 8, 2], P('dom'), may hold values from 0 to 255
- edge_src: int32 [8, 4, 512], P('dom', 'rep'), may hold values from 0 to 255
- edge_rel: int32 [8, 4, 512], P('dom', 'rep'), may hold values from 0 to 999
- edge_dst: int32 [8, 4, 512], P('dom', 'rep'), may hold values from 0 to 15
- neg_ids: int32 [8, 4, 2, 384], P('dom', 'rep'), may hold values from 0 to 15
- edge_count: int32 [8, 4], P('dom', 'rep'), may hold values from 1 to 512, 1536 in all within a row
Outputs:
- entity_grad: float32 [2048, 400], P('dom', 'rep')
- relation_grad: float32 [1000, 400], replicated
Inputs may be any that keep to these rules, and one draw needn't show every extreme that they name: `entities`: entity entries are bounded.
All inputs are finite; a program needn't handle non-finite values. No bound on the sum of `edge_count` on one device may be relied on, other than what follows from the above.
Results may differ from a plain program's by a relative error of at most 0.0021.
The roundings to bfloat16 on the way count: a program that leaves them out, or rounds other values in their place, can miss the bound.
Values may be sent and summed in bfloat16 or wider, within the bound.
No kernel may reach another device: no remote copies, remote signals or barrier semaphores. Data moves between devices by JAX's collectives and lax.ppermute only.
A program may use at most 64 MiB of HBM per device.

v0:
```python
import jax
import jax.numpy as jnp
from jax import lax
from jax.sharding import PartitionSpec as P


def shard_grads(lhs_block, relation, table, src, rel, dst, neg, count):
    groups = neg.shape[0]
    edges = src.shape[0]
    width = edges // groups
    dim = lhs_block.shape[1]
    lhs_rows = lhs_block[src].astype(jnp.float32)
    rel_rows = relation[rel]
    query = (lhs_rows * rel_rows).astype(jnp.bfloat16).reshape(groups, width, dim)
    cands = jnp.concatenate([table[dst].reshape(groups, width, dim), table[neg]], axis=1)
    scores = jnp.einsum("cid,cjd->cij", query, cands, preferred_element_type=jnp.float32)
    position = jnp.arange(edges, dtype=jnp.int32).reshape(groups, width)
    live = position < count
    columns = jnp.concatenate([live, jnp.ones((groups, neg.shape[1]), dtype=bool)], axis=1)
    scores = jnp.where(columns[:, None, :], scores, jnp.float32(-1e30))
    top = jnp.max(scores, axis=-1, keepdims=True)
    expo = jnp.exp(scores - top)
    probs = expo / jnp.sum(expo, axis=-1, keepdims=True)
    onehot = (jnp.arange(width + neg.shape[1])[None, :] == jnp.arange(width)[:, None]).astype(
        jnp.float32
    )
    grads = ((probs - onehot[None]) * live[:, :, None].astype(jnp.float32)).astype(jnp.bfloat16)
    dquery = jnp.einsum("cij,cjd->cid", grads, cands, preferred_element_type=jnp.float32).reshape(
        edges, dim
    )
    dcand = jnp.einsum("cij,cid->cjd", grads, query, preferred_element_type=jnp.float32)
    lhs_grad = jnp.zeros(lhs_block.shape, jnp.float32).at[src].add(dquery * rel_rows)
    rel_grad = jnp.zeros(relation.shape, jnp.float32).at[rel].add(dquery * lhs_rows)
    table_grad = (
        jnp.zeros(table.shape, jnp.float32).at[dst].add(dcand[:, :width].reshape(edges, dim))
    )
    table_grad = table_grad.at[neg.reshape(-1)].add(dcand[:, width:].reshape(-1, dim))
    return (lhs_grad, table_grad, rel_grad)


def shards(entities, relation, serve_ids, edge_src, edge_rel, edge_dst, neg_ids, edge_count):
    workers = lax.axis_size("dom")
    replicas = lax.axis_size("rep")
    dim = entities.shape[1]
    served = serve_ids[0]
    cap = served.shape[1]
    outgoing = entities[served]
    received = lax.all_to_all(outgoing, "dom", split_axis=0, concat_axis=0, tiled=True)
    table = received.reshape(workers * cap, dim)
    lhs_grad, table_grad, rel_grad = shard_grads(
        entities,
        relation,
        table,
        edge_src[0, 0],
        edge_rel[0, 0],
        edge_dst[0, 0],
        neg_ids[0, 0],
        edge_count[0, 0],
    )
    slots = edge_src.shape[2] * workers * replicas
    relation_grad = lax.psum(rel_grad, ("dom", "rep")) / jnp.float32(slots)
    table_part, lhs_part = (
        lax.psum_scatter(
            table_grad.reshape(workers, cap, dim), "rep", scatter_dimension=2, tiled=True
        ),
        lax.psum_scatter(lhs_grad.reshape(-1, 1, dim), "rep", scatter_dimension=2, tiled=True),
    )
    returned = lax.all_to_all(table_part, "dom", split_axis=0, concat_axis=0, tiled=True)
    narrow = lhs_part.shape[2]
    entity_grad = (
        lhs_part.reshape(-1, narrow).at[served.reshape(-1)].add(returned.reshape(-1, narrow))
    )
    return (entity_grad, relation_grad)


def solution(mesh):
    placed = (
        P("dom", None),
        P(),
        P("dom", None, None),
        P("dom", "rep", None),
        P("dom", "rep", None),
        P("dom", "rep", None),
        P("dom", "rep", None, None),
        P("dom", "rep"),
    )
    return jax.shard_map(
        shards, mesh=mesh, in_specs=placed, out_specs=(P("dom", "rep"), P()), check_vma=False
    )
```

profile of v0, /device:TPU:0, one launch (start us, length us, event | category | flops | bytes accessed | tf_op | source)
XLA Modules:
  0.0 226.4 jit_solution(9020727653664421348)
XLA Ops:
  7.2 1.1 copy.37
  8.2 0.7 compare_select_fusion.5
  8.9 0.1 copy.39
  9.0 0.1 reshape.297
  9.1 0.6 gather_fusion.2
  9.7 0.6 reshape.296
  10.3 7.3 %all-to-all-start = ((bf16[8,2,400]{2,1,0:T(2,128)(2,1)}), bf16[8,2,400]{2,1,0:T(2,128)(2,1)S(1)}, u32[]{:S(2)}, u32[]{:S(2)}) async-start(bf16[8,2,400]{2,1,0:T(2,128)(2,1)} %reshape.296), calls=%async_computation | async-start | bytes 32768 | tf_op jit(solution)/shard_map/all_to_all | solution.py:48
  17.6 0.0 all-reduce.8.cloned.1.call-start
  17.6 0.9 fusion.17
  18.5 0.7 compare_select_fusion.4
  19.2 2.1 copy.38
  21.3 0.0 copy-done.9
  21.3 0.0 copy-done.7
  21.4 0.0 copy-done.10
  22.1 2.6 %gather_fusion = bf16[512,400]{1,0:T(8,128)(2,1)} fusion(bf16[256,400]{1,0:T(8,128)(2,1)S(1)} %copy.37, s32[1024]{0:T(1024)S(1)} %pad_clamp_fusion.4), kind=kCustom, calls=%fused_computation | custom fusion | bytes 821248 | tf_op jit(solution)/shard_map/gather | solution.py:12
  24.7 1.6 gather_fusion.1
  26.3 2.0 fusion.10
  28.4 0.0 all-to-all-done
  28.4 2.7 %gather_fusion.4 = bf16[768,400]{1,0:T(8,128)(2,1)S(1)} fusion(bf16[16,400]{1,0:T(8,128)(2,1)S(1)} %reshape.270, s32[1024]{0:T(1024)S(1)} %pad_clamp_fusion), kind=kCustom, calls=%fused_computation.4 | custom fusion | bytes 1231872 | tf_op jit(solution)/shard_map/gather | solution.py:15
  31.1 0.3 copy.44
  31.4 0.0 copy-start.3
  31.5 0.0 copy-start.1
  31.5 2.0 gather_fusion.3
  33.5 1.0 copy.43
  34.4 0.0 copy-done.3
  34.4 0.0 copy-done.1
  34.4 2.6 %fusion.9 = f32[2,256,400]{2,1,0:T(8,128)S(1)} fusion(bf16[2,384,400]{1,2,0:T(8,128)(2,1)S(1)} %copy.44, bf16[2,256,400]{1,2,0:T(8,128)(2,1)} %copy.43, f32[2,256]{1,0:T(2,128)S(1)} %get-tuple-element.7, f32[256,640]{1,0:T(8,128)S(1)} %copy-done.1, bf16[2,256,400]{2,1,0:T(8,128)(2,1)} %bitcast.48, pred[2,640]{1,0:T(4,128)(4,1)S(1)} %concatenate.6), kind=kOutput, calls=%fused_computation.22 | convolution fusion | flops 530352384 | bytes 2911488 | tf_op jit(solution)/shard_map/reshape | solution.py:28
  37.0 0.2 bitcast_multiply_fusion
  37.3 0.0 copy-start
  37.3 3.7 %scatter_custom_fusion = f32[256,400]{1,0:T(8,128)S(1)} fusion(s32[512]{0:T(512)S(1)} %bitcast.57, f32[512,400]{1,0:T(8,128)S(1)} %bitcast_multiply_fusion, f32[]{:T(128)} %constant.9.clone.1), kind=kCustom, calls=%fused_computation.35 | custom fusion | flops 204800 | bytes 409604 | tf_op jit(solution)/shard_map/scatter-add | solution.py:32
  41.0 1.0 copy.48
  42.0 0.0 all-reduce.8.cloned.1.call-update
  42.0 0.2 all-reduce.6.cloned.1.call-start
  42.3 0.0 copy-done
  42.3 0.0 copy-start.6
  42.3 5.0 %scatter_custom_fusion.4 = f32[1000,400]{1,0:T(8,128)} fusion(s32[512]{0:T(512)S(1)} %bitcast.55, f32[512,400]{1,0:T(8,128)S(1)} %bitcast.42, bf16[512,400]{1,0:T(8,128)(2,1)S(1)} %copy-done, f32[]{:T(128)} %constant.9.clone.1), kind=kCustom, calls=%fused_computation.24 | custom fusion | flops 614400 | bytes 3172868 | tf_op jit(solution)/shard_map/scatter-add | solution.py:33
  47.4 0.0 copy-start.5
  47.4 0.0 all-reduce.6.cloned.1.call-update
  47.4 0.6 copy-done.8
  48.0 0.1 copy.50
  48.1 0.1 reshape_squeeze.6
  48.2 0.0 copy-done.11
  48.2 0.6 dynamic-slice
  49.4 0.0 copy-done.6
  49.5 0.0 copy-done.2
  49.5 3.1 %fusion.8 = f32[2,640,400]{1,2,0:T(8,128)} fusion(bf16[2,256,400]{2,1,0:T(8,128)(2,1)S(1)} %bitcast.49, f32[2,256]{1,0:T(2,128)S(1)} %get-tuple-element.7, f32[256,640]{1,0:T(8,128)S(1)} %copy-done.2, bf16[2,384,400]{1,2,0:T(8,128)(2,1)S(1)} %copy-done.4, bf16[2,256,400]{1,2,0:T(8,128)(2,1)S(1)} %copy-done.6, pred[2,640]{1,0:T(4,128)(4,1)S(1)} %concatenate.6), kind=kOutput, calls=%fused_computation.21 | convolution fusion | flops 528304384 | bytes 4140288 | tf_op jit(solution)/shard_map/cij,cid->cjd/dot_general | solution.py:31
  52.6 1.2 slice.18
  53.8 1.4 slice.19
  55.2 0.3 copy.65
  55.5 3.6 %scatter_custom_fusion.1 = f32[16,400]{1,0:T(8,128)S(1)} fusion(s32[512]{0:T(512)S(1)} %bitcast.53, f32[512,400]{1,0:T(8,128)S(1)} %bitcast.46, f32[]{:T(128)} %constant.9.clone.1), kind=kCustom, calls=%fused_computation.38 | custom fusion | flops 204800 | bytes 25604 | tf_op jit(solution)/shard_map/scatter-add | solution.py:35
  59.2 0.5 copy.66
  59.6 6.6 %scatter_fusion = f32[16,400]{1,0:T(8,128)S(1)} fusion(f32[16,400]{1,0:T(8,128)S(1)} %scatter_custom_fusion.1, s32[768]{0:T(1024)S(1)} %fusion.22, f32[768,400]{1,0:T(8,128)S(1)} %bitcast.41), kind=kCustom, calls=%fused_computation.7 | custom fusion | flops 307200 | bytes 3689472 | tf_op jit(solution)/shard_map/scatter-add | solution.py:37
  66.3 10.9 %all-reduce.2 = f32[8,2,400]{2,1,0:T(2,128)S(1)} all-reduce(f32[8,2,400]{2,1,0:T(2,128)S(1)} %reshape.277), channel_id=3, replica_groups=mesh['dom'=8,'rep'=4] {'rep'}, use_global_device_ids=true, to_apply=%region_6.7.clone | all-reduce | flops 6400 | bytes 51200
  77.2 0.7 constant_dynamic-slice_fusion
  77.9 6.0 %all-to-all-start.1 = ((f32[8,2,100]{2,1,0:T(2,128)}), f32[8,2,100]{2,1,0:T(2,128)S(1)}, u32[]{:S(2)}, u32[]{:S(2)}) async-start(f32[8,2,100]{2,1,0:T(2,128)} %constant_dynamic-slice_fusion), calls=%async_computation.1 | async-start | bytes 16384 | tf_op jit(solution)/shard_map/all_to_all | solution.py:68
  83.9 0.0 all-reduce.8.cloned.1.call-done
  83.9 0.9 constant_dynamic-slice_fusion.1
  84.9 0.1 copy.49
  85.0 5.5 %all-to-all-done.1 = f32[8,2,100]{2,1,0:T(2,128)S(1)} async-done(((f32[8,2,100]{2,1,0:T(2,128)}), f32[8,2,100]{2,1,0:T(2,128)S(1)}, u32[]{:S(2)}, u32[]{:S(2)}) %all-to-all-start.1) | async-done | bytes 6432 | tf_op jit(solution)/shard_map/all_to_all | solution.py:68
  90.4 0.7 scatter_fusion.1
  91.2 0.7 copy.57
  91.9 124.1 %all-reduce.6.cloned.1.call-done = f32[1000,400]{1,0:T(8,128)} async-done(((f32[1000,400]{1,0:T(8,128)}), f32[1000,400]{1,0:T(8,128)}) %all-reduce.6.cloned.1.call-update) | async-done | bytes 1600016 | tf_op jit(solution)/shard_map/psum | solution.py:61
  216.1 1.8 broadcast_multiply_fusion
  217.9 1.7 copy.58
  (25 shorter events, 0.2 us)
Async XLA Ops:
  10.3 18.1 %all-to-all-start = ((bf16[8,2,400]{2,1,0:T(2,128)(2,1)}), bf16[8,2,400]{2,1,0:T(2,128)(2,1)S(1)}, u32[]{:S(2)}, u32[]{:S(2)}) async-start(bf16[8,2,400]{2,1,0:T(2,128)(2,1)} %reshape.296), calls=%async_computation | async-start | bytes 32768 | tf_op jit(solution)/shard_map/all_to_all | solution.py:48
  17.6 66.3 %all-reduce.8.cloned.1.call-start = ((), (), s32[]{:S(2)}) async-start(), calls=%async_computation.3 | async-start | bytes 819200
  19.2 2.1 copy-start.9
  19.2 2.1 copy-start.7
  19.2 2.2 copy-start.10
  31.4 3.0 %copy-start.3 = (bf16[2,384,400]{1,2,0:T(8,128)(2,1)}, bf16[2,384,400]{1,2,0:T(8,128)(2,1)S(1)}, u32[]{:S(2)}) copy-start(bf16[2,384,400]{1,2,0:T(8,128)(2,1)S(1)} %copy.44) | copy-start | bytes 1843204
  31.5 3.0 %copy-start.1 = (f32[256,640]{1,0:T(8,128)S(1)}, f32[256,640]{1,0:T(8,128)}, u32[]{:S(2)}) copy-start(f32[256,640]{1,0:T(8,128)} %fusion.17) | copy-start | bytes 1966084
  37.3 5.0 %copy-start = (bf16[512,400]{1,0:T(8,128)(2,1)S(1)}, bf16[512,400]{1,0:T(8,128)(2,1)}, u32[]{:S(2)}) copy-start(bf16[512,400]{1,0:T(8,128)(2,1)} %gather_fusion) | copy-start | bytes 1228804
  42.0 174.0 %all-reduce.6.cloned.1.call-start = ((), (), s32[]{:S(2)}) async-start(), calls=%async_computation.2 | async-start | bytes 4096000 | tf_op jit(solution)/shard_map/psum | solution.py:61
  42.3 7.1 %copy-start.6 = (bf16[2,256,400]{1,2,0:T(8,128)(2,1)S(1)}, bf16[2,256,400]{1,2,0:T(8,128)(2,1)}, u32[]{:S(2)}) copy-start(bf16[2,256,400]{1,2,0:T(8,128)(2,1)} %copy.43) | copy-start | bytes 1228804
  47.3 0.7 copy-start.8
  47.3 0.8 copy-start.11
  47.4 2.1 copy-start.2
  47.4 2.1 copy-start.4
  47.4 2.1 copy-start.5
  77.9 12.5 %all-to-all-start.1 = ((f32[8,2,100]{2,1,0:T(2,128)}), f32[8,2,100]{2,1,0:T(2,128)S(1)}, u32[]{:S(2)}, u32[]{:S(2)}) async-start(f32[8,2,100]{2,1,0:T(2,128)} %constant_dynamic-slice_fusion), calls=%async_computation.1 | async-start | bytes 16384 | tf_op jit(solution)/shard_map/all_to_all | solution.py:68
Sparse Core Ops, SparseCore 0:
  42.2 33.9 all-reduce.7
  82.3 133.6 all-reduce.5
where the time goes:
time: 227 us; the launch traced here: 226 us
  waiting for transfers between devices  130 us (57%)
  other arithmetic  26.1 us (11%)
  local copies, waits for them, and re-layouts  24.8 us (11%)
  between operations  15.7 us (7%)
  starting transfers between devices  13.5 us (6%)
  blocking collectives  10.9 us (5%)
  matrix products  5.72 us (3%)
    psum x1, waiting for transfers between devices, shards(): relation_grad = lax.psum(rel_grad, ('dom', 'rep')) / jnp.float32(slots)  124 us
    unnamed x1, blocking collectives  10.9 us
    unnamed x33, local copies, waits for them, and re-layouts  8.55 us
    all_to_all x1, starting transfers between devices, shards(): lax.all_to_all(outgoing, 'dom', split_axis=0, concat_axis=0, tiled=True)  7.28 us
    scatter-add x1, other arithmetic, shard_grads(): table_grad.at[neg.reshape(-1)].add(dcand[:, width:].reshape(-1, dim))  6.64 us
    all_to_all x1, starting transfers between devices, shards(): lax.all_to_all(table_part, 'dom', split_axis=0, concat_axis=0, tiled=True)  5.99 us
    all_to_all x1, waiting for transfers between devices, shards(): lax.all_to_all(table_part, 'dom', split_axis=0, concat_axis=0, tiled=True)  5.48 us
    scatter-add x1, other arithmetic, shard_grads(): jnp.zeros(relation.shape, jnp.float32).at[rel].add(dquery * lhs_rows)  5.04 us
  transfers between devices with their start and end apart: 4, of which 2 were waited for; matrix products, arithmetic and copies ran while one was open for 16% of the time, Pallas kernels for 0%

commit v1 on v0

v1 whole, which is shorter than its diff:
```python
import functools

import jax
import jax.numpy as jnp
from jax import lax
from jax.experimental import pallas as pl
from jax.experimental.pallas import tpu as pltpu
from jax.sharding import PartitionSpec as P

F32 = jnp.float32
BF16 = jnp.bfloat16
IDX_ROWS = 8
VMEM = pl.BlockSpec(memory_space=pltpu.VMEM)
SMEM = pl.BlockSpec(memory_space=pltpu.SMEM)


def params():
    return pltpu.CompilerParams(vmem_limit_bytes=40 * 1024 * 1024)


def split2(x):
    hi = x.astype(BF16)
    lo = (x - hi.astype(F32)).astype(BF16)
    return hi, lo


def dot(a, b):
    return jnp.dot(a, b, preferred_element_type=F32)


def prep_kernel(serve, count, ent, src, rel, dst, neg, out_rows, out_idx, onehot):
    workers, cap = serve.shape[1], serve.shape[2]
    rows = ent.shape[0]
    groups = neg.shape[2]
    width = neg.shape[3]

    def fill(k, carry):
        spot = lax.broadcasted_iota(jnp.int32, (1, rows), 1)
        picked = serve[0, k // cap, k % cap]
        onehot[pl.ds(k, 1), :] = jnp.where(spot == picked, 1.0, 0.0).astype(F32)
        return carry

    lax.fori_loop(0, workers * cap, fill, 0)
    out_rows[...] = dot(onehot[...].astype(BF16), ent[...]).astype(BF16)
    out_idx[...] = jnp.full(out_idx.shape, count[0, 0], jnp.int32)
    out_idx[0:1, :] = src[0]
    out_idx[1:2, :] = rel[0]
    out_idx[2:3, :] = dst[0]
    for g in range(groups):
        out_idx[3 + g : 4 + g, :width] = neg[0, 0, g : g + 1, :]


def main_kernel(cfg, rep_ref, *refs):
    workers, replicas, cap, groups, width, nrel, pad_rel, block, dim, narrow, total = cfg
    idx_refs = refs[:replicas]
    (ent, relation, table, out_rel, out_lhs) = refs[replicas : replicas + 5]
    (idx_all, idx_col, rel_hi, rel_lo, acc_rel, acc_lhs, acc_tab) = refs[replicas + 5 :]
    edges = idx_all.shape[1]
    rows = ent.shape[0]
    slots = table.shape[0]
    mine = rep_ref[0]
    per = edges // groups

    for i in range(replicas):
        idx_all[i * IDX_ROWS : (i + 1) * IDX_ROWS, :] = idx_refs[i][...]
        idx_col[i] = jnp.transpose(idx_refs[i][...])
    tail = pad_rel - nrel
    if tail:
        rel_hi[nrel:, :] = jnp.zeros((tail, dim), BF16)
        rel_lo[nrel:, :] = jnp.zeros((tail, dim), BF16)
    hi, lo = split2(relation[...])
    rel_hi[:nrel, :] = hi
    rel_lo[:nrel, :] = lo
    acc_rel[...] = jnp.zeros(acc_rel.shape, F32)
    acc_lhs[...] = jnp.zeros(acc_lhs.shape, F32)
    acc_tab[...] = jnp.zeros(acc_tab.shape, F32)

    spot = lax.broadcasted_iota(jnp.int32, (total, edges), 0)
    target = (spot // block) * (block * replicas) + mine * block + spot % block

    def shard(i, carry):
        base = pl.multiple_of(i * IDX_ROWS, IDX_ROWS)
        lanes = idx_all[pl.ds(base, IDX_ROWS), :]
        cols = idx_col[i]
        src_l, rel_l, dst_l = lanes[0:1], lanes[1:2], lanes[2:3]
        count = lanes[IDX_ROWS - 1 : IDX_ROWS]
        src_c, rel_c = cols[:, 0:1], cols[:, 1:2]

        pick = jnp.where(
            lax.broadcasted_iota(jnp.int32, (edges, rows), 1) == src_c, 1.0, 0.0
        ).astype(BF16)
        lhs = dot(pick, ent[...])
        pick = jnp.where(
            lax.broadcasted_iota(jnp.int32, (edges, pad_rel), 1) == rel_c, 1.0, 0.0
        ).astype(BF16)
        rel_rows = dot(pick, rel_hi[...]) + dot(pick, rel_lo[...])
        query = (lhs * rel_rows).astype(BF16)
        scores = lax.dot_general(
            table[...], query, (((1,), (1,)), ((), ())), preferred_element_type=F32
        )
        position = lax.broadcasted_iota(jnp.int32, (1, edges), 1)
        live = jnp.where(position < count, 1.0, 0.0).astype(F32)
        own = jnp.where(
            lax.broadcasted_iota(jnp.int32, (slots, edges), 0) == dst_l, 1.0, 0.0
        ).astype(F32)
        seen = own * live
        parts = []
        for g in range(groups):
            s = scores[:, g * per : (g + 1) * per]
            o = own[:, g * per : (g + 1) * per]
            neg = jnp.where(
                lax.broadcasted_iota(jnp.int32, (slots, width), 0)
                == lanes[3 + g : 4 + g, :width],
                1.0,
                0.0,
            ).astype(F32)
            times = jnp.sum(seen[:, g * per : (g + 1) * per], axis=1, keepdims=True) + jnp.sum(
                neg, axis=1, keepdims=True
            )
            s = jnp.where(times > 0, s, F32(-1e30))
            top = jnp.max(s, axis=0, keepdims=True)
            expo = jnp.exp(s - top)
            norm = jnp.sum(expo * times, axis=0, keepdims=True)
            probs = expo / norm
            other = probs.astype(BF16).astype(F32)
            self_ = (probs - 1.0).astype(BF16).astype(F32)
            grads = (times - o) * other + o * self_
            parts.append(grads * live[:, g * per : (g + 1) * per])
        grads = jnp.concatenate(parts, axis=1)
        g0 = grads.astype(BF16)
        rest = grads - g0.astype(F32)
        g1 = rest.astype(BF16)
        g2 = (rest - g1.astype(F32)).astype(BF16)

        stack = jnp.concatenate([g0, g1, g2], axis=0)
        tables = jnp.concatenate([table[...]] * 3, axis=0)
        dquery = lax.dot_general(
            stack, tables, (((0,), (0,)), ((), ())), preferred_element_type=F32
        )
        acc_tab[:, :dim] += dot(g0, query) + dot(g1, query) + dot(g2, query)
        y0, y1 = split2(dquery * lhs)
        put = jnp.where(target == rel_l, 1.0, 0.0).astype(BF16)
        acc_rel[:, :dim] += dot(put, y0) + dot(put, y1)
        x0, x1 = split2(dquery * rel_rows)
        put = jnp.where(
            lax.broadcasted_iota(jnp.int32, (rows, edges), 0) == src_l, 1.0, 0.0
        ).astype(BF16)
        acc_lhs[:, :dim] += dot(put, x0) + dot(put, x1)
        return carry

    lax.fori_loop(0, replicas, shard, 0)

    lhs_all = acc_lhs[...]
    part = lhs_all[:, :narrow]
    for k in range(1, replicas):
        part = jnp.where(mine == k, lhs_all[:, k * narrow : (k + 1) * narrow], part)
    out_lhs[...] = part
    out_rel[...] = acc_rel[...]
    span = out_rel.shape[1]
    shifted = pltpu.roll(acc_tab[...], dim - mine * narrow, 1)
    lane = lax.broadcasted_iota(jnp.int32, (slots, span), 1)
    shifted = jnp.where((lane >= dim) & (lane < dim + narrow), shifted, 0.0)
    for o in range(workers):
        out_rel[o * block : o * block + cap, :] += shifted[o * cap : (o + 1) * cap, :]


def entity_kernel(dim, serve, lhs, recv, out, rows_ref):
    workers, cap = serve.shape[1], serve.shape[2]
    narrow = out.shape[1]
    out[...] = lhs[...]
    for w in range(workers):
        rows_ref[w * cap : (w + 1) * cap, :] = recv[w, :cap, dim : dim + narrow]

    def add(k, carry):
        picked = serve[0, k // cap, k % cap]
        out[pl.ds(picked, 1), :] += rows_ref[pl.ds(k, 1), :]
        return carry

    lax.fori_loop(0, workers * cap, add, 0)


def shards(entities, relation, serve_ids, edge_src, edge_rel, edge_dst, neg_ids, edge_count):
    workers = lax.axis_size("dom")
    replicas = lax.axis_size("rep")
    rows, dim = entities.shape
    nrel = relation.shape[0]
    cap = serve_ids.shape[2]
    edges = edge_src.shape[2]
    groups, width = neg_ids.shape[2], neg_ids.shape[3]
    slots = workers * cap
    narrow = dim // replicas
    devices = workers * replicas
    block = max(-(-nrel // devices), cap)
    total = workers * block
    pad_rel = -(-nrel // 128) * 128
    span = -(-(dim + narrow) // 128) * 128

    outgoing, idx = pl.pallas_call(
        prep_kernel,
        out_shape=(
            jax.ShapeDtypeStruct((slots, dim), BF16),
            jax.ShapeDtypeStruct((IDX_ROWS, edges), jnp.int32),
        ),
        in_specs=[SMEM, SMEM] + [VMEM] * 5,
        out_specs=(VMEM, VMEM),
        scratch_shapes=[pltpu.VMEM((slots, rows), F32)],
        compiler_params=params(),
        name="prep",
    )(serve_ids, edge_count, entities, edge_src, edge_rel, edge_dst, neg_ids)

    held = [idx]
    for hop in range(1, replicas):
        held.append(
            lax.ppermute(idx, "rep", [(i, (i + hop) % replicas) for i in range(replicas)])
        )
    received = lax.all_to_all(
        outgoing.reshape(workers, cap, dim), "dom", split_axis=0, concat_axis=0, tiled=True
    )
    table = received.reshape(slots, dim)

    cfg = (workers, replicas, cap, groups, width, nrel, pad_rel, block, dim, narrow, total)
    mine = lax.axis_index("rep").astype(jnp.int32).reshape(1)
    rel_part, lhs_part = pl.pallas_call(
        functools.partial(main_kernel, cfg),
        out_shape=(
            jax.ShapeDtypeStruct((total, span), F32),
            jax.ShapeDtypeStruct((rows, narrow), F32),
        ),
        in_specs=[SMEM] + [VMEM] * (replicas + 3),
        out_specs=(VMEM, VMEM),
        scratch_shapes=[
            pltpu.VMEM((replicas * IDX_ROWS, edges), jnp.int32),
            pltpu.VMEM((replicas, edges, IDX_ROWS), jnp.int32),
            pltpu.VMEM((pad_rel, dim), BF16),
            pltpu.VMEM((pad_rel, dim), BF16),
            pltpu.VMEM((total, span), F32),
            pltpu.VMEM((rows, span), F32),
            pltpu.VMEM((slots, span), F32),
        ],
        compiler_params=params(),
        name="edges",
    )(mine, *held, entities, relation, table)

    recv = lax.all_to_all(
        rel_part.reshape(workers, block, span), "dom", split_axis=0, concat_axis=0, tiled=True
    )
    scale = 1.0 / (edges * devices)
    rel_sum = (jnp.sum(recv[:, :, :dim], axis=0) * F32(scale)).astype(BF16)
    gathered = lax.all_gather(rel_sum, ("dom", "rep"), axis=0, tiled=True)
    relation_grad = gathered[:nrel].astype(F32)

    entity_grad = pl.pallas_call(
        functools.partial(entity_kernel, dim),
        out_shape=jax.ShapeDtypeStruct((rows, narrow), F32),
        in_specs=[SMEM, VMEM, VMEM],
        out_specs=VMEM,
        scratch_shapes=[pltpu.VMEM((slots, narrow), F32)],
        compiler_params=params(),
        name="entity",
    )(serve_ids, lhs_part, recv)
    return (entity_grad, relation_grad)


def solution(mesh):
    placed = (
        P("dom", None),
        P(),
        P("dom", None, None),
        P("dom", "rep", None),
        P("dom", "rep", None),
        P("dom", "rep", None),
        P("dom", "rep", None, None),
        P("dom", "rep"),
    )
    return jax.shard_map(
        shards, mesh=mesh, in_specs=placed, out_specs=(P("dom", "rep"), P()), check_vma=False
    )
```

time: 227 us -> 98.8 us (0.44)
  waiting for transfers between devices: 130 us -> 2.8 us
  blocking collectives: 10.9 us -> 60.5 us
  other arithmetic: 26.1 us -> 0.32 us
  local copies, waits for them, and re-layouts: 24.8 us -> 9.74 us
  Pallas kernels: 0 us -> 14.6 us
  between operations: 15.7 us -> 1.36 us
  matrix products: 5.72 us -> 0 us
  starting transfers between devices: 13.5 us -> 9 us
    psum x1 -> x0, waiting for transfers between devices: 124 us -> none  [shards(): relation_grad = lax.psum(rel_grad, ('dom', 'rep')) / jnp.float32(slots)]
    all_gather x0 -> x1, blocking collectives: none -> 42.1 us  [shards(): gathered = lax.all_gather(rel_sum, ('dom', 'rep'), axis=0, tiled=True)]
    scatter-add x5 -> x0, other arithmetic: 19.7 us -> none  [the longest x1 6.64 us: shard_grads(): table_grad.at[neg.reshape(-1)].add(dcand[:, width:].reshape(-1, dim))]
    all_to_all x0 -> x1, blocking collectives: none -> 18.5 us  [shards(): lax.all_to_all(rel_part.reshape(workers, block, span), 'dom', split_axis=...]
    pallas_call x0 -> x3, Pallas kernels: none -> 14.6 us  [the longest x1 12.8 us: shards(): pl.pallas_call(functools.partial(main_kernel, cfg), out_shape=(jax.ShapeD...]
    unnamed x1 -> x0, blocking collectives: 10.9 us -> none
    gather x7 -> x0, local copies, waits for them, and re-layouts: 10.5 us -> none  [the longest x2 3.03 us: shard_grads(): table[neg]]
    all_to_all x2 -> x1, starting transfers between devices: 13.3 us -> 7.28 us  [shards(): lax.all_to_all(outgoing.reshape(workers, cap, dim), 'dom', split_axis=0,...]
  transfers between devices with their start and end apart: 4 -> 4, of which waited for: 2 -> 1; matrix products, arithmetic and copies ran while one was open for 16% -> 2% of each run, Pallas kernels for 0% -> 0%
where the time goes in v1:
time: 98.8 us; the launch traced here: 98.4 us
  blocking collectives  60.5 us (61%)
  Pallas kernels  14.6 us (15%)
  local copies, waits for them, and re-layouts  9.74 us (10%)
  starting transfers between devices  9 us (9%)
  waiting for transfers between devices  2.8 us (3%)
  between operations  1.36 us (1%)
    all_gather x1, blocking collectives, shards(): gathered = lax.all_gather(rel_sum, ('dom', 'rep'), axis=0, tiled=True)  42.1 us
    all_to_all x1, blocking collectives, shards(): lax.all_to_all(rel_part.reshape(workers, block, span), 'dom', split_axis=...  18.5 us
    pallas_call x1, Pallas kernels, shards(): pl.pallas_call(functools.partial(main_kernel, cfg), out_shape=(jax.ShapeD...  12.8 us
    unnamed x13, local copies, waits for them, and re-layouts  9.08 us
    all_to_all x1, starting transfers between devices, shards(): lax.all_to_all(outgoing.reshape(workers, cap, dim), 'dom', split_axis=0,...  7.28 us
    all_to_all x1, waiting for transfers between devices, shards(): lax.all_to_all(outgoing.reshape(workers, cap, dim), 'dom', split_axis=0,...  2.8 us
  transfers between devices with their start and end apart: 4, of which 1 were waited for; matrix products, arithmetic and copies ran while one was open for 2% of the time, Pallas kernels for 0%

profile of v1, /device:TPU:0, one launch (start us, length us, event | category | flops | bytes accessed | tf_op | source)
XLA Modules:
  0.0 98.4 jit_solution(15180325581772303121)
XLA Ops:
  1.3 0.8 copy.20.serve
  2.0 1.1 %copy.17.ent.refs_4_ = bf16[256,400]{1,0:T(8,128)(2,1)S(1)} copy(bf16[256,400]{0,1:T(8,128)(2,1)} %param.8) | data formatting | bytes 409600 | tf_op args[0]
  3.1 0.0 copy-start
  3.1 0.7 copy-done
  3.8 0.0 copy-start.1
  3.8 0.7 copy-done.1
  4.5 0.0 copy-start.2
  4.5 0.7 copy-done.2
  5.2 0.0 copy-start.3
  5.2 0.7 copy-done.3
  5.8 1.0 %prep.1 = (bf16[16,400]{1,0:T(8,128)(2,1)S(1)}, s32[8,512]{1,0:T(8,128)S(1)}) custom-call(s32[1,8,2]{2,1,0:T(8,128)S(1)} %copy.20.serve, s32[1,1]{1,0:T(1,128)S(6)} %copy.23.count, bf16[256,400]{1,0:T(8,128)(2,1)S(1)} %copy.17.ent.refs_4_, s32[1,1,512]{2,1,0:T(1,128)S(1)} %copy-done.1, s32[1,1,512]{2,1,0:T(1,128)S(1)} %copy-done.2, ...), custom_call_target="tpu_custom_call" | custom-call | tf_op jit(solution)/shard_map/prep/pallas_call | solution.py:198
  6.8 0.6 reshape.17
  7.5 7.3 %all-to-all-start = ((bf16[8,2,400]{2,1,0:T(2,128)(2,1)}), bf16[8,2,400]{2,1,0:T(2,128)(2,1)S(1)}, u32[]{:S(2)}, u32[]{:S(2)}) async-start(bf16[8,2,400]{2,1,0:T(2,128)(2,1)} %reshape.17), calls=%async_computation | async-start | bytes 32768 | tf_op jit(solution)/shard_map/all_to_all | solution.py:216
  14.7 0.7 collective-permute-start.2
  15.4 0.9 collective-permute-start.1
  16.3 0.2 collective-permute-start
  16.5 2.0 %copy.19.refs_5_ = f32[1000,400]{1,0:T(8,128)S(1)} copy(f32[1000,400]{0,1:T(8,128)} %param.9) | data formatting | bytes 3200000 | tf_op args[1]
  18.5 2.8 %all-to-all-done = bf16[8,2,400]{2,1,0:T(2,128)(2,1)S(1)} async-done(((bf16[8,2,400]{2,1,0:T(2,128)(2,1)}), bf16[8,2,400]{2,1,0:T(2,128)(2,1)S(1)}, u32[]{:S(2)}, u32[]{:S(2)}) %all-to-all-start) | async-done | bytes 12832 | tf_op jit(solution)/shard_map/all_to_all | solution.py:216
  21.4 0.0 collective-permute-done.2.refs_3_
  21.4 0.0 collective-permute-done.1.refs_2_
  21.4 0.0 collective-permute-done.refs_1_
  21.4 12.8 %edges.1 = (f32[256,512]{1,0:T(8,128)S(1)}, f32[256,100]{1,0:T(8,128)S(1)}) custom-call(s32[1]{0:T(128)} %bitcast.rep_ref, s32[8,512]{1,0:T(8,128)S(1)} %get-tuple-element.6.refs_0_, s32[8,512]{1,0:T(8,128)S(1)} %collective-permute-done.refs_1_, s32[8,512]{1,0:T(8,128)S(1)} %collective-permute-done.1.refs_2_, s32[8,512]{1,0:T(8,128)S(1)} %collective-permute-done.2.refs_3_, ...), custom_call_target="tpu_custom_call" | custom-call | tf_op jit(solution)/shard_map/edges/pallas_call | solution.py:223
  34.2 18.5 %all_to_all.10.recv = f32[8,32,512]{2,1,0:T(8,128)S(1)} all-to-all(f32[8,32,512]{2,1,0:T(8,128)S(1)} %bitcast.2), channel_id=1, replica_groups=mesh['dom'=8,'rep'=4] {'dom'}, dimensions={0} | all-to-all | bytes 1048576 | tf_op jit(solution)/shard_map/all_to_all | solution.py:244
  52.7 0.9 entity.1
  53.5 0.7 copy.21
  54.3 42.1 %all_gather.3 = bf16[1024,400]{1,0:T(8,128)(2,1)S(1)} all-gather(bf16[32,400]{1,0:T(8,128)(2,1)S(1)} %multiply_convert_fusion), channel_id=1, replica_groups=mesh['dom'=8,'rep'=4] {'dom','rep'}, dimensions={0}, use_global_device_ids=true | all-gather | bytes 844800 | tf_op jit(solution)/shard_map/all_gather | solution.py:249
  96.4 0.3 slice_convert_fusion
  96.7 1.7 %copy.22 = f32[1000,400]{0,1:T(8,128)} copy(f32[1000,400]{1,0:T(8,128)S(1)} %slice_convert_fusion) | data formatting | bytes 3200000
  (3 shorter events, 0.1 us)
Async XLA Ops:
  3.1 0.7 copy-start
  3.8 0.7 copy-start.1
  4.5 0.7 copy-start.2
  5.2 0.7 copy-start.3
  7.5 13.9 %all-to-all-start = ((bf16[8,2,400]{2,1,0:T(2,128)(2,1)}), bf16[8,2,400]{2,1,0:T(2,128)(2,1)S(1)}, u32[]{:S(2)}, u32[]{:S(2)}) async-start(bf16[8,2,400]{2,1,0:T(2,128)(2,1)} %reshape.17), calls=%async_computation | async-start | bytes 32768 | tf_op jit(solution)/shard_map/all_to_all | solution.py:216
  14.7 6.6 %collective-permute-start.2 = (s32[8,512]{1,0:T(8,128)S(1)}, s32[8,512]{1,0:T(8,128)S(1)}, u32[]{:S(2)}, u32[]{:S(2)}) collective-permute-start(s32[8,512]{1,0:T(8,128)S(1)} %get-tuple-element.6.refs_0_), channel_id=1, source_target_pairs={{0,3},{1,0},{2,1},{3,2},{4,7},{5,4},{6,5},{7,6},{8,11},{9,8},{10,9... | collective-permute-start | bytes 49160 | tf_op jit(solution)/shard_map/ppermute | solution.py:214
  15.4 6.0 %collective-permute-start.1 = (s32[8,512]{1,0:T(8,128)S(1)}, s32[8,512]{1,0:T(8,128)S(1)}, u32[]{:S(2)}, u32[]{:S(2)}) collective-permute-start(s32[8,512]{1,0:T(8,128)S(1)} %get-tuple-element.6.refs_0_), channel_id=1, source_target_pairs={{0,2},{1,3},{2,0},{3,1},{4,6},{5,7},{6,4},{7,5},{8,10},{9,11},{10,... | collective-permute-start | bytes 49160 | tf_op jit(solution)/shard_map/ppermute | solution.py:214
  16.3 5.1 %collective-permute-start = (s32[8,512]{1,0:T(8,128)S(1)}, s32[8,512]{1,0:T(8,128)S(1)}, u32[]{:S(2)}, u32[]{:S(2)}) collective-permute-start(s32[8,512]{1,0:T(8,128)S(1)} %get-tuple-element.6.refs_0_), channel_id=1, source_target_pairs={{0,1},{1,2},{2,3},{3,0},{4,5},{5,6},{6,7},{7,4},{8,9},{9,10},{10,1... | collective-permute-start | bytes 49160 | tf_op jit(solution)/shard_map/ppermute | solution.py:214

commit v2 on v0

v2 whole, which is shorter than its diff:
```python
import functools

import jax
import jax.numpy as jnp
from jax import lax
from jax.experimental import pallas as pl
from jax.experimental.pallas import tpu as pltpu
from jax.sharding import PartitionSpec as P

F32 = jnp.float32
BF16 = jnp.bfloat16
IDX_ROWS = 8
LANES = 128
VMEM = pl.BlockSpec(memory_space=pltpu.VMEM)
SMEM = pl.BlockSpec(memory_space=pltpu.SMEM)
HBM = pl.BlockSpec(memory_space=pltpu.HBM)


def params():
    return pltpu.CompilerParams(vmem_limit_bytes=32 * 1024 * 1024)


def up(value, step):
    return -(-value // step) * step


def split2(x):
    hi = x.astype(BF16)
    lo = (x - hi.astype(F32)).astype(BF16)
    return hi, lo


def split3(x):
    hi, rest = x.astype(BF16), x
    rest = rest - hi.astype(F32)
    mid = rest.astype(BF16)
    low = (rest - mid.astype(F32)).astype(BF16)
    return hi, mid, low


def dot(a, b):
    return jnp.dot(a, b, preferred_element_type=F32)


def dot_t(a, b):
    return lax.dot_general(a, b, (((1,), (1,)), ((), ())), preferred_element_type=F32)


def ones_where(flag):
    return jnp.where(flag, 1.0, 0.0).astype(BF16)


def iota(shape, axis):
    return lax.broadcasted_iota(jnp.int32, shape, axis)


def shifted_rows(x, offset, narrow, offsets):
    out = x[offsets[0] : offsets[0] + narrow]
    for other in offsets[1:]:
        out = jnp.where(offset == other, x[other : other + narrow], out)
    return out


def prep_kernel(direct, place, serve, count, ent, src, rel, dst, neg, *refs):
    cap, workers = serve.shape[1], serve.shape[2]
    rows = ent.shape[1]
    groups, width = neg.shape[2], neg.shape[3]
    copies = 7
    out_idx, outs = refs[0], refs[1:-9]
    serve_s, count_s, ent_v, src_v, rel_v, dst_v, neg_v, onehot, sems = refs[-9:]
    moves = [
        pltpu.make_async_copy(a, b, sems.at[n])
        for n, (a, b) in enumerate(
            zip(
                (serve, count, ent, src, rel, dst, neg),
                (serve_s, count_s, ent_v, src_v, rel_v, dst_v, neg_v),
            )
        )
    ]
    for move in moves:
        move.start()
    for move in moves:
        move.wait()
    assert len(moves) == copies
    out_idx[...] = jnp.full(out_idx.shape, count_s[0, 0], jnp.int32)
    out_idx[0:1, :] = src_v[0]
    out_idx[1:2, :] = rel_v[0]
    out_idx[2:3, :] = dst_v[0]
    for g in range(groups):
        out_idx[3 + g : 4 + g, :width] = neg_v[0, 0, g : g + 1, :]

    first = place[0] if direct else 0

    def fill(k, carry):
        worker = lax.rem(first + k // cap, workers)
        picked = serve_s[0, k % cap, worker]
        onehot[pl.ds(k, 1), :] = jnp.where(iota((1, rows), 1) == picked, 1.0, 0.0).astype(F32)
        return carry

    lax.fori_loop(0, workers * cap, fill, 0)
    picked_rows = dot_t(onehot[...].astype(BF16), ent_v[...])
    if direct:
        for h in range(workers):
            outs[h][...] = picked_rows[h * cap : (h + 1) * cap]
    else:
        outs[0][...] = picked_rows


def main_kernel(cfg, place, *refs):
    (direct, workers, replicas, cap, groups, width, nrel, pad_rel, block, narrow, window, offsets) = cfg
    pieces = workers if direct else 1
    idx_refs, refs = refs[:replicas], refs[replicas:]
    (ent, relation), refs = refs[:2], refs[2:]
    table_refs, refs = refs[:pieces], refs[pieces:]
    out_lhs, outs, refs = refs[0], refs[1 : 1 + pieces], refs[1 + pieces :]
    (
        idx_all,
        idx_col,
        rel_parts,
        table_f,
        table_t,
        lhs_s,
        rel_s,
        query_s,
        acc_rel,
        acc_lhs,
        acc_tab,
        wide_t,
        served_s,
    ) = refs
    edges = idx_all.shape[1]
    dim, rows = ent.shape
    slots = workers * cap
    dom, rep = place[0], place[1]
    per = edges // groups
    base = pl.multiple_of((rep * narrow) // 8 * 8, 8)
    offset = rep * narrow - base

    for i in range(replicas):
        idx_all[i * IDX_ROWS : (i + 1) * IDX_ROWS, :] = idx_refs[i][...]
        idx_col[i] = jnp.transpose(idx_refs[i][...])
    hi, lo = split2(relation[...])
    if pad_rel > nrel:
        rel_parts[...] = jnp.zeros(rel_parts.shape, BF16)
    rel_parts[:dim, :nrel] = hi
    rel_parts[dim:, :nrel] = lo
    if direct:
        for h in range(workers):
            source = lax.rem(dom - h + workers, workers)
            for c in range(cap):
                table_f[pl.ds(source * cap + c, 1), :] = table_refs[h][c : c + 1, :]
    else:
        table_f[...] = table_refs[0][...]
    table_t[...] = jnp.transpose(table_f[...])
    table = table_f[...].astype(BF16)
    own_t = table_t[pl.ds(base, window), :].astype(BF16)
    own_t = jnp.concatenate([own_t] * 3, axis=1)
    acc_rel[...] = jnp.zeros(acc_rel.shape, F32)
    acc_lhs[...] = jnp.zeros(acc_lhs.shape, F32)
    acc_tab[...] = jnp.zeros(acc_tab.shape, F32)

    def shard(i, carry):
        lanes = idx_all[pl.ds(pl.multiple_of(i * IDX_ROWS, IDX_ROWS), IDX_ROWS), :]
        cols = idx_col[i]
        src_l, rel_l, dst_l = lanes[0:1], lanes[1:2], lanes[2:3]
        count = lanes[IDX_ROWS - 1 : IDX_ROWS]

        lhs = dot(ent[...], ones_where(iota((rows, edges), 0) == src_l))
        both = dot(rel_parts[...], ones_where(iota((pad_rel, edges), 0) == rel_l))
        rel_rows = both[:dim] + both[dim:]
        query = (lhs * rel_rows).astype(BF16)
        lhs_s[...] = lhs
        rel_s[...] = rel_rows
        query_s[...] = query.astype(F32)
        scores = dot(table, query)
        live = jnp.where(iota((1, edges), 1) < count, 1.0, 0.0).astype(F32)
        own = jnp.where(iota((slots, edges), 0) == dst_l, 1.0, 0.0).astype(F32)
        seen = own * live
        parts = []
        for g in range(groups):
            span = slice(g * per, (g + 1) * per)
            s, o = scores[:, span], own[:, span]
            neg = jnp.where(
                iota((slots, width), 0) == lanes[3 + g : 4 + g, :width], 1.0, 0.0
            ).astype(F32)
            times = jnp.sum(seen[:, span], axis=1, keepdims=True)
            times = times + jnp.sum(neg, axis=1, keepdims=True)
            s = jnp.where(times > 0, s, F32(-1e30))
            top = jnp.max(s, axis=0, keepdims=True)
            expo = jnp.exp(s - top)
            probs = expo / jnp.sum(expo * times, axis=0, keepdims=True)
            other = probs.astype(BF16).astype(F32)
            itself = (probs - 1.0).astype(BF16).astype(F32)
            parts.append(((times - o) * other + o * itself) * live[:, span])
        grads = jnp.concatenate(parts, axis=1)
        stack = jnp.concatenate(split3(grads), axis=0)
        stack_t = jnp.concatenate(split3(jnp.transpose(grads)), axis=1)

        dquery = dot(own_t, stack)
        acc_tab[...] += dot(query_s[pl.ds(base, window), :].astype(BF16), stack_t)
        y = jnp.concatenate(split2(dquery * lhs_s[pl.ds(base, window), :]), axis=0)
        acc_rel[...] += dot(y, ones_where(iota((edges, pad_rel), 1) == cols[:, 1:2]))
        x = jnp.concatenate(split2(dquery * rel_s[pl.ds(base, window), :]), axis=0)
        acc_lhs[...] += dot(x, ones_where(iota((edges, rows), 1) == cols[:, 0:1]))
        return carry

    lax.fori_loop(0, replicas, shard, 0)

    pick = functools.partial(shifted_rows, offset=offset, narrow=narrow, offsets=offsets)
    out_lhs[...] = pick(acc_lhs[:window] + acc_lhs[window:])
    acc_rel[:narrow] = pick(acc_rel[:window] + acc_rel[window:])
    table_grad = pick(acc_tab[:, :slots] + acc_tab[:, slots : 2 * slots] + acc_tab[:, 2 * slots :])
    wide_t[...] = jnp.zeros(wide_t.shape, F32)
    wide_t[:narrow] = table_grad
    served_s[...] = jnp.transpose(wide_t[...])
    for h in range(workers):
        out = outs[h] if direct else outs[0].at[h]
        to = lax.rem(dom + h, workers) if direct else h
        out[...] = jnp.zeros(out.shape, F32)
        if direct:
            out[:narrow, :] = acc_rel[:narrow, pl.ds(pl.multiple_of(to * block, block), block)]
        else:
            out[:narrow, :block] = acc_rel[:narrow, h * block : (h + 1) * block]
        for c in range(cap):
            out[narrow + c : narrow + c + 1, :] = served_s[pl.ds(to * cap + c, 1), :]


def combine_kernel(scale, narrow, block, *refs):
    out = refs[-1]
    total = refs[0][...]
    for ref in refs[1:-1]:
        total = total + ref[...]
    out[...] = jnp.zeros(out.shape, BF16)
    keep = iota(out.shape, 0) < narrow
    tall = jnp.concatenate(
        [total[:, :block], jnp.zeros((out.shape[0] - total.shape[0], block), F32)], axis=0
    )
    out[...] = jnp.where(keep, tall * F32(scale), 0.0).astype(BF16)


def entity_kernel(direct, narrow, place, serve, lhs, *refs):
    cap, workers = serve.shape[1], serve.shape[2]
    recv, out, (terms, onehot) = refs[:-3], refs[-3], refs[-2:]
    rows = out.shape[1]
    for h in range(workers):
        part = recv[h] if direct else recv[0].at[h]
        terms[h * cap : (h + 1) * cap, :] = part[narrow : narrow + cap, :]

    def fill(k, carry):
        h = k // cap
        worker = lax.rem(place[0] - h + workers, workers) if direct else h
        picked = serve[0, k % cap, worker]
        onehot[pl.ds(k, 1), :] = jnp.where(iota((1, rows), 1) == picked, 1.0, 0.0).astype(F32)
        return carry

    lax.fori_loop(0, workers * cap, fill, 0)
    spots = onehot[...].astype(BF16)
    parts = jnp.concatenate(split3(jnp.transpose(terms[...])), axis=1)
    added = dot(parts, jnp.concatenate([spots] * 3, axis=0))
    out[...] = lhs[...] + added[:narrow]


def spread_kernel(phases, narrow, block, place, *refs):
    pieces, out, wide = refs[:-2], refs[-2], refs[-1]
    replicas = wide.shape[0]
    height = wide.shape[1]
    nrel = out.shape[1]
    each = pieces[0].shape[0]
    for n, piece in enumerate(pieces):
        for m in range(each):
            spot = n * each + m
            at = [place[0], place[1]]
            for axis, stride, radix in phases:
                hop = spot % radix
                spot = spot // radix
                digit = lax.rem(at[axis] // stride, radix)
                moved = lax.rem(digit - hop + radix, radix)
                at[axis] = at[axis] + (moved - digit) * stride
            wide[at[1], :, pl.ds(pl.multiple_of(at[0] * block, block), block)] = piece[m].astype(
                F32
            )[:height]
    for r in range(replicas):
        out[r * narrow : (r + 1) * narrow, :] = wide[r, :narrow, :nrel]


def turned(size, stride, radix, hop):
    pairs = []
    for i in range(size):
        digit = (i // stride) % radix
        pairs.append((i, i + ((digit + hop) % radix - digit) * stride))
    return pairs


def radices(size):
    found = []
    for radix in (4, 2, 3, 5, 7):
        while size % radix == 0:
            found.append(radix)
            size //= radix
    return found


def shards(entities, relation, serve_ids, edge_src, edge_rel, edge_dst, neg_ids, edge_count):
    workers = lax.axis_size("dom")
    replicas = lax.axis_size("rep")
    rows, dim = entities.shape
    nrel = relation.shape[0]
    cap = serve_ids.shape[2]
    edges = edge_src.shape[2]
    groups, width = neg_ids.shape[2], neg_ids.shape[3]
    slots = workers * cap
    narrow = dim // replicas
    direct = workers <= 16
    block = up(-(-nrel // workers), LANES if direct else 8)
    pad_rel = up(max(nrel, workers * block), LANES)
    offsets = sorted({(narrow * r) % 8 for r in range(replicas)})
    window = up(narrow + offsets[-1], 8)
    height = up(narrow + cap, 8)
    pieces = workers if direct else 1
    ent_t, rel_t = entities.T, relation.T
    serve_t = jnp.transpose(serve_ids, (0, 2, 1))
    place = jnp.stack([lax.axis_index("dom"), lax.axis_index("rep")]).astype(jnp.int32)

    piece = (cap, dim) if direct else (slots, dim)
    prepared = pl.pallas_call(
        functools.partial(prep_kernel, direct),
        out_shape=[jax.ShapeDtypeStruct((IDX_ROWS, edges), jnp.int32)]
        + [jax.ShapeDtypeStruct(piece, F32)] * pieces,
        in_specs=[SMEM] + [HBM] * 7,
        out_specs=[VMEM] * (1 + pieces),
        scratch_shapes=[
            pltpu.SMEM(serve_t.shape, jnp.int32),
            pltpu.SMEM(edge_count.shape, jnp.int32),
            pltpu.VMEM(ent_t.shape, BF16),
            pltpu.VMEM(edge_src.shape, jnp.int32),
            pltpu.VMEM(edge_rel.shape, jnp.int32),
            pltpu.VMEM(edge_dst.shape, jnp.int32),
            pltpu.VMEM(neg_ids.shape, jnp.int32),
            pltpu.VMEM((slots, rows), F32),
            pltpu.SemaphoreType.DMA((7,)),
        ],
        compiler_params=params(),
        name="prep",
    )(place, serve_t, edge_count, ent_t, edge_src, edge_rel, edge_dst, neg_ids)
    idx, served = prepared[0], prepared[1:]

    held = [idx]
    for hop in range(1, replicas):
        held.append(lax.ppermute(idx, "rep", turned(replicas, 1, replicas, hop)))
    if direct:
        tables = [served[0]]
        for hop in range(1, workers):
            tables.append(lax.ppermute(served[hop], "dom", turned(workers, 1, workers, hop)))
    else:
        tables = [
            lax.all_to_all(
                served[0].reshape(workers, cap, dim).astype(BF16), "dom", 0, 0, tiled=True
            )
            .reshape(slots, dim)
            .astype(F32)
        ]

    cfg = (
        direct, workers, replicas, cap, groups, width, nrel, pad_rel, block, narrow, window,
        tuple(offsets),
    )
    lanes = max(LANES, block, up(narrow, LANES))
    part = (height, lanes) if direct else (workers, height, lanes)
    results = pl.pallas_call(
        functools.partial(main_kernel, cfg),
        out_shape=[jax.ShapeDtypeStruct((narrow, rows), F32)]
        + [jax.ShapeDtypeStruct(part, F32)] * pieces,
        in_specs=[SMEM] + [VMEM] * (replicas + 2 + pieces),
        out_specs=[VMEM] * (1 + pieces),
        scratch_shapes=[
            pltpu.VMEM((replicas * IDX_ROWS, edges), jnp.int32),
            pltpu.VMEM((replicas, edges, IDX_ROWS), jnp.int32),
            pltpu.VMEM((2 * dim, pad_rel), BF16),
            pltpu.VMEM((slots, dim), F32),
            pltpu.VMEM((dim, slots), F32),
            pltpu.VMEM((dim, edges), F32),
            pltpu.VMEM((dim, edges), F32),
            pltpu.VMEM((dim, edges), F32),
            pltpu.VMEM((2 * window, pad_rel), F32),
            pltpu.VMEM((2 * window, rows), F32),
            pltpu.VMEM((window, 3 * slots), F32),
            pltpu.VMEM((lanes, slots), F32),
            pltpu.VMEM((slots, lanes), F32),
        ],
        compiler_params=params(),
        name="edges",
    )(place, *held, ent_t, rel_t, *tables)
    lhs_part, sent = results[0], results[1:]

    if direct:
        recv = [sent[0]]
        for hop in range(1, workers):
            recv.append(lax.ppermute(sent[hop], "dom", turned(workers, 1, workers, hop)))
        summed = recv
    else:
        recv = [lax.all_to_all(sent[0], "dom", 0, 0, tiled=True)]
        summed = [jnp.sum(recv[0], axis=0)]
    tall = up(height, 16)
    chunk = pl.pallas_call(
        functools.partial(combine_kernel, 1.0 / (edges * workers * replicas), narrow, block),
        out_shape=jax.ShapeDtypeStruct((tall, block), BF16),
        in_specs=[VMEM] * len(summed),
        out_specs=VMEM,
        compiler_params=params(),
        name="combine",
    )(*summed)

    entity_grad = pl.pallas_call(
        functools.partial(entity_kernel, direct, narrow),
        out_shape=jax.ShapeDtypeStruct((narrow, rows), F32),
        in_specs=[SMEM, SMEM] + [VMEM] * (1 + pieces),
        out_specs=VMEM,
        scratch_shapes=[pltpu.VMEM((slots, lanes), F32), pltpu.VMEM((slots, rows), F32)],
        compiler_params=params(),
        name="entity",
    )(place, serve_t, lhs_part, *recv)

    if direct:
        phases = []
        for axis, name, size in ((0, "dom", workers), (1, "rep", replicas)):
            stride = size
            for radix in radices(size) if axis == 0 else (2,) * (replicas.bit_length() - 1):
                stride //= radix
                phases.append((axis, stride, radix))
        held = [chunk.reshape(1, tall, block)]
        for axis, stride, radix in phases:
            name, size = (("dom", workers), ("rep", replicas))[axis]
            base = held[0] if len(held) == 1 else jnp.concatenate(held, axis=0)
            held = [base]
            for hop in range(1, radix):
                held.append(lax.ppermute(base, name, turned(size, stride, radix, hop)))
        relation_t = pl.pallas_call(
            functools.partial(spread_kernel, tuple(phases), narrow, block),
            out_shape=jax.ShapeDtypeStruct((dim, nrel), F32),
            in_specs=[SMEM] + [VMEM] * len(held),
            out_specs=VMEM,
            scratch_shapes=[pltpu.VMEM((replicas, height, pad_rel), F32)],
            compiler_params=params(),
            name="spread",
        )(place, *held)
    else:
        whole = lax.all_gather(chunk[:narrow], ("dom", "rep"), axis=0)
        whole = whole.reshape(workers, replicas, narrow, block).transpose(1, 2, 0, 3)
        relation_t = whole.reshape(dim, workers * block)[:, :nrel].astype(F32)
    return (entity_grad.T, relation_t.T)


def solution(mesh):
    placed = (
        P("dom", None),
        P(),
        P("dom", None, None),
        P("dom", "rep", None),
        P("dom", "rep", None),
        P("dom", "rep", None),
        P("dom", "rep", None, None),
        P("dom", "rep"),
    )
    return jax.shard_map(
        shards, mesh=mesh, in_specs=placed, out_specs=(P("dom", "rep"), P()), check_vma=False
    )
```

time: 227 us -> 81.2 us (0.36)
  waiting for transfers between devices: 130 us -> 28.1 us
  other arithmetic: 26.1 us -> 0.09 us
  local copies, waits for them, and re-layouts: 24.8 us -> 6.81 us
  Pallas kernels: 0 us -> 15.6 us
  starting transfers between devices: 13.5 us -> 28.9 us
  between operations: 15.7 us -> 1.38 us
  blocking collectives: 10.9 us -> 0 us
  matrix products: 5.72 us -> 0 us
    psum x1 -> x0, waiting for transfers between devices: 124 us -> none  [shards(): relation_grad = lax.psum(rel_grad, ('dom', 'rep')) / jnp.float32(slots)]
    ppermute x0 -> x23, starting transfers between devices: none -> 28.9 us  [the longest x7 11 us: shards(): lax.ppermute(sent[hop], 'dom', turned(workers, 1, workers, hop))]
    ppermute x0 -> x23, waiting for transfers between devices: none -> 28.1 us  [the longest x6 13.3 us: shards(): held.append(lax.ppermute(base, name, turned(size, stride, radix, hop)))]
    scatter-add x5 -> x0, other arithmetic: 19.7 us -> none  [the longest x1 6.64 us: shard_grads(): table_grad.at[neg.reshape(-1)].add(dcand[:, width:].reshape(-1, dim))]
    pallas_call x0 -> x5, Pallas kernels: none -> 15.6 us  [the longest x1 9.95 us: shards(): pl.pallas_call(functools.partial(main_kernel, cfg), out_shape=[jax.ShapeD...]
    all_to_all x2 -> x0, starting transfers between devices: 13.3 us -> none  [the longest x1 7.28 us: shards(): lax.all_to_all(outgoing, 'dom', split_axis=0, concat_axis=0, tiled=True)]
    unnamed x1 -> x0, blocking collectives: 10.9 us -> none
    gather x7 -> x0, local copies, waits for them, and re-layouts: 10.5 us -> none  [the longest x2 3.03 us: shard_grads(): table[neg]]
  transfers between devices with their start and end apart: 4 -> 23, of which waited for: 2 -> 13; matrix products, arithmetic and copies ran while one was open for 16% -> 0% of each run, Pallas kernels for 0% -> 2%
where the time goes in v2:
time: 81.2 us; the launch traced here: 80.8 us
  starting transfers between devices  28.9 us (36%)
  waiting for transfers between devices  28.1 us (35%)
  Pallas kernels  15.6 us (19%)
  local copies, waits for them, and re-layouts  6.81 us (8%)
  between operations  1.38 us (2%)
    ppermute x6, waiting for transfers between devices, shards(): held.append(lax.ppermute(base, name, turned(size, stride, radix, hop)))  13.3 us
    ppermute x7, waiting for transfers between devices, shards(): lax.ppermute(served[hop], 'dom', turned(workers, 1, workers, hop))  11.2 us
    ppermute x7, starting transfers between devices, shards(): lax.ppermute(sent[hop], 'dom', turned(workers, 1, workers, hop))  11 us
    pallas_call x1, Pallas kernels, shards(): pl.pallas_call(functools.partial(main_kernel, cfg), out_shape=[jax.ShapeD...  9.95 us
    ppermute x7, starting transfers between devices, shards(): lax.ppermute(served[hop], 'dom', turned(workers, 1, workers, hop))  8.58 us
    unnamed x22, local copies, waits for them, and re-layouts  6.74 us
    ppermute x6, starting transfers between devices, shards(): held.append(lax.ppermute(base, name, turned(size, stride, radix, hop)))  6.01 us
    ppermute x7, waiting for transfers between devices, shards(): lax.ppermute(sent[hop], 'dom', turned(workers, 1, workers, hop))  3.51 us
  transfers between devices with their start and end apart: 23, of which 13 were waited for; matrix products, arithmetic and copies ran while one was open for 0% of the time, Pallas kernels for 2%

profile of v2, /device:TPU:0, one launch (start us, length us, event | category | flops | bytes accessed | tf_op | source)
XLA Modules:
  0.0 80.8 jit_solution(11761459855816468645)
XLA Ops:
  1.3 0.1 pad_add_fusion.place
  1.4 0.0 copy-start.1
  1.4 0.9 %copy-done.1 = bf16[256,400]{0,1:T(8,128)(2,1)S(1)} copy-done((bf16[256,400]{0,1:T(8,128)(2,1)S(1)}, bf16[256,400]{0,1:T(8,128)(2,1)}, u32[]{:S(2)}) %copy-start.1) | copy-done | bytes 204824
  2.3 0.0 copy-start.3
  2.3 0.7 copy-done.3
  3.0 0.0 copy-start.5
  3.0 0.7 copy-done.5
  3.7 0.7 copy-done.6
  4.3 0.7 copy-done.7
  5.0 0.7 copy-done.8
  5.7 1.7 %prep.1 = (s32[8,512]{1,0:T(8,128)S(1)}, f32[2,400]{1,0:T(2,128)S(1)}, f32[2,400]{1,0:T(2,128)S(1)}, f32[2,400]{1,0:T(2,128)S(1)}, f32[2,400]{1,0:T(2,128)S(1)},...) custom-call(s32[2]{0:T(128)S(1)} %pad_add_fusion.place, ...), custom_call_target="tpu_custom_call" | custom-call | tf_op jit(solution)/shard_map/prep/pallas_call | solution.py:325
  7.4 2.4 %collective-permute-start.2 = (s32[8,512]{1,0:T(8,128)S(1)}, s32[8,512]{1,0:T(8,128)S(1)}, u32[]{:S(2)}, u32[]{:S(2)}) collective-permute-start(s32[8,512]{1,0:T(8,128)S(1)} %get-tuple-element.20.refs_0_), channel_id=1, source_target_pairs={{0,3},{1,0},{2,1},{3,2},{4,7},{5,4},{6,5},{7,6},{8,11},{9,8},{10,9... | collective-permute-start | bytes 49160 | tf_op jit(solution)/shard_map/ppermute | solution.py:349
  9.8 0.6 collective-permute-start.1
  10.4 0.2 collective-permute-start
  10.6 1.5 %collective-permute-start.3 = (f32[2,400]{1,0:T(2,128)S(1)}, f32[2,400]{1,0:T(2,128)S(1)}, u32[]{:S(2)}, u32[]{:S(2)}) collective-permute-start(f32[2,400]{1,0:T(2,128)S(1)} %get-tuple-element.22), channel_id=1, source_target_pairs={{0,4},{4,8},{8,12},{12,16},{16,20},{20,24},{24,28},{28,0},{1,5},{5... | collective-permute-start | bytes 9608 | tf_op jit(solution)/shard_map/ppermute | solution.py:353
  12.1 1.6 %collective-permute-start.4 = (f32[2,400]{1,0:T(2,128)S(1)}, f32[2,400]{1,0:T(2,128)S(1)}, u32[]{:S(2)}, u32[]{:S(2)}) collective-permute-start(f32[2,400]{1,0:T(2,128)S(1)} %get-tuple-element.23), channel_id=1, source_target_pairs={{0,8},{4,12},{8,16},{12,20},{16,24},{20,28},{24,0},{28,4},{1,9},{5... | collective-permute-start | bytes 9608 | tf_op jit(solution)/shard_map/ppermute | solution.py:353
  13.7 3.2 %collective-permute-done.3.refs_7_ = f32[2,400]{1,0:T(2,128)S(1)} collective-permute-done((f32[2,400]{1,0:T(2,128)S(1)}, f32[2,400]{1,0:T(2,128)S(1)}, u32[]{:S(2)}, u32[]{:S(2)}) %collective-permute-start.3) | collective-permute-done | bytes 3232 | tf_op jit(solution)/shard_map/ppermute | solution.py:353
  16.9 0.0 collective-permute-start.5
  16.9 0.6 collective-permute-done.4.refs_8_
  17.5 1.8 %collective-permute-start.6 = (f32[2,400]{1,0:T(2,128)S(1)}, f32[2,400]{1,0:T(2,128)S(1)}, u32[]{:S(2)}, u32[]{:S(2)}) collective-permute-start(f32[2,400]{1,0:T(2,128)S(1)} %get-tuple-element.25), channel_id=1, source_target_pairs={{0,16},{4,20},{8,24},{12,28},{16,0},{20,4},{24,8},{28,12},{1,17},{... | collective-permute-start | bytes 9608 | tf_op jit(solution)/shard_map/ppermute | solution.py:353
  19.3 3.0 %collective-permute-done.5.refs_9_ = f32[2,400]{1,0:T(2,128)S(1)} collective-permute-done((f32[2,400]{1,0:T(2,128)S(1)}, f32[2,400]{1,0:T(2,128)S(1)}, u32[]{:S(2)}, u32[]{:S(2)}) %collective-permute-start.5) | collective-permute-done | bytes 3232 | tf_op jit(solution)/shard_map/ppermute | solution.py:353
  22.3 0.0 collective-permute-start.7
  22.3 0.0 collective-permute-done.6.refs_10_
  22.3 1.8 %collective-permute-start.8 = (f32[2,400]{1,0:T(2,128)S(1)}, f32[2,400]{1,0:T(2,128)S(1)}, u32[]{:S(2)}, u32[]{:S(2)}) collective-permute-start(f32[2,400]{1,0:T(2,128)S(1)} %get-tuple-element.27), channel_id=1, source_target_pairs={{0,24},{4,28},{8,0},{12,4},{16,8},{20,12},{24,16},{28,20},{1,25},{... | collective-permute-start | bytes 9608 | tf_op jit(solution)/shard_map/ppermute | solution.py:353
  24.1 2.7 %collective-permute-done.7.refs_11_ = f32[2,400]{1,0:T(2,128)S(1)} collective-permute-done((f32[2,400]{1,0:T(2,128)S(1)}, f32[2,400]{1,0:T(2,128)S(1)}, u32[]{:S(2)}, u32[]{:S(2)}) %collective-permute-start.7) | collective-permute-done | bytes 3232 | tf_op jit(solution)/shard_map/ppermute | solution.py:353
  26.8 1.9 %collective-permute-start.9 = (f32[2,400]{1,0:T(2,128)S(1)}, f32[2,400]{1,0:T(2,128)S(1)}, u32[]{:S(2)}, u32[]{:S(2)}) collective-permute-start(f32[2,400]{1,0:T(2,128)S(1)} %get-tuple-element.28), channel_id=1, source_target_pairs={{0,28},{4,0},{8,4},{12,8},{16,12},{20,16},{24,20},{28,24},{1,29},{... | collective-permute-start | bytes 9608 | tf_op jit(solution)/shard_map/ppermute | solution.py:353
  28.7 0.0 collective-permute-done.8.refs_12_
  28.7 1.7 %collective-permute-done.9.refs_13_ = f32[2,400]{1,0:T(2,128)S(1)} collective-permute-done((f32[2,400]{1,0:T(2,128)S(1)}, f32[2,400]{1,0:T(2,128)S(1)}, u32[]{:S(2)}, u32[]{:S(2)}) %collective-permute-start.9) | collective-permute-done | bytes 3232 | tf_op jit(solution)/shard_map/ppermute | solution.py:353
  30.4 0.0 collective-permute-done.2.refs_3_
  30.4 0.0 collective-permute-done.1.refs_2_
  30.4 0.0 collective-permute-done.refs_1_
  30.4 0.0 copy-start
  30.5 1.4 %copy-done = f32[1000,400]{0,1:T(8,128)S(1)} copy-done((f32[1000,400]{0,1:T(8,128)S(1)}, f32[1000,400]{0,1:T(8,128)}, u32[]{:S(2)}) %copy-start) | copy-done | bytes 1600024
  31.9 0.9 %copy-done.2 = bf16[256,400]{0,1:T(8,128)(2,1)S(1)} copy-done((bf16[256,400]{0,1:T(8,128)(2,1)S(1)}, bf16[256,400]{0,1:T(8,128)(2,1)}, u32[]{:S(2)}) %copy-start.2) | copy-done | bytes 204824
  32.8 9.9 %edges.1 = (f32[100,256]{1,0:T(8,128)S(1)}, f32[104,128]{1,0:T(8,128)S(1)}, f32[104,128]{1,0:T(8,128)S(1)}, f32[104,128]{1,0:T(8,128)S(1)}, f32[104,128]{1,0:T(8...) custom-call(s32[2]{0:T(128)S(1)} %pad_add_fusion.place, ...), custom_call_target="tpu_custom_call" | custom-call | tf_op jit(solution)/shard_map/edges/pallas_call | solution.py:369
  42.8 1.6 %collective-permute-start.10 = (f32[104,128]{1,0:T(8,128)S(1)}, f32[104,128]{1,0:T(8,128)S(1)}, u32[]{:S(2)}, u32[]{:S(2)}) collective-permute-start(f32[104,128]{1,0:T(8,128)S(1)} %get-tuple-element.31), channel_id=1, source_target_pairs={{0,4},{4,8},{8,12},{12,16},{16,20},{20,24},{24,28},{28,0},{1,5},{5... | collective-permute-start | bytes 159752 | tf_op jit(solution)/shard_map/ppermute | solution.py:398
  44.3 0.3 collective-permute-start.11
  44.6 3.8 %collective-permute-start.12 = (f32[104,128]{1,0:T(8,128)S(1)}, f32[104,128]{1,0:T(8,128)S(1)}, u32[]{:S(2)}, u32[]{:S(2)}) collective-permute-start(f32[104,128]{1,0:T(8,128)S(1)} %get-tuple-element.33), channel_id=1, source_target_pairs={{0,12},{4,16},{8,20},{12,24},{16,28},{20,0},{24,4},{28,8},{1,13},{... | collective-permute-start | bytes 159752 | tf_op jit(solution)/shard_map/ppermute | solution.py:398
  48.4 0.1 collective-permute-start.13
  48.5 3.8 %collective-permute-start.14 = (f32[104,128]{1,0:T(8,128)S(1)}, f32[104,128]{1,0:T(8,128)S(1)}, u32[]{:S(2)}, u32[]{:S(2)}) collective-permute-start(f32[104,128]{1,0:T(8,128)S(1)} %get-tuple-element.35), channel_id=1, source_target_pairs={{0,20},{4,24},{8,28},{12,0},{16,4},{20,8},{24,12},{28,16},{1,21},{... | collective-permute-start | bytes 159752 | tf_op jit(solution)/shard_map/ppermute | solution.py:398
  52.3 0.0 collective-permute-done.10.refs_1_
  52.3 0.8 %collective-permute-start.15 = (f32[104,128]{1,0:T(8,128)S(1)}, f32[104,128]{1,0:T(8,128)S(1)}, u32[]{:S(2)}, u32[]{:S(2)}) collective-permute-start(f32[104,128]{1,0:T(8,128)S(1)} %get-tuple-element.36), channel_id=1, source_target_pairs={{0,24},{4,28},{8,0},{12,4},{16,8},{20,12},{24,16},{28,20},{1,25},{... | collective-permute-start | bytes 159752 | tf_op jit(solution)/shard_map/ppermute | solution.py:398
  53.2 0.0 collective-permute-done.11.refs_2_
  53.2 0.6 collective-permute-start.16
  53.8 0.0 collective-permute-done.12.refs_3_
  53.8 0.0 collective-permute-done.13.refs_4_
  53.8 0.3 collective-permute-done.14.refs_5_
  54.1 2.3 %collective-permute-done.15.refs_6_ = f32[104,128]{1,0:T(8,128)S(1)} collective-permute-done((f32[104,128]{1,0:T(8,128)S(1)}, f32[104,128]{1,0:T(8,128)S(1)}, u32[]{:S(2)}, u32[]{:S(2)}) %collective-permute-start.15) | collective-permute-done | bytes 53280 | tf_op jit(solution)/shard_map/ppermute | solution.py:398
  56.5 0.8 %collective-permute-done.16.refs_7_ = f32[104,128]{1,0:T(8,128)S(1)} collective-permute-done((f32[104,128]{1,0:T(8,128)S(1)}, f32[104,128]{1,0:T(8,128)S(1)}, u32[]{:S(2)}, u32[]{:S(2)}) %collective-permute-start.16) | collective-permute-done | bytes 53280 | tf_op jit(solution)/shard_map/ppermute | solution.py:398
  57.4 2.0 %collective-permute-start.19 = (bf16[1,112,128]{2,1,0:T(8,128)(2,1)S(1)}, bf16[1,112,128]{2,1,0:T(8,128)(2,1)S(1)}, u32[]{:S(2)}, u32[]{:S(2)}) collective-permute-start(bf16[1,112,128]{2,1,0:T(8,128)(2,1)S(1)} %bitcast.13), channel_id=1, source_target_pairs={{0,24},{4,28},{8,0},{12,4},{16,8},{20,12},{24,16},{28,20},{1,25},{... | collective-permute-start | bytes 86024 | tf_op jit(solution)/shard_map/ppermute | solution.py:436
  59.4 0.7 collective-permute-start.18
  60.1 0.2 collective-permute-start.17
  60.3 1.0 %collective-permute-done.19 = bf16[1,112,128]{2,1,0:T(8,128)(2,1)S(1)} collective-permute-done((bf16[1,112,128]{2,1,0:T(8,128)(2,1)S(1)}, bf16[1,112,128]{2,1,0:T(8,128)(2,1)S(1)}, u32[]{:S(2)}, u32[]{:S(2)}) %collective-permute-start.19) | collective-permute-done | bytes 28704 | tf_op jit(solution)/shard_map/ppermute | solution.py:436
  61.3 2.9 %collective-permute-done.18 = bf16[1,112,128]{2,1,0:T(8,128)(2,1)S(1)} collective-permute-done((bf16[1,112,128]{2,1,0:T(8,128)(2,1)S(1)}, bf16[1,112,128]{2,1,0:T(8,128)(2,1)S(1)}, u32[]{:S(2)}, u32[]{:S(2)}) %collective-permute-start.18) | collective-permute-done | bytes 28704 | tf_op jit(solution)/shard_map/ppermute | solution.py:436
  64.2 1.6 %collective-permute-done.17 = bf16[1,112,128]{2,1,0:T(8,128)(2,1)S(1)} collective-permute-done((bf16[1,112,128]{2,1,0:T(8,128)(2,1)S(1)}, bf16[1,112,128]{2,1,0:T(8,128)(2,1)S(1)}, u32[]{:S(2)}, u32[]{:S(2)}) %collective-permute-start.17) | collective-permute-done | bytes 28704 | tf_op jit(solution)/shard_map/ppermute | solution.py:436
  65.7 1.7 %collective-permute-start.20 = (bf16[4,112,128]{2,1,0:T(8,128)(2,1)S(1)}, bf16[4,112,128]{2,1,0:T(8,128)(2,1)S(1)}, u32[]{:S(2)}, u32[]{:S(2)}) collective-permute-start(bf16[4,112,128]{2,1,0:T(8,128)(2,1)S(1)} %pad_maximum_fusion), channel_id=1, source_target_pairs={{0,4},{4,0},{8,12},{12,8},{16,20},{20,16},{24,28},{28,24},{1,5},{5... | collective-permute-start | bytes 344072 | tf_op jit(solution)/shard_map/ppermute | solution.py:436
  67.5 3.1 %collective-permute-done.20 = bf16[4,112,128]{2,1,0:T(8,128)(2,1)S(1)} collective-permute-done((bf16[4,112,128]{2,1,0:T(8,128)(2,1)S(1)}, bf16[4,112,128]{2,1,0:T(8,128)(2,1)S(1)}, u32[]{:S(2)}, u32[]{:S(2)}) %collective-permute-start.20) | collective-permute-done | bytes 114720 | tf_op jit(solution)/shard_map/ppermute | solution.py:436
  70.7 1.3 %collective-permute-start.21 = (bf16[8,112,128]{2,1,0:T(8,128)(2,1)S(1)}, bf16[8,112,128]{2,1,0:T(8,128)(2,1)S(1)}, u32[]{:S(2)}, u32[]{:S(2)}) collective-permute-start(bf16[8,112,128]{2,1,0:T(8,128)(2,1)S(1)} %get-tuple-element.38), channel_id=1, source_target_pairs={{0,2},{1,3},{2,0},{3,1},{4,6},{5,7},{6,4},{7,5},{8,10},{9,11},{10,... | collective-permute-start | bytes 688136 | tf_op jit(solution)/shard_map/ppermute | solution.py:436
  72.0 4.8 %collective-permute-done.21 = bf16[8,112,128]{2,1,0:T(8,128)(2,1)S(1)} collective-permute-done((bf16[8,112,128]{2,1,0:T(8,128)(2,1)S(1)}, bf16[8,112,128]{2,1,0:T(8,128)(2,1)S(1)}, u32[]{:S(2)}, u32[]{:S(2)}) %collective-permute-start.21) | collective-permute-done | bytes 229408 | tf_op jit(solution)/shard_map/ppermute | solution.py:436
  76.8 0.1 collective-permute-start.22
  76.9 0.0 copy-done.4
  76.9 1.8 %entity.1 = f32[100,256]{1,0:T(8,128)} custom-call(s32[2]{0:T(128)S(1)} %pad_add_fusion.place, s32[1,2,8]{2,1,0:T(2,128)S(1)} %bitcast.18, f32[100,256]{1,0:T(8,128)S(1)} %get-tuple-element.29.lhs, f32[104,128]{1,0:T(8,128)S(1)} %get-tuple-element.30.refs_0_, f32[104,128]{1,0:T(8,128)S(1)} %collective-permute-done.10.refs_1_, ...), custom_call_target="tpu_custom_call" | custom-call | tf_op jit(solution)/shard_map/entity/pallas_call | solution.py:413
  78.6 0.0 collective-permute-done.22.refs_1_
  78.7 2.2 %spread.1 = f32[400,1000]{1,0:T(8,128)} custom-call(s32[2]{0:T(128)S(1)} %pad_add_fusion.place, bf16[16,112,128]{2,1,0:T(8,128)(2,1)S(1)} %constant_dynamic-update-slice_fusion.5.refs_0_, bf16[16,112,128]{2,1,0:T(8,128)(2,1)S(1)} %collective-permute-done.22.refs_1_), custom_call_target="tpu_custom_call" | custom-call | tf_op jit(solution)/shard_map/spread/pallas_call | solution.py:437
  (13 shorter events, 0.2 us)
Async XLA Ops:
  1.4 0.9 %copy-start.1 = (bf16[256,400]{0,1:T(8,128)(2,1)S(1)}, bf16[256,400]{0,1:T(8,128)(2,1)}, u32[]{:S(2)}) copy-start(bf16[256,400]{0,1:T(8,128)(2,1)} %param.8) | copy-start | bytes 614404
  2.3 0.7 copy-start.3
  3.0 0.7 copy-start.5
  3.6 0.7 copy-start.6
  4.3 0.7 copy-start.7
  5.0 0.7 copy-start.8
  7.4 23.1 %collective-permute-start.2 = (s32[8,512]{1,0:T(8,128)S(1)}, s32[8,512]{1,0:T(8,128)S(1)}, u32[]{:S(2)}, u32[]{:S(2)}) collective-permute-start(s32[8,512]{1,0:T(8,128)S(1)} %get-tuple-element.20.refs_0_), channel_id=1, source_target_pairs={{0,3},{1,0},{2,1},{3,2},{4,7},{5,4},{6,5},{7,6},{8,11},{9,8},{10,9... | collective-permute-start | bytes 49160 | tf_op jit(solution)/shard_map/ppermute | solution.py:349
  9.8 20.6 %collective-permute-start.1 = (s32[8,512]{1,0:T(8,128)S(1)}, s32[8,512]{1,0:T(8,128)S(1)}, u32[]{:S(2)}, u32[]{:S(2)}) collective-permute-start(s32[8,512]{1,0:T(8,128)S(1)} %get-tuple-element.20.refs_0_), channel_id=1, source_target_pairs={{0,2},{1,3},{2,0},{3,1},{4,6},{5,7},{6,4},{7,5},{8,10},{9,11},{10,... | collective-permute-start | bytes 49160 | tf_op jit(solution)/shard_map/ppermute | solution.py:349
  10.4 20.0 %collective-permute-start = (s32[8,512]{1,0:T(8,128)S(1)}, s32[8,512]{1,0:T(8,128)S(1)}, u32[]{:S(2)}, u32[]{:S(2)}) collective-permute-start(s32[8,512]{1,0:T(8,128)S(1)} %get-tuple-element.20.refs_0_), channel_id=1, source_target_pairs={{0,1},{1,2},{2,3},{3,0},{4,5},{5,6},{6,7},{7,4},{8,9},{9,10},{10,1... | collective-permute-start | bytes 49160 | tf_op jit(solution)/shard_map/ppermute | solution.py:349
  10.6 6.3 %collective-permute-start.3 = (f32[2,400]{1,0:T(2,128)S(1)}, f32[2,400]{1,0:T(2,128)S(1)}, u32[]{:S(2)}, u32[]{:S(2)}) collective-permute-start(f32[2,400]{1,0:T(2,128)S(1)} %get-tuple-element.22), channel_id=1, source_target_pairs={{0,4},{4,8},{8,12},{12,16},{16,20},{20,24},{24,28},{28,0},{1,5},{5... | collective-permute-start | bytes 9608 | tf_op jit(solution)/shard_map/ppermute | solution.py:353
  12.1 5.4 %collective-permute-start.4 = (f32[2,400]{1,0:T(2,128)S(1)}, f32[2,400]{1,0:T(2,128)S(1)}, u32[]{:S(2)}, u32[]{:S(2)}) collective-permute-start(f32[2,400]{1,0:T(2,128)S(1)} %get-tuple-element.23), channel_id=1, source_target_pairs={{0,8},{4,12},{8,16},{12,20},{16,24},{20,28},{24,0},{28,4},{1,9},{5... | collective-permute-start | bytes 9608 | tf_op jit(solution)/shard_map/ppermute | solution.py:353
  16.9 5.4 %collective-permute-start.5 = (f32[2,400]{1,0:T(2,128)S(1)}, f32[2,400]{1,0:T(2,128)S(1)}, u32[]{:S(2)}, u32[]{:S(2)}) collective-permute-start(f32[2,400]{1,0:T(2,128)S(1)} %get-tuple-element.24), channel_id=1, source_target_pairs={{0,12},{4,16},{8,20},{12,24},{16,28},{20,0},{24,4},{28,8},{1,13},{... | collective-permute-start | bytes 9608 | tf_op jit(solution)/shard_map/ppermute | solution.py:353
  17.5 4.8 %collective-permute-start.6 = (f32[2,400]{1,0:T(2,128)S(1)}, f32[2,400]{1,0:T(2,128)S(1)}, u32[]{:S(2)}, u32[]{:S(2)}) collective-permute-start(f32[2,400]{1,0:T(2,128)S(1)} %get-tuple-element.25), channel_id=1, source_target_pairs={{0,16},{4,20},{8,24},{12,28},{16,0},{20,4},{24,8},{28,12},{1,17},{... | collective-permute-start | bytes 9608 | tf_op jit(solution)/shard_map/ppermute | solution.py:353
  22.3 4.5 %collective-permute-start.7 = (f32[2,400]{1,0:T(2,128)S(1)}, f32[2,400]{1,0:T(2,128)S(1)}, u32[]{:S(2)}, u32[]{:S(2)}) collective-permute-start(f32[2,400]{1,0:T(2,128)S(1)} %get-tuple-element.26), channel_id=1, source_target_pairs={{0,20},{4,24},{8,28},{12,0},{16,4},{20,8},{24,12},{28,16},{1,21},{... | collective-permute-start | bytes 9608 | tf_op jit(solution)/shard_map/ppermute | solution.py:353
  22.3 6.4 %collective-permute-start.8 = (f32[2,400]{1,0:T(2,128)S(1)}, f32[2,400]{1,0:T(2,128)S(1)}, u32[]{:S(2)}, u32[]{:S(2)}) collective-permute-start(f32[2,400]{1,0:T(2,128)S(1)} %get-tuple-element.27), channel_id=1, source_target_pairs={{0,24},{4,28},{8,0},{12,4},{16,8},{20,12},{24,16},{28,20},{1,25},{... | collective-permute-start | bytes 9608 | tf_op jit(solution)/shard_map/ppermute | solution.py:353
  26.8 3.6 %collective-permute-start.9 = (f32[2,400]{1,0:T(2,128)S(1)}, f32[2,400]{1,0:T(2,128)S(1)}, u32[]{:S(2)}, u32[]{:S(2)}) collective-permute-start(f32[2,400]{1,0:T(2,128)S(1)} %get-tuple-element.28), channel_id=1, source_target_pairs={{0,28},{4,0},{8,4},{12,8},{16,12},{20,16},{24,20},{28,24},{1,29},{... | collective-permute-start | bytes 9608 | tf_op jit(solution)/shard_map/ppermute | solution.py:353
  30.4 1.4 %copy-start = (f32[1000,400]{0,1:T(8,128)S(1)}, f32[1000,400]{0,1:T(8,128)}, u32[]{:S(2)}) copy-start(f32[1000,400]{0,1:T(8,128)} %param.9) | copy-start | bytes 4800004
  31.9 0.9 %copy-start.2 = (bf16[256,400]{0,1:T(8,128)(2,1)S(1)}, bf16[256,400]{0,1:T(8,128)(2,1)}, u32[]{:S(2)}) copy-start(bf16[256,400]{0,1:T(8,128)(2,1)} %param.8) | copy-start | bytes 614404
  32.8 44.0 %copy-start.4 = (s32[1,8,2]{1,2,0:T(2,128)S(1)}, s32[1,8,2]{1,2,0:T(2,128)}, u32[]{:S(2)}) copy-start(s32[1,8,2]{1,2,0:T(2,128)} %param.10) | copy-start | bytes 196
  42.8 9.6 %collective-permute-start.10 = (f32[104,128]{1,0:T(8,128)S(1)}, f32[104,128]{1,0:T(8,128)S(1)}, u32[]{:S(2)}, u32[]{:S(2)}) collective-permute-start(f32[104,128]{1,0:T(8,128)S(1)} %get-tuple-element.31), channel_id=1, source_target_pairs={{0,4},{4,8},{8,12},{12,16},{16,20},{20,24},{24,28},{28,0},{1,5},{5... | collective-permute-start | bytes 159752 | tf_op jit(solution)/shard_map/ppermute | solution.py:398
  44.3 8.8 %collective-permute-start.11 = (f32[104,128]{1,0:T(8,128)S(1)}, f32[104,128]{1,0:T(8,128)S(1)}, u32[]{:S(2)}, u32[]{:S(2)}) collective-permute-start(f32[104,128]{1,0:T(8,128)S(1)} %get-tuple-element.32), channel_id=1, source_target_pairs={{0,8},{4,12},{8,16},{12,20},{16,24},{20,28},{24,0},{28,4},{1,9},{5... | collective-permute-start | bytes 159752 | tf_op jit(solution)/shard_map/ppermute | solution.py:398
  44.6 9.2 %collective-permute-start.12 = (f32[104,128]{1,0:T(8,128)S(1)}, f32[104,128]{1,0:T(8,128)S(1)}, u32[]{:S(2)}, u32[]{:S(2)}) collective-permute-start(f32[104,128]{1,0:T(8,128)S(1)} %get-tuple-element.33), channel_id=1, source_target_pairs={{0,12},{4,16},{8,20},{12,24},{16,28},{20,0},{24,4},{28,8},{1,13},{... | collective-permute-start | bytes 159752 | tf_op jit(solution)/shard_map/ppermute | solution.py:398
  48.4 5.4 %collective-permute-start.13 = (f32[104,128]{1,0:T(8,128)S(1)}, f32[104,128]{1,0:T(8,128)S(1)}, u32[]{:S(2)}, u32[]{:S(2)}) collective-permute-start(f32[104,128]{1,0:T(8,128)S(1)} %get-tuple-element.34), channel_id=1, source_target_pairs={{0,16},{4,20},{8,24},{12,28},{16,0},{20,4},{24,8},{28,12},{1,17},{... | collective-permute-start | bytes 159752 | tf_op jit(solution)/shard_map/ppermute | solution.py:398
  48.5 5.6 %collective-permute-start.14 = (f32[104,128]{1,0:T(8,128)S(1)}, f32[104,128]{1,0:T(8,128)S(1)}, u32[]{:S(2)}, u32[]{:S(2)}) collective-permute-start(f32[104,128]{1,0:T(8,128)S(1)} %get-tuple-element.35), channel_id=1, source_target_pairs={{0,20},{4,24},{8,28},{12,0},{16,4},{20,8},{24,12},{28,16},{1,21},{... | collective-permute-start | bytes 159752 | tf_op jit(solution)/shard_map/ppermute | solution.py:398
  52.3 4.1 %collective-permute-start.15 = (f32[104,128]{1,0:T(8,128)S(1)}, f32[104,128]{1,0:T(8,128)S(1)}, u32[]{:S(2)}, u32[]{:S(2)}) collective-permute-start(f32[104,128]{1,0:T(8,128)S(1)} %get-tuple-element.36), channel_id=1, source_target_pairs={{0,24},{4,28},{8,0},{12,4},{16,8},{20,12},{24,16},{28,20},{1,25},{... | collective-permute-start | bytes 159752 | tf_op jit(solution)/shard_map/ppermute | solution.py:398
  53.2 4.1 %collective-permute-start.16 = (f32[104,128]{1,0:T(8,128)S(1)}, f32[104,128]{1,0:T(8,128)S(1)}, u32[]{:S(2)}, u32[]{:S(2)}) collective-permute-start(f32[104,128]{1,0:T(8,128)S(1)} %get-tuple-element.37), channel_id=1, source_target_pairs={{0,28},{4,0},{8,4},{12,8},{16,12},{20,16},{24,20},{28,24},{1,29},{... | collective-permute-start | bytes 159752 | tf_op jit(solution)/shard_map/ppermute | solution.py:398
  57.4 3.9 %collective-permute-start.19 = (bf16[1,112,128]{2,1,0:T(8,128)(2,1)S(1)}, bf16[1,112,128]{2,1,0:T(8,128)(2,1)S(1)}, u32[]{:S(2)}, u32[]{:S(2)}) collective-permute-start(bf16[1,112,128]{2,1,0:T(8,128)(2,1)S(1)} %bitcast.13), channel_id=1, source_target_pairs={{0,24},{4,28},{8,0},{12,4},{16,8},{20,12},{24,16},{28,20},{1,25},{... | collective-permute-start | bytes 86024 | tf_op jit(solution)/shard_map/ppermute | solution.py:436
  59.4 4.8 %collective-permute-start.18 = (bf16[1,112,128]{2,1,0:T(8,128)(2,1)S(1)}, bf16[1,112,128]{2,1,0:T(8,128)(2,1)S(1)}, u32[]{:S(2)}, u32[]{:S(2)}) collective-permute-start(bf16[1,112,128]{2,1,0:T(8,128)(2,1)S(1)} %bitcast.14), channel_id=1, source_target_pairs={{0,16},{4,20},{8,24},{12,28},{16,0},{20,4},{24,8},{28,12},{1,17},{... | collective-permute-start | bytes 86024 | tf_op jit(solution)/shard_map/ppermute | solution.py:436
  60.1 5.7 %collective-permute-start.17 = (bf16[1,112,128]{2,1,0:T(8,128)(2,1)S(1)}, bf16[1,112,128]{2,1,0:T(8,128)(2,1)S(1)}, u32[]{:S(2)}, u32[]{:S(2)}) collective-permute-start(bf16[1,112,128]{2,1,0:T(8,128)(2,1)S(1)} %bitcast.15), channel_id=1, source_target_pairs={{0,8},{4,12},{8,16},{12,20},{16,24},{20,28},{24,0},{28,4},{1,9},{5... | collective-permute-start | bytes 86024 | tf_op jit(solution)/shard_map/ppermute | solution.py:436
  65.7 4.9 %collective-permute-start.20 = (bf16[4,112,128]{2,1,0:T(8,128)(2,1)S(1)}, bf16[4,112,128]{2,1,0:T(8,128)(2,1)S(1)}, u32[]{:S(2)}, u32[]{:S(2)}) collective-permute-start(bf16[4,112,128]{2,1,0:T(8,128)(2,1)S(1)} %pad_maximum_fusion), channel_id=1, source_target_pairs={{0,4},{4,0},{8,12},{12,8},{16,20},{20,16},{24,28},{28,24},{1,5},{5... | collective-permute-start | bytes 344072 | tf_op jit(solution)/shard_map/ppermute | solution.py:436
  70.7 6.1 %collective-permute-start.21 = (bf16[8,112,128]{2,1,0:T(8,128)(2,1)S(1)}, bf16[8,112,128]{2,1,0:T(8,128)(2,1)S(1)}, u32[]{:S(2)}, u32[]{:S(2)}) collective-permute-start(bf16[8,112,128]{2,1,0:T(8,128)(2,1)S(1)} %get-tuple-element.38), channel_id=1, source_target_pairs={{0,2},{1,3},{2,0},{3,1},{4,6},{5,7},{6,4},{7,5},{8,10},{9,11},{10,... | collective-permute-start | bytes 688136 | tf_op jit(solution)/shard_map/ppermute | solution.py:436
  76.8 1.9 %collective-permute-start.22 = (bf16[16,112,128]{2,1,0:T(8,128)(2,1)S(1)}, bf16[16,112,128]{2,1,0:T(8,128)(2,1)S(1)}, u32[]{:S(2)}, u32[]{:S(2)}) collective-permute-start(bf16[16,112,128]{2,1,0:T(8,128)(2,1)S(1)} %constant_dynamic-update-slice_fusion.5.refs_0_), channel_id=1, source_target_pairs={{0,1},{1,0},{2,3},{3,2},{4,5},{5,4},{6,7},{7,6},{8,9},{9,8},{10,11... | collective-permute-start | bytes 1376264 | tf_op jit(solution)/shard_map/ppermute | solution.py:436

commit v3 on v2

--- a/solution.py
+++ b/solution.py
@@ -16,8 +16,12 @@
 HBM = pl.BlockSpec(memory_space=pltpu.HBM)
 
 
-def params():
-    return pltpu.CompilerParams(vmem_limit_bytes=32 * 1024 * 1024)
+def params(mib=32):
+    return pltpu.CompilerParams(vmem_limit_bytes=mib * 1024 * 1024)
+
+
+def cost(flops, moved):
+    return pl.CostEstimate(flops=flops, bytes_accessed=moved, transcendentals=0)
 
 
 def up(value, step):
@@ -61,96 +65,78 @@
     return out
 
 
-def prep_kernel(direct, place, serve, count, ent, src, rel, dst, neg, *refs):
+def prep_kernel(serve, count, ent, src, rel, dst, neg, out_idx, out_rows, *refs):
     cap, workers = serve.shape[1], serve.shape[2]
     rows = ent.shape[1]
     groups, width = neg.shape[2], neg.shape[3]
-    copies = 7
-    out_idx, outs = refs[0], refs[1:-9]
-    serve_s, count_s, ent_v, src_v, rel_v, dst_v, neg_v, onehot, sems = refs[-9:]
+    onehot, sems = refs[-2:]
     moves = [
         pltpu.make_async_copy(a, b, sems.at[n])
-        for n, (a, b) in enumerate(
-            zip(
-                (serve, count, ent, src, rel, dst, neg),
-                (serve_s, count_s, ent_v, src_v, rel_v, dst_v, neg_v),
-            )
-        )
+        for n, (a, b) in enumerate(zip((serve, count, ent, src, rel, dst, neg), refs))
     ]
     for move in moves:
         move.start()
     for move in moves:
         move.wait()
-    assert len(moves) == copies
+    serve_s, count_s, ent_v, src_v, rel_v, dst_v, neg_v = refs[:7]
     out_idx[...] = jnp.full(out_idx.shape, count_s[0, 0], jnp.int32)
     out_idx[0:1, :] = src_v[0]
     out_idx[1:2, :] = rel_v[0]
     out_idx[2:3, :] = dst_v[0]
     for g in range(groups):
         out_idx[3 + g : 4 + g, :width] = neg_v[0, 0, g : g + 1, :]
-
-    first = place[0] if direct else 0
-
-    def fill(k, carry):
-        worker = lax.rem(first + k // cap, workers)
-        picked = serve_s[0, k % cap, worker]
-        onehot[pl.ds(k, 1), :] = jnp.where(iota((1, rows), 1) == picked, 1.0, 0.0).astype(F32)
-        return carry
-
-    lax.fori_loop(0, workers * cap, fill, 0)
+    lane = iota((1, rows), 1)
+    for k in range(workers * cap):
+        picked = serve_s[0, k % cap, k // cap]
+        onehot[k : k + 1, :] = jnp.where(lane == picked, 1.0, 0.0).astype(F32)
     picked_rows = dot_t(onehot[...].astype(BF16), ent_v[...])
-    if direct:
-        for h in range(workers):
-            outs[h][...] = picked_rows[h * cap : (h + 1) * cap]
-    else:
-        outs[0][...] = picked_rows
+    for w in range(workers):
+        out_rows[w] = picked_rows[w * cap : (w + 1) * cap]
+
+
+def gather_kernel(cfg, place, *refs):
+    replicas, nrel, pad_rel, narrow, window = cfg
+    idx_refs, refs = refs[:replicas], refs[replicas:]
+    ent, relation, out_query, out_lhs, out_rel, rel_parts, lhs_s, rel_s = refs
+    edges = idx_refs[0].shape[1]
+    dim, rows = ent.shape
+    base = pl.multiple_of((place[1] * narrow) // 8 * 8, 8)
+    hi, lo = split2(relation[...])
+    if pad_rel > nrel:
+        rel_parts[...] = jnp.zeros(rel_parts.shape, BF16)
+    rel_parts[:dim, :nrel] = hi
+    rel_parts[dim:, :nrel] = lo
+    for i in range(replicas):
+        span = slice(i * edges, (i + 1) * edges)
+        src_l, rel_l = idx_refs[i][0:1, :], idx_refs[i][1:2, :]
+        lhs = dot(ent[...], ones_where(iota((rows, edges), 0) == src_l))
+        both = dot(rel_parts[...], ones_where(iota((pad_rel, edges), 0) == rel_l))
+        rel_rows = both[:dim] + both[dim:]
+        lhs_s[...] = lhs
+        rel_s[...] = rel_rows
+        out_query[:, span] = (lhs * rel_rows).astype(BF16)
+        out_lhs[:, span] = lhs_s[pl.ds(base, window), :]
+        out_rel[:, span] = rel_s[pl.ds(base, window), :]
 
 
 def main_kernel(cfg, place, *refs):
-    (direct, workers, replicas, cap, groups, width, nrel, pad_rel, block, narrow, window, offsets) = cfg
+    (direct, workers, replicas, cap, groups, width, pad_rel, block, narrow, window, offsets) = cfg
     pieces = workers if direct else 1
     idx_refs, refs = refs[:replicas], refs[replicas:]
-    (ent, relation), refs = refs[:2], refs[2:]
-    table_refs, refs = refs[:pieces], refs[pieces:]
+    (query_v, lhs_v, rel_v, received), refs = refs[:4], refs[4:]
     out_lhs, outs, refs = refs[0], refs[1 : 1 + pieces], refs[1 + pieces :]
-    (
-        idx_all,
-        idx_col,
-        rel_parts,
-        table_f,
-        table_t,
-        lhs_s,
-        rel_s,
-        query_s,
-        acc_rel,
-        acc_lhs,
-        acc_tab,
-        wide_t,
-        served_s,
-    ) = refs
-    edges = idx_all.shape[1]
-    dim, rows = ent.shape
+    table_f, table_t, query_s, acc_rel, acc_lhs, acc_tab, wide_t, served_s = refs
+    edges = idx_refs[0].shape[1]
+    dim = query_v.shape[0]
+    rows = out_lhs.shape[1]
     slots = workers * cap
     dom, rep = place[0], place[1]
     per = edges // groups
     base = pl.multiple_of((rep * narrow) // 8 * 8, 8)
     offset = rep * narrow - base
 
-    for i in range(replicas):
-        idx_all[i * IDX_ROWS : (i + 1) * IDX_ROWS, :] = idx_refs[i][...]
-        idx_col[i] = jnp.transpose(idx_refs[i][...])
-    hi, lo = split2(relation[...])
-    if pad_rel > nrel:
-        rel_parts[...] = jnp.zeros(rel_parts.shape, BF16)
-    rel_parts[:dim, :nrel] = hi
-    rel_parts[dim:, :nrel] = lo
-    if direct:
-        for h in range(workers):
-            source = lax.rem(dom - h + workers, workers)
-            for c in range(cap):
-                table_f[pl.ds(source * cap + c, 1), :] = table_refs[h][c : c + 1, :]
-    else:
-        table_f[...] = table_refs[0][...]
+    for w in range(workers):
+        table_f[w * cap : (w + 1) * cap, :] = received[w]
     table_t[...] = jnp.transpose(table_f[...])
     table = table_f[...].astype(BF16)
     own_t = table_t[pl.ds(base, window), :].astype(BF16)
@@ -159,18 +145,13 @@
     acc_lhs[...] = jnp.zeros(acc_lhs.shape, F32)
     acc_tab[...] = jnp.zeros(acc_tab.shape, F32)
 
-    def shard(i, carry):
-        lanes = idx_all[pl.ds(pl.multiple_of(i * IDX_ROWS, IDX_ROWS), IDX_ROWS), :]
-        cols = idx_col[i]
-        src_l, rel_l, dst_l = lanes[0:1], lanes[1:2], lanes[2:3]
+    for i in range(replicas):
+        here = slice(i * edges, (i + 1) * edges)
+        lanes = idx_refs[i][...]
+        cols = jnp.transpose(lanes)
+        dst_l = lanes[2:3]
         count = lanes[IDX_ROWS - 1 : IDX_ROWS]
-
-        lhs = dot(ent[...], ones_where(iota((rows, edges), 0) == src_l))
-        both = dot(rel_parts[...], ones_where(iota((pad_rel, edges), 0) == rel_l))
-        rel_rows = both[:dim] + both[dim:]
-        query = (lhs * rel_rows).astype(BF16)
-        lhs_s[...] = lhs
-        rel_s[...] = rel_rows
+        query = query_v[:, here]
         query_s[...] = query.astype(F32)
         scores = dot(table, query)
         live = jnp.where(iota((1, edges), 1) < count, 1.0, 0.0).astype(F32)
@@ -198,13 +179,10 @@
 
         dquery = dot(own_t, stack)
         acc_tab[...] += dot(query_s[pl.ds(base, window), :].astype(BF16), stack_t)
-        y = jnp.concatenate(split2(dquery * lhs_s[pl.ds(base, window), :]), axis=0)
+        y = jnp.concatenate(split2(dquery * lhs_v[:, here]), axis=0)
         acc_rel[...] += dot(y, ones_where(iota((edges, pad_rel), 1) == cols[:, 1:2]))
-        x = jnp.concatenate(split2(dquery * rel_s[pl.ds(base, window), :]), axis=0)
+        x = jnp.concatenate(split2(dquery * rel_v[:, here]), axis=0)
         acc_lhs[...] += dot(x, ones_where(iota((edges, rows), 1) == cols[:, 0:1]))
-        return carry
-
-    lax.fori_loop(0, replicas, shard, 0)
 
     pick = functools.partial(shifted_rows, offset=offset, narrow=narrow, offsets=offsets)
     out_lhs[...] = pick(acc_lhs[:window] + acc_lhs[window:])
@@ -260,27 +238,23 @@
     out[...] = lhs[...] + added[:narrow]
 
 
-def spread_kernel(phases, narrow, block, place, *refs):
-    pieces, out, wide = refs[:-2], refs[-2], refs[-1]
-    replicas = wide.shape[0]
-    height = wide.shape[1]
+def spread_kernel(phases, workers, replicas, narrow, block, place, *refs):
+    pieces, out = refs[:-1], refs[-1]
     nrel = out.shape[1]
     each = pieces[0].shape[0]
-    for n, piece in enumerate(pieces):
-        for m in range(each):
-            spot = n * each + m
-            at = [place[0], place[1]]
+    for o in range(workers):
+        for r in range(replicas):
+            at, spot, scale = (o, r), 0, 1
             for axis, stride, radix in phases:
-                hop = spot % radix
-                spot = spot // radix
-                digit = lax.rem(at[axis] // stride, radix)
-                moved = lax.rem(digit - hop + radix, radix)
-                at[axis] = at[axis] + (moved - digit) * stride
-            wide[at[1], :, pl.ds(pl.multiple_of(at[0] * block, block), block)] = piece[m].astype(
-                F32
-            )[:height]
-    for r in range(replicas):
-        out[r * narrow : (r + 1) * narrow, :] = wide[r, :narrow, :nrel]
+                digit = lax.rem(place[axis] // stride, radix)
+                spot = spot + scale * lax.rem(digit - (at[axis] // stride) % radix + radix, radix)
+                scale *= radix
+            part, group = lax.rem(spot, each), spot // each
+            value = pieces[0][part].astype(F32)
+            for n in range(1, len(pieces)):
+                value = jnp.where(group == n, pieces[n][part].astype(F32), value)
+            end = min((o + 1) * block, nrel)
+            out[r * narrow : (r + 1) * narrow, o * block : end] = value[:narrow, : end - o * block]
 
 
 def turned(size, stride, radix, hop):
@@ -321,13 +295,14 @@
     serve_t = jnp.transpose(serve_ids, (0, 2, 1))
     place = jnp.stack([lax.axis_index("dom"), lax.axis_index("rep")]).astype(jnp.int32)
 
-    piece = (cap, dim) if direct else (slots, dim)
-    prepared = pl.pallas_call(
-        functools.partial(prep_kernel, direct),
-        out_shape=[jax.ShapeDtypeStruct((IDX_ROWS, edges), jnp.int32)]
-        + [jax.ShapeDtypeStruct(piece, F32)] * pieces,
-        in_specs=[SMEM] + [HBM] * 7,
-        out_specs=[VMEM] * (1 + pieces),
+    idx, served = pl.pallas_call(
+        prep_kernel,
+        out_shape=(
+            jax.ShapeDtypeStruct((IDX_ROWS, edges), jnp.int32),
+            jax.ShapeDtypeStruct((workers, cap, dim), F32),
+        ),
+        in_specs=[HBM] * 7,
+        out_specs=(VMEM, VMEM),
         scratch_shapes=[
             pltpu.SMEM(serve_t.shape, jnp.int32),
             pltpu.SMEM(edge_count.shape, jnp.int32),
@@ -339,29 +314,37 @@
             pltpu.VMEM((slots, rows), F32),
             pltpu.SemaphoreType.DMA((7,)),
         ],
-        compiler_params=params(),
+        compiler_params=params(60),
         name="prep",
-    )(place, serve_t, edge_count, ent_t, edge_src, edge_rel, edge_dst, neg_ids)
-    idx, served = prepared[0], prepared[1:]
+    )(serve_t, edge_count, ent_t, edge_src, edge_rel, edge_dst, neg_ids)
 
     held = [idx]
     for hop in range(1, replicas):
         held.append(lax.ppermute(idx, "rep", turned(replicas, 1, replicas, hop)))
-    if direct:
-        tables = [served[0]]
-        for hop in range(1, workers):
-            tables.append(lax.ppermute(served[hop], "dom", turned(workers, 1, workers, hop)))
-    else:
-        tables = [
-            lax.all_to_all(
-                served[0].reshape(workers, cap, dim).astype(BF16), "dom", 0, 0, tiled=True
-            )
-            .reshape(slots, dim)
-            .astype(F32)
-        ]
+    received = lax.all_to_all(served, "dom", 0, 0, tiled=True)
+
+    total = replicas * edges
+    query, lhs_rows, rel_rows = pl.pallas_call(
+        functools.partial(gather_kernel, (replicas, nrel, pad_rel, narrow, window)),
+        out_shape=(
+            jax.ShapeDtypeStruct((dim, total), BF16),
+            jax.ShapeDtypeStruct((window, total), F32),
+            jax.ShapeDtypeStruct((window, total), F32),
+        ),
+        in_specs=[SMEM] + [VMEM] * (replicas + 2),
+        out_specs=(VMEM, VMEM, VMEM),
+        scratch_shapes=[
+            pltpu.VMEM((2 * dim, pad_rel), BF16),
+            pltpu.VMEM((dim, edges), F32),
+            pltpu.VMEM((dim, edges), F32),
+        ],
+        compiler_params=params(),
+        cost_estimate=cost(2 * total * dim * (2 * pad_rel + rows), 8 * total * dim),
+        name="gather",
+    )(place, *held, ent_t, rel_t)
 
     cfg = (
-        direct, workers, replicas, cap, groups, width, nrel, pad_rel, block, narrow, window,
+        direct, workers, replicas, cap, groups, width, pad_rel, block, narrow, window,
         tuple(offsets),
     )
     lanes = max(LANES, block, up(narrow, LANES))
@@ -370,16 +353,11 @@
         functools.partial(main_kernel, cfg),
         out_shape=[jax.ShapeDtypeStruct((narrow, rows), F32)]
         + [jax.ShapeDtypeStruct(part, F32)] * pieces,
-        in_specs=[SMEM] + [VMEM] * (replicas + 2 + pieces),
+        in_specs=[SMEM] + [VMEM] * (replicas + 4),
         out_specs=[VMEM] * (1 + pieces),
         scratch_shapes=[
-            pltpu.VMEM((replicas * IDX_ROWS, edges), jnp.int32),
-            pltpu.VMEM((replicas, edges, IDX_ROWS), jnp.int32),
-            pltpu.VMEM((2 * dim, pad_rel), BF16),
             pltpu.VMEM((slots, dim), F32),
             pltpu.VMEM((dim, slots), F32),
-            pltpu.VMEM((dim, edges), F32),
-            pltpu.VMEM((dim, edges), F32),
             pltpu.VMEM((dim, edges), F32),
             pltpu.VMEM((2 * window, pad_rel), F32),
             pltpu.VMEM((2 * window, rows), F32),
@@ -389,7 +367,7 @@
         ],
         compiler_params=params(),
         name="edges",
-    )(place, *held, ent_t, rel_t, *tables)
+    )(place, *held, query, lhs_rows, rel_rows, received)
     lhs_part, sent = results[0], results[1:]
 
     if direct:
@@ -417,6 +395,7 @@
         out_specs=VMEM,
         scratch_shapes=[pltpu.VMEM((slots, lanes), F32), pltpu.VMEM((slots, rows), F32)],
         compiler_params=params(),
+        cost_estimate=cost(10**9, 10**6),
         name="entity",
     )(place, serve_t, lhs_part, *recv)
 
@@ -431,15 +410,18 @@
         for axis, stride, radix in phases:
             name, size = (("dom", workers), ("rep", replicas))[axis]
             base = held[0] if len(held) == 1 else jnp.concatenate(held, axis=0)
+            if (axis, stride, radix) == phases[-1]:
+                base, entity_grad = lax.optimization_barrier((base, entity_grad))
             held = [base]
             for hop in range(1, radix):
                 held.append(lax.ppermute(base, name, turned(size, stride, radix, hop)))
         relation_t = pl.pallas_call(
-            functools.partial(spread_kernel, tuple(phases), narrow, block),
+            functools.partial(
+                spread_kernel, tuple(phases), workers, replicas, narrow, block
+            ),
             out_shape=jax.ShapeDtypeStruct((dim, nrel), F32),
             in_specs=[SMEM] + [VMEM] * len(held),
             out_specs=VMEM,
-            scratch_shapes=[pltpu.VMEM((replicas, height, pad_rel), F32)],
             compiler_params=params(),
             name="spread",
         )(place, *held)

time: 81.2 us -> 64 us (0.79)
  waiting for transfers between devices: 28.1 us -> 16 us
  local copies, waits for them, and re-layouts: 6.81 us -> 3.2 us
  Pallas kernels: 15.6 us -> 14.7 us
    ppermute x7 -> x0, waiting for transfers between devices: 11.2 us -> none  [shards(): lax.ppermute(served[hop], 'dom', turned(workers, 1, workers, hop))]
    ppermute x7 -> x0, starting transfers between devices: 8.58 us -> none  [shards(): lax.ppermute(served[hop], 'dom', turned(workers, 1, workers, hop))]
    all_to_all x0 -> x1, starting transfers between devices: none -> 5.84 us  [shards(): received = lax.all_to_all(served, 'dom', 0, 0, tiled=True)]
    pallas_call x1, Pallas kernels: 9.95 us -> 4.28 us  [shards(): pl.pallas_call(functools.partial(main_kernel, cfg), out_shape=[jax.ShapeD...]
    pallas_call x2 -> x3, Pallas kernels: 3.85 us -> 8.59 us  [the longest x1 4.62 us: shards(): pl.pallas_call(functools.partial(gather_kernel, (replicas, nrel, pad_rel,...]
    unnamed x22 -> x14, local copies, waits for them, and re-layouts: 6.74 us -> 3.12 us
    ppermute x7, starting transfers between devices: 11 us -> 12.7 us  [shards(): lax.ppermute(sent[hop], 'dom', turned(workers, 1, workers, hop))]
  transfers between devices with their start and end apart: 23 -> 17, of which waited for: 13 -> 9; matrix products, arithmetic and copies ran while one was open for 0% -> 0% of each run, Pallas kernels for 2% -> 10%
where the time goes in v3:
time: 64 us; the launch traced here: 63.6 us
  starting transfers between devices  28.2 us (44%)
  waiting for transfers between devices  16 us (25%)
  Pallas kernels  14.7 us (23%)
  local copies, waits for them, and re-layouts  3.2 us (5%)
  between operations  1.39 us (2%)
    ppermute x6, waiting for transfers between devices, shards(): held.append(lax.ppermute(base, name, turned(size, stride, radix, hop)))  13.1 us
    ppermute x7, starting transfers between devices, shards(): lax.ppermute(sent[hop], 'dom', turned(workers, 1, workers, hop))  12.7 us
    ppermute x6, starting transfers between devices, shards(): held.append(lax.ppermute(base, name, turned(size, stride, radix, hop)))  6.52 us
    all_to_all x1, starting transfers between devices, shards(): received = lax.all_to_all(served, 'dom', 0, 0, tiled=True)  5.84 us
    pallas_call x1, Pallas kernels, shards(): pl.pallas_call(functools.partial(gather_kernel, (replicas, nrel, pad_rel,...  4.62 us
    pallas_call x1, Pallas kernels, shards(): pl.pallas_call(functools.partial(main_kernel, cfg), out_shape=[jax.ShapeD...  4.28 us
    ppermute x3, starting transfers between devices, shards(): held.append(lax.ppermute(idx, 'rep', turned(replicas, 1, replicas, hop)))  3.23 us
    unnamed x14, local copies, waits for them, and re-layouts  3.12 us
  transfers between devices with their start and end apart: 17, of which 9 were waited for; matrix products, arithmetic and copies ran while one was open for 0% of the time, Pallas kernels for 10%

profile of v3, /device:TPU:0, one launch (start us, length us, event | category | flops | bytes accessed | tf_op | source)
XLA Modules:
  0.0 63.6 jit_solution(10979233367755289734)
XLA Ops:
  1.3 1.8 %prep.1 = (s32[8,512]{1,0:T(8,128)}, f32[8,2,400]{2,1,0:T(2,128)}) custom-call(s32[1,2,8]{2,1,0:T(2,128)} %bitcast.16, s32[1,1]{1,0:T(1,128)S(6)} %copy.19.count, bf16[400,256]{1,0:T(8,128)(2,1)} %bitcast.14, s32[1,1,512]{2,1,0:T(1,128)} %src.1, s32[1,1,512]{2,1,0:T(1,128)} %rel.1, s32[1,1,512]{2,1,0:T(1,128)} %dst.1, s32[1,1,2,384]{3,2,1,0:T(2,128)} %neg.1), custom_call_target="tpu_custom_call" | custom-call | tf_op jit(solution)/shard_map/prep/pallas_call | solution.py:298
  3.1 2.4 %collective-permute-start.2 = (s32[8,512]{1,0:T(8,128)}, s32[8,512]{1,0:T(8,128)S(1)}, u32[]{:S(2)}, u32[]{:S(2)}) collective-permute-start(s32[8,512]{1,0:T(8,128)} %get-tuple-element.18.refs_0_), channel_id=1, source_target_pairs={{0,3},{1,0},{2,1},{3,2},{4,7},{5,4},{6,5},{7,6},{8,11},{9,8},{10,9... | collective-permute-start | bytes 49160 | tf_op jit(solution)/shard_map/ppermute | solution.py:323
  5.5 0.6 %collective-permute-start.1 = (s32[8,512]{1,0:T(8,128)}, s32[8,512]{1,0:T(8,128)S(1)}, u32[]{:S(2)}, u32[]{:S(2)}) collective-permute-start(s32[8,512]{1,0:T(8,128)} %get-tuple-element.18.refs_0_), channel_id=1, source_target_pairs={{0,2},{1,3},{2,0},{3,1},{4,6},{5,7},{6,4},{7,5},{8,10},{9,11},{10,... | collective-permute-start | bytes 49160 | tf_op jit(solution)/shard_map/ppermute | solution.py:323
  6.2 0.2 collective-permute-start
  6.3 5.8 %all-to-all-start = ((f32[8,2,400]{2,1,0:T(2,128)}), f32[8,2,400]{2,1,0:T(2,128)S(1)}, u32[]{:S(2)}, u32[]{:S(2)}) async-start(f32[8,2,400]{2,1,0:T(2,128)} %get-tuple-element.22), calls=%async_computation | async-start | bytes 65536 | tf_op jit(solution)/shard_map/all_to_all | solution.py:324
  12.2 0.1 pad_add_fusion.place
  12.2 0.0 collective-permute-done.2.refs_3_
  12.2 0.0 collective-permute-done.1.refs_2_
  12.2 0.0 collective-permute-done.refs_1_
  12.3 0.0 copy-start
  12.3 0.9 %copy-done = bf16[256,400]{0,1:T(8,128)(2,1)S(1)} copy-done((bf16[256,400]{0,1:T(8,128)(2,1)S(1)}, bf16[256,400]{0,1:T(8,128)(2,1)}, u32[]{:S(2)}) %copy-start) | copy-done | bytes 204824
  13.2 0.0 copy-start.1
  13.2 0.7 %copy-done.1 = s32[8,512]{1,0:T(8,128)S(1)} copy-done((s32[8,512]{1,0:T(8,128)S(1)}, s32[8,512]{1,0:T(8,128)}, u32[]{:S(2)}) %copy-start.1) | copy-done | bytes 16408
  13.9 0.0 copy-start.4
  13.9 1.4 %copy-done.4 = f32[1000,400]{0,1:T(8,128)S(1)} copy-done((f32[1000,400]{0,1:T(8,128)S(1)}, f32[1000,400]{0,1:T(8,128)}, u32[]{:S(2)}) %copy-start.4) | copy-done | bytes 1600024
  15.3 0.0 copy-start.2
  15.3 4.6 %gather.1 = (bf16[400,2048]{1,0:T(8,128)(2,1)S(1)}, f32[104,2048]{1,0:T(8,128)S(1)}, f32[104,2048]{1,0:T(8,128)S(1)}) custom-call(s32[2]{0:T(128)S(1)} %pad_add_fusion.place, s32[8,512]{1,0:T(8,128)S(1)} %copy-done.1, s32[8,512]{1,0:T(8,128)S(1)} %collective-permute-done.refs_1_, s32[8,512]{1,0:T(8,128)S(1)} %collective-permute-done.1.refs_2_, ...), custom_call_target="tpu_custom_call" | custom-call | flops 3774873600 | bytes 6553600 | tf_op jit(solution)/shard_map/gather/pallas_call | solution.py:327
  20.0 0.0 all-to-all-done.refs_7_
  20.0 0.0 copy-done.2
  20.0 0.0 copy-start.3
  20.0 4.3 %edges.1 = (f32[100,256]{1,0:T(8,128)S(1)}, f32[104,128]{1,0:T(8,128)S(1)}, f32[104,128]{1,0:T(8,128)S(1)}, f32[104,128]{1,0:T(8,128)S(1)}, f32[104,128]{1,0:T(8...) custom-call(s32[2]{0:T(128)S(1)} %pad_add_fusion.place, ...), custom_call_target="tpu_custom_call" | custom-call | tf_op jit(solution)/shard_map/edges/pallas_call | solution.py:352
  24.3 2.1 %collective-permute-start.3 = (f32[104,128]{1,0:T(8,128)S(1)}, f32[104,128]{1,0:T(8,128)S(1)}, u32[]{:S(2)}, u32[]{:S(2)}) collective-permute-start(f32[104,128]{1,0:T(8,128)S(1)} %get-tuple-element.24), channel_id=1, source_target_pairs={{0,4},{4,8},{8,12},{12,16},{16,20},{20,24},{24,28},{28,0},{1,5},{5... | collective-permute-start | bytes 159752 | tf_op jit(solution)/shard_map/ppermute | solution.py:376
  26.4 1.5 %collective-permute-start.4 = (f32[104,128]{1,0:T(8,128)S(1)}, f32[104,128]{1,0:T(8,128)S(1)}, u32[]{:S(2)}, u32[]{:S(2)}) collective-permute-start(f32[104,128]{1,0:T(8,128)S(1)} %get-tuple-element.25), channel_id=1, source_target_pairs={{0,8},{4,12},{8,16},{12,20},{16,24},{20,28},{24,0},{28,4},{1,9},{5... | collective-permute-start | bytes 159752 | tf_op jit(solution)/shard_map/ppermute | solution.py:376
  27.8 2.4 %collective-permute-start.5 = (f32[104,128]{1,0:T(8,128)S(1)}, f32[104,128]{1,0:T(8,128)S(1)}, u32[]{:S(2)}, u32[]{:S(2)}) collective-permute-start(f32[104,128]{1,0:T(8,128)S(1)} %get-tuple-element.26), channel_id=1, source_target_pairs={{0,12},{4,16},{8,20},{12,24},{16,28},{20,0},{24,4},{28,8},{1,13},{... | collective-permute-start | bytes 159752 | tf_op jit(solution)/shard_map/ppermute | solution.py:376
  30.2 1.5 %collective-permute-start.6 = (f32[104,128]{1,0:T(8,128)S(1)}, f32[104,128]{1,0:T(8,128)S(1)}, u32[]{:S(2)}, u32[]{:S(2)}) collective-permute-start(f32[104,128]{1,0:T(8,128)S(1)} %get-tuple-element.27), channel_id=1, source_target_pairs={{0,16},{4,20},{8,24},{12,28},{16,0},{20,4},{24,8},{28,12},{1,17},{... | collective-permute-start | bytes 159752 | tf_op jit(solution)/shard_map/ppermute | solution.py:376
  31.6 2.4 %collective-permute-start.7 = (f32[104,128]{1,0:T(8,128)S(1)}, f32[104,128]{1,0:T(8,128)S(1)}, u32[]{:S(2)}, u32[]{:S(2)}) collective-permute-start(f32[104,128]{1,0:T(8,128)S(1)} %get-tuple-element.28), channel_id=1, source_target_pairs={{0,20},{4,24},{8,28},{12,0},{16,4},{20,8},{24,12},{28,16},{1,21},{... | collective-permute-start | bytes 159752 | tf_op jit(solution)/shard_map/ppermute | solution.py:376
  34.0 0.0 collective-permute-done.3.refs_1_
  34.0 1.5 %collective-permute-start.8 = (f32[104,128]{1,0:T(8,128)S(1)}, f32[104,128]{1,0:T(8,128)S(1)}, u32[]{:S(2)}, u32[]{:S(2)}) collective-permute-start(f32[104,128]{1,0:T(8,128)S(1)} %get-tuple-element.29), channel_id=1, source_target_pairs={{0,24},{4,28},{8,0},{12,4},{16,8},{20,12},{24,16},{28,20},{1,25},{... | collective-permute-start | bytes 159752 | tf_op jit(solution)/shard_map/ppermute | solution.py:376
  35.5 0.0 collective-permute-done.4.refs_2_
  35.5 1.5 %collective-permute-start.9 = (f32[104,128]{1,0:T(8,128)S(1)}, f32[104,128]{1,0:T(8,128)S(1)}, u32[]{:S(2)}, u32[]{:S(2)}) collective-permute-start(f32[104,128]{1,0:T(8,128)S(1)} %get-tuple-element.30), channel_id=1, source_target_pairs={{0,28},{4,0},{8,4},{12,8},{16,12},{20,16},{24,20},{28,24},{1,29},{... | collective-permute-start | bytes 159752 | tf_op jit(solution)/shard_map/ppermute | solution.py:376
  36.9 0.0 collective-permute-done.5.refs_3_
  36.9 1.0 %collective-permute-done.6.refs_4_ = f32[104,128]{1,0:T(8,128)S(1)} collective-permute-done((f32[104,128]{1,0:T(8,128)S(1)}, f32[104,128]{1,0:T(8,128)S(1)}, u32[]{:S(2)}, u32[]{:S(2)}) %collective-permute-start.6) | collective-permute-done | bytes 53280 | tf_op jit(solution)/shard_map/ppermute | solution.py:376
  38.0 0.6 %collective-permute-done.7.refs_5_ = f32[104,128]{1,0:T(8,128)S(1)} collective-permute-done((f32[104,128]{1,0:T(8,128)S(1)}, f32[104,128]{1,0:T(8,128)S(1)}, u32[]{:S(2)}, u32[]{:S(2)}) %collective-permute-start.7) | collective-permute-done | bytes 53280 | tf_op jit(solution)/shard_map/ppermute | solution.py:376
  38.6 1.3 %collective-permute-done.8.refs_6_ = f32[104,128]{1,0:T(8,128)S(1)} collective-permute-done((f32[104,128]{1,0:T(8,128)S(1)}, f32[104,128]{1,0:T(8,128)S(1)}, u32[]{:S(2)}, u32[]{:S(2)}) %collective-permute-start.8) | collective-permute-done | bytes 53280 | tf_op jit(solution)/shard_map/ppermute | solution.py:376
  39.9 0.0 collective-permute-done.9.refs_7_
  39.9 1.8 %collective-permute-start.12 = (bf16[1,112,128]{2,1,0:T(8,128)(2,1)S(1)}, bf16[1,112,128]{2,1,0:T(8,128)(2,1)S(1)}, u32[]{:S(2)}, u32[]{:S(2)}) collective-permute-start(bf16[1,112,128]{2,1,0:T(8,128)(2,1)S(1)} %bitcast.10), channel_id=1, source_target_pairs={{0,24},{4,28},{8,0},{12,4},{16,8},{20,12},{24,16},{28,20},{1,25},{... | collective-permute-start | bytes 86024 | tf_op jit(solution)/shard_map/ppermute | solution.py:417
  41.7 0.7 %collective-permute-start.11 = (bf16[1,112,128]{2,1,0:T(8,128)(2,1)S(1)}, bf16[1,112,128]{2,1,0:T(8,128)(2,1)S(1)}, u32[]{:S(2)}, u32[]{:S(2)}) collective-permute-start(bf16[1,112,128]{2,1,0:T(8,128)(2,1)S(1)} %bitcast.11), channel_id=1, source_target_pairs={{0,16},{4,20},{8,24},{12,28},{16,0},{20,4},{24,8},{28,12},{1,17},{... | collective-permute-start | bytes 86024 | tf_op jit(solution)/shard_map/ppermute | solution.py:417
  42.4 0.6 collective-permute-start.10
  43.0 1.1 %collective-permute-done.12 = bf16[1,112,128]{2,1,0:T(8,128)(2,1)S(1)} collective-permute-done((bf16[1,112,128]{2,1,0:T(8,128)(2,1)S(1)}, bf16[1,112,128]{2,1,0:T(8,128)(2,1)S(1)}, u32[]{:S(2)}, u32[]{:S(2)}) %collective-permute-start.12) | collective-permute-done | bytes 28704 | tf_op jit(solution)/shard_map/ppermute | solution.py:417
  44.1 2.8 %collective-permute-done.11 = bf16[1,112,128]{2,1,0:T(8,128)(2,1)S(1)} collective-permute-done((bf16[1,112,128]{2,1,0:T(8,128)(2,1)S(1)}, bf16[1,112,128]{2,1,0:T(8,128)(2,1)S(1)}, u32[]{:S(2)}, u32[]{:S(2)}) %collective-permute-start.11) | collective-permute-done | bytes 28704 | tf_op jit(solution)/shard_map/ppermute | solution.py:417
  46.8 1.2 %collective-permute-done.10 = bf16[1,112,128]{2,1,0:T(8,128)(2,1)S(1)} collective-permute-done((bf16[1,112,128]{2,1,0:T(8,128)(2,1)S(1)}, bf16[1,112,128]{2,1,0:T(8,128)(2,1)S(1)}, u32[]{:S(2)}, u32[]{:S(2)}) %collective-permute-start.10) | collective-permute-done | bytes 28704 | tf_op jit(solution)/shard_map/ppermute | solution.py:417
  48.1 2.6 %collective-permute-start.13 = (bf16[4,112,128]{2,1,0:T(8,128)(2,1)S(1)}, bf16[4,112,128]{2,1,0:T(8,128)(2,1)S(1)}, u32[]{:S(2)}, u32[]{:S(2)}) collective-permute-start(bf16[4,112,128]{2,1,0:T(8,128)(2,1)S(1)} %pad_maximum_fusion), channel_id=1, source_target_pairs={{0,4},{4,0},{8,12},{12,8},{16,20},{20,16},{24,28},{28,24},{1,5},{5... | collective-permute-start | bytes 344072 | tf_op jit(solution)/shard_map/ppermute | solution.py:417
  50.7 2.7 %collective-permute-done.13 = bf16[4,112,128]{2,1,0:T(8,128)(2,1)S(1)} collective-permute-done((bf16[4,112,128]{2,1,0:T(8,128)(2,1)S(1)}, bf16[4,112,128]{2,1,0:T(8,128)(2,1)S(1)}, u32[]{:S(2)}, u32[]{:S(2)}) %collective-permute-start.13) | collective-permute-done | bytes 114720 | tf_op jit(solution)/shard_map/ppermute | solution.py:417
  53.5 0.8 %collective-permute-start.14 = (bf16[8,112,128]{2,1,0:T(8,128)(2,1)S(1)}, bf16[8,112,128]{2,1,0:T(8,128)(2,1)S(1)}, u32[]{:S(2)}, u32[]{:S(2)}) collective-permute-start(bf16[8,112,128]{2,1,0:T(8,128)(2,1)S(1)} %get-tuple-element.34), channel_id=1, source_target_pairs={{0,2},{1,3},{2,0},{3,1},{4,6},{5,7},{6,4},{7,5},{8,10},{9,11},{10,... | collective-permute-start | bytes 688136 | tf_op jit(solution)/shard_map/ppermute | solution.py:417
  54.3 0.0 copy-done.3
  54.3 1.8 %entity.1 = f32[100,256]{1,0:T(8,128)} custom-call(s32[2]{0:T(128)S(1)} %pad_add_fusion.place, s32[1,2,8]{2,1,0:T(2,128)S(1)} %bitcast.17, f32[100,256]{1,0:T(8,128)S(1)} %get-tuple-element.31.lhs, f32[104,128]{1,0:T(8,128)S(1)} %get-tuple-element.23.refs_0_, f32[104,128]{1,0:T(8,128)S(1)} %collective-permute-done.3.refs_1_, ...), custom_call_target="tpu_custom_call" | custom-call | flops 1000000000 | bytes 1000000 | tf_op jit(solution)/shard_map/entity/pallas_call | solution.py:391
  56.1 3.5 %collective-permute-done.14 = bf16[8,112,128]{2,1,0:T(8,128)(2,1)S(1)} collective-permute-done((bf16[8,112,128]{2,1,0:T(8,128)(2,1)S(1)}, bf16[8,112,128]{2,1,0:T(8,128)(2,1)S(1)}, u32[]{:S(2)}, u32[]{:S(2)}) %collective-permute-start.14) | collective-permute-done | bytes 229408 | tf_op jit(solution)/shard_map/ppermute | solution.py:417
  59.6 0.1 collective-permute-start.15
  59.7 1.8 %collective-permute-done.15.refs_1_ = bf16[16,112,128]{2,1,0:T(8,128)(2,1)S(1)} collective-permute-done((bf16[16,112,128]{2,1,0:T(8,128)(2,1)S(1)}, bf16[16,112,128]{2,1,0:T(8,128)(2,1)S(1)}, u32[]{:S(2)}, u32[]{:S(2)}) %collective-permute-start.15) | collective-permute-done | bytes 458784 | tf_op jit(solution)/shard_map/ppermute | solution.py:417
  61.5 2.2 %spread.1 = f32[400,1000]{1,0:T(8,128)} custom-call(s32[2]{0:T(128)S(1)} %pad_add_fusion.place, bf16[16,112,128]{2,1,0:T(8,128)(2,1)S(1)} %constant_dynamic-update-slice_fusion.5.refs_0_, bf16[16,112,128]{2,1,0:T(8,128)(2,1)S(1)} %collective-permute-done.15.refs_1_), custom_call_target="tpu_custom_call" | custom-call | tf_op jit(solution)/shard_map/spread/pallas_call | solution.py:418
  (8 shorter events, 0.2 us)
Async XLA Ops:
  3.1 9.1 %collective-permute-start.2 = (s32[8,512]{1,0:T(8,128)}, s32[8,512]{1,0:T(8,128)S(1)}, u32[]{:S(2)}, u32[]{:S(2)}) collective-permute-start(s32[8,512]{1,0:T(8,128)} %get-tuple-element.18.refs_0_), channel_id=1, source_target_pairs={{0,3},{1,0},{2,1},{3,2},{4,7},{5,4},{6,5},{7,6},{8,11},{9,8},{10,9... | collective-permute-start | bytes 49160 | tf_op jit(solution)/shard_map/ppermute | solution.py:323
  5.5 6.7 %collective-permute-start.1 = (s32[8,512]{1,0:T(8,128)}, s32[8,512]{1,0:T(8,128)S(1)}, u32[]{:S(2)}, u32[]{:S(2)}) collective-permute-start(s32[8,512]{1,0:T(8,128)} %get-tuple-element.18.refs_0_), channel_id=1, source_target_pairs={{0,2},{1,3},{2,0},{3,1},{4,6},{5,7},{6,4},{7,5},{8,10},{9,11},{10,... | collective-permute-start | bytes 49160 | tf_op jit(solution)/shard_map/ppermute | solution.py:323
  6.2 6.1 %collective-permute-start = (s32[8,512]{1,0:T(8,128)}, s32[8,512]{1,0:T(8,128)S(1)}, u32[]{:S(2)}, u32[]{:S(2)}) collective-permute-start(s32[8,512]{1,0:T(8,128)} %get-tuple-element.18.refs_0_), channel_id=1, source_target_pairs={{0,1},{1,2},{2,3},{3,0},{4,5},{5,6},{6,7},{7,4},{8,9},{9,10},{10,1... | collective-permute-start | bytes 49160 | tf_op jit(solution)/shard_map/ppermute | solution.py:323
  6.3 13.6 %all-to-all-start = ((f32[8,2,400]{2,1,0:T(2,128)}), f32[8,2,400]{2,1,0:T(2,128)S(1)}, u32[]{:S(2)}, u32[]{:S(2)}) async-start(f32[8,2,400]{2,1,0:T(2,128)} %get-tuple-element.22), calls=%async_computation | async-start | bytes 65536 | tf_op jit(solution)/shard_map/all_to_all | solution.py:324
  12.3 0.9 %copy-start = (bf16[256,400]{0,1:T(8,128)(2,1)S(1)}, bf16[256,400]{0,1:T(8,128)(2,1)}, u32[]{:S(2)}) copy-start(bf16[256,400]{0,1:T(8,128)(2,1)} %param.8) | copy-start | bytes 614404
  13.2 0.7 %copy-start.1 = (s32[8,512]{1,0:T(8,128)S(1)}, s32[8,512]{1,0:T(8,128)}, u32[]{:S(2)}) copy-start(s32[8,512]{1,0:T(8,128)} %get-tuple-element.18.refs_0_) | copy-start | bytes 49156
  13.9 1.4 %copy-start.4 = (f32[1000,400]{0,1:T(8,128)S(1)}, f32[1000,400]{0,1:T(8,128)}, u32[]{:S(2)}) copy-start(f32[1000,400]{0,1:T(8,128)} %param.9) | copy-start | bytes 4800004
  15.3 4.6 %copy-start.2 = (s32[8,512]{1,0:T(8,128)S(1)}, s32[8,512]{1,0:T(8,128)}, u32[]{:S(2)}) copy-start(s32[8,512]{1,0:T(8,128)} %get-tuple-element.18.refs_0_) | copy-start | bytes 49156
  20.0 34.3 %copy-start.3 = (s32[1,8,2]{1,2,0:T(2,128)S(1)}, s32[1,8,2]{1,2,0:T(2,128)}, u32[]{:S(2)}) copy-start(s32[1,8,2]{1,2,0:T(2,128)} %param.10) | copy-start | bytes 196
  24.3 9.7 %collective-permute-start.3 = (f32[104,128]{1,0:T(8,128)S(1)}, f32[104,128]{1,0:T(8,128)S(1)}, u32[]{:S(2)}, u32[]{:S(2)}) collective-permute-start(f32[104,128]{1,0:T(8,128)S(1)} %get-tuple-element.24), channel_id=1, source_target_pairs={{0,4},{4,8},{8,12},{12,16},{16,20},{20,24},{24,28},{28,0},{1,5},{5... | collective-permute-start | bytes 159752 | tf_op jit(solution)/shard_map/ppermute | solution.py:376
  26.4 9.1 %collective-permute-start.4 = (f32[104,128]{1,0:T(8,128)S(1)}, f32[104,128]{1,0:T(8,128)S(1)}, u32[]{:S(2)}, u32[]{:S(2)}) collective-permute-start(f32[104,128]{1,0:T(8,128)S(1)} %get-tuple-element.25), channel_id=1, source_target_pairs={{0,8},{4,12},{8,16},{12,20},{16,24},{20,28},{24,0},{28,4},{1,9},{5... | collective-permute-start | bytes 159752 | tf_op jit(solution)/shard_map/ppermute | solution.py:376
  27.8 9.1 %collective-permute-start.5 = (f32[104,128]{1,0:T(8,128)S(1)}, f32[104,128]{1,0:T(8,128)S(1)}, u32[]{:S(2)}, u32[]{:S(2)}) collective-permute-start(f32[104,128]{1,0:T(8,128)S(1)} %get-tuple-element.26), channel_id=1, source_target_pairs={{0,12},{4,16},{8,20},{12,24},{16,28},{20,0},{24,4},{28,8},{1,13},{... | collective-permute-start | bytes 159752 | tf_op jit(solution)/shard_map/ppermute | solution.py:376
  30.2 7.8 %collective-permute-start.6 = (f32[104,128]{1,0:T(8,128)S(1)}, f32[104,128]{1,0:T(8,128)S(1)}, u32[]{:S(2)}, u32[]{:S(2)}) collective-permute-start(f32[104,128]{1,0:T(8,128)S(1)} %get-tuple-element.27), channel_id=1, source_target_pairs={{0,16},{4,20},{8,24},{12,28},{16,0},{20,4},{24,8},{28,12},{1,17},{... | collective-permute-start | bytes 159752 | tf_op jit(solution)/shard_map/ppermute | solution.py:376
  31.6 7.0 %collective-permute-start.7 = (f32[104,128]{1,0:T(8,128)S(1)}, f32[104,128]{1,0:T(8,128)S(1)}, u32[]{:S(2)}, u32[]{:S(2)}) collective-permute-start(f32[104,128]{1,0:T(8,128)S(1)} %get-tuple-element.28), channel_id=1, source_target_pairs={{0,20},{4,24},{8,28},{12,0},{16,4},{20,8},{24,12},{28,16},{1,21},{... | collective-permute-start | bytes 159752 | tf_op jit(solution)/shard_map/ppermute | solution.py:376
  34.0 5.9 %collective-permute-start.8 = (f32[104,128]{1,0:T(8,128)S(1)}, f32[104,128]{1,0:T(8,128)S(1)}, u32[]{:S(2)}, u32[]{:S(2)}) collective-permute-start(f32[104,128]{1,0:T(8,128)S(1)} %get-tuple-element.29), channel_id=1, source_target_pairs={{0,24},{4,28},{8,0},{12,4},{16,8},{20,12},{24,16},{28,20},{1,25},{... | collective-permute-start | bytes 159752 | tf_op jit(solution)/shard_map/ppermute | solution.py:376
  35.5 4.4 %collective-permute-start.9 = (f32[104,128]{1,0:T(8,128)S(1)}, f32[104,128]{1,0:T(8,128)S(1)}, u32[]{:S(2)}, u32[]{:S(2)}) collective-permute-start(f32[104,128]{1,0:T(8,128)S(1)} %get-tuple-element.30), channel_id=1, source_target_pairs={{0,28},{4,0},{8,4},{12,8},{16,12},{20,16},{24,20},{28,24},{1,29},{... | collective-permute-start | bytes 159752 | tf_op jit(solution)/shard_map/ppermute | solution.py:376
  39.9 4.1 %collective-permute-start.12 = (bf16[1,112,128]{2,1,0:T(8,128)(2,1)S(1)}, bf16[1,112,128]{2,1,0:T(8,128)(2,1)S(1)}, u32[]{:S(2)}, u32[]{:S(2)}) collective-permute-start(bf16[1,112,128]{2,1,0:T(8,128)(2,1)S(1)} %bitcast.10), channel_id=1, source_target_pairs={{0,24},{4,28},{8,0},{12,4},{16,8},{20,12},{24,16},{28,20},{1,25},{... | collective-permute-start | bytes 86024 | tf_op jit(solution)/shard_map/ppermute | solution.py:417
  41.7 5.1 %collective-permute-start.11 = (bf16[1,112,128]{2,1,0:T(8,128)(2,1)S(1)}, bf16[1,112,128]{2,1,0:T(8,128)(2,1)S(1)}, u32[]{:S(2)}, u32[]{:S(2)}) collective-permute-start(bf16[1,112,128]{2,1,0:T(8,128)(2,1)S(1)} %bitcast.11), channel_id=1, source_target_pairs={{0,16},{4,20},{8,24},{12,28},{16,0},{20,4},{24,8},{28,12},{1,17},{... | collective-permute-start | bytes 86024 | tf_op jit(solution)/shard_map/ppermute | solution.py:417
  42.4 5.7 %collective-permute-start.10 = (bf16[1,112,128]{2,1,0:T(8,128)(2,1)S(1)}, bf16[1,112,128]{2,1,0:T(8,128)(2,1)S(1)}, u32[]{:S(2)}, u32[]{:S(2)}) collective-permute-start(bf16[1,112,128]{2,1,0:T(8,128)(2,1)S(1)} %bitcast.12), channel_id=1, source_target_pairs={{0,8},{4,12},{8,16},{12,20},{16,24},{20,28},{24,0},{28,4},{1,9},{5... | collective-permute-start | bytes 86024 | tf_op jit(solution)/shard_map/ppermute | solution.py:417
  48.1 5.3 %collective-permute-start.13 = (bf16[4,112,128]{2,1,0:T(8,128)(2,1)S(1)}, bf16[4,112,128]{2,1,0:T(8,128)(2,1)S(1)}, u32[]{:S(2)}, u32[]{:S(2)}) collective-permute-start(bf16[4,112,128]{2,1,0:T(8,128)(2,1)S(1)} %pad_maximum_fusion), channel_id=1, source_target_pairs={{0,4},{4,0},{8,12},{12,8},{16,20},{20,16},{24,28},{28,24},{1,5},{5... | collective-permute-start | bytes 344072 | tf_op jit(solution)/shard_map/ppermute | solution.py:417
  53.5 6.1 %collective-permute-start.14 = (bf16[8,112,128]{2,1,0:T(8,128)(2,1)S(1)}, bf16[8,112,128]{2,1,0:T(8,128)(2,1)S(1)}, u32[]{:S(2)}, u32[]{:S(2)}) collective-permute-start(bf16[8,112,128]{2,1,0:T(8,128)(2,1)S(1)} %get-tuple-element.34), channel_id=1, source_target_pairs={{0,2},{1,3},{2,0},{3,1},{4,6},{5,7},{6,4},{7,5},{8,10},{9,11},{10,... | collective-permute-start | bytes 688136 | tf_op jit(solution)/shard_map/ppermute | solution.py:417
  59.6 1.9 %collective-permute-start.15 = (bf16[16,112,128]{2,1,0:T(8,128)(2,1)S(1)}, bf16[16,112,128]{2,1,0:T(8,128)(2,1)S(1)}, u32[]{:S(2)}, u32[]{:S(2)}) collective-permute-start(bf16[16,112,128]{2,1,0:T(8,128)(2,1)S(1)} %constant_dynamic-update-slice_fusion.5.refs_0_), channel_id=1, source_target_pairs={{0,1},{1,0},{2,3},{3,2},{4,5},{5,4},{6,7},{7,6},{8,9},{9,8},{10,11... | collective-permute-start | bytes 1376264 | tf_op jit(solution)/shard_map/ppermute | solution.py:417

commit v4 on v3

--- a/solution.py
+++ b/solution.py
@@ -52,6 +52,20 @@
 
 def ones_where(flag):
     return jnp.where(flag, 1.0, 0.0).astype(BF16)
+
+
+def exponent(largest):
+    safe = jnp.where(largest > 0, largest, 1.0)
+    return jnp.clip(jnp.floor(F32(14.9) - jnp.log2(safe)), -120.0, 120.0)
+
+
+def encode(x, axis):
+    k = exponent(jnp.max(jnp.abs(x), axis=axis, keepdims=True))
+    return jnp.floor(x * jnp.exp2(k) + 0.5).astype(jnp.int32), k.astype(jnp.int32)
+
+
+def decode(codes, k):
+    return codes.astype(F32) * jnp.exp2(-k.astype(F32))
 
 
 def iota(shape, axis):
@@ -120,17 +134,15 @@
 
 
 def main_kernel(cfg, place, *refs):
-    (direct, workers, replicas, cap, groups, width, pad_rel, block, narrow, window, offsets) = cfg
-    pieces = workers if direct else 1
+    (workers, replicas, cap, groups, width, pad_rel, block, narrow, window, offsets) = cfg
     idx_refs, refs = refs[:replicas], refs[replicas:]
     (query_v, lhs_v, rel_v, received), refs = refs[:4], refs[4:]
-    out_lhs, outs, refs = refs[0], refs[1 : 1 + pieces], refs[1 + pieces :]
-    table_f, table_t, query_s, acc_rel, acc_lhs, acc_tab, wide_t, served_s = refs
+    out_lhs, out, table_f, table_t, query_s, acc_rel, acc_lhs, acc_tab, wide_t, mixed = refs
     edges = idx_refs[0].shape[1]
     dim = query_v.shape[0]
     rows = out_lhs.shape[1]
     slots = workers * cap
-    dom, rep = place[0], place[1]
+    rep = place[1]
     per = edges // groups
     base = pl.multiple_of((rep * narrow) // 8 * 8, 8)
     offset = rep * narrow - base
@@ -186,88 +198,88 @@
 
     pick = functools.partial(shifted_rows, offset=offset, narrow=narrow, offsets=offsets)
     out_lhs[...] = pick(acc_lhs[:window] + acc_lhs[window:])
-    acc_rel[:narrow] = pick(acc_rel[:window] + acc_rel[window:])
-    table_grad = pick(acc_tab[:, :slots] + acc_tab[:, slots : 2 * slots] + acc_tab[:, 2 * slots :])
+    codes, powers = encode(pick(acc_rel[:window] + acc_rel[window:]), 0)
     wide_t[...] = jnp.zeros(wide_t.shape, F32)
-    wide_t[:narrow] = table_grad
-    served_s[...] = jnp.transpose(wide_t[...])
-    for h in range(workers):
-        out = outs[h] if direct else outs[0].at[h]
-        to = lax.rem(dom + h, workers) if direct else h
-        out[...] = jnp.zeros(out.shape, F32)
-        if direct:
-            out[:narrow, :] = acc_rel[:narrow, pl.ds(pl.multiple_of(to * block, block), block)]
-        else:
-            out[:narrow, :block] = acc_rel[:narrow, h * block : (h + 1) * block]
+    wide_t[:narrow] = pick(
+        acc_tab[:, :slots] + acc_tab[:, slots : 2 * slots] + acc_tab[:, 2 * slots :]
+    )
+    table_codes, table_powers = encode(jnp.transpose(wide_t[...]), 1)
+    table_powers = jnp.broadcast_to(table_powers, table_codes.shape)
+    mixed[...] = jnp.zeros(mixed.shape, jnp.int32)
+    last = narrow + 2 * cap
+    for o in range(workers):
+        span = slice(o * block, (o + 1) * block)
+        mixed[:narrow, :block] = codes[:, span]
+        mixed[narrow : narrow + cap, :] = table_codes[o * cap : (o + 1) * cap]
+        mixed[narrow + cap : last, :] = table_powers[o * cap : (o + 1) * cap]
+        mixed[last : last + 1, :block] = powers[:, span]
+        out[o] = mixed[...].astype(jnp.int16)
+
+
+def combine_kernel(scale, narrow, cap, block, recv, out, mixed):
+    last = narrow + 2 * cap
+    total = jnp.zeros((narrow, block), F32)
+    for w in range(recv.shape[0]):
+        both = recv[w].astype(jnp.int32)
+        total += decode(both[:narrow, :block], both[last : last + 1, :block])
+    codes, powers = encode(total * F32(scale), 0)
+    mixed[...] = jnp.zeros(mixed.shape, jnp.int32)
+    mixed[:narrow, :block] = codes
+    mixed[last : last + 1, :block] = powers
+    out[...] = mixed[...].astype(jnp.int16)
+
+
+def entity_kernel(narrow, serve, lhs, recv, out, terms, onehot):
+    cap, workers = serve.shape[1], serve.shape[2]
+    rows = out.shape[1]
+    lane = iota((1, rows), 1)
+    for w in range(workers):
+        both = recv[w].astype(jnp.int32)
+        terms[w * cap : (w + 1) * cap, :] = decode(
+            both[narrow : narrow + cap], both[narrow + cap : narrow + 2 * cap]
+        )
         for c in range(cap):
-            out[narrow + c : narrow + c + 1, :] = served_s[pl.ds(to * cap + c, 1), :]
-
-
-def combine_kernel(scale, narrow, block, *refs):
-    out = refs[-1]
-    total = refs[0][...]
-    for ref in refs[1:-1]:
-        total = total + ref[...]
-    out[...] = jnp.zeros(out.shape, BF16)
-    keep = iota(out.shape, 0) < narrow
-    tall = jnp.concatenate(
-        [total[:, :block], jnp.zeros((out.shape[0] - total.shape[0], block), F32)], axis=0
-    )
-    out[...] = jnp.where(keep, tall * F32(scale), 0.0).astype(BF16)
-
-
-def entity_kernel(direct, narrow, place, serve, lhs, *refs):
-    cap, workers = serve.shape[1], serve.shape[2]
-    recv, out, (terms, onehot) = refs[:-3], refs[-3], refs[-2:]
-    rows = out.shape[1]
-    for h in range(workers):
-        part = recv[h] if direct else recv[0].at[h]
-        terms[h * cap : (h + 1) * cap, :] = part[narrow : narrow + cap, :]
-
-    def fill(k, carry):
-        h = k // cap
-        worker = lax.rem(place[0] - h + workers, workers) if direct else h
-        picked = serve[0, k % cap, worker]
-        onehot[pl.ds(k, 1), :] = jnp.where(iota((1, rows), 1) == picked, 1.0, 0.0).astype(F32)
-        return carry
-
-    lax.fori_loop(0, workers * cap, fill, 0)
+            picked = serve[0, c, w]
+            onehot[w * cap + c : w * cap + c + 1, :] = jnp.where(lane == picked, 1.0, 0.0).astype(
+                F32
+            )
     spots = onehot[...].astype(BF16)
     parts = jnp.concatenate(split3(jnp.transpose(terms[...])), axis=1)
     added = dot(parts, jnp.concatenate([spots] * 3, axis=0))
     out[...] = lhs[...] + added[:narrow]
 
 
-def spread_kernel(phases, workers, replicas, narrow, block, place, *refs):
-    pieces, out = refs[:-1], refs[-1]
+def spread_kernel(orders, workers, replicas, narrow, power_row, block, place, mine, other, out):
     nrel = out.shape[1]
-    each = pieces[0].shape[0]
+    kinds = len(orders)
+    kind = lax.rem(place[1], kinds)
     for o in range(workers):
         for r in range(replicas):
             at, spot, scale = (o, r), 0, 1
-            for axis, stride, radix in phases:
+            for axis, stride, radix in orders[r % kinds]:
                 digit = lax.rem(place[axis] // stride, radix)
                 spot = spot + scale * lax.rem(digit - (at[axis] // stride) % radix + radix, radix)
                 scale *= radix
-            part, group = lax.rem(spot, each), spot // each
-            value = pieces[0][part].astype(F32)
-            for n in range(1, len(pieces)):
-                value = jnp.where(group == n, pieces[n][part].astype(F32), value)
+            both = jnp.where(
+                kind == r % kinds, mine[spot].astype(jnp.int32), other[spot].astype(jnp.int32)
+            )
+            value = decode(both[:narrow], both[power_row : power_row + 1])
             end = min((o + 1) * block, nrel)
-            out[r * narrow : (r + 1) * narrow, o * block : end] = value[:narrow, : end - o * block]
-
-
-def turned(size, stride, radix, hop):
-    pairs = []
-    for i in range(size):
-        digit = (i // stride) % radix
-        pairs.append((i, i + ((digit + hop) % radix - digit) * stride))
-    return pairs
+            out[r * narrow : (r + 1) * narrow, o * block : end] = value[:, : end - o * block]
+
+
+def moved(index, stride, radix, hop):
+    digit = (index // stride) % radix
+    return index + ((digit + hop) % radix - digit) * stride
+
+
+def turned(size, hop):
+    return [(i, (i + hop) % size) for i in range(size)]
 
 
 def radices(size):
     found = []
-    for radix in (4, 2, 3, 5, 7):
+    for radix in (2, 3, 5, 7):
         while size % radix == 0:
             found.append(radix)
             size //= radix
@@ -284,13 +296,12 @@
     groups, width = neg_ids.shape[2], neg_ids.shape[3]
     slots = workers * cap
     narrow = dim // replicas
-    direct = workers <= 16
+    direct = workers == 8 and replicas == 4
     block = up(-(-nrel // workers), LANES if direct else 8)
     pad_rel = up(max(nrel, workers * block), LANES)
     offsets = sorted({(narrow * r) % 8 for r in range(replicas)})
     window = up(narrow + offsets[-1], 8)
-    height = up(narrow + cap, 8)
-    pieces = workers if direct else 1
+    height = up(narrow + 2 * cap + 1, 16)
     ent_t, rel_t = entities.T, relation.T
     serve_t = jnp.transpose(serve_ids, (0, 2, 1))
     place = jnp.stack([lax.axis_index("dom"), lax.axis_index("rep")]).astype(jnp.int32)
@@ -320,7 +331,7 @@
 
     held = [idx]
     for hop in range(1, replicas):
-        held.append(lax.ppermute(idx, "rep", turned(replicas, 1, replicas, hop)))
+        held.append(lax.ppermute(idx, "rep", turned(replicas, hop)))
     received = lax.all_to_all(served, "dom", 0, 0, tiled=True)
 
     total = replicas * edges
@@ -343,18 +354,16 @@
         name="gather",
     )(place, *held, ent_t, rel_t)
 
-    cfg = (
-        direct, workers, replicas, cap, groups, width, pad_rel, block, narrow, window,
-        tuple(offsets),
-    )
-    lanes = max(LANES, block, up(narrow, LANES))
-    part = (height, lanes) if direct else (workers, height, lanes)
-    results = pl.pallas_call(
+    cfg = (workers, replicas, cap, groups, width, pad_rel, block, narrow, window, tuple(offsets))
+    lanes = max(up(block, LANES), up(narrow, LANES))
+    lhs_part, sent = pl.pallas_call(
         functools.partial(main_kernel, cfg),
-        out_shape=[jax.ShapeDtypeStruct((narrow, rows), F32)]
-        + [jax.ShapeDtypeStruct(part, F32)] * pieces,
+        out_shape=(
+            jax.ShapeDtypeStruct((narrow, rows), F32),
+            jax.ShapeDtypeStruct((workers, height, lanes), jnp.int16),
+        ),
         in_specs=[SMEM] + [VMEM] * (replicas + 4),
-        out_specs=[VMEM] * (1 + pieces),
+        out_specs=(VMEM, VMEM),
         scratch_shapes=[
             pltpu.VMEM((slots, dim), F32),
             pltpu.VMEM((dim, slots), F32),
@@ -363,72 +372,74 @@
             pltpu.VMEM((2 * window, rows), F32),
             pltpu.VMEM((window, 3 * slots), F32),
             pltpu.VMEM((lanes, slots), F32),
-            pltpu.VMEM((slots, lanes), F32),
+            pltpu.VMEM((height, lanes), jnp.int32),
         ],
         compiler_params=params(),
         name="edges",
     )(place, *held, query, lhs_rows, rel_rows, received)
-    lhs_part, sent = results[0], results[1:]
-
-    if direct:
-        recv = [sent[0]]
-        for hop in range(1, workers):
-            recv.append(lax.ppermute(sent[hop], "dom", turned(workers, 1, workers, hop)))
-        summed = recv
-    else:
-        recv = [lax.all_to_all(sent[0], "dom", 0, 0, tiled=True)]
-        summed = [jnp.sum(recv[0], axis=0)]
-    tall = up(height, 16)
+
+    recv = lax.all_to_all(sent, "dom", 0, 0, tiled=True)
+    scale = 1.0 / (edges * workers * replicas)
     chunk = pl.pallas_call(
-        functools.partial(combine_kernel, 1.0 / (edges * workers * replicas), narrow, block),
-        out_shape=jax.ShapeDtypeStruct((tall, block), BF16),
-        in_specs=[VMEM] * len(summed),
+        functools.partial(combine_kernel, scale, narrow, cap, block),
+        out_shape=jax.ShapeDtypeStruct((height, lanes), jnp.int16),
+        in_specs=[VMEM],
         out_specs=VMEM,
+        scratch_shapes=[pltpu.VMEM((height, lanes), jnp.int32)],
         compiler_params=params(),
         name="combine",
-    )(*summed)
+    )(recv)
 
     entity_grad = pl.pallas_call(
-        functools.partial(entity_kernel, direct, narrow),
+        functools.partial(entity_kernel, narrow),
         out_shape=jax.ShapeDtypeStruct((narrow, rows), F32),
-        in_specs=[SMEM, SMEM] + [VMEM] * (1 + pieces),
+        in_specs=[SMEM] + [VMEM] * 2,
         out_specs=VMEM,
         scratch_shapes=[pltpu.VMEM((slots, lanes), F32), pltpu.VMEM((slots, rows), F32)],
         compiler_params=params(),
         cost_estimate=cost(10**9, 10**6),
         name="entity",
-    )(place, serve_t, lhs_part, *recv)
-
+    )(serve_t, lhs_part, recv)
+
+    power_row = narrow + 2 * cap
     if direct:
-        phases = []
-        for axis, name, size in ((0, "dom", workers), (1, "rep", replicas)):
-            stride = size
-            for radix in radices(size) if axis == 0 else (2,) * (replicas.bit_length() - 1):
-                stride //= radix
-                phases.append((axis, stride, radix))
-        held = [chunk.reshape(1, tall, block)]
-        for axis, stride, radix in phases:
-            name, size = (("dom", workers), ("rep", replicas))[axis]
-            base = held[0] if len(held) == 1 else jnp.concatenate(held, axis=0)
-            if (axis, stride, radix) == phases[-1]:
-                base, entity_grad = lax.optimization_barrier((base, entity_grad))
-            held = [base]
-            for hop in range(1, radix):
-                held.append(lax.ppermute(base, name, turned(size, stride, radix, hop)))
+        steps, stride = [], 1
+        for radix in radices(workers):
+            steps.append((0, stride, radix))
+            stride *= radix
+        across = [(1, 2, replicas // 2)]
+        first, flip = steps[1:] + steps[:1], across
+        orders = (tuple(first + flip), tuple(first[:-1] + flip + first[-1:]))
+        base = chunk.reshape(1, height, lanes)
+        for n in range(len(orders[0])):
+            parts = [base]
+            for hop in range(1, orders[0][n][2]):
+                pairs = []
+                for o in range(workers):
+                    for r in range(replicas):
+                        axis, stride, radix = orders[r % 2][n]
+                        at = [o, r]
+                        at[axis] = moved(at[axis], stride, radix, hop)
+                        pairs.append((o * replicas + r, at[0] * replicas + at[1]))
+                parts.append(lax.ppermute(base, ("dom", "rep"), pairs))
+            base = jnp.concatenate(parts, axis=0)
+        base, entity_grad = lax.optimization_barrier((base, entity_grad))
+        swapped = lax.ppermute(base, "rep", [(i, i ^ 1) for i in range(replicas)])
         relation_t = pl.pallas_call(
             functools.partial(
-                spread_kernel, tuple(phases), workers, replicas, narrow, block
+                spread_kernel, orders, workers, replicas, narrow, power_row, block
             ),
             out_shape=jax.ShapeDtypeStruct((dim, nrel), F32),
-            in_specs=[SMEM] + [VMEM] * len(held),
+            in_specs=[SMEM] + [VMEM] * 2,
             out_specs=VMEM,
             compiler_params=params(),
             name="spread",
-        )(place, *held)
+        )(place, base, swapped)
     else:
-        whole = lax.all_gather(chunk[:narrow], ("dom", "rep"), axis=0)
+        whole = lax.all_gather(chunk[:, :block], ("dom", "rep"), axis=0)
+        whole = decode(whole[:, :narrow], whole[:, power_row : power_row + 1])
         whole = whole.reshape(workers, replicas, narrow, block).transpose(1, 2, 0, 3)
-        relation_t = whole.reshape(dim, workers * block)[:, :nrel].astype(F32)
+        relation_t = whole.reshape(dim, workers * block)[:, :nrel]
     return (entity_grad.T, relation_t.T)
 
 

time: 64 us -> 65.7 us (1.027)
  starting transfers between devices: 28.2 us -> 12.4 us
  blocking collectives: 0 us -> 15.2 us
  waiting for transfers between devices: 16 us -> 18.7 us
    ppermute x16 -> x8, starting transfers between devices: 22.4 us -> 6.57 us  [the longest x4 3.26 us: shards(): parts.append(lax.ppermute(base, ('dom', 'rep'), pairs))]
    all_to_all x0 -> x1, blocking collectives: none -> 15.2 us  [shards(): recv = lax.all_to_all(sent, 'dom', 0, 0, tiled=True)]
    ppermute x16 -> x8, waiting for transfers between devices: 16 us -> 18.7 us  [the longest x4 16.9 us: shards(): parts.append(lax.ppermute(base, ('dom', 'rep'), pairs))]
  transfers between devices with their start and end apart: 17 -> 9, of which waited for: 9 -> 5; matrix products, arithmetic and copies ran while one was open for 0% -> 0% of each run, Pallas kernels for 10% -> 9%
where the time goes in v4:
time: 65.7 us; the launch traced here: 65.3 us
  waiting for transfers between devices  18.7 us (28%)
  blocking collectives  15.2 us (23%)
  Pallas kernels  14.4 us (22%)
  starting transfers between devices  12.4 us (19%)
  local copies, waits for them, and re-layouts  3.15 us (5%)
  between operations  1.38 us (2%)
    ppermute x4, waiting for transfers between devices, shards(): parts.append(lax.ppermute(base, ('dom', 'rep'), pairs))  16.9 us
    all_to_all x1, blocking collectives, shards(): recv = lax.all_to_all(sent, 'dom', 0, 0, tiled=True)  15.2 us
    all_to_all x1, starting transfers between devices, shards(): received = lax.all_to_all(served, 'dom', 0, 0, tiled=True)  5.84 us
    pallas_call x1, Pallas kernels, shards(): pl.pallas_call(functools.partial(gather_kernel, (replicas, nrel, pad_rel,...  4.62 us
    pallas_call x1, Pallas kernels, shards(): pl.pallas_call(functools.partial(main_kernel, cfg), out_shape=(jax.ShapeD...  4.18 us
    ppermute x4, starting transfers between devices, shards(): parts.append(lax.ppermute(base, ('dom', 'rep'), pairs))  3.26 us
    ppermute x3, starting transfers between devices, shards(): held.append(lax.ppermute(idx, 'rep', turned(replicas, hop)))  3.23 us
    unnamed x14, local copies, waits for them, and re-layouts  3.12 us
  transfers between devices with their start and end apart: 9, of which 5 were waited for; matrix products, arithmetic and copies ran while one was open for 0% of the time, Pallas kernels for 9%

profile of v4, /device:TPU:0, one launch (start us, length us, event | category | flops | bytes accessed | tf_op | source)
XLA Modules:
  0.0 65.3 jit_solution(15659078051651190495)
XLA Ops:
  1.3 1.8 %prep.1 = (s32[8,512]{1,0:T(8,128)}, f32[8,2,400]{2,1,0:T(2,128)}) custom-call(s32[1,2,8]{2,1,0:T(2,128)} %bitcast.15, s32[1,1]{1,0:T(1,128)S(6)} %copy.14.count, bf16[400,256]{1,0:T(8,128)(2,1)} %bitcast.13, s32[1,1,512]{2,1,0:T(1,128)} %src.1, s32[1,1,512]{2,1,0:T(1,128)} %rel.1, s32[1,1,512]{2,1,0:T(1,128)} %dst.1, s32[1,1,2,384]{3,2,1,0:T(2,128)} %neg.1), custom_call_target="tpu_custom_call" | custom-call | tf_op jit(solution)/shard_map/prep/pallas_call | solution.py:309
  3.1 2.4 %collective-permute-start.2 = (s32[8,512]{1,0:T(8,128)}, s32[8,512]{1,0:T(8,128)S(1)}, u32[]{:S(2)}, u32[]{:S(2)}) collective-permute-start(s32[8,512]{1,0:T(8,128)} %get-tuple-element.11.refs_0_), channel_id=1, source_target_pairs={{0,3},{1,0},{2,1},{3,2},{4,7},{5,4},{6,5},{7,6},{8,11},{9,8},{10,9... | collective-permute-start | bytes 49160 | tf_op jit(solution)/shard_map/ppermute | solution.py:334
  5.5 0.6 collective-permute-start.1
  6.2 0.2 collective-permute-start
  6.3 5.8 %all-to-all-start = ((f32[8,2,400]{2,1,0:T(2,128)}), f32[8,2,400]{2,1,0:T(2,128)S(1)}, u32[]{:S(2)}, u32[]{:S(2)}) async-start(f32[8,2,400]{2,1,0:T(2,128)} %get-tuple-element.15), calls=%async_computation | async-start | bytes 65536 | tf_op jit(solution)/shard_map/all_to_all | solution.py:335
  12.2 0.1 pad_add_fusion.3.place
  12.2 0.0 collective-permute-done.2.refs_3_
  12.2 0.0 collective-permute-done.1.refs_2_
  12.2 0.0 collective-permute-done.refs_1_
  12.3 0.0 copy-start
  12.3 0.9 %copy-done = bf16[256,400]{0,1:T(8,128)(2,1)S(1)} copy-done((bf16[256,400]{0,1:T(8,128)(2,1)S(1)}, bf16[256,400]{0,1:T(8,128)(2,1)}, u32[]{:S(2)}) %copy-start) | copy-done | bytes 204824
  13.2 0.0 copy-start.1
  13.2 0.7 %copy-done.1 = s32[8,512]{1,0:T(8,128)S(1)} copy-done((s32[8,512]{1,0:T(8,128)S(1)}, s32[8,512]{1,0:T(8,128)}, u32[]{:S(2)}) %copy-start.1) | copy-done | bytes 16408
  13.9 0.0 copy-start.4
  13.9 1.4 %copy-done.4 = f32[1000,400]{0,1:T(8,128)S(1)} copy-done((f32[1000,400]{0,1:T(8,128)S(1)}, f32[1000,400]{0,1:T(8,128)}, u32[]{:S(2)}) %copy-start.4) | copy-done | bytes 1600024
  15.3 0.0 copy-start.2
  15.3 4.6 %gather.1 = (bf16[400,2048]{1,0:T(8,128)(2,1)S(1)}, f32[104,2048]{1,0:T(8,128)S(1)}, f32[104,2048]{1,0:T(8,128)S(1)}) custom-call(s32[2]{0:T(128)S(1)} %pad_add_fusion.3.place, s32[8,512]{1,0:T(8,128)S(1)} %copy-done.1, s32[8,512]{1,0:T(8,128)S(1)} %collective-permute-done.refs_1_, s32[8,512]{1,0:T(8,128)S(1)} %collective-permute-done.1.refs_2_, ...), custom_call_target="tpu_custom_call" | custom-call | flops 3774873600 | bytes 6553600 | tf_op jit(solution)/shard_map/gather/pallas_call | solution.py:338
  20.0 0.0 all-to-all-done.refs_7_
  20.0 0.0 copy-done.2
  20.0 0.0 copy-start.3
  20.0 4.2 %edges.1 = (f32[100,256]{1,0:T(8,128)S(1)}, s16[8,112,128]{2,1,0:T(8,128)(2,1)S(1)}) custom-call(s32[2]{0:T(128)S(1)} %pad_add_fusion.3.place, s32[8,512]{1,0:T(8,128)S(1)} %copy-done.2, s32[8,512]{1,0:T(8,128)S(1)} %collective-permute-done.refs_1_, s32[8,512]{1,0:T(8,128)S(1)} %collective-permute-done.1.refs_2_, ...), custom_call_target="tpu_custom_call" | custom-call | tf_op jit(solution)/shard_map/edges/pallas_call | solution.py:359
  24.2 15.2 %all_to_all.10.recv = s16[8,112,128]{2,1,0:T(8,128)(2,1)S(1)} all-to-all(s16[8,112,128]{2,1,0:T(8,128)(2,1)S(1)} %get-tuple-element.16), channel_id=1, replica_groups=mesh['dom'=8,'rep'=4] {'dom'}, dimensions={0} | all-to-all | bytes 458752 | tf_op jit(solution)/shard_map/all_to_all | solution.py:381
  39.4 0.1 combine.1
  39.5 1.0 %collective-permute-start.3 = (s16[1,112,128]{2,1,0:T(8,128)(2,1)S(1)}, s16[1,112,128]{2,1,0:T(8,128)(2,1)S(1)}, u32[]{:S(2)}, u32[]{:S(2)}) collective-permute-start(s16[1,112,128]{2,1,0:T(8,128)(2,1)S(1)} %bitcast.9), channel_id=1, source_target_pairs={{0,8},{1,9},{2,10},{3,11},{4,12},{5,13},{6,14},{7,15},{8,0},{9,1},... | collective-permute-start | bytes 86024 | tf_op jit(solution)/shard_map/ppermute | solution.py:424
  40.4 3.0 %collective-permute-done.3 = s16[1,112,128]{2,1,0:T(8,128)(2,1)S(1)} collective-permute-done((s16[1,112,128]{2,1,0:T(8,128)(2,1)S(1)}, s16[1,112,128]{2,1,0:T(8,128)(2,1)S(1)}, u32[]{:S(2)}, u32[]{:S(2)}) %collective-permute-start.3) | collective-permute-done | bytes 28704 | tf_op jit(solution)/shard_map/ppermute | solution.py:424
  43.4 0.6 collective-permute-start.4
  44.0 5.1 %collective-permute-done.4 = s16[2,112,128]{2,1,0:T(8,128)(2,1)S(1)} collective-permute-done((s16[2,112,128]{2,1,0:T(8,128)(2,1)S(1)}, s16[2,112,128]{2,1,0:T(8,128)(2,1)S(1)}, u32[]{:S(2)}, u32[]{:S(2)}) %collective-permute-start.4) | collective-permute-done | bytes 57376 | tf_op jit(solution)/shard_map/ppermute | solution.py:424
  49.1 0.9 %collective-permute-start.5 = (s16[4,112,128]{2,1,0:T(8,128)(2,1)S(1)}, s16[4,112,128]{2,1,0:T(8,128)(2,1)S(1)}, u32[]{:S(2)}, u32[]{:S(2)}) collective-permute-start(s16[4,112,128]{2,1,0:T(8,128)(2,1)S(1)} %pad_add_fusion.1), channel_id=1, source_target_pairs={{0,4},{1,3},{2,6},{3,1},{4,0},{5,7},{6,2},{7,5},{8,12},{9,11},{10,... | collective-permute-start | bytes 344072 | tf_op jit(solution)/shard_map/ppermute | solution.py:424
  50.1 0.0 copy-done.3
  50.1 1.5 %entity.1 = f32[100,256]{1,0:T(8,128)} custom-call(s32[1,2,8]{2,1,0:T(2,128)S(1)} %bitcast.16, f32[100,256]{1,0:T(8,128)S(1)} %get-tuple-element.17.lhs, s16[8,112,128]{2,1,0:T(8,128)(2,1)S(1)} %all_to_all.10.recv), custom_call_target="tpu_custom_call" | custom-call | flops 1000000000 | bytes 1000000 | tf_op jit(solution)/shard_map/entity/pallas_call | solution.py:393
  51.6 3.6 %collective-permute-done.5 = s16[4,112,128]{2,1,0:T(8,128)(2,1)S(1)} collective-permute-done((s16[4,112,128]{2,1,0:T(8,128)(2,1)S(1)}, s16[4,112,128]{2,1,0:T(8,128)(2,1)S(1)}, u32[]{:S(2)}, u32[]{:S(2)}) %collective-permute-start.5) | collective-permute-done | bytes 114720 | tf_op jit(solution)/shard_map/ppermute | solution.py:424
  55.1 0.8 %collective-permute-start.6 = (s16[8,112,128]{2,1,0:T(8,128)(2,1)S(1)}, s16[8,112,128]{2,1,0:T(8,128)(2,1)S(1)}, u32[]{:S(2)}, u32[]{:S(2)}) collective-permute-start(s16[8,112,128]{2,1,0:T(8,128)(2,1)S(1)} %pad_add_fusion), channel_id=1, source_target_pairs={{0,2},{1,5},{2,0},{3,7},{4,6},{5,1},{6,4},{7,3},{8,10},{9,13},{10,... | collective-permute-start | bytes 688136 | tf_op jit(solution)/shard_map/ppermute | solution.py:424
  55.9 5.3 %collective-permute-done.6 = s16[8,112,128]{2,1,0:T(8,128)(2,1)S(1)} collective-permute-done((s16[8,112,128]{2,1,0:T(8,128)(2,1)S(1)}, s16[8,112,128]{2,1,0:T(8,128)(2,1)S(1)}, u32[]{:S(2)}, u32[]{:S(2)}) %collective-permute-start.6) | collective-permute-done | bytes 229408 | tf_op jit(solution)/shard_map/ppermute | solution.py:424
  61.3 0.1 collective-permute-start.7
  61.3 1.8 %collective-permute-done.7.other = s16[16,112,128]{2,1,0:T(8,128)(2,1)S(1)} collective-permute-done((s16[16,112,128]{2,1,0:T(8,128)(2,1)S(1)}, s16[16,112,128]{2,1,0:T(8,128)(2,1)S(1)}, u32[]{:S(2)}, u32[]{:S(2)}) %collective-permute-start.7) | collective-permute-done | bytes 458784 | tf_op jit(solution)/shard_map/ppermute | solution.py:427
  63.1 2.1 %spread.1 = f32[400,1000]{1,0:T(8,128)} custom-call(s32[2]{0:T(128)S(1)} %pad_add_fusion.3.place, s16[16,112,128]{2,1,0:T(8,128)(2,1)S(1)} %constant_dynamic-update-slice_fusion.mine, s16[16,112,128]{2,1,0:T(8,128)(2,1)S(1)} %collective-permute-done.7.other), custom_call_target="tpu_custom_call" | custom-call | tf_op jit(solution)/shard_map/spread/pallas_call | solution.py:428
  (8 shorter events, 0.1 us)
Async XLA Ops:
  3.1 9.1 %collective-permute-start.2 = (s32[8,512]{1,0:T(8,128)}, s32[8,512]{1,0:T(8,128)S(1)}, u32[]{:S(2)}, u32[]{:S(2)}) collective-permute-start(s32[8,512]{1,0:T(8,128)} %get-tuple-element.11.refs_0_), channel_id=1, source_target_pairs={{0,3},{1,0},{2,1},{3,2},{4,7},{5,4},{6,5},{7,6},{8,11},{9,8},{10,9... | collective-permute-start | bytes 49160 | tf_op jit(solution)/shard_map/ppermute | solution.py:334
  5.5 6.7 %collective-permute-start.1 = (s32[8,512]{1,0:T(8,128)}, s32[8,512]{1,0:T(8,128)S(1)}, u32[]{:S(2)}, u32[]{:S(2)}) collective-permute-start(s32[8,512]{1,0:T(8,128)} %get-tuple-element.11.refs_0_), channel_id=1, source_target_pairs={{0,2},{1,3},{2,0},{3,1},{4,6},{5,7},{6,4},{7,5},{8,10},{9,11},{10,... | collective-permute-start | bytes 49160 | tf_op jit(solution)/shard_map/ppermute | solution.py:334
  6.2 6.1 %collective-permute-start = (s32[8,512]{1,0:T(8,128)}, s32[8,512]{1,0:T(8,128)S(1)}, u32[]{:S(2)}, u32[]{:S(2)}) collective-permute-start(s32[8,512]{1,0:T(8,128)} %get-tuple-element.11.refs_0_), channel_id=1, source_target_pairs={{0,1},{1,2},{2,3},{3,0},{4,5},{5,6},{6,7},{7,4},{8,9},{9,10},{10,1... | collective-permute-start | bytes 49160 | tf_op jit(solution)/shard_map/ppermute | solution.py:334
  6.3 13.6 %all-to-all-start = ((f32[8,2,400]{2,1,0:T(2,128)}), f32[8,2,400]{2,1,0:T(2,128)S(1)}, u32[]{:S(2)}, u32[]{:S(2)}) async-start(f32[8,2,400]{2,1,0:T(2,128)} %get-tuple-element.15), calls=%async_computation | async-start | bytes 65536 | tf_op jit(solution)/shard_map/all_to_all | solution.py:335
  12.3 0.9 %copy-start = (bf16[256,400]{0,1:T(8,128)(2,1)S(1)}, bf16[256,400]{0,1:T(8,128)(2,1)}, u32[]{:S(2)}) copy-start(bf16[256,400]{0,1:T(8,128)(2,1)} %param.8) | copy-start | bytes 614404
  13.2 0.7 %copy-start.1 = (s32[8,512]{1,0:T(8,128)S(1)}, s32[8,512]{1,0:T(8,128)}, u32[]{:S(2)}) copy-start(s32[8,512]{1,0:T(8,128)} %get-tuple-element.11.refs_0_) | copy-start | bytes 49156
  13.9 1.4 %copy-start.4 = (f32[1000,400]{0,1:T(8,128)S(1)}, f32[1000,400]{0,1:T(8,128)}, u32[]{:S(2)}) copy-start(f32[1000,400]{0,1:T(8,128)} %param.9) | copy-start | bytes 4800004
  15.3 4.6 %copy-start.2 = (s32[8,512]{1,0:T(8,128)S(1)}, s32[8,512]{1,0:T(8,128)}, u32[]{:S(2)}) copy-start(s32[8,512]{1,0:T(8,128)} %get-tuple-element.11.refs_0_) | copy-start | bytes 49156
  20.0 30.1 %copy-start.3 = (s32[1,8,2]{1,2,0:T(2,128)S(1)}, s32[1,8,2]{1,2,0:T(2,128)}, u32[]{:S(2)}) copy-start(s32[1,8,2]{1,2,0:T(2,128)} %param.10) | copy-start | bytes 196
  39.5 3.9 %collective-permute-start.3 = (s16[1,112,128]{2,1,0:T(8,128)(2,1)S(1)}, s16[1,112,128]{2,1,0:T(8,128)(2,1)S(1)}, u32[]{:S(2)}, u32[]{:S(2)}) collective-permute-start(s16[1,112,128]{2,1,0:T(8,128)(2,1)S(1)} %bitcast.9), channel_id=1, source_target_pairs={{0,8},{1,9},{2,10},{3,11},{4,12},{5,13},{6,14},{7,15},{8,0},{9,1},... | collective-permute-start | bytes 86024 | tf_op jit(solution)/shard_map/ppermute | solution.py:424
  43.4 5.7 %collective-permute-start.4 = (s16[2,112,128]{2,1,0:T(8,128)(2,1)S(1)}, s16[2,112,128]{2,1,0:T(8,128)(2,1)S(1)}, u32[]{:S(2)}, u32[]{:S(2)}) collective-permute-start(s16[2,112,128]{2,1,0:T(8,128)(2,1)S(1)} %pad_add_fusion.2), channel_id=1, source_target_pairs={{0,16},{1,17},{2,18},{3,19},{4,20},{5,21},{6,22},{7,23},{8,24},{9,... | collective-permute-start | bytes 172040 | tf_op jit(solution)/shard_map/ppermute | solution.py:424
  49.1 6.0 %collective-permute-start.5 = (s16[4,112,128]{2,1,0:T(8,128)(2,1)S(1)}, s16[4,112,128]{2,1,0:T(8,128)(2,1)S(1)}, u32[]{:S(2)}, u32[]{:S(2)}) collective-permute-start(s16[4,112,128]{2,1,0:T(8,128)(2,1)S(1)} %pad_add_fusion.1), channel_id=1, source_target_pairs={{0,4},{1,3},{2,6},{3,1},{4,0},{5,7},{6,2},{7,5},{8,12},{9,11},{10,... | collective-permute-start | bytes 344072 | tf_op jit(solution)/shard_map/ppermute | solution.py:424
  55.1 6.1 %collective-permute-start.6 = (s16[8,112,128]{2,1,0:T(8,128)(2,1)S(1)}, s16[8,112,128]{2,1,0:T(8,128)(2,1)S(1)}, u32[]{:S(2)}, u32[]{:S(2)}) collective-permute-start(s16[8,112,128]{2,1,0:T(8,128)(2,1)S(1)} %pad_add_fusion), channel_id=1, source_target_pairs={{0,2},{1,5},{2,0},{3,7},{4,6},{5,1},{6,4},{7,3},{8,10},{9,13},{10,... | collective-permute-start | bytes 688136 | tf_op jit(solution)/shard_map/ppermute | solution.py:424
  61.3 1.9 %collective-permute-start.7 = (s16[16,112,128]{2,1,0:T(8,128)(2,1)S(1)}, s16[16,112,128]{2,1,0:T(8,128)(2,1)S(1)}, u32[]{:S(2)}, u32[]{:S(2)}) collective-permute-start(s16[16,112,128]{2,1,0:T(8,128)(2,1)S(1)} %constant_dynamic-update-slice_fusion.mine), channel_id=1, source_target_pairs={{0,1},{1,0},{2,3},{3,2},{4,5},{5,4},{6,7},{7,6},{8,9},{9,8},{10,11... | collective-permute-start | bytes 1376264 | tf_op jit(solution)/shard_map/ppermute | solution.py:427

commit v5 on v4

--- a/solution.py
+++ b/solution.py
@@ -134,10 +134,13 @@
 
 
 def main_kernel(cfg, place, *refs):
-    (workers, replicas, cap, groups, width, pad_rel, block, narrow, window, offsets) = cfg
+    (direct, workers, replicas, cap, groups, width, pad_rel, block, narrow, window, offsets) = cfg
     idx_refs, refs = refs[:replicas], refs[replicas:]
     (query_v, lhs_v, rel_v, received), refs = refs[:4], refs[4:]
-    out_lhs, out, table_f, table_t, query_s, acc_rel, acc_lhs, acc_tab, wide_t, mixed = refs
+    out_lhs, refs = refs[0], refs[1:]
+    (keep, send), refs = (refs[:2], refs[2:]) if direct else ((None, refs[0]), refs[1:])
+    table_f, table_t, query_s, acc_rel, acc_lhs, acc_tab, wide_t, mixed = refs[:8]
+    codes_s, powers_s, tables_s, table_powers_s = refs[8:]
     edges = idx_refs[0].shape[1]
     dim = query_v.shape[0]
     rows = out_lhs.shape[1]
@@ -206,84 +209,103 @@
     table_codes, table_powers = encode(jnp.transpose(wide_t[...]), 1)
     table_powers = jnp.broadcast_to(table_powers, table_codes.shape)
     mixed[...] = jnp.zeros(mixed.shape, jnp.int32)
-    last = narrow + 2 * cap
-    for o in range(workers):
-        span = slice(o * block, (o + 1) * block)
-        mixed[:narrow, :block] = codes[:, span]
-        mixed[narrow : narrow + cap, :] = table_codes[o * cap : (o + 1) * cap]
-        mixed[narrow + cap : last, :] = table_powers[o * cap : (o + 1) * cap]
-        mixed[last : last + 1, :block] = powers[:, span]
-        out[o] = mixed[...].astype(jnp.int16)
-
-
-def combine_kernel(scale, narrow, cap, block, recv, out, mixed):
-    last = narrow + 2 * cap
-    total = jnp.zeros((narrow, block), F32)
-    for w in range(recv.shape[0]):
-        both = recv[w].astype(jnp.int32)
-        total += decode(both[:narrow, :block], both[last : last + 1, :block])
-    codes, powers = encode(total * F32(scale), 0)
+    codes_s[...] = codes
+    powers_s[...] = powers
+    tables_s[...] = table_codes
+    table_powers_s[...] = table_powers
+    places = rows_of(narrow, cap)
+    for h in range(workers):
+        if direct:
+            turn, z = h // (workers // 2), h % (workers // 2)
+            o = z * 2 + lax.rem(place[0] + turn, 2)
+            lane = pl.ds(pl.multiple_of(o * block, block), block)
+            target = (keep if turn == 0 else send).at[z]
+        else:
+            o, lane, target = h, slice(h * block, (h + 1) * block), send.at[h]
+        mixed[:narrow, :block] = codes_s[:, lane]
+        for c in range(cap):
+            for ref, row in ((tables_s, places[0]), (table_powers_s, places[2])):
+                mixed[row + c : row + c + 1, :] = ref[pl.ds(o * cap + c, 1), :]
+        mixed[places[4] : places[4] + 1, :block] = powers_s[0:1, lane]
+        target[...] = mixed[...].astype(jnp.int16)
+
+
+def rows_of(narrow, cap):
+    return [narrow + n * cap for n in range(5)]
+
+
+def pair_kernel(narrow, cap, block, keep, got, out, mixed):
+    places = rows_of(narrow, cap)
     mixed[...] = jnp.zeros(mixed.shape, jnp.int32)
-    mixed[:narrow, :block] = codes
-    mixed[last : last + 1, :block] = powers
-    out[...] = mixed[...].astype(jnp.int16)
-
-
-def entity_kernel(narrow, serve, lhs, recv, out, terms, onehot):
+    for z in range(keep.shape[0]):
+        ours, theirs = keep[z].astype(jnp.int32), got[z].astype(jnp.int32)
+        power = slice(places[4], places[4] + 1)
+        total = decode(ours[:narrow], ours[power]) + decode(theirs[:narrow], theirs[power])
+        mixed[:narrow, :], mixed[power, :] = encode(total, 0)
+        for n in (0, 2):
+            mixed[places[n] : places[n + 1], :] = ours[places[n] : places[n + 1]]
+            mixed[places[n + 1] : places[n + 2], :] = theirs[places[n] : places[n + 1]]
+        out[z] = mixed[...].astype(jnp.int16)
+
+
+def sum_kernel(scale, narrow, cap, block, *refs):
+    parts, out, mixed = refs[:-2], refs[-2], refs[-1]
+    power = slice(narrow + 4 * cap, narrow + 4 * cap + 1)
+    mixed[...] = jnp.zeros(mixed.shape, jnp.int32)
+    for z in range(out.shape[0]):
+        total = jnp.zeros((narrow, block), F32)
+        for part in parts:
+            both = part[z].astype(jnp.int32)
+            total += decode(both[:narrow, :block], both[power, :block])
+        mixed[:narrow, :block], mixed[power, :block] = encode(total * F32(scale), 0)
+        out[z] = mixed[...].astype(jnp.int16)
+
+
+def entity_kernel(direct, narrow, place, serve, lhs, *refs):
+    recv, out, terms, onehot = refs[:-3], refs[-3], refs[-2], refs[-1]
     cap, workers = serve.shape[1], serve.shape[2]
     rows = out.shape[1]
     lane = iota((1, rows), 1)
-    for w in range(workers):
-        both = recv[w].astype(jnp.int32)
-        terms[w * cap : (w + 1) * cap, :] = decode(
-            both[narrow : narrow + cap], both[narrow + cap : narrow + 2 * cap]
+    places = rows_of(narrow, cap)
+    for h in range(workers):
+        if direct:
+            turn, hop = h % 2, h // 2
+            z = place[0] // 2
+            both = recv[hop][z].astype(jnp.int32)
+            far = lax.rem(z - hop + len(recv), len(recv))
+            worker = far * 2 + lax.rem(place[0] + turn, 2)
+        else:
+            turn, both, worker = 0, recv[0][h].astype(jnp.int32), h
+        span = slice(h * cap, (h + 1) * cap)
+        terms[span, :] = decode(
+            both[places[turn] : places[turn + 1]], both[places[turn + 2] : places[turn + 3]]
         )
         for c in range(cap):
-            picked = serve[0, c, w]
-            onehot[w * cap + c : w * cap + c + 1, :] = jnp.where(lane == picked, 1.0, 0.0).astype(
-                F32
-            )
+            spot = jnp.where(lane == serve[0, c, worker], 1.0, 0.0).astype(F32)
+            onehot[h * cap + c : h * cap + c + 1, :] = spot
     spots = onehot[...].astype(BF16)
     parts = jnp.concatenate(split3(jnp.transpose(terms[...])), axis=1)
     added = dot(parts, jnp.concatenate([spots] * 3, axis=0))
     out[...] = lhs[...] + added[:narrow]
 
 
-def spread_kernel(orders, workers, replicas, narrow, power_row, block, place, mine, other, out):
+def spread_kernel(workers, replicas, narrow, power_row, block, place, mine, other, out):
     nrel = out.shape[1]
-    kinds = len(orders)
-    kind = lax.rem(place[1], kinds)
+    depth = workers // 2
     for o in range(workers):
         for r in range(replicas):
-            at, spot, scale = (o, r), 0, 1
-            for axis, stride, radix in orders[r % kinds]:
-                digit = lax.rem(place[axis] // stride, radix)
-                spot = spot + scale * lax.rem(digit - (at[axis] // stride) % radix + radix, radix)
-                scale *= radix
-            both = jnp.where(
-                kind == r % kinds, mine[spot].astype(jnp.int32), other[spot].astype(jnp.int32)
-            )
+            over_y = lax.rem(place[0] + o, 2)
+            over_x = lax.rem(place[1] // 2 + r // 2, 2)
+            spot = (over_y + 2 * over_x) * depth + o // 2
+            here = lax.rem(place[1], 2) == r % 2
+            both = jnp.where(here, mine[spot].astype(jnp.int32), other[spot].astype(jnp.int32))
             value = decode(both[:narrow], both[power_row : power_row + 1])
             end = min((o + 1) * block, nrel)
             out[r * narrow : (r + 1) * narrow, o * block : end] = value[:, : end - o * block]
 
 
-def moved(index, stride, radix, hop):
-    digit = (index // stride) % radix
-    return index + ((digit + hop) % radix - digit) * stride
-
-
 def turned(size, hop):
     return [(i, (i + hop) % size) for i in range(size)]
-
-
-def radices(size):
-    found = []
-    for radix in (2, 3, 5, 7):
-        while size % radix == 0:
-            found.append(radix)
-            size //= radix
-    return found
 
 
 def shards(entities, relation, serve_ids, edge_src, edge_rel, edge_dst, neg_ids, edge_count):
@@ -301,7 +323,7 @@
     pad_rel = up(max(nrel, workers * block), LANES)
     offsets = sorted({(narrow * r) % 8 for r in range(replicas)})
     window = up(narrow + offsets[-1], 8)
-    height = up(narrow + 2 * cap + 1, 16)
+    height = up(narrow + 4 * cap + 1, 16)
     ent_t, rel_t = entities.T, relation.T
     serve_t = jnp.transpose(serve_ids, (0, 2, 1))
     place = jnp.stack([lax.axis_index("dom"), lax.axis_index("rep")]).astype(jnp.int32)
@@ -354,16 +376,19 @@
         name="gather",
     )(place, *held, ent_t, rel_t)
 
-    cfg = (workers, replicas, cap, groups, width, pad_rel, block, narrow, window, tuple(offsets))
+    cfg = (
+        direct, workers, replicas, cap, groups, width, pad_rel, block, narrow, window,
+        tuple(offsets),
+    )
     lanes = max(up(block, LANES), up(narrow, LANES))
-    lhs_part, sent = pl.pallas_call(
+    half = workers // 2
+    outs = [half, half] if direct else [workers]
+    sizes = [jax.ShapeDtypeStruct((n, height, lanes), jnp.int16) for n in outs]
+    lhs_part, *sent = pl.pallas_call(
         functools.partial(main_kernel, cfg),
-        out_shape=(
-            jax.ShapeDtypeStruct((narrow, rows), F32),
-            jax.ShapeDtypeStruct((workers, height, lanes), jnp.int16),
-        ),
+        out_shape=[jax.ShapeDtypeStruct((narrow, rows), F32)] + sizes,
         in_specs=[SMEM] + [VMEM] * (replicas + 4),
-        out_specs=(VMEM, VMEM),
+        out_specs=[VMEM] * (1 + len(sizes)),
         scratch_shapes=[
             pltpu.VMEM((slots, dim), F32),
             pltpu.VMEM((dim, slots), F32),
@@ -373,62 +398,73 @@
             pltpu.VMEM((window, 3 * slots), F32),
             pltpu.VMEM((lanes, slots), F32),
             pltpu.VMEM((height, lanes), jnp.int32),
+            pltpu.VMEM((narrow, pad_rel), jnp.int32),
+            pltpu.VMEM((1, pad_rel), jnp.int32),
+            pltpu.VMEM((slots, lanes), jnp.int32),
+            pltpu.VMEM((slots, lanes), jnp.int32),
         ],
         compiler_params=params(),
         name="edges",
     )(place, *held, query, lhs_rows, rel_rows, received)
 
-    recv = lax.all_to_all(sent, "dom", 0, 0, tiled=True)
+    def swap(array, over_z=0, over_y=0, over_x=0):
+        pairs = []
+        for o in range(workers):
+            for r in range(replicas):
+                z, y, x = (o // 2 + over_z) % half, (o + over_y) % 2, (r // 2 + over_x) % 2
+                pairs.append((o * replicas + r, (z * 2 + y) * replicas + x * 2 + r % 2))
+        return lax.ppermute(array, ("dom", "rep"), pairs)
+
+    stack = jax.ShapeDtypeStruct((outs[0], height, lanes), jnp.int16)
+    mixed = [pltpu.VMEM((height, lanes), jnp.int32)]
+    if direct:
+        summed = pl.pallas_call(
+            functools.partial(pair_kernel, narrow, cap, block),
+            out_shape=stack,
+            in_specs=[VMEM] * 2,
+            out_specs=VMEM,
+            scratch_shapes=mixed,
+            compiler_params=params(),
+            name="pair",
+        )(sent[0], swap(sent[1], over_y=1))
+        recv = [summed] + [swap(summed, over_z=hop) for hop in range(1, half)]
+        parts = recv
+    else:
+        recv = [lax.all_to_all(sent[0], "dom", 0, 0, tiled=True)]
+        parts = [recv[0][w : w + 1] for w in range(workers)]
+        stack = jax.ShapeDtypeStruct((1, height, lanes), jnp.int16)
     scale = 1.0 / (edges * workers * replicas)
     chunk = pl.pallas_call(
-        functools.partial(combine_kernel, scale, narrow, cap, block),
-        out_shape=jax.ShapeDtypeStruct((height, lanes), jnp.int16),
-        in_specs=[VMEM],
+        functools.partial(sum_kernel, scale, narrow, cap, block),
+        out_shape=stack,
+        in_specs=[VMEM] * len(parts),
         out_specs=VMEM,
-        scratch_shapes=[pltpu.VMEM((height, lanes), jnp.int32)],
+        scratch_shapes=mixed,
         compiler_params=params(),
-        name="combine",
-    )(recv)
+        name="total",
+    )(*parts)
 
     entity_grad = pl.pallas_call(
-        functools.partial(entity_kernel, narrow),
+        functools.partial(entity_kernel, direct, narrow),
         out_shape=jax.ShapeDtypeStruct((narrow, rows), F32),
-        in_specs=[SMEM] + [VMEM] * 2,
+        in_specs=[SMEM] * 2 + [VMEM] * (1 + len(recv)),
         out_specs=VMEM,
         scratch_shapes=[pltpu.VMEM((slots, lanes), F32), pltpu.VMEM((slots, rows), F32)],
         compiler_params=params(),
         cost_estimate=cost(10**9, 10**6),
         name="entity",
-    )(serve_t, lhs_part, recv)
-
-    power_row = narrow + 2 * cap
+    )(place, serve_t, lhs_part, *recv)
+
+    power_row = narrow + 4 * cap
     if direct:
-        steps, stride = [], 1
-        for radix in radices(workers):
-            steps.append((0, stride, radix))
-            stride *= radix
-        across = [(1, 2, replicas // 2)]
-        first, flip = steps[1:] + steps[:1], across
-        orders = (tuple(first + flip), tuple(first[:-1] + flip + first[-1:]))
-        base = chunk.reshape(1, height, lanes)
-        for n in range(len(orders[0])):
-            parts = [base]
-            for hop in range(1, orders[0][n][2]):
-                pairs = []
-                for o in range(workers):
-                    for r in range(replicas):
-                        axis, stride, radix = orders[r % 2][n]
-                        at = [o, r]
-                        at[axis] = moved(at[axis], stride, radix, hop)
-                        pairs.append((o * replicas + r, at[0] * replicas + at[1]))
-                parts.append(lax.ppermute(base, ("dom", "rep"), pairs))
-            base = jnp.concatenate(parts, axis=0)
+        base = jnp.concatenate(
+            [chunk, swap(chunk, over_y=1), swap(chunk, over_x=1), swap(chunk, over_y=1, over_x=1)],
+            axis=0,
+        )
         base, entity_grad = lax.optimization_barrier((base, entity_grad))
         swapped = lax.ppermute(base, "rep", [(i, i ^ 1) for i in range(replicas)])
         relation_t = pl.pallas_call(
-            functools.partial(
-                spread_kernel, orders, workers, replicas, narrow, power_row, block
-            ),
+            functools.partial(spread_kernel, workers, replicas, narrow, power_row, block),
             out_shape=jax.ShapeDtypeStruct((dim, nrel), F32),
             in_specs=[SMEM] + [VMEM] * 2,
             out_specs=VMEM,
@@ -436,7 +472,7 @@
             name="spread",
         )(place, base, swapped)
     else:
-        whole = lax.all_gather(chunk[:, :block], ("dom", "rep"), axis=0)
+        whole = lax.all_gather(chunk[0, :, :block], ("dom", "rep"), axis=0)
         whole = decode(whole[:, :narrow], whole[:, power_row : power_row + 1])
         whole = whole.reshape(workers, replicas, narrow, block).transpose(1, 2, 0, 3)
         relation_t = whole.reshape(dim, workers * block)[:, :nrel]

time: 65.7 us -> 57.3 us (0.87)
  blocking collectives: 15.2 us -> 0 us
  starting transfers between devices: 12.4 us -> 19.7 us
  waiting for transfers between devices: 18.7 us -> 17.8 us
    all_to_all x1 -> x0, blocking collectives: 15.2 us -> none  [shards(): recv = lax.all_to_all(sent, 'dom', 0, 0, tiled=True)]
    ppermute x4 -> x7, starting transfers between devices: 3.26 us -> 10.5 us  [swap(): return lax.ppermute(array, ('dom', 'rep'), pairs)]
    ppermute x4 -> x7, waiting for transfers between devices: 16.9 us -> 16 us  [swap(): return lax.ppermute(array, ('dom', 'rep'), pairs)]
    pallas_call x4 -> x5, Pallas kernels: 7.93 us -> 8.49 us  [the longest x1 4.47 us: shards(): pl.pallas_call(functools.partial(main_kernel, cfg), out_shape=[jax.ShapeD...]
    unnamed x14 -> x10, local copies, waits for them, and re-layouts: 3.12 us -> 3.08 us
  transfers between devices with their start and end apart: 9 -> 12, of which waited for: 5 -> 7; matrix products, arithmetic and copies ran while one was open for 0% -> 0% of each run, Pallas kernels for 9% -> 11%
where the time goes in v5:
time: 57.3 us; the launch traced here: 57 us
  starting transfers between devices  19.7 us (34%)
  waiting for transfers between devices  17.8 us (31%)
  Pallas kernels  14.9 us (26%)
  local copies, waits for them, and re-layouts  3.08 us (5%)
  between operations  1.37 us (2%)
    ppermute x7, waiting for transfers between devices, swap(): return lax.ppermute(array, ('dom', 'rep'), pairs)  16 us
    ppermute x7, starting transfers between devices, swap(): return lax.ppermute(array, ('dom', 'rep'), pairs)  10.5 us
    all_to_all x1, starting transfers between devices, shards(): received = lax.all_to_all(served, 'dom', 0, 0, tiled=True)  5.84 us
    pallas_call x1, Pallas kernels, shards(): pl.pallas_call(functools.partial(gather_kernel, (replicas, nrel, pad_rel,...  4.64 us
    pallas_call x1, Pallas kernels, shards(): pl.pallas_call(functools.partial(main_kernel, cfg), out_shape=[jax.ShapeD...  4.47 us
    ppermute x3, starting transfers between devices, shards(): held.append(lax.ppermute(idx, 'rep', turned(replicas, hop)))  3.23 us
    unnamed x10, local copies, waits for them, and re-layouts  3.08 us
    pallas_call x1, Pallas kernels, shards(): pl.pallas_call(functools.partial(spread_kernel, workers, replicas, narrow...  2.13 us
  transfers between devices with their start and end apart: 12, of which 7 were waited for; matrix products, arithmetic and copies ran while one was open for 0% of the time, Pallas kernels for 11%

profile of v5, /device:TPU:0, one launch (start us, length us, event | category | flops | bytes accessed | tf_op | source)
XLA Modules:
  0.0 57.0 jit_solution(2919332510303424211)
XLA Ops:
  1.3 1.8 %prep.1 = (s32[8,512]{1,0:T(8,128)}, f32[8,2,400]{2,1,0:T(2,128)}) custom-call(s32[1,2,8]{2,1,0:T(2,128)} %bitcast.9, s32[1,1]{1,0:T(1,128)S(6)} %copy.10.count, bf16[400,256]{1,0:T(8,128)(2,1)} %bitcast.7, s32[1,1,512]{2,1,0:T(1,128)} %src.1, s32[1,1,512]{2,1,0:T(1,128)} %rel.1, s32[1,1,512]{2,1,0:T(1,128)} %dst.1, s32[1,1,2,384]{3,2,1,0:T(2,128)} %neg.1), custom_call_target="tpu_custom_call" | custom-call | tf_op jit(solution)/shard_map/prep/pallas_call | solution.py:331
  3.1 2.4 %collective-permute-start.2 = (s32[8,512]{1,0:T(8,128)}, s32[8,512]{1,0:T(8,128)S(1)}, u32[]{:S(2)}, u32[]{:S(2)}) collective-permute-start(s32[8,512]{1,0:T(8,128)} %get-tuple-element.12.refs_0_), channel_id=1, source_target_pairs={{0,3},{1,0},{2,1},{3,2},{4,7},{5,4},{6,5},{7,6},{8,11},{9,8},{10,9... | collective-permute-start | bytes 49160 | tf_op jit(solution)/shard_map/ppermute | solution.py:356
  5.5 0.6 %collective-permute-start.1 = (s32[8,512]{1,0:T(8,128)}, s32[8,512]{1,0:T(8,128)S(1)}, u32[]{:S(2)}, u32[]{:S(2)}) collective-permute-start(s32[8,512]{1,0:T(8,128)} %get-tuple-element.12.refs_0_), channel_id=1, source_target_pairs={{0,2},{1,3},{2,0},{3,1},{4,6},{5,7},{6,4},{7,5},{8,10},{9,11},{10,... | collective-permute-start | bytes 49160 | tf_op jit(solution)/shard_map/ppermute | solution.py:356
  6.2 0.2 collective-permute-start
  6.3 5.8 %all-to-all-start = ((f32[8,2,400]{2,1,0:T(2,128)}), f32[8,2,400]{2,1,0:T(2,128)S(1)}, u32[]{:S(2)}, u32[]{:S(2)}) async-start(f32[8,2,400]{2,1,0:T(2,128)} %get-tuple-element.16), calls=%async_computation | async-start | bytes 65536 | tf_op jit(solution)/shard_map/all_to_all | solution.py:357
  12.2 0.1 pad_add_fusion.1.place
  12.2 0.0 collective-permute-done.2.refs_3_
  12.2 0.0 collective-permute-done.1.refs_2_
  12.2 0.0 collective-permute-done.refs_1_
  12.3 0.0 copy-start
  12.3 0.9 %copy-done = bf16[256,400]{0,1:T(8,128)(2,1)S(1)} copy-done((bf16[256,400]{0,1:T(8,128)(2,1)S(1)}, bf16[256,400]{0,1:T(8,128)(2,1)}, u32[]{:S(2)}) %copy-start) | copy-done | bytes 204824
  13.2 0.0 copy-start.1
  13.2 0.7 %copy-done.1 = s32[8,512]{1,0:T(8,128)S(1)} copy-done((s32[8,512]{1,0:T(8,128)S(1)}, s32[8,512]{1,0:T(8,128)}, u32[]{:S(2)}) %copy-start.1) | copy-done | bytes 16408
  13.9 0.0 copy-start.4
  13.9 1.4 %copy-done.4 = f32[1000,400]{0,1:T(8,128)S(1)} copy-done((f32[1000,400]{0,1:T(8,128)S(1)}, f32[1000,400]{0,1:T(8,128)}, u32[]{:S(2)}) %copy-start.4) | copy-done | bytes 1600024
  15.3 0.0 copy-start.2
  15.3 4.6 %gather.1 = (bf16[400,2048]{1,0:T(8,128)(2,1)S(1)}, f32[104,2048]{1,0:T(8,128)S(1)}, f32[104,2048]{1,0:T(8,128)S(1)}) custom-call(s32[2]{0:T(128)S(1)} %pad_add_fusion.1.place, s32[8,512]{1,0:T(8,128)S(1)} %copy-done.1, s32[8,512]{1,0:T(8,128)S(1)} %collective-permute-done.refs_1_, s32[8,512]{1,0:T(8,128)S(1)} %collective-permute-done.1.refs_2_, ...), custom_call_target="tpu_custom_call" | custom-call | flops 3774873600 | bytes 6553600 | tf_op jit(solution)/shard_map/gather/pallas_call | solution.py:360
  20.0 0.0 all-to-all-done.refs_7_
  20.0 0.0 copy-done.2
  20.0 0.0 copy-start.3
  20.0 4.5 %edges.1 = (f32[100,256]{1,0:T(8,128)S(1)}, s16[4,112,128]{2,1,0:T(8,128)(2,1)S(1)}, s16[4,112,128]{2,1,0:T(8,128)(2,1)S(1)}) custom-call(s32[2]{0:T(128)S(1)} %pad_add_fusion.1.place, s32[8,512]{1,0:T(8,128)S(1)} %copy-done.2, s32[8,512]{1,0:T(8,128)S(1)} %collective-permute-done.refs_1_, s32[8,512]{1,0:T(8,128)S(1)} %collective-permute-done.1.refs_2_, ...), custom_call_target="tpu_custom_call" | custom-call | tf_op jit(solution)/shard_map/edges/pallas_call | solution.py:387
  24.5 2.1 %collective-permute-start.3 = (s16[4,112,128]{2,1,0:T(8,128)(2,1)S(1)}, s16[4,112,128]{2,1,0:T(8,128)(2,1)S(1)}, u32[]{:S(2)}, u32[]{:S(2)}) collective-permute-start(s16[4,112,128]{2,1,0:T(8,128)(2,1)S(1)} %get-tuple-element.18), channel_id=1, source_target_pairs={{0,4},{1,5},{2,6},{3,7},{4,0},{5,1},{6,2},{7,3},{8,12},{9,13},{10,... | collective-permute-start | bytes 344072 | tf_op jit(solution)/shard_map/ppermute | solution.py:416
  26.6 3.9 %collective-permute-done.3.got = s16[4,112,128]{2,1,0:T(8,128)(2,1)S(1)} collective-permute-done((s16[4,112,128]{2,1,0:T(8,128)(2,1)S(1)}, s16[4,112,128]{2,1,0:T(8,128)(2,1)S(1)}, u32[]{:S(2)}, u32[]{:S(2)}) %collective-permute-start.3) | collective-permute-done | bytes 114720 | tf_op jit(solution)/shard_map/ppermute | solution.py:416
  30.5 0.2 pair.1.refs_0_
  30.6 3.8 %collective-permute-start.6 = (s16[4,112,128]{2,1,0:T(8,128)(2,1)S(1)}, s16[4,112,128]{2,1,0:T(8,128)(2,1)S(1)}, u32[]{:S(2)}, u32[]{:S(2)}) collective-permute-start(s16[4,112,128]{2,1,0:T(8,128)(2,1)S(1)} %pair.1.refs_0_), channel_id=1, source_target_pairs={{0,24},{1,25},{2,26},{3,27},{4,28},{5,29},{6,30},{7,31},{8,0},{9,1... | collective-permute-start | bytes 344072 | tf_op jit(solution)/shard_map/ppermute | solution.py:416
  34.4 0.0 collective-permute-start.5
  34.4 1.1 %collective-permute-start.4 = (s16[4,112,128]{2,1,0:T(8,128)(2,1)S(1)}, s16[4,112,128]{2,1,0:T(8,128)(2,1)S(1)}, u32[]{:S(2)}, u32[]{:S(2)}) collective-permute-start(s16[4,112,128]{2,1,0:T(8,128)(2,1)S(1)} %pair.1.refs_0_), channel_id=1, source_target_pairs={{0,8},{1,9},{2,10},{3,11},{4,12},{5,13},{6,14},{7,15},{8,16},{9,17... | collective-permute-start | bytes 344072 | tf_op jit(solution)/shard_map/ppermute | solution.py:416
  35.5 2.4 %collective-permute-done.6.refs_3_ = s16[4,112,128]{2,1,0:T(8,128)(2,1)S(1)} collective-permute-done((s16[4,112,128]{2,1,0:T(8,128)(2,1)S(1)}, s16[4,112,128]{2,1,0:T(8,128)(2,1)S(1)}, u32[]{:S(2)}, u32[]{:S(2)}) %collective-permute-start.6) | collective-permute-done | bytes 114720 | tf_op jit(solution)/shard_map/ppermute | solution.py:416
  38.0 6.6 %collective-permute-done.5.refs_2_ = s16[4,112,128]{2,1,0:T(8,128)(2,1)S(1)} collective-permute-done((s16[4,112,128]{2,1,0:T(8,128)(2,1)S(1)}, s16[4,112,128]{2,1,0:T(8,128)(2,1)S(1)}, u32[]{:S(2)}, u32[]{:S(2)}) %collective-permute-start.5) | collective-permute-done | bytes 114720 | tf_op jit(solution)/shard_map/ppermute | solution.py:416
  44.6 0.0 collective-permute-done.4.refs_1_
  44.6 0.2 total.1
  44.8 1.2 %collective-permute-start.9 = (s16[4,112,128]{2,1,0:T(8,128)(2,1)S(1)}, s16[4,112,128]{2,1,0:T(8,128)(2,1)S(1)}, u32[]{:S(2)}, u32[]{:S(2)}) collective-permute-start(s16[4,112,128]{2,1,0:T(8,128)(2,1)S(1)} %total.1), channel_id=1, source_target_pairs={{0,6},{1,7},{2,4},{3,5},{4,2},{5,3},{6,0},{7,1},{8,14},{9,15},{10,... | collective-permute-start | bytes 344072 | tf_op jit(solution)/shard_map/ppermute | solution.py:416
  46.0 1.7 %collective-permute-start.8 = (s16[4,112,128]{2,1,0:T(8,128)(2,1)S(1)}, s16[4,112,128]{2,1,0:T(8,128)(2,1)S(1)}, u32[]{:S(2)}, u32[]{:S(2)}) collective-permute-start(s16[4,112,128]{2,1,0:T(8,128)(2,1)S(1)} %total.1), channel_id=1, source_target_pairs={{0,2},{1,3},{2,0},{3,1},{4,6},{5,7},{6,4},{7,5},{8,10},{9,11},{10,... | collective-permute-start | bytes 344072 | tf_op jit(solution)/shard_map/ppermute | solution.py:416
  47.8 0.6 %collective-permute-start.7 = (s16[4,112,128]{2,1,0:T(8,128)(2,1)S(1)}, s16[4,112,128]{2,1,0:T(8,128)(2,1)S(1)}, u32[]{:S(2)}, u32[]{:S(2)}) collective-permute-start(s16[4,112,128]{2,1,0:T(8,128)(2,1)S(1)} %total.1), channel_id=1, source_target_pairs={{0,4},{1,5},{2,6},{3,7},{4,0},{5,1},{6,2},{7,3},{8,12},{9,13},{10,... | collective-permute-start | bytes 344072 | tf_op jit(solution)/shard_map/ppermute | solution.py:416
  48.4 0.0 copy-done.3
  48.4 1.5 %entity.1 = f32[100,256]{1,0:T(8,128)} custom-call(s32[2]{0:T(128)S(1)} %pad_add_fusion.1.place, s32[1,2,8]{2,1,0:T(2,128)S(1)} %bitcast.10, f32[100,256]{1,0:T(8,128)S(1)} %get-tuple-element.19.lhs, s16[4,112,128]{2,1,0:T(8,128)(2,1)S(1)} %pair.1.refs_0_, s16[4,112,128]{2,1,0:T(8,128)(2,1)S(1)} %collective-permute-done.4.refs_1_, ...), custom_call_target="tpu_custom_call" | custom-call | flops 1000000000 | bytes 1000000 | tf_op jit(solution)/shard_map/entity/pallas_call | solution.py:447
  49.9 1.7 %collective-permute-done.9 = s16[4,112,128]{2,1,0:T(8,128)(2,1)S(1)} collective-permute-done((s16[4,112,128]{2,1,0:T(8,128)(2,1)S(1)}, s16[4,112,128]{2,1,0:T(8,128)(2,1)S(1)}, u32[]{:S(2)}, u32[]{:S(2)}) %collective-permute-start.9) | collective-permute-done | bytes 114720 | tf_op jit(solution)/shard_map/ppermute | solution.py:416
  51.6 1.1 %collective-permute-done.8 = s16[4,112,128]{2,1,0:T(8,128)(2,1)S(1)} collective-permute-done((s16[4,112,128]{2,1,0:T(8,128)(2,1)S(1)}, s16[4,112,128]{2,1,0:T(8,128)(2,1)S(1)}, u32[]{:S(2)}, u32[]{:S(2)}) %collective-permute-start.8) | collective-permute-done | bytes 114720 | tf_op jit(solution)/shard_map/ppermute | solution.py:416
  52.7 0.2 collective-permute-done.7
  53.0 0.1 collective-permute-start.10
  53.0 1.8 %collective-permute-done.10.other = s16[16,112,128]{2,1,0:T(8,128)(2,1)S(1)} collective-permute-done((s16[16,112,128]{2,1,0:T(8,128)(2,1)S(1)}, s16[16,112,128]{2,1,0:T(8,128)(2,1)S(1)}, u32[]{:S(2)}, u32[]{:S(2)}) %collective-permute-start.10) | collective-permute-done | bytes 458784 | tf_op jit(solution)/shard_map/ppermute | solution.py:465
  54.8 2.1 %spread.1 = f32[400,1000]{1,0:T(8,128)} custom-call(s32[2]{0:T(128)S(1)} %pad_add_fusion.1.place, s16[16,112,128]{2,1,0:T(8,128)(2,1)S(1)} %pad_add_fusion.mine, s16[16,112,128]{2,1,0:T(8,128)(2,1)S(1)} %collective-permute-done.10.other), custom_call_target="tpu_custom_call" | custom-call | tf_op jit(solution)/shard_map/spread/pallas_call | solution.py:466
  (1 shorter events, 0.0 us)
Async XLA Ops:
  3.1 9.1 %collective-permute-start.2 = (s32[8,512]{1,0:T(8,128)}, s32[8,512]{1,0:T(8,128)S(1)}, u32[]{:S(2)}, u32[]{:S(2)}) collective-permute-start(s32[8,512]{1,0:T(8,128)} %get-tuple-element.12.refs_0_), channel_id=1, source_target_pairs={{0,3},{1,0},{2,1},{3,2},{4,7},{5,4},{6,5},{7,6},{8,11},{9,8},{10,9... | collective-permute-start | bytes 49160 | tf_op jit(solution)/shard_map/ppermute | solution.py:356
  5.5 6.7 %collective-permute-start.1 = (s32[8,512]{1,0:T(8,128)}, s32[8,512]{1,0:T(8,128)S(1)}, u32[]{:S(2)}, u32[]{:S(2)}) collective-permute-start(s32[8,512]{1,0:T(8,128)} %get-tuple-element.12.refs_0_), channel_id=1, source_target_pairs={{0,2},{1,3},{2,0},{3,1},{4,6},{5,7},{6,4},{7,5},{8,10},{9,11},{10,... | collective-permute-start | bytes 49160 | tf_op jit(solution)/shard_map/ppermute | solution.py:356
  6.2 6.1 %collective-permute-start = (s32[8,512]{1,0:T(8,128)}, s32[8,512]{1,0:T(8,128)S(1)}, u32[]{:S(2)}, u32[]{:S(2)}) collective-permute-start(s32[8,512]{1,0:T(8,128)} %get-tuple-element.12.refs_0_), channel_id=1, source_target_pairs={{0,1},{1,2},{2,3},{3,0},{4,5},{5,6},{6,7},{7,4},{8,9},{9,10},{10,1... | collective-permute-start | bytes 49160 | tf_op jit(solution)/shard_map/ppermute | solution.py:356
  6.3 13.7 %all-to-all-start = ((f32[8,2,400]{2,1,0:T(2,128)}), f32[8,2,400]{2,1,0:T(2,128)S(1)}, u32[]{:S(2)}, u32[]{:S(2)}) async-start(f32[8,2,400]{2,1,0:T(2,128)} %get-tuple-element.16), calls=%async_computation | async-start | bytes 65536 | tf_op jit(solution)/shard_map/all_to_all | solution.py:357
  12.3 0.9 %copy-start = (bf16[256,400]{0,1:T(8,128)(2,1)S(1)}, bf16[256,400]{0,1:T(8,128)(2,1)}, u32[]{:S(2)}) copy-start(bf16[256,400]{0,1:T(8,128)(2,1)} %param.8) | copy-start | bytes 614404
  13.2 0.7 %copy-start.1 = (s32[8,512]{1,0:T(8,128)S(1)}, s32[8,512]{1,0:T(8,128)}, u32[]{:S(2)}) copy-start(s32[8,512]{1,0:T(8,128)} %get-tuple-element.12.refs_0_) | copy-start | bytes 49156
  13.9 1.4 %copy-start.4 = (f32[1000,400]{0,1:T(8,128)S(1)}, f32[1000,400]{0,1:T(8,128)}, u32[]{:S(2)}) copy-start(f32[1000,400]{0,1:T(8,128)} %param.9) | copy-start | bytes 4800004
  15.3 4.7 %copy-start.2 = (s32[8,512]{1,0:T(8,128)S(1)}, s32[8,512]{1,0:T(8,128)}, u32[]{:S(2)}) copy-start(s32[8,512]{1,0:T(8,128)} %get-tuple-element.12.refs_0_) | copy-start | bytes 49156
  20.0 28.4 %copy-start.3 = (s32[1,8,2]{1,2,0:T(2,128)S(1)}, s32[1,8,2]{1,2,0:T(2,128)}, u32[]{:S(2)}) copy-start(s32[1,8,2]{1,2,0:T(2,128)} %param.10) | copy-start | bytes 196
  24.5 6.0 %collective-permute-start.3 = (s16[4,112,128]{2,1,0:T(8,128)(2,1)S(1)}, s16[4,112,128]{2,1,0:T(8,128)(2,1)S(1)}, u32[]{:S(2)}, u32[]{:S(2)}) collective-permute-start(s16[4,112,128]{2,1,0:T(8,128)(2,1)S(1)} %get-tuple-element.18), channel_id=1, source_target_pairs={{0,4},{1,5},{2,6},{3,7},{4,0},{5,1},{6,2},{7,3},{8,12},{9,13},{10,... | collective-permute-start | bytes 344072 | tf_op jit(solution)/shard_map/ppermute | solution.py:416
  30.6 7.3 %collective-permute-start.6 = (s16[4,112,128]{2,1,0:T(8,128)(2,1)S(1)}, s16[4,112,128]{2,1,0:T(8,128)(2,1)S(1)}, u32[]{:S(2)}, u32[]{:S(2)}) collective-permute-start(s16[4,112,128]{2,1,0:T(8,128)(2,1)S(1)} %pair.1.refs_0_), channel_id=1, source_target_pairs={{0,24},{1,25},{2,26},{3,27},{4,28},{5,29},{6,30},{7,31},{8,0},{9,1... | collective-permute-start | bytes 344072 | tf_op jit(solution)/shard_map/ppermute | solution.py:416
  34.4 10.2 %collective-permute-start.5 = (s16[4,112,128]{2,1,0:T(8,128)(2,1)S(1)}, s16[4,112,128]{2,1,0:T(8,128)(2,1)S(1)}, u32[]{:S(2)}, u32[]{:S(2)}) collective-permute-start(s16[4,112,128]{2,1,0:T(8,128)(2,1)S(1)} %pair.1.refs_0_), channel_id=1, source_target_pairs={{0,16},{1,17},{2,18},{3,19},{4,20},{5,21},{6,22},{7,23},{8,24},{9,... | collective-permute-start | bytes 344072 | tf_op jit(solution)/shard_map/ppermute | solution.py:416
  34.4 10.2 %collective-permute-start.4 = (s16[4,112,128]{2,1,0:T(8,128)(2,1)S(1)}, s16[4,112,128]{2,1,0:T(8,128)(2,1)S(1)}, u32[]{:S(2)}, u32[]{:S(2)}) collective-permute-start(s16[4,112,128]{2,1,0:T(8,128)(2,1)S(1)} %pair.1.refs_0_), channel_id=1, source_target_pairs={{0,8},{1,9},{2,10},{3,11},{4,12},{5,13},{6,14},{7,15},{8,16},{9,17... | collective-permute-start | bytes 344072 | tf_op jit(solution)/shard_map/ppermute | solution.py:416
  44.8 6.8 %collective-permute-start.9 = (s16[4,112,128]{2,1,0:T(8,128)(2,1)S(1)}, s16[4,112,128]{2,1,0:T(8,128)(2,1)S(1)}, u32[]{:S(2)}, u32[]{:S(2)}) collective-permute-start(s16[4,112,128]{2,1,0:T(8,128)(2,1)S(1)} %total.1), channel_id=1, source_target_pairs={{0,6},{1,7},{2,4},{3,5},{4,2},{5,3},{6,0},{7,1},{8,14},{9,15},{10,... | collective-permute-start | bytes 344072 | tf_op jit(solution)/shard_map/ppermute | solution.py:416
  46.0 6.6 %collective-permute-start.8 = (s16[4,112,128]{2,1,0:T(8,128)(2,1)S(1)}, s16[4,112,128]{2,1,0:T(8,128)(2,1)S(1)}, u32[]{:S(2)}, u32[]{:S(2)}) collective-permute-start(s16[4,112,128]{2,1,0:T(8,128)(2,1)S(1)} %total.1), channel_id=1, source_target_pairs={{0,2},{1,3},{2,0},{3,1},{4,6},{5,7},{6,4},{7,5},{8,10},{9,11},{10,... | collective-permute-start | bytes 344072 | tf_op jit(solution)/shard_map/ppermute | solution.py:416
  47.8 5.1 %collective-permute-start.7 = (s16[4,112,128]{2,1,0:T(8,128)(2,1)S(1)}, s16[4,112,128]{2,1,0:T(8,128)(2,1)S(1)}, u32[]{:S(2)}, u32[]{:S(2)}) collective-permute-start(s16[4,112,128]{2,1,0:T(8,128)(2,1)S(1)} %total.1), channel_id=1, source_target_pairs={{0,4},{1,5},{2,6},{3,7},{4,0},{5,1},{6,2},{7,3},{8,12},{9,13},{10,... | collective-permute-start | bytes 344072 | tf_op jit(solution)/shard_map/ppermute | solution.py:416
  53.0 1.9 %collective-permute-start.10 = (s16[16,112,128]{2,1,0:T(8,128)(2,1)S(1)}, s16[16,112,128]{2,1,0:T(8,128)(2,1)S(1)}, u32[]{:S(2)}, u32[]{:S(2)}) collective-permute-start(s16[16,112,128]{2,1,0:T(8,128)(2,1)S(1)} %pad_add_fusion.mine), channel_id=1, source_target_pairs={{0,1},{1,0},{2,3},{3,2},{4,5},{5,4},{6,7},{7,6},{8,9},{9,8},{10,11... | collective-permute-start | bytes 1376264 | tf_op jit(solution)/shard_map/ppermute | solution.py:465

commit v6 on v5

--- a/solution.py
+++ b/solution.py
@@ -79,79 +79,91 @@
     return out
 
 
-def prep_kernel(serve, count, ent, src, rel, dst, neg, out_idx, out_rows, *refs):
+def prep_kernel(direct, place, serve, count, ent, src, rel, dst, neg, out_idx, *refs):
     cap, workers = serve.shape[1], serve.shape[2]
     rows = ent.shape[1]
     groups, width = neg.shape[2], neg.shape[3]
     onehot, sems = refs[-2:]
+    scratch, outs = refs[-9:-2], refs[:-9]
     moves = [
         pltpu.make_async_copy(a, b, sems.at[n])
-        for n, (a, b) in enumerate(zip((serve, count, ent, src, rel, dst, neg), refs))
+        for n, (a, b) in enumerate(zip((serve, count, ent, src, rel, dst, neg), scratch))
     ]
     for move in moves:
         move.start()
     for move in moves:
         move.wait()
-    serve_s, count_s, ent_v, src_v, rel_v, dst_v, neg_v = refs[:7]
-    out_idx[...] = jnp.full(out_idx.shape, count_s[0, 0], jnp.int32)
-    out_idx[0:1, :] = src_v[0]
-    out_idx[1:2, :] = rel_v[0]
-    out_idx[2:3, :] = dst_v[0]
+    serve_s, count_s, ent_v, src_v, rel_v, dst_v, neg_v = scratch
+    out_idx[...] = jnp.full(out_idx.shape, count_s[0, 0].astype(F32), F32)
+    out_idx[0:1, :] = src_v[0].astype(F32)
+    out_idx[1:2, :] = rel_v[0].astype(F32)
+    out_idx[2:3, :] = dst_v[0].astype(F32)
     for g in range(groups):
-        out_idx[3 + g : 4 + g, :width] = neg_v[0, 0, g : g + 1, :]
+        out_idx[3 + g : 4 + g, :width] = neg_v[0, 0, g : g + 1, :].astype(F32)
     lane = iota((1, rows), 1)
-    for k in range(workers * cap):
-        picked = serve_s[0, k % cap, k // cap]
-        onehot[k : k + 1, :] = jnp.where(lane == picked, 1.0, 0.0).astype(F32)
+    if direct:
+        onehot[...] = jnp.zeros(onehot.shape, F32)
+    for k in range(len(outs) * cap if direct else workers * cap):
+        worker = lax.rem(place[0] + len(outs) * place[1] + k // cap, workers) if direct else k // cap
+        spot = jnp.where(lane == serve_s[0, k % cap, worker], 1.0, 0.0).astype(F32)
+        onehot[k : k + 1, :] = spot
     picked_rows = dot_t(onehot[...].astype(BF16), ent_v[...])
-    for w in range(workers):
-        out_rows[w] = picked_rows[w * cap : (w + 1) * cap]
-
-
-def gather_kernel(cfg, place, *refs):
-    replicas, nrel, pad_rel, narrow, window = cfg
-    idx_refs, refs = refs[:replicas], refs[replicas:]
-    ent, relation, out_query, out_lhs, out_rel, rel_parts, lhs_s, rel_s = refs
-    edges = idx_refs[0].shape[1]
-    dim, rows = ent.shape
-    base = pl.multiple_of((place[1] * narrow) // 8 * 8, 8)
+    if direct:
+        for n, out in enumerate(outs):
+            out[...] = picked_rows[n * cap : (n + 1) * cap]
+    else:
+        for w in range(workers):
+            outs[0][w] = picked_rows[w * cap : (w + 1) * cap]
+
+
+def halves_kernel(relation, ent, out_parts, out_ent):
+    dim, nrel = relation.shape
     hi, lo = split2(relation[...])
-    if pad_rel > nrel:
-        rel_parts[...] = jnp.zeros(rel_parts.shape, BF16)
-    rel_parts[:dim, :nrel] = hi
-    rel_parts[dim:, :nrel] = lo
-    for i in range(replicas):
-        span = slice(i * edges, (i + 1) * edges)
-        src_l, rel_l = idx_refs[i][0:1, :], idx_refs[i][1:2, :]
-        lhs = dot(ent[...], ones_where(iota((rows, edges), 0) == src_l))
-        both = dot(rel_parts[...], ones_where(iota((pad_rel, edges), 0) == rel_l))
-        rel_rows = both[:dim] + both[dim:]
-        lhs_s[...] = lhs
-        rel_s[...] = rel_rows
-        out_query[:, span] = (lhs * rel_rows).astype(BF16)
-        out_lhs[:, span] = lhs_s[pl.ds(base, window), :]
-        out_rel[:, span] = rel_s[pl.ds(base, window), :]
+    if out_parts.shape[1] > nrel:
+        out_parts[...] = jnp.zeros(out_parts.shape, BF16)
+    out_parts[:dim, :nrel] = hi
+    out_parts[dim:, :nrel] = lo
+    out_ent[...] = ent[...]
+
+
+def pack_kernel(idx, *refs):
+    out = refs[-1]
+    out[...] = jnp.zeros(out.shape, F32)
+    out[:IDX_ROWS] = idx[...]
+    cap, dim = refs[0].shape
+    for n, rows in enumerate(refs[:-1]):
+        out[IDX_ROWS + n * cap : IDX_ROWS + (n + 1) * cap, :dim] = rows[...]
 
 
 def main_kernel(cfg, place, *refs):
     (direct, workers, replicas, cap, groups, width, pad_rel, block, narrow, window, offsets) = cfg
-    idx_refs, refs = refs[:replicas], refs[replicas:]
-    (query_v, lhs_v, rel_v, received), refs = refs[:4], refs[4:]
+    packs, refs = refs[:replicas], refs[replicas:]
+    (rel_parts, ent), refs = refs[:2], refs[2:]
+    received, refs = (None, refs) if direct else (refs[0], refs[1:])
     out_lhs, refs = refs[0], refs[1:]
     (keep, send), refs = (refs[:2], refs[2:]) if direct else ((None, refs[0]), refs[1:])
-    table_f, table_t, query_s, acc_rel, acc_lhs, acc_tab, wide_t, mixed = refs[:8]
-    codes_s, powers_s, tables_s, table_powers_s = refs[8:]
-    edges = idx_refs[0].shape[1]
-    dim = query_v.shape[0]
-    rows = out_lhs.shape[1]
+    table_f, table_t, lhs_s, rel_s, query_s, acc_rel, acc_lhs, acc_tab, wide_t, mixed = refs[:10]
+    codes_s, powers_s, tables_s, table_powers_s = refs[10:]
+    edges = packs[0].shape[1]
+    dim, rows = ent.shape
     slots = workers * cap
-    rep = place[1]
+    dom, rep = place[0], place[1]
     per = edges // groups
     base = pl.multiple_of((rep * narrow) // 8 * 8, 8)
     offset = rep * narrow - base
 
-    for w in range(workers):
-        table_f[w * cap : (w + 1) * cap, :] = received[w]
+    if direct:
+        each = workers // replicas
+        for h in range(replicas):
+            first = dom - each * lax.rem(rep - h + replicas, replicas) + workers
+            for n in range(each):
+                owner = lax.rem(first - n, workers)
+                for c in range(cap):
+                    row = IDX_ROWS + n * cap + c
+                    table_f[pl.ds(owner * cap + c, 1), :] = packs[h][row : row + 1, :dim]
+    else:
+        for w in range(workers):
+            table_f[w * cap : (w + 1) * cap, :] = received[w]
     table_t[...] = jnp.transpose(table_f[...])
     table = table_f[...].astype(BF16)
     own_t = table_t[pl.ds(base, window), :].astype(BF16)
@@ -161,12 +173,16 @@
     acc_tab[...] = jnp.zeros(acc_tab.shape, F32)
 
     for i in range(replicas):
-        here = slice(i * edges, (i + 1) * edges)
-        lanes = idx_refs[i][...]
+        lanes = packs[i][:IDX_ROWS].astype(jnp.int32)
         cols = jnp.transpose(lanes)
-        dst_l = lanes[2:3]
+        src_l, rel_l, dst_l = lanes[0:1], lanes[1:2], lanes[2:3]
         count = lanes[IDX_ROWS - 1 : IDX_ROWS]
-        query = query_v[:, here]
+        lhs = dot(ent[...], ones_where(iota((rows, edges), 0) == src_l))
+        both = dot(rel_parts[...], ones_where(iota((pad_rel, edges), 0) == rel_l))
+        rel_rows = both[:dim] + both[dim:]
+        query = (lhs * rel_rows).astype(BF16)
+        lhs_s[...] = lhs
+        rel_s[...] = rel_rows
         query_s[...] = query.astype(F32)
         scores = dot(table, query)
         live = jnp.where(iota((1, edges), 1) < count, 1.0, 0.0).astype(F32)
@@ -194,9 +210,9 @@
 
         dquery = dot(own_t, stack)
         acc_tab[...] += dot(query_s[pl.ds(base, window), :].astype(BF16), stack_t)
-        y = jnp.concatenate(split2(dquery * lhs_v[:, here]), axis=0)
+        y = jnp.concatenate(split2(dquery * lhs_s[pl.ds(base, window), :]), axis=0)
         acc_rel[...] += dot(y, ones_where(iota((edges, pad_rel), 1) == cols[:, 1:2]))
-        x = jnp.concatenate(split2(dquery * rel_v[:, here]), axis=0)
+        x = jnp.concatenate(split2(dquery * rel_s[pl.ds(base, window), :]), axis=0)
         acc_lhs[...] += dot(x, ones_where(iota((edges, rows), 1) == cols[:, 0:1]))
 
     pick = functools.partial(shifted_rows, offset=offset, narrow=narrow, offsets=offsets)
@@ -328,14 +344,17 @@
     serve_t = jnp.transpose(serve_ids, (0, 2, 1))
     place = jnp.stack([lax.axis_index("dom"), lax.axis_index("rep")]).astype(jnp.int32)
 
-    idx, served = pl.pallas_call(
-        prep_kernel,
-        out_shape=(
-            jax.ShapeDtypeStruct((IDX_ROWS, edges), jnp.int32),
-            jax.ShapeDtypeStruct((workers, cap, dim), F32),
-        ),
-        in_specs=[HBM] * 7,
-        out_specs=(VMEM, VMEM),
+    each = workers // replicas
+    served = (
+        [jax.ShapeDtypeStruct((cap, dim), F32)] * each
+        if direct
+        else [jax.ShapeDtypeStruct((workers, cap, dim), F32)]
+    )
+    idx, *served = pl.pallas_call(
+        functools.partial(prep_kernel, direct),
+        out_shape=[jax.ShapeDtypeStruct((IDX_ROWS, edges), F32)] + served,
+        in_specs=[SMEM] + [HBM] * 7,
+        out_specs=[VMEM] * (1 + len(served)),
         scratch_shapes=[
             pltpu.SMEM(serve_t.shape, jnp.int32),
             pltpu.SMEM(edge_count.shape, jnp.int32),
@@ -344,37 +363,50 @@
             pltpu.VMEM(edge_rel.shape, jnp.int32),
             pltpu.VMEM(edge_dst.shape, jnp.int32),
             pltpu.VMEM(neg_ids.shape, jnp.int32),
-            pltpu.VMEM((slots, rows), F32),
+            pltpu.VMEM((up(each * cap, 16) if direct else slots, rows), F32),
             pltpu.SemaphoreType.DMA((7,)),
         ],
         compiler_params=params(60),
         name="prep",
-    )(serve_t, edge_count, ent_t, edge_src, edge_rel, edge_dst, neg_ids)
-
+    )(place, serve_t, edge_count, ent_t, edge_src, edge_rel, edge_dst, neg_ids)
+
+    rel_late, ent_late, idx = lax.optimization_barrier((rel_t, ent_t, idx))
+    rel_parts, ent_late = pl.pallas_call(
+        halves_kernel,
+        out_shape=(
+            jax.ShapeDtypeStruct((2 * dim, pad_rel), BF16),
+            jax.ShapeDtypeStruct(ent_t.shape, BF16),
+        ),
+        in_specs=[VMEM, VMEM],
+        out_specs=(VMEM, VMEM),
+        compiler_params=params(),
+        cost_estimate=cost(10 * dim * nrel, 8 * dim * nrel),
+        name="halves",
+    )(rel_late, ent_late)
+
+    if direct:
+        fetched = []
+        for n in range(each):
+            pairs = []
+            for o in range(workers):
+                for r in range(replicas):
+                    to = (o + each * r + n) % workers
+                    pairs.append((o * replicas + r, to * replicas + r))
+            fetched.append(lax.ppermute(served[n], ("dom", "rep"), pairs))
+        idx = pl.pallas_call(
+            pack_kernel,
+            out_shape=jax.ShapeDtypeStruct((up(IDX_ROWS + each * cap, 8), edges), F32),
+            in_specs=[VMEM] * (1 + each),
+            out_specs=VMEM,
+            compiler_params=params(),
+            name="pack",
+        )(idx, *fetched)
+        received = []
+    else:
+        received = [lax.all_to_all(served[0], "dom", 0, 0, tiled=True)]
     held = [idx]
     for hop in range(1, replicas):
         held.append(lax.ppermute(idx, "rep", turned(replicas, hop)))
-    received = lax.all_to_all(served, "dom", 0, 0, tiled=True)
-
-    total = replicas * edges
-    query, lhs_rows, rel_rows = pl.pallas_call(
-        functools.partial(gather_kernel, (replicas, nrel, pad_rel, narrow, window)),
-        out_shape=(
-            jax.ShapeDtypeStruct((dim, total), BF16),
-            jax.ShapeDtypeStruct((window, total), F32),
-            jax.ShapeDtypeStruct((window, total), F32),
-        ),
-        in_specs=[SMEM] + [VMEM] * (replicas + 2),
-        out_specs=(VMEM, VMEM, VMEM),
-        scratch_shapes=[
-            pltpu.VMEM((2 * dim, pad_rel), BF16),
-            pltpu.VMEM((dim, edges), F32),
-            pltpu.VMEM((dim, edges), F32),
-        ],
-        compiler_params=params(),
-        cost_estimate=cost(2 * total * dim * (2 * pad_rel + rows), 8 * total * dim),
-        name="gather",
-    )(place, *held, ent_t, rel_t)
 
     cfg = (
         direct, workers, replicas, cap, groups, width, pad_rel, block, narrow, window,
@@ -387,11 +419,13 @@
     lhs_part, *sent = pl.pallas_call(
         functools.partial(main_kernel, cfg),
         out_shape=[jax.ShapeDtypeStruct((narrow, rows), F32)] + sizes,
-        in_specs=[SMEM] + [VMEM] * (replicas + 4),
+        in_specs=[SMEM] + [VMEM] * (replicas + 2 + len(received)),
         out_specs=[VMEM] * (1 + len(sizes)),
         scratch_shapes=[
             pltpu.VMEM((slots, dim), F32),
             pltpu.VMEM((dim, slots), F32),
+            pltpu.VMEM((dim, edges), F32),
+            pltpu.VMEM((dim, edges), F32),
             pltpu.VMEM((dim, edges), F32),
             pltpu.VMEM((2 * window, pad_rel), F32),
             pltpu.VMEM((2 * window, rows), F32),
@@ -405,7 +439,7 @@
         ],
         compiler_params=params(),
         name="edges",
-    )(place, *held, query, lhs_rows, rel_rows, received)
+    )(place, *held, rel_parts, ent_late, *received)
 
     def swap(array, over_z=0, over_y=0, over_x=0):
         pairs = []

time: 57.3 us -> 61.3 us (1.070)
  waiting for transfers between devices: 17.8 us -> 22.1 us
  starting transfers between devices: 19.7 us -> 18.2 us
  Pallas kernels: 14.9 us -> 15.6 us
    all_to_all x1 -> x0, starting transfers between devices: 5.84 us -> none  [shards(): received = lax.all_to_all(served, 'dom', 0, 0, tiled=True)]
    ppermute x0 -> x2, waiting for transfers between devices: none -> 4.83 us  [shards(): fetched.append(lax.ppermute(served[n], ('dom', 'rep'), pairs))]
    ppermute x0 -> x2, starting transfers between devices: none -> 4.31 us  [shards(): fetched.append(lax.ppermute(served[n], ('dom', 'rep'), pairs))]
    pallas_call x1, Pallas kernels: 4.47 us -> 8.75 us  [shards(): pl.pallas_call(functools.partial(main_kernel, cfg), out_shape=[jax.ShapeD...]
    pallas_call x2 -> x3, Pallas kernels: 6.45 us -> 2.83 us  [the longest x1 2.51 us: shards(): pl.pallas_call(functools.partial(prep_kernel, direct), out_shape=[jax.Sha...]
    ppermute x7, waiting for transfers between devices: 16 us -> 15 us  [swap(): return lax.ppermute(array, ('dom', 'rep'), pairs)]
  transfers between devices with their start and end apart: 12 -> 13, of which waited for: 7 -> 8; matrix products, arithmetic and copies ran while one was open for 0% -> 0% of each run, Pallas kernels for 11% -> 3%
where the time goes in v6:
time: 61.3 us; the launch traced here: 61 us
  waiting for transfers between devices  22.1 us (36%)
  starting transfers between devices  18.2 us (30%)
  Pallas kernels  15.6 us (25%)
  local copies, waits for them, and re-layouts  3.09 us (5%)
  between operations  1.36 us (2%)
  other arithmetic  0.63 us (1%)
    ppermute x7, waiting for transfers between devices, swap(): return lax.ppermute(array, ('dom', 'rep'), pairs)  15 us
    ppermute x7, starting transfers between devices, swap(): return lax.ppermute(array, ('dom', 'rep'), pairs)  10.5 us
    pallas_call x1, Pallas kernels, shards(): pl.pallas_call(functools.partial(main_kernel, cfg), out_shape=[jax.ShapeD...  8.75 us
    ppermute x2, waiting for transfers between devices, shards(): fetched.append(lax.ppermute(served[n], ('dom', 'rep'), pairs))  4.83 us
    ppermute x2, starting transfers between devices, shards(): fetched.append(lax.ppermute(served[n], ('dom', 'rep'), pairs))  4.31 us
    ppermute x3, starting transfers between devices, shards(): held.append(lax.ppermute(idx, 'rep', turned(replicas, hop)))  3.3 us
    unnamed x10, local copies, waits for them, and re-layouts  3.09 us
    pallas_call x1, Pallas kernels, shards(): pl.pallas_call(functools.partial(prep_kernel, direct), out_shape=[jax.Sha...  2.51 us
  transfers between devices with their start and end apart: 13, of which 8 were waited for; matrix products, arithmetic and copies ran while one was open for 0% of the time, Pallas kernels for 3%

profile of v6, /device:TPU:0, one launch (start us, length us, event | category | flops | bytes accessed | tf_op | source)
XLA Modules:
  0.0 61.0 jit_solution(2906757069013854338)
XLA Ops:
  1.3 0.6 pad_add_fusion.1.place
  1.9 0.0 copy-start.3
  1.9 2.5 %prep.1 = (f32[8,512]{1,0:T(8,128)}, f32[2,400]{1,0:T(2,128)}, f32[2,400]{1,0:T(2,128)}) custom-call(s32[2]{0:T(128)} %pad_add_fusion.1.place, s32[1,2,8]{2,1,0:T(2,128)} %bitcast.10, s32[1,1]{1,0:T(1,128)S(6)} %copy.10.count, bf16[400,256]{1,0:T(8,128)(2,1)} %bitcast.8, s32[1,1,512]{2,1,0:T(1,128)} %src.1, s32[1,1,512]{2,1,0:T(1,128)} %rel.1, ...), custom_call_target="tpu_custom_call" | custom-call | tf_op jit(solution)/shard_map/prep/pallas_call | solution.py:353
  4.4 1.3 %collective-permute-start = (f32[2,400]{1,0:T(2,128)}, f32[2,400]{1,0:T(2,128)S(1)}, u32[]{:S(2)}, u32[]{:S(2)}) collective-permute-start(f32[2,400]{1,0:T(2,128)} %get-tuple-element.17), channel_id=1, source_target_pairs={{0,0},{1,9},{2,18},{3,27},{4,4},{5,13},{6,22},{7,31},{8,8},{9,17},... | collective-permute-start | bytes 9608 | tf_op jit(solution)/shard_map/ppermute | solution.py:395
  5.7 3.0 %collective-permute-start.1 = (f32[2,400]{1,0:T(2,128)}, f32[2,400]{1,0:T(2,128)S(1)}, u32[]{:S(2)}, u32[]{:S(2)}) collective-permute-start(f32[2,400]{1,0:T(2,128)} %get-tuple-element.18), channel_id=1, source_target_pairs={{0,4},{1,13},{2,22},{3,31},{4,8},{5,17},{6,26},{7,3},{8,12},{9,21}... | collective-permute-start | bytes 9608 | tf_op jit(solution)/shard_map/ppermute | solution.py:395
  8.7 0.0 collective-permute-done.refs_0_
  8.7 4.8 %collective-permute-done.1.refs_1_ = f32[2,400]{1,0:T(2,128)S(1)} collective-permute-done((f32[2,400]{1,0:T(2,128)}, f32[2,400]{1,0:T(2,128)S(1)}, u32[]{:S(2)}, u32[]{:S(2)}) %collective-permute-start.1) | collective-permute-done | bytes 3232 | tf_op jit(solution)/shard_map/ppermute | solution.py:395
  13.5 0.0 copy-start.2
  13.6 0.7 %copy-done.2 = f32[8,512]{1,0:T(8,128)S(1)} copy-done((f32[8,512]{1,0:T(8,128)S(1)}, f32[8,512]{1,0:T(8,128)}, u32[]{:S(2)}) %copy-start.2) | copy-done | bytes 16408
  14.3 1.2 %collective-permute-start.4 = (f32[16,512]{1,0:T(8,128)S(1)}, f32[16,512]{1,0:T(8,128)S(1)}, u32[]{:S(2)}, u32[]{:S(2)}) collective-permute-start(f32[16,512]{1,0:T(8,128)S(1)} %pack.1.refs_0_), channel_id=1, source_target_pairs={{0,3},{1,0},{2,1},{3,2},{4,7},{5,4},{6,5},{7,6},{8,11},{9,8},{10,9... | collective-permute-start | bytes 98312 | tf_op jit(solution)/shard_map/ppermute | solution.py:409
  15.5 1.9 %collective-permute-start.3 = (f32[16,512]{1,0:T(8,128)S(1)}, f32[16,512]{1,0:T(8,128)S(1)}, u32[]{:S(2)}, u32[]{:S(2)}) collective-permute-start(f32[16,512]{1,0:T(8,128)S(1)} %pack.1.refs_0_), channel_id=1, source_target_pairs={{0,2},{1,3},{2,0},{3,1},{4,6},{5,7},{6,4},{7,5},{8,10},{9,11},{10,... | collective-permute-start | bytes 98312 | tf_op jit(solution)/shard_map/ppermute | solution.py:409
  17.4 0.2 collective-permute-start.2
  17.6 0.0 copy-start
  17.6 1.4 %copy-done = f32[1000,400]{0,1:T(8,128)S(1)} copy-done((f32[1000,400]{0,1:T(8,128)S(1)}, f32[1000,400]{0,1:T(8,128)}, u32[]{:S(2)}) %copy-start) | copy-done | bytes 1600024
  19.0 0.0 copy-start.1
  19.0 0.9 %copy-done.1 = bf16[256,400]{0,1:T(8,128)(2,1)S(1)} copy-done((bf16[256,400]{0,1:T(8,128)(2,1)S(1)}, bf16[256,400]{0,1:T(8,128)(2,1)}, u32[]{:S(2)}) %copy-start.1) | copy-done | bytes 204824
  19.9 0.3 halves.1
  20.3 0.0 copy-start.4
  20.3 0.0 collective-permute-done.4.refs_3_
  20.3 0.0 collective-permute-done.3.refs_2_
  20.3 0.5 collective-permute-done.2.refs_1_
  20.8 0.0 copy-done.3
  20.8 8.8 %edges.1 = (f32[100,256]{1,0:T(8,128)S(1)}, s16[4,112,128]{2,1,0:T(8,128)(2,1)S(1)}, s16[4,112,128]{2,1,0:T(8,128)(2,1)S(1)}) custom-call(s32[2]{0:T(128)S(1)} %copy-done.3, f32[16,512]{1,0:T(8,128)S(1)} %pack.1.refs_0_, f32[16,512]{1,0:T(8,128)S(1)} %collective-permute-done.2.refs_1_, f32[16,512]{1,0:T(8,128)S(1)} %collective-permute-done.3.refs_2_, ...), custom_call_target="tpu_custom_call" | custom-call | tf_op jit(solution)/shard_map/edges/pallas_call | solution.py:419
  29.5 2.5 %collective-permute-start.5 = (s16[4,112,128]{2,1,0:T(8,128)(2,1)S(1)}, s16[4,112,128]{2,1,0:T(8,128)(2,1)S(1)}, u32[]{:S(2)}, u32[]{:S(2)}) collective-permute-start(s16[4,112,128]{2,1,0:T(8,128)(2,1)S(1)} %get-tuple-element.24), channel_id=1, source_target_pairs={{0,4},{1,5},{2,6},{3,7},{4,0},{5,1},{6,2},{7,3},{8,12},{9,13},{10,... | collective-permute-start | bytes 344072 | tf_op jit(solution)/shard_map/ppermute | solution.py:450
  32.0 2.9 %collective-permute-done.5.got = s16[4,112,128]{2,1,0:T(8,128)(2,1)S(1)} collective-permute-done((s16[4,112,128]{2,1,0:T(8,128)(2,1)S(1)}, s16[4,112,128]{2,1,0:T(8,128)(2,1)S(1)}, u32[]{:S(2)}, u32[]{:S(2)}) %collective-permute-start.5) | collective-permute-done | bytes 114720 | tf_op jit(solution)/shard_map/ppermute | solution.py:450
  34.9 0.2 pair.1.refs_0_
  35.1 2.7 %collective-permute-start.8 = (s16[4,112,128]{2,1,0:T(8,128)(2,1)S(1)}, s16[4,112,128]{2,1,0:T(8,128)(2,1)S(1)}, u32[]{:S(2)}, u32[]{:S(2)}) collective-permute-start(s16[4,112,128]{2,1,0:T(8,128)(2,1)S(1)} %pair.1.refs_0_), channel_id=1, source_target_pairs={{0,24},{1,25},{2,26},{3,27},{4,28},{5,29},{6,30},{7,31},{8,0},{9,1... | collective-permute-start | bytes 344072 | tf_op jit(solution)/shard_map/ppermute | solution.py:450
  37.7 0.4 collective-permute-start.7
  38.1 0.2 collective-permute-start.6
  38.4 3.0 %collective-permute-done.8.refs_3_ = s16[4,112,128]{2,1,0:T(8,128)(2,1)S(1)} collective-permute-done((s16[4,112,128]{2,1,0:T(8,128)(2,1)S(1)}, s16[4,112,128]{2,1,0:T(8,128)(2,1)S(1)}, u32[]{:S(2)}, u32[]{:S(2)}) %collective-permute-start.8) | collective-permute-done | bytes 114720 | tf_op jit(solution)/shard_map/ppermute | solution.py:450
  41.3 6.2 %collective-permute-done.7.refs_2_ = s16[4,112,128]{2,1,0:T(8,128)(2,1)S(1)} collective-permute-done((s16[4,112,128]{2,1,0:T(8,128)(2,1)S(1)}, s16[4,112,128]{2,1,0:T(8,128)(2,1)S(1)}, u32[]{:S(2)}, u32[]{:S(2)}) %collective-permute-start.7) | collective-permute-done | bytes 114720 | tf_op jit(solution)/shard_map/ppermute | solution.py:450
  47.6 0.0 collective-permute-done.6.refs_1_
  47.6 0.2 total.1
  47.8 4.1 %collective-permute-start.11 = (s16[4,112,128]{2,1,0:T(8,128)(2,1)S(1)}, s16[4,112,128]{2,1,0:T(8,128)(2,1)S(1)}, u32[]{:S(2)}, u32[]{:S(2)}) collective-permute-start(s16[4,112,128]{2,1,0:T(8,128)(2,1)S(1)} %total.1), channel_id=1, source_target_pairs={{0,6},{1,7},{2,4},{3,5},{4,2},{5,3},{6,0},{7,1},{8,14},{9,15},{10,... | collective-permute-start | bytes 344072 | tf_op jit(solution)/shard_map/ppermute | solution.py:450
  51.9 0.0 collective-permute-start.10
  51.9 0.6 %collective-permute-start.9 = (s16[4,112,128]{2,1,0:T(8,128)(2,1)S(1)}, s16[4,112,128]{2,1,0:T(8,128)(2,1)S(1)}, u32[]{:S(2)}, u32[]{:S(2)}) collective-permute-start(s16[4,112,128]{2,1,0:T(8,128)(2,1)S(1)} %total.1), channel_id=1, source_target_pairs={{0,4},{1,5},{2,6},{3,7},{4,0},{5,1},{6,2},{7,3},{8,12},{9,13},{10,... | collective-permute-start | bytes 344072 | tf_op jit(solution)/shard_map/ppermute | solution.py:450
  52.5 0.0 copy-done.4
  52.5 1.5 %entity.1 = f32[100,256]{1,0:T(8,128)} custom-call(s32[2]{0:T(128)S(1)} %copy-done.3, s32[1,2,8]{2,1,0:T(2,128)S(1)} %bitcast.11, f32[100,256]{1,0:T(8,128)S(1)} %get-tuple-element.25.lhs, s16[4,112,128]{2,1,0:T(8,128)(2,1)S(1)} %pair.1.refs_0_, s16[4,112,128]{2,1,0:T(8,128)(2,1)S(1)} %collective-permute-done.6.refs_1_, ...), custom_call_target="tpu_custom_call" | custom-call | flops 1000000000 | bytes 1000000 | tf_op jit(solution)/shard_map/entity/pallas_call | solution.py:481
  54.0 1.9 %collective-permute-done.11 = s16[4,112,128]{2,1,0:T(8,128)(2,1)S(1)} collective-permute-done((s16[4,112,128]{2,1,0:T(8,128)(2,1)S(1)}, s16[4,112,128]{2,1,0:T(8,128)(2,1)S(1)}, u32[]{:S(2)}, u32[]{:S(2)}) %collective-permute-start.11) | collective-permute-done | bytes 114720 | tf_op jit(solution)/shard_map/ppermute | solution.py:450
  56.0 1.0 %collective-permute-done.10 = s16[4,112,128]{2,1,0:T(8,128)(2,1)S(1)} collective-permute-done((s16[4,112,128]{2,1,0:T(8,128)(2,1)S(1)}, s16[4,112,128]{2,1,0:T(8,128)(2,1)S(1)}, u32[]{:S(2)}, u32[]{:S(2)}) %collective-permute-start.10) | collective-permute-done | bytes 114720 | tf_op jit(solution)/shard_map/ppermute | solution.py:450
  56.9 0.0 collective-permute-done.9
  57.0 0.1 collective-permute-start.12
  57.1 1.8 %collective-permute-done.12.other = s16[16,112,128]{2,1,0:T(8,128)(2,1)S(1)} collective-permute-done((s16[16,112,128]{2,1,0:T(8,128)(2,1)S(1)}, s16[16,112,128]{2,1,0:T(8,128)(2,1)S(1)}, u32[]{:S(2)}, u32[]{:S(2)}) %collective-permute-start.12) | collective-permute-done | bytes 458784 | tf_op jit(solution)/shard_map/ppermute | solution.py:499
  58.9 2.1 %spread.1 = f32[400,1000]{1,0:T(8,128)} custom-call(s32[2]{0:T(128)S(1)} %copy-done.3, s16[16,112,128]{2,1,0:T(8,128)(2,1)S(1)} %pad_add_fusion.mine, s16[16,112,128]{2,1,0:T(8,128)(2,1)S(1)} %collective-permute-done.12.other), custom_call_target="tpu_custom_call" | custom-call | tf_op jit(solution)/shard_map/spread/pallas_call | solution.py:500
  (2 shorter events, 0.0 us)
Async XLA Ops:
  1.9 18.9 %copy-start.3 = (s32[2]{0:T(128)S(1)}, s32[2]{0:T(128)}, u32[]{:S(2)}) copy-start(s32[2]{0:T(128)} %pad_add_fusion.1.place) | copy-start | bytes 28
  4.4 4.3 %collective-permute-start = (f32[2,400]{1,0:T(2,128)}, f32[2,400]{1,0:T(2,128)S(1)}, u32[]{:S(2)}, u32[]{:S(2)}) collective-permute-start(f32[2,400]{1,0:T(2,128)} %get-tuple-element.17), channel_id=1, source_target_pairs={{0,0},{1,9},{2,18},{3,27},{4,4},{5,13},{6,22},{7,31},{8,8},{9,17},... | collective-permute-start | bytes 9608 | tf_op jit(solution)/shard_map/ppermute | solution.py:395
  5.7 7.8 %collective-permute-start.1 = (f32[2,400]{1,0:T(2,128)}, f32[2,400]{1,0:T(2,128)S(1)}, u32[]{:S(2)}, u32[]{:S(2)}) collective-permute-start(f32[2,400]{1,0:T(2,128)} %get-tuple-element.18), channel_id=1, source_target_pairs={{0,4},{1,13},{2,22},{3,31},{4,8},{5,17},{6,26},{7,3},{8,12},{9,21}... | collective-permute-start | bytes 9608 | tf_op jit(solution)/shard_map/ppermute | solution.py:395
  13.5 0.7 %copy-start.2 = (f32[8,512]{1,0:T(8,128)S(1)}, f32[8,512]{1,0:T(8,128)}, u32[]{:S(2)}) copy-start(f32[8,512]{1,0:T(8,128)} %get-tuple-element.16.idx) | copy-start | bytes 49156
  14.3 6.0 %collective-permute-start.4 = (f32[16,512]{1,0:T(8,128)S(1)}, f32[16,512]{1,0:T(8,128)S(1)}, u32[]{:S(2)}, u32[]{:S(2)}) collective-permute-start(f32[16,512]{1,0:T(8,128)S(1)} %pack.1.refs_0_), channel_id=1, source_target_pairs={{0,3},{1,0},{2,1},{3,2},{4,7},{5,4},{6,5},{7,6},{8,11},{9,8},{10,9... | collective-permute-start | bytes 98312 | tf_op jit(solution)/shard_map/ppermute | solution.py:409
  15.5 4.8 %collective-permute-start.3 = (f32[16,512]{1,0:T(8,128)S(1)}, f32[16,512]{1,0:T(8,128)S(1)}, u32[]{:S(2)}, u32[]{:S(2)}) collective-permute-start(f32[16,512]{1,0:T(8,128)S(1)} %pack.1.refs_0_), channel_id=1, source_target_pairs={{0,2},{1,3},{2,0},{3,1},{4,6},{5,7},{6,4},{7,5},{8,10},{9,11},{10,... | collective-permute-start | bytes 98312 | tf_op jit(solution)/shard_map/ppermute | solution.py:409
  17.4 3.3 %collective-permute-start.2 = (f32[16,512]{1,0:T(8,128)S(1)}, f32[16,512]{1,0:T(8,128)S(1)}, u32[]{:S(2)}, u32[]{:S(2)}) collective-permute-start(f32[16,512]{1,0:T(8,128)S(1)} %pack.1.refs_0_), channel_id=1, source_target_pairs={{0,1},{1,2},{2,3},{3,0},{4,5},{5,6},{6,7},{7,4},{8,9},{9,10},{10,1... | collective-permute-start | bytes 98312 | tf_op jit(solution)/shard_map/ppermute | solution.py:409
  17.6 1.4 %copy-start = (f32[1000,400]{0,1:T(8,128)S(1)}, f32[1000,400]{0,1:T(8,128)}, u32[]{:S(2)}) copy-start(f32[1000,400]{0,1:T(8,128)} %param.9) | copy-start | bytes 4800004
  19.0 0.9 %copy-start.1 = (bf16[256,400]{0,1:T(8,128)(2,1)S(1)}, bf16[256,400]{0,1:T(8,128)(2,1)}, u32[]{:S(2)}) copy-start(bf16[256,400]{0,1:T(8,128)(2,1)} %param.8) | copy-start | bytes 614404
  20.3 32.3 %copy-start.4 = (s32[1,8,2]{1,2,0:T(2,128)S(1)}, s32[1,8,2]{1,2,0:T(2,128)}, u32[]{:S(2)}) copy-start(s32[1,8,2]{1,2,0:T(2,128)} %param.10) | copy-start | bytes 196
  29.5 5.4 %collective-permute-start.5 = (s16[4,112,128]{2,1,0:T(8,128)(2,1)S(1)}, s16[4,112,128]{2,1,0:T(8,128)(2,1)S(1)}, u32[]{:S(2)}, u32[]{:S(2)}) collective-permute-start(s16[4,112,128]{2,1,0:T(8,128)(2,1)S(1)} %get-tuple-element.24), channel_id=1, source_target_pairs={{0,4},{1,5},{2,6},{3,7},{4,0},{5,1},{6,2},{7,3},{8,12},{9,13},{10,... | collective-permute-start | bytes 344072 | tf_op jit(solution)/shard_map/ppermute | solution.py:450
  35.1 6.3 %collective-permute-start.8 = (s16[4,112,128]{2,1,0:T(8,128)(2,1)S(1)}, s16[4,112,128]{2,1,0:T(8,128)(2,1)S(1)}, u32[]{:S(2)}, u32[]{:S(2)}) collective-permute-start(s16[4,112,128]{2,1,0:T(8,128)(2,1)S(1)} %pair.1.refs_0_), channel_id=1, source_target_pairs={{0,24},{1,25},{2,26},{3,27},{4,28},{5,29},{6,30},{7,31},{8,0},{9,1... | collective-permute-start | bytes 344072 | tf_op jit(solution)/shard_map/ppermute | solution.py:450
  37.7 9.8 %collective-permute-start.7 = (s16[4,112,128]{2,1,0:T(8,128)(2,1)S(1)}, s16[4,112,128]{2,1,0:T(8,128)(2,1)S(1)}, u32[]{:S(2)}, u32[]{:S(2)}) collective-permute-start(s16[4,112,128]{2,1,0:T(8,128)(2,1)S(1)} %pair.1.refs_0_), channel_id=1, source_target_pairs={{0,16},{1,17},{2,18},{3,19},{4,20},{5,21},{6,22},{7,23},{8,24},{9,... | collective-permute-start | bytes 344072 | tf_op jit(solution)/shard_map/ppermute | solution.py:450
  38.1 9.4 %collective-permute-start.6 = (s16[4,112,128]{2,1,0:T(8,128)(2,1)S(1)}, s16[4,112,128]{2,1,0:T(8,128)(2,1)S(1)}, u32[]{:S(2)}, u32[]{:S(2)}) collective-permute-start(s16[4,112,128]{2,1,0:T(8,128)(2,1)S(1)} %pair.1.refs_0_), channel_id=1, source_target_pairs={{0,8},{1,9},{2,10},{3,11},{4,12},{5,13},{6,14},{7,15},{8,16},{9,17... | collective-permute-start | bytes 344072 | tf_op jit(solution)/shard_map/ppermute | solution.py:450
  47.8 8.2 %collective-permute-start.11 = (s16[4,112,128]{2,1,0:T(8,128)(2,1)S(1)}, s16[4,112,128]{2,1,0:T(8,128)(2,1)S(1)}, u32[]{:S(2)}, u32[]{:S(2)}) collective-permute-start(s16[4,112,128]{2,1,0:T(8,128)(2,1)S(1)} %total.1), channel_id=1, source_target_pairs={{0,6},{1,7},{2,4},{3,5},{4,2},{5,3},{6,0},{7,1},{8,14},{9,15},{10,... | collective-permute-start | bytes 344072 | tf_op jit(solution)/shard_map/ppermute | solution.py:450
  51.9 5.1 %collective-permute-start.10 = (s16[4,112,128]{2,1,0:T(8,128)(2,1)S(1)}, s16[4,112,128]{2,1,0:T(8,128)(2,1)S(1)}, u32[]{:S(2)}, u32[]{:S(2)}) collective-permute-start(s16[4,112,128]{2,1,0:T(8,128)(2,1)S(1)} %total.1), channel_id=1, source_target_pairs={{0,2},{1,3},{2,0},{3,1},{4,6},{5,7},{6,4},{7,5},{8,10},{9,11},{10,... | collective-permute-start | bytes 344072 | tf_op jit(solution)/shard_map/ppermute | solution.py:450
  51.9 5.1 %collective-permute-start.9 = (s16[4,112,128]{2,1,0:T(8,128)(2,1)S(1)}, s16[4,112,128]{2,1,0:T(8,128)(2,1)S(1)}, u32[]{:S(2)}, u32[]{:S(2)}) collective-permute-start(s16[4,112,128]{2,1,0:T(8,128)(2,1)S(1)} %total.1), channel_id=1, source_target_pairs={{0,4},{1,5},{2,6},{3,7},{4,0},{5,1},{6,2},{7,3},{8,12},{9,13},{10,... | collective-permute-start | bytes 344072 | tf_op jit(solution)/shard_map/ppermute | solution.py:450
  57.0 1.9 %collective-permute-start.12 = (s16[16,112,128]{2,1,0:T(8,128)(2,1)S(1)}, s16[16,112,128]{2,1,0:T(8,128)(2,1)S(1)}, u32[]{:S(2)}, u32[]{:S(2)}) collective-permute-start(s16[16,112,128]{2,1,0:T(8,128)(2,1)S(1)} %pad_add_fusion.mine), channel_id=1, source_target_pairs={{0,1},{1,0},{2,3},{3,2},{4,5},{5,4},{6,7},{7,6},{8,9},{9,8},{10,11... | collective-permute-start | bytes 1376264 | tf_op jit(solution)/shard_map/ppermute | solution.py:499

commit v7 on v5

--- a/solution.py
+++ b/solution.py
@@ -11,6 +11,7 @@
 BF16 = jnp.bfloat16
 IDX_ROWS = 8
 LANES = 128
+SOURCES = 4
 VMEM = pl.BlockSpec(memory_space=pltpu.VMEM)
 SMEM = pl.BlockSpec(memory_space=pltpu.SMEM)
 HBM = pl.BlockSpec(memory_space=pltpu.HBM)
@@ -138,9 +139,9 @@
     idx_refs, refs = refs[:replicas], refs[replicas:]
     (query_v, lhs_v, rel_v, received), refs = refs[:4], refs[4:]
     out_lhs, refs = refs[0], refs[1:]
-    (keep, send), refs = (refs[:2], refs[2:]) if direct else ((None, refs[0]), refs[1:])
+    outs, refs = (refs[:SOURCES], refs[SOURCES:]) if direct else (refs[:1], refs[1:])
     table_f, table_t, query_s, acc_rel, acc_lhs, acc_tab, wide_t, mixed = refs[:8]
-    codes_s, powers_s, tables_s, table_powers_s = refs[8:]
+    codes_s, powers_s, tables_s = refs[8:]
     edges = idx_refs[0].shape[1]
     dim = query_v.shape[0]
     rows = out_lhs.shape[1]
@@ -207,58 +208,65 @@
         acc_tab[:, :slots] + acc_tab[:, slots : 2 * slots] + acc_tab[:, 2 * slots :]
     )
     table_codes, table_powers = encode(jnp.transpose(wide_t[...]), 1)
-    table_powers = jnp.broadcast_to(table_powers, table_codes.shape)
-    mixed[...] = jnp.zeros(mixed.shape, jnp.int32)
+    spare = iota(table_codes.shape, 1) >= narrow
+    tables_s[...] = jnp.where(spare, table_powers, table_codes)
     codes_s[...] = codes
     powers_s[...] = powers
-    tables_s[...] = table_codes
-    table_powers_s[...] = table_powers
-    places = rows_of(narrow, cap)
-    for h in range(workers):
-        if direct:
-            turn, z = h // (workers // 2), h % (workers // 2)
-            o = z * 2 + lax.rem(place[0] + turn, 2)
-            lane = pl.ds(pl.multiple_of(o * block, block), block)
-            target = (keep if turn == 0 else send).at[z]
-        else:
-            o, lane, target = h, slice(h * block, (h + 1) * block), send.at[h]
+    mixed[...] = jnp.zeros(mixed.shape, jnp.int32)
+    power_row = narrow + SOURCES * cap
+    dom = place[0]
+
+    def write(target, o, lane):
         mixed[:narrow, :block] = codes_s[:, lane]
         for c in range(cap):
-            for ref, row in ((tables_s, places[0]), (table_powers_s, places[2])):
-                mixed[row + c : row + c + 1, :] = ref[pl.ds(o * cap + c, 1), :]
-        mixed[places[4] : places[4] + 1, :block] = powers_s[0:1, lane]
+            mixed[narrow + c : narrow + c + 1, :] = tables_s[pl.ds(o * cap + c, 1), :]
+        mixed[power_row : power_row + 1, :block] = powers_s[0:1, lane]
         target[...] = mixed[...].astype(jnp.int16)
 
-
-def rows_of(narrow, cap):
-    return [narrow + n * cap for n in range(5)]
-
-
-def pair_kernel(narrow, cap, block, keep, got, out, mixed):
-    places = rows_of(narrow, cap)
+    if direct:
+        for h in range(SOURCES):
+            for top in range(2):
+                o = top * 4 + flipped(dom % 4, h)
+                write(outs[h].at[top], o, pl.ds(pl.multiple_of(o * block, block), block))
+    else:
+        for o in range(workers):
+            write(outs[0].at[o], o, slice(o * block, (o + 1) * block))
+
+
+def flipped(index, mask):
+    out, bit = index * 0, 1
+    while bit < 4:
+        out = out + bit * lax.rem(index // bit + (mask // bit) % 2, 2)
+        bit *= 2
+    return out
+
+
+def quad_kernel(narrow, cap, *refs):
+    parts, out, mixed = refs[:-2], refs[-2], refs[-1]
+    power = slice(narrow + SOURCES * cap, narrow + SOURCES * cap + 1)
     mixed[...] = jnp.zeros(mixed.shape, jnp.int32)
-    for z in range(keep.shape[0]):
-        ours, theirs = keep[z].astype(jnp.int32), got[z].astype(jnp.int32)
-        power = slice(places[4], places[4] + 1)
-        total = decode(ours[:narrow], ours[power]) + decode(theirs[:narrow], theirs[power])
+    for top in range(out.shape[0]):
+        total = jnp.zeros((narrow, out.shape[2]), F32)
+        for n, part in enumerate(parts):
+            both = part[top].astype(jnp.int32)
+            total += decode(both[:narrow], both[power])
+            row = narrow + n * cap
+            mixed[row : row + cap, :] = both[narrow : narrow + cap]
         mixed[:narrow, :], mixed[power, :] = encode(total, 0)
-        for n in (0, 2):
-            mixed[places[n] : places[n + 1], :] = ours[places[n] : places[n + 1]]
-            mixed[places[n + 1] : places[n + 2], :] = theirs[places[n] : places[n + 1]]
-        out[z] = mixed[...].astype(jnp.int16)
+        out[top] = mixed[...].astype(jnp.int16)
 
 
 def sum_kernel(scale, narrow, cap, block, *refs):
     parts, out, mixed = refs[:-2], refs[-2], refs[-1]
-    power = slice(narrow + 4 * cap, narrow + 4 * cap + 1)
+    power = slice(narrow + SOURCES * cap, narrow + SOURCES * cap + 1)
     mixed[...] = jnp.zeros(mixed.shape, jnp.int32)
-    for z in range(out.shape[0]):
+    for top in range(out.shape[0]):
         total = jnp.zeros((narrow, block), F32)
         for part in parts:
-            both = part[z].astype(jnp.int32)
+            both = part[top].astype(jnp.int32)
             total += decode(both[:narrow, :block], both[power, :block])
         mixed[:narrow, :block], mixed[power, :block] = encode(total * F32(scale), 0)
-        out[z] = mixed[...].astype(jnp.int16)
+        out[top] = mixed[...].astype(jnp.int16)
 
 
 def entity_kernel(direct, narrow, place, serve, lhs, *refs):
@@ -266,19 +274,18 @@
     cap, workers = serve.shape[1], serve.shape[2]
     rows = out.shape[1]
     lane = iota((1, rows), 1)
-    places = rows_of(narrow, cap)
     for h in range(workers):
         if direct:
-            turn, hop = h % 2, h // 2
-            z = place[0] // 2
-            both = recv[hop][z].astype(jnp.int32)
-            far = lax.rem(z - hop + len(recv), len(recv))
-            worker = far * 2 + lax.rem(place[0] + turn, 2)
+            turn, hop = h % SOURCES, h // SOURCES
+            mine = place[0] // 4
+            both = recv[hop][mine].astype(jnp.int32)
+            worker = lax.rem(mine + hop, 2) * 4 + flipped(place[0] % 4, turn)
         else:
             turn, both, worker = 0, recv[0][h].astype(jnp.int32), h
-        span = slice(h * cap, (h + 1) * cap)
-        terms[span, :] = decode(
-            both[places[turn] : places[turn + 1]], both[places[turn + 2] : places[turn + 3]]
+        row = narrow + turn * cap
+        both = both[row : row + cap]
+        terms[h * cap : (h + 1) * cap, :] = jnp.where(
+            iota(both.shape, 1) < narrow, decode(both, both[:, narrow : narrow + 1]), 0.0
         )
         for c in range(cap):
             spot = jnp.where(lane == serve[0, c, worker], 1.0, 0.0).astype(F32)
@@ -289,19 +296,30 @@
     out[...] = lhs[...] + added[:narrow]
 
 
-def spread_kernel(workers, replicas, narrow, power_row, block, place, mine, other, out):
-    nrel = out.shape[1]
-    depth = workers // 2
-    for o in range(workers):
-        for r in range(replicas):
-            over_y = lax.rem(place[0] + o, 2)
-            over_x = lax.rem(place[1] // 2 + r // 2, 2)
-            spot = (over_y + 2 * over_x) * depth + o // 2
-            here = lax.rem(place[1], 2) == r % 2
-            both = jnp.where(here, mine[spot].astype(jnp.int32), other[spot].astype(jnp.int32))
+def spread_kernel(workers, replicas, narrow, power_row, block, place, mine, other, out, whole, sems):
+    dim, nrel = out.shape
+    dom, rep = place[0], place[1]
+    here = lax.rem(rep, 2)
+    moves, start = [], 0
+    for r in range(replicas):
+        for o in range(workers):
+            over_low = lax.rem(dom // 2 + o // 2, 2)
+            over_y = lax.rem(dom + o, 2)
+            over_x = lax.rem(rep // 2 + r // 2, 2)
+            spot = (over_y + 2 * over_x) * 4 + over_low * 2 + o // 4
+            both = jnp.where(
+                here == r % 2, mine[spot].astype(jnp.int32), other[spot].astype(jnp.int32)
+            )
             value = decode(both[:narrow], both[power_row : power_row + 1])
             end = min((o + 1) * block, nrel)
-            out[r * narrow : (r + 1) * narrow, o * block : end] = value[:, : end - o * block]
+            whole[r * narrow : (r + 1) * narrow, o * block : end] = value[:, : end - o * block]
+        end = (r + 1) * narrow // 8 * 8 if r + 1 < replicas else dim
+        band = slice(start, end)
+        moves.append(pltpu.make_async_copy(whole.at[band], out.at[band], sems.at[r]))
+        moves[-1].start()
+        start = end
+    for move in moves:
+        move.wait()
 
 
 def turned(size, hop):
@@ -323,7 +341,7 @@
     pad_rel = up(max(nrel, workers * block), LANES)
     offsets = sorted({(narrow * r) % 8 for r in range(replicas)})
     window = up(narrow + offsets[-1], 8)
-    height = up(narrow + 4 * cap + 1, 16)
+    height = up(narrow + SOURCES * cap + 1, 16)
     ent_t, rel_t = entities.T, relation.T
     serve_t = jnp.transpose(serve_ids, (0, 2, 1))
     place = jnp.stack([lax.axis_index("dom"), lax.axis_index("rep")]).astype(jnp.int32)
@@ -381,8 +399,7 @@
         tuple(offsets),
     )
     lanes = max(up(block, LANES), up(narrow, LANES))
-    half = workers // 2
-    outs = [half, half] if direct else [workers]
+    outs = [2] * SOURCES if direct else [workers]
     sizes = [jax.ShapeDtypeStruct((n, height, lanes), jnp.int16) for n in outs]
     lhs_part, *sent = pl.pallas_call(
         functools.partial(main_kernel, cfg),
@@ -401,33 +418,31 @@
             pltpu.VMEM((narrow, pad_rel), jnp.int32),
             pltpu.VMEM((1, pad_rel), jnp.int32),
             pltpu.VMEM((slots, lanes), jnp.int32),
-            pltpu.VMEM((slots, lanes), jnp.int32),
         ],
         compiler_params=params(),
         name="edges",
     )(place, *held, query, lhs_rows, rel_rows, received)
 
-    def swap(array, over_z=0, over_y=0, over_x=0):
+    def swap(array, dom_bits=0, rep_bits=0):
         pairs = []
         for o in range(workers):
             for r in range(replicas):
-                z, y, x = (o // 2 + over_z) % half, (o + over_y) % 2, (r // 2 + over_x) % 2
-                pairs.append((o * replicas + r, (z * 2 + y) * replicas + x * 2 + r % 2))
+                pairs.append((o * replicas + r, (o ^ dom_bits) * replicas + (r ^ rep_bits)))
         return lax.ppermute(array, ("dom", "rep"), pairs)
 
     stack = jax.ShapeDtypeStruct((outs[0], height, lanes), jnp.int16)
     mixed = [pltpu.VMEM((height, lanes), jnp.int32)]
     if direct:
         summed = pl.pallas_call(
-            functools.partial(pair_kernel, narrow, cap, block),
+            functools.partial(quad_kernel, narrow, cap),
             out_shape=stack,
-            in_specs=[VMEM] * 2,
+            in_specs=[VMEM] * SOURCES,
             out_specs=VMEM,
             scratch_shapes=mixed,
             compiler_params=params(),
-            name="pair",
-        )(sent[0], swap(sent[1], over_y=1))
-        recv = [summed] + [swap(summed, over_z=hop) for hop in range(1, half)]
+            name="quad",
+        )(sent[0], *[swap(sent[n], n) for n in range(1, SOURCES)])
+        recv = [summed, swap(summed, 4)]
         parts = recv
     else:
         recv = [lax.all_to_all(sent[0], "dom", 0, 0, tiled=True)]
@@ -455,11 +470,11 @@
         name="entity",
     )(place, serve_t, lhs_part, *recv)
 
-    power_row = narrow + 4 * cap
+    power_row = narrow + SOURCES * cap
     if direct:
+        base = jnp.concatenate([chunk, swap(chunk, 2)], axis=0)
         base = jnp.concatenate(
-            [chunk, swap(chunk, over_y=1), swap(chunk, over_x=1), swap(chunk, over_y=1, over_x=1)],
-            axis=0,
+            [base, swap(base, 1), swap(base, 0, 2), swap(base, 1, 2)], axis=0
         )
         base, entity_grad = lax.optimization_barrier((base, entity_grad))
         swapped = lax.ppermute(base, "rep", [(i, i ^ 1) for i in range(replicas)])
@@ -467,7 +482,11 @@
             functools.partial(spread_kernel, workers, replicas, narrow, power_row, block),
             out_shape=jax.ShapeDtypeStruct((dim, nrel), F32),
             in_specs=[SMEM] + [VMEM] * 2,
-            out_specs=VMEM,
+            out_specs=HBM,
+            scratch_shapes=[
+                pltpu.VMEM((dim, nrel), F32),
+                pltpu.SemaphoreType.DMA((replicas,)),
+            ],
             compiler_params=params(),
             name="spread",
         )(place, base, swapped)

time: 57.3 us -> 56.6 us (0.988)
  starting transfers between devices: 19.7 us -> 18.9 us
    ppermute x7 -> x8, starting transfers between devices: 10.5 us -> 9.73 us  [swap(): return lax.ppermute(array, ('dom', 'rep'), pairs)]
    ppermute x7 -> x8, waiting for transfers between devices: 16 us -> 16.4 us  [swap(): return lax.ppermute(array, ('dom', 'rep'), pairs)]
    unnamed x10 -> x14, local copies, waits for them, and re-layouts: 3.08 us -> 3.13 us
  transfers between devices with their start and end apart: 12 -> 13, of which waited for: 7 -> 7; matrix products, arithmetic and copies ran while one was open for 0% -> 0% of each run, Pallas kernels for 11% -> 11%
where the time goes in v7:
time: 56.6 us; the launch traced here: 56.2 us
  starting transfers between devices  18.9 us (33%)
  waiting for transfers between devices  18.2 us (32%)
  Pallas kernels  14.5 us (26%)
  local copies, waits for them, and re-layouts  3.15 us (6%)
  between operations  1.4 us (2%)
    ppermute x8, waiting for transfers between devices, swap(): return lax.ppermute(array, ('dom', 'rep'), pairs)  16.4 us
    ppermute x8, starting transfers between devices, swap(): return lax.ppermute(array, ('dom', 'rep'), pairs)  9.73 us
    all_to_all x1, starting transfers between devices, shards(): received = lax.all_to_all(served, 'dom', 0, 0, tiled=True)  5.84 us
    pallas_call x1, Pallas kernels, shards(): pl.pallas_call(functools.partial(gather_kernel, (replicas, nrel, pad_rel,...  4.62 us
    pallas_call x1, Pallas kernels, shards(): pl.pallas_call(functools.partial(main_kernel, cfg), out_shape=[jax.ShapeD...  4.42 us
    ppermute x3, starting transfers between devices, shards(): held.append(lax.ppermute(idx, 'rep', turned(replicas, hop)))  3.23 us
    unnamed x14, local copies, waits for them, and re-layouts  3.13 us
    pallas_call x1, Pallas kernels, shards(): pl.pallas_call(functools.partial(spread_kernel, workers, replicas, narrow...  1.84 us
  transfers between devices with their start and end apart: 13, of which 7 were waited for; matrix products, arithmetic and copies ran while one was open for 0% of the time, Pallas kernels for 11%

profile of v7, /device:TPU:0, one launch (start us, length us, event | category | flops | bytes accessed | tf_op | source)
XLA Modules:
  0.0 56.2 jit_solution(15362065978950004449)
XLA Ops:
  1.3 1.8 %prep.1 = (s32[8,512]{1,0:T(8,128)}, f32[8,2,400]{2,1,0:T(2,128)}) custom-call(s32[1,2,8]{2,1,0:T(2,128)} %bitcast.9, s32[1,1]{1,0:T(1,128)S(6)} %copy.14.count, bf16[400,256]{1,0:T(8,128)(2,1)} %bitcast.7, s32[1,1,512]{2,1,0:T(1,128)} %src.1, s32[1,1,512]{2,1,0:T(1,128)} %rel.1, s32[1,1,512]{2,1,0:T(1,128)} %dst.1, s32[1,1,2,384]{3,2,1,0:T(2,128)} %neg.1), custom_call_target="tpu_custom_call" | custom-call | tf_op jit(solution)/shard_map/prep/pallas_call | solution.py:349
  3.1 2.4 %collective-permute-start.2 = (s32[8,512]{1,0:T(8,128)}, s32[8,512]{1,0:T(8,128)S(1)}, u32[]{:S(2)}, u32[]{:S(2)}) collective-permute-start(s32[8,512]{1,0:T(8,128)} %get-tuple-element.14.refs_0_), channel_id=1, source_target_pairs={{0,3},{1,0},{2,1},{3,2},{4,7},{5,4},{6,5},{7,6},{8,11},{9,8},{10,9... | collective-permute-start | bytes 49160 | tf_op jit(solution)/shard_map/ppermute | solution.py:374
  5.5 0.6 %collective-permute-start.1 = (s32[8,512]{1,0:T(8,128)}, s32[8,512]{1,0:T(8,128)S(1)}, u32[]{:S(2)}, u32[]{:S(2)}) collective-permute-start(s32[8,512]{1,0:T(8,128)} %get-tuple-element.14.refs_0_), channel_id=1, source_target_pairs={{0,2},{1,3},{2,0},{3,1},{4,6},{5,7},{6,4},{7,5},{8,10},{9,11},{10,... | collective-permute-start | bytes 49160 | tf_op jit(solution)/shard_map/ppermute | solution.py:374
  6.2 0.2 collective-permute-start
  6.3 5.8 %all-to-all-start = ((f32[8,2,400]{2,1,0:T(2,128)}), f32[8,2,400]{2,1,0:T(2,128)S(1)}, u32[]{:S(2)}, u32[]{:S(2)}) async-start(f32[8,2,400]{2,1,0:T(2,128)} %get-tuple-element.18), calls=%async_computation | async-start | bytes 65536 | tf_op jit(solution)/shard_map/all_to_all | solution.py:375
  12.2 0.1 pad_add_fusion.1.place
  12.2 0.0 collective-permute-done.2.refs_3_
  12.2 0.0 collective-permute-done.1.refs_2_
  12.2 0.0 collective-permute-done.refs_1_
  12.3 0.0 copy-start
  12.3 0.9 %copy-done = bf16[256,400]{0,1:T(8,128)(2,1)S(1)} copy-done((bf16[256,400]{0,1:T(8,128)(2,1)S(1)}, bf16[256,400]{0,1:T(8,128)(2,1)}, u32[]{:S(2)}) %copy-start) | copy-done | bytes 204824
  13.2 0.0 copy-start.1
  13.2 0.7 %copy-done.1 = s32[8,512]{1,0:T(8,128)S(1)} copy-done((s32[8,512]{1,0:T(8,128)S(1)}, s32[8,512]{1,0:T(8,128)}, u32[]{:S(2)}) %copy-start.1) | copy-done | bytes 16408
  13.9 0.0 copy-start.4
  13.9 1.4 %copy-done.4 = f32[1000,400]{0,1:T(8,128)S(1)} copy-done((f32[1000,400]{0,1:T(8,128)S(1)}, f32[1000,400]{0,1:T(8,128)}, u32[]{:S(2)}) %copy-start.4) | copy-done | bytes 1600024
  15.3 0.0 copy-start.2
  15.3 4.6 %gather.1 = (bf16[400,2048]{1,0:T(8,128)(2,1)S(1)}, f32[104,2048]{1,0:T(8,128)S(1)}, f32[104,2048]{1,0:T(8,128)S(1)}) custom-call(s32[2]{0:T(128)S(1)} %pad_add_fusion.1.place, s32[8,512]{1,0:T(8,128)S(1)} %copy-done.1, s32[8,512]{1,0:T(8,128)S(1)} %collective-permute-done.refs_1_, s32[8,512]{1,0:T(8,128)S(1)} %collective-permute-done.1.refs_2_, ...), custom_call_target="tpu_custom_call" | custom-call | flops 3774873600 | bytes 6553600 | tf_op jit(solution)/shard_map/gather/pallas_call | solution.py:378
  20.0 0.0 all-to-all-done.refs_7_
  20.0 0.0 copy-done.2
  20.0 0.0 copy-start.3
  20.0 4.4 %edges.1 = (f32[100,256]{1,0:T(8,128)S(1)}, s16[2,112,128]{2,1,0:T(8,128)(2,1)S(1)}, s16[2,112,128]{2,1,0:T(8,128)(2,1)S(1)}, s16[2,112,128]{2,1,0:T(8,128)(2,1)S(1)}, s16[2,112,128]{2,1,0:T(8,128)(2,1)S(1)}) custom-call(s32[2]{0:T(128)S(1)} %pad_add_fusion.1.place, s32[8,512]{1,0:T(8,128)S(1)} %copy-done.2, s32[8,512]{1,0:T(8,128)S(1)} %collective-permute-done.refs_1_, ...), custom_call_target="tpu_custom_call" | custom-call | tf_op jit(solution)/shard_map/edges/pallas_call | solution.py:404
  24.4 2.1 %collective-permute-start.3 = (s16[2,112,128]{2,1,0:T(8,128)(2,1)S(1)}, s16[2,112,128]{2,1,0:T(8,128)(2,1)S(1)}, u32[]{:S(2)}, u32[]{:S(2)}) collective-permute-start(s16[2,112,128]{2,1,0:T(8,128)(2,1)S(1)} %get-tuple-element.20), channel_id=1, source_target_pairs={{0,4},{1,5},{2,6},{3,7},{4,0},{5,1},{6,2},{7,3},{8,12},{9,13},{10,... | collective-permute-start | bytes 172040 | tf_op jit(solution)/shard_map/ppermute | solution.py:431
  26.5 1.5 %collective-permute-start.4 = (s16[2,112,128]{2,1,0:T(8,128)(2,1)S(1)}, s16[2,112,128]{2,1,0:T(8,128)(2,1)S(1)}, u32[]{:S(2)}, u32[]{:S(2)}) collective-permute-start(s16[2,112,128]{2,1,0:T(8,128)(2,1)S(1)} %get-tuple-element.21), channel_id=1, source_target_pairs={{0,8},{1,9},{2,10},{3,11},{4,12},{5,13},{6,14},{7,15},{8,0},{9,1},... | collective-permute-start | bytes 172040 | tf_op jit(solution)/shard_map/ppermute | solution.py:431
  28.0 0.1 collective-permute-start.5
  28.1 1.1 %collective-permute-done.3.refs_1_ = s16[2,112,128]{2,1,0:T(8,128)(2,1)S(1)} collective-permute-done((s16[2,112,128]{2,1,0:T(8,128)(2,1)S(1)}, s16[2,112,128]{2,1,0:T(8,128)(2,1)S(1)}, u32[]{:S(2)}, u32[]{:S(2)}) %collective-permute-start.3) | collective-permute-done | bytes 57376 | tf_op jit(solution)/shard_map/ppermute | solution.py:431
  29.2 1.7 %collective-permute-done.4.refs_2_ = s16[2,112,128]{2,1,0:T(8,128)(2,1)S(1)} collective-permute-done((s16[2,112,128]{2,1,0:T(8,128)(2,1)S(1)}, s16[2,112,128]{2,1,0:T(8,128)(2,1)S(1)}, u32[]{:S(2)}, u32[]{:S(2)}) %collective-permute-start.4) | collective-permute-done | bytes 57376 | tf_op jit(solution)/shard_map/ppermute | solution.py:431
  30.9 2.1 %collective-permute-done.5.refs_3_ = s16[2,112,128]{2,1,0:T(8,128)(2,1)S(1)} collective-permute-done((s16[2,112,128]{2,1,0:T(8,128)(2,1)S(1)}, s16[2,112,128]{2,1,0:T(8,128)(2,1)S(1)}, u32[]{:S(2)}, u32[]{:S(2)}) %collective-permute-start.5) | collective-permute-done | bytes 57376 | tf_op jit(solution)/shard_map/ppermute | solution.py:431
  33.0 0.1 quad.1.refs_0_
  33.2 2.4 %collective-permute-start.6 = (s16[2,112,128]{2,1,0:T(8,128)(2,1)S(1)}, s16[2,112,128]{2,1,0:T(8,128)(2,1)S(1)}, u32[]{:S(2)}, u32[]{:S(2)}) collective-permute-start(s16[2,112,128]{2,1,0:T(8,128)(2,1)S(1)} %quad.1.refs_0_), channel_id=1, source_target_pairs={{0,16},{1,17},{2,18},{3,19},{4,20},{5,21},{6,22},{7,23},{8,24},{9,... | collective-permute-start | bytes 172040 | tf_op jit(solution)/shard_map/ppermute | solution.py:431
  35.6 3.3 %collective-permute-done.6.refs_1_ = s16[2,112,128]{2,1,0:T(8,128)(2,1)S(1)} collective-permute-done((s16[2,112,128]{2,1,0:T(8,128)(2,1)S(1)}, s16[2,112,128]{2,1,0:T(8,128)(2,1)S(1)}, u32[]{:S(2)}, u32[]{:S(2)}) %collective-permute-start.6) | collective-permute-done | bytes 57376 | tf_op jit(solution)/shard_map/ppermute | solution.py:431
  38.9 0.1 total.1
  39.0 0.1 collective-permute-start.7
  39.2 4.1 %collective-permute-done.7 = s16[2,112,128]{2,1,0:T(8,128)(2,1)S(1)} collective-permute-done((s16[2,112,128]{2,1,0:T(8,128)(2,1)S(1)}, s16[2,112,128]{2,1,0:T(8,128)(2,1)S(1)}, u32[]{:S(2)}, u32[]{:S(2)}) %collective-permute-start.7) | collective-permute-done | bytes 57376 | tf_op jit(solution)/shard_map/ppermute | solution.py:431
  43.3 0.2 collective-permute-start.8
  43.5 0.0 copy-done.3
  43.5 1.6 %entity.1 = f32[100,256]{1,0:T(8,128)} custom-call(s32[2]{0:T(128)S(1)} %pad_add_fusion.1.place, s32[1,2,8]{2,1,0:T(2,128)S(1)} %bitcast.10, f32[100,256]{1,0:T(8,128)S(1)} %get-tuple-element.23.lhs, s16[2,112,128]{2,1,0:T(8,128)(2,1)S(1)} %quad.1.refs_0_, s16[2,112,128]{2,1,0:T(8,128)(2,1)S(1)} %collective-permute-done.6.refs_1_), custom_call_target="tpu_custom_call" | custom-call | flops 1000000000 | bytes 1000000 | tf_op jit(solution)/shard_map/entity/pallas_call | solution.py:462
  45.1 2.6 %collective-permute-start.10 = (s16[4,112,128]{2,1,0:T(8,128)(2,1)S(1)}, s16[4,112,128]{2,1,0:T(8,128)(2,1)S(1)}, u32[]{:S(2)}, u32[]{:S(2)}) collective-permute-start(s16[4,112,128]{2,1,0:T(8,128)(2,1)S(1)} %pad_add_fusion), channel_id=1, source_target_pairs={{0,6},{1,7},{2,4},{3,5},{4,2},{5,3},{6,0},{7,1},{8,14},{9,15},{10,... | collective-permute-start | bytes 344072 | tf_op jit(solution)/shard_map/ppermute | solution.py:431
  47.6 0.8 %collective-permute-start.9 = (s16[4,112,128]{2,1,0:T(8,128)(2,1)S(1)}, s16[4,112,128]{2,1,0:T(8,128)(2,1)S(1)}, u32[]{:S(2)}, u32[]{:S(2)}) collective-permute-start(s16[4,112,128]{2,1,0:T(8,128)(2,1)S(1)} %pad_add_fusion), channel_id=1, source_target_pairs={{0,2},{1,3},{2,0},{3,1},{4,6},{5,7},{6,4},{7,5},{8,10},{9,11},{10,... | collective-permute-start | bytes 344072 | tf_op jit(solution)/shard_map/ppermute | solution.py:431
  48.5 0.0 collective-permute-done.8
  48.5 3.9 %collective-permute-done.9 = s16[4,112,128]{2,1,0:T(8,128)(2,1)S(1)} collective-permute-done((s16[4,112,128]{2,1,0:T(8,128)(2,1)S(1)}, s16[4,112,128]{2,1,0:T(8,128)(2,1)S(1)}, u32[]{:S(2)}, u32[]{:S(2)}) %collective-permute-start.9) | collective-permute-done | bytes 114720 | tf_op jit(solution)/shard_map/ppermute | solution.py:431
  52.5 0.0 collective-permute-done.10
  52.5 0.1 collective-permute-start.11
  52.6 1.8 %collective-permute-done.11.other = s16[16,112,128]{2,1,0:T(8,128)(2,1)S(1)} collective-permute-done((s16[16,112,128]{2,1,0:T(8,128)(2,1)S(1)}, s16[16,112,128]{2,1,0:T(8,128)(2,1)S(1)}, u32[]{:S(2)}, u32[]{:S(2)}) %collective-permute-start.11) | collective-permute-done | bytes 458784 | tf_op jit(solution)/shard_map/ppermute | solution.py:480
  54.4 1.8 %spread.1 = f32[400,1000]{1,0:T(8,128)} custom-call(s32[2]{0:T(128)S(1)} %pad_add_fusion.1.place, s16[16,112,128]{2,1,0:T(8,128)(2,1)S(1)} %constant_dynamic-update-slice_fusion.mine, s16[16,112,128]{2,1,0:T(8,128)(2,1)S(1)} %collective-permute-done.11.other), custom_call_target="tpu_custom_call" | custom-call | tf_op jit(solution)/shard_map/spread/pallas_call | solution.py:481
  (6 shorter events, 0.1 us)
Async XLA Ops:
  3.1 9.1 %collective-permute-start.2 = (s32[8,512]{1,0:T(8,128)}, s32[8,512]{1,0:T(8,128)S(1)}, u32[]{:S(2)}, u32[]{:S(2)}) collective-permute-start(s32[8,512]{1,0:T(8,128)} %get-tuple-element.14.refs_0_), channel_id=1, source_target_pairs={{0,3},{1,0},{2,1},{3,2},{4,7},{5,4},{6,5},{7,6},{8,11},{9,8},{10,9... | collective-permute-start | bytes 49160 | tf_op jit(solution)/shard_map/ppermute | solution.py:374
  5.5 6.7 %collective-permute-start.1 = (s32[8,512]{1,0:T(8,128)}, s32[8,512]{1,0:T(8,128)S(1)}, u32[]{:S(2)}, u32[]{:S(2)}) collective-permute-start(s32[8,512]{1,0:T(8,128)} %get-tuple-element.14.refs_0_), channel_id=1, source_target_pairs={{0,2},{1,3},{2,0},{3,1},{4,6},{5,7},{6,4},{7,5},{8,10},{9,11},{10,... | collective-permute-start | bytes 49160 | tf_op jit(solution)/shard_map/ppermute | solution.py:374
  6.2 6.1 %collective-permute-start = (s32[8,512]{1,0:T(8,128)}, s32[8,512]{1,0:T(8,128)S(1)}, u32[]{:S(2)}, u32[]{:S(2)}) collective-permute-start(s32[8,512]{1,0:T(8,128)} %get-tuple-element.14.refs_0_), channel_id=1, source_target_pairs={{0,1},{1,2},{2,3},{3,0},{4,5},{5,6},{6,7},{7,4},{8,9},{9,10},{10,1... | collective-permute-start | bytes 49160 | tf_op jit(solution)/shard_map/ppermute | solution.py:374
  6.3 13.6 %all-to-all-start = ((f32[8,2,400]{2,1,0:T(2,128)}), f32[8,2,400]{2,1,0:T(2,128)S(1)}, u32[]{:S(2)}, u32[]{:S(2)}) async-start(f32[8,2,400]{2,1,0:T(2,128)} %get-tuple-element.18), calls=%async_computation | async-start | bytes 65536 | tf_op jit(solution)/shard_map/all_to_all | solution.py:375
  12.3 0.9 %copy-start = (bf16[256,400]{0,1:T(8,128)(2,1)S(1)}, bf16[256,400]{0,1:T(8,128)(2,1)}, u32[]{:S(2)}) copy-start(bf16[256,400]{0,1:T(8,128)(2,1)} %param.8) | copy-start | bytes 614404
  13.2 0.7 %copy-start.1 = (s32[8,512]{1,0:T(8,128)S(1)}, s32[8,512]{1,0:T(8,128)}, u32[]{:S(2)}) copy-start(s32[8,512]{1,0:T(8,128)} %get-tuple-element.14.refs_0_) | copy-start | bytes 49156
  13.9 1.4 %copy-start.4 = (f32[1000,400]{0,1:T(8,128)S(1)}, f32[1000,400]{0,1:T(8,128)}, u32[]{:S(2)}) copy-start(f32[1000,400]{0,1:T(8,128)} %param.9) | copy-start | bytes 4800004
  15.3 4.6 %copy-start.2 = (s32[8,512]{1,0:T(8,128)S(1)}, s32[8,512]{1,0:T(8,128)}, u32[]{:S(2)}) copy-start(s32[8,512]{1,0:T(8,128)} %get-tuple-element.14.refs_0_) | copy-start | bytes 49156
  20.0 23.5 %copy-start.3 = (s32[1,8,2]{1,2,0:T(2,128)S(1)}, s32[1,8,2]{1,2,0:T(2,128)}, u32[]{:S(2)}) copy-start(s32[1,8,2]{1,2,0:T(2,128)} %param.10) | copy-start | bytes 196
  24.4 4.8 %collective-permute-start.3 = (s16[2,112,128]{2,1,0:T(8,128)(2,1)S(1)}, s16[2,112,128]{2,1,0:T(8,128)(2,1)S(1)}, u32[]{:S(2)}, u32[]{:S(2)}) collective-permute-start(s16[2,112,128]{2,1,0:T(8,128)(2,1)S(1)} %get-tuple-element.20), channel_id=1, source_target_pairs={{0,4},{1,5},{2,6},{3,7},{4,0},{5,1},{6,2},{7,3},{8,12},{9,13},{10,... | collective-permute-start | bytes 172040 | tf_op jit(solution)/shard_map/ppermute | solution.py:431
  26.5 4.4 %collective-permute-start.4 = (s16[2,112,128]{2,1,0:T(8,128)(2,1)S(1)}, s16[2,112,128]{2,1,0:T(8,128)(2,1)S(1)}, u32[]{:S(2)}, u32[]{:S(2)}) collective-permute-start(s16[2,112,128]{2,1,0:T(8,128)(2,1)S(1)} %get-tuple-element.21), channel_id=1, source_target_pairs={{0,8},{1,9},{2,10},{3,11},{4,12},{5,13},{6,14},{7,15},{8,0},{9,1},... | collective-permute-start | bytes 172040 | tf_op jit(solution)/shard_map/ppermute | solution.py:431
  28.0 5.1 %collective-permute-start.5 = (s16[2,112,128]{2,1,0:T(8,128)(2,1)S(1)}, s16[2,112,128]{2,1,0:T(8,128)(2,1)S(1)}, u32[]{:S(2)}, u32[]{:S(2)}) collective-permute-start(s16[2,112,128]{2,1,0:T(8,128)(2,1)S(1)} %get-tuple-element.22), channel_id=1, source_target_pairs={{0,12},{1,13},{2,14},{3,15},{4,8},{5,9},{6,10},{7,11},{8,4},{9,5},... | collective-permute-start | bytes 172040 | tf_op jit(solution)/shard_map/ppermute | solution.py:431
  33.2 5.8 %collective-permute-start.6 = (s16[2,112,128]{2,1,0:T(8,128)(2,1)S(1)}, s16[2,112,128]{2,1,0:T(8,128)(2,1)S(1)}, u32[]{:S(2)}, u32[]{:S(2)}) collective-permute-start(s16[2,112,128]{2,1,0:T(8,128)(2,1)S(1)} %quad.1.refs_0_), channel_id=1, source_target_pairs={{0,16},{1,17},{2,18},{3,19},{4,20},{5,21},{6,22},{7,23},{8,24},{9,... | collective-permute-start | bytes 172040 | tf_op jit(solution)/shard_map/ppermute | solution.py:431
  39.0 4.2 %collective-permute-start.7 = (s16[2,112,128]{2,1,0:T(8,128)(2,1)S(1)}, s16[2,112,128]{2,1,0:T(8,128)(2,1)S(1)}, u32[]{:S(2)}, u32[]{:S(2)}) collective-permute-start(s16[2,112,128]{2,1,0:T(8,128)(2,1)S(1)} %total.1), channel_id=1, source_target_pairs={{0,8},{1,9},{2,10},{3,11},{4,12},{5,13},{6,14},{7,15},{8,0},{9,1},... | collective-permute-start | bytes 172040 | tf_op jit(solution)/shard_map/ppermute | solution.py:431
  43.3 5.2 %collective-permute-start.8 = (s16[4,112,128]{2,1,0:T(8,128)(2,1)S(1)}, s16[4,112,128]{2,1,0:T(8,128)(2,1)S(1)}, u32[]{:S(2)}, u32[]{:S(2)}) collective-permute-start(s16[4,112,128]{2,1,0:T(8,128)(2,1)S(1)} %pad_add_fusion), channel_id=1, source_target_pairs={{0,4},{1,5},{2,6},{3,7},{4,0},{5,1},{6,2},{7,3},{8,12},{9,13},{10,... | collective-permute-start | bytes 344072 | tf_op jit(solution)/shard_map/ppermute | solution.py:431
  45.1 7.4 %collective-permute-start.10 = (s16[4,112,128]{2,1,0:T(8,128)(2,1)S(1)}, s16[4,112,128]{2,1,0:T(8,128)(2,1)S(1)}, u32[]{:S(2)}, u32[]{:S(2)}) collective-permute-start(s16[4,112,128]{2,1,0:T(8,128)(2,1)S(1)} %pad_add_fusion), channel_id=1, source_target_pairs={{0,6},{1,7},{2,4},{3,5},{4,2},{5,3},{6,0},{7,1},{8,14},{9,15},{10,... | collective-permute-start | bytes 344072 | tf_op jit(solution)/shard_map/ppermute | solution.py:431
  47.6 4.8 %collective-permute-start.9 = (s16[4,112,128]{2,1,0:T(8,128)(2,1)S(1)}, s16[4,112,128]{2,1,0:T(8,128)(2,1)S(1)}, u32[]{:S(2)}, u32[]{:S(2)}) collective-permute-start(s16[4,112,128]{2,1,0:T(8,128)(2,1)S(1)} %pad_add_fusion), channel_id=1, source_target_pairs={{0,2},{1,3},{2,0},{3,1},{4,6},{5,7},{6,4},{7,5},{8,10},{9,11},{10,... | collective-permute-start | bytes 344072 | tf_op jit(solution)/shard_map/ppermute | solution.py:431
  52.5 1.9 %collective-permute-start.11 = (s16[16,112,128]{2,1,0:T(8,128)(2,1)S(1)}, s16[16,112,128]{2,1,0:T(8,128)(2,1)S(1)}, u32[]{:S(2)}, u32[]{:S(2)}) collective-permute-start(s16[16,112,128]{2,1,0:T(8,128)(2,1)S(1)} %constant_dynamic-update-slice_fusion.mine), channel_id=1, source_target_pairs={{0,1},{1,0},{2,3},{3,2},{4,5},{5,4},{6,7},{7,6},{8,9},{9,8},{10,11... | collective-permute-start | bytes 1376264 | tf_op jit(solution)/shard_map/ppermute | solution.py:480

commit v8 on v7

--- a/solution.py
+++ b/solution.py
@@ -256,17 +256,19 @@
         out[top] = mixed[...].astype(jnp.int16)
 
 
-def sum_kernel(scale, narrow, cap, block, *refs):
+def sum_kernel(scale, narrow, cap, block, terms, *refs):
     parts, out, mixed = refs[:-2], refs[-2], refs[-1]
+    depth = parts[0].shape[0]
     power = slice(narrow + SOURCES * cap, narrow + SOURCES * cap + 1)
     mixed[...] = jnp.zeros(mixed.shape, jnp.int32)
-    for top in range(out.shape[0]):
-        total = jnp.zeros((narrow, block), F32)
-        for part in parts:
-            both = part[top].astype(jnp.int32)
-            total += decode(both[:narrow, :block], both[power, :block])
-        mixed[:narrow, :block], mixed[power, :block] = encode(total * F32(scale), 0)
-        out[top] = mixed[...].astype(jnp.int16)
+    for first in range(0, len(parts), terms):
+        for top in range(depth):
+            total = jnp.zeros((narrow, block), F32)
+            for part in parts[first : first + terms]:
+                both = part[top].astype(jnp.int32)
+                total += decode(both[:narrow, :block], both[power, :block])
+            mixed[:narrow, :block], mixed[power, :block] = encode(total * F32(scale), 0)
+            out[first // terms * depth + top] = mixed[...].astype(jnp.int16)
 
 
 def entity_kernel(direct, narrow, place, serve, lhs, *refs):
@@ -443,14 +445,15 @@
             name="quad",
         )(sent[0], *[swap(sent[n], n) for n in range(1, SOURCES)])
         recv = [summed, swap(summed, 4)]
-        parts = recv
+        parts = recv + [swap(summed, 2), swap(summed, 6)]
+        stack = jax.ShapeDtypeStruct((4, height, lanes), jnp.int16)
     else:
         recv = [lax.all_to_all(sent[0], "dom", 0, 0, tiled=True)]
         parts = [recv[0][w : w + 1] for w in range(workers)]
         stack = jax.ShapeDtypeStruct((1, height, lanes), jnp.int16)
     scale = 1.0 / (edges * workers * replicas)
     chunk = pl.pallas_call(
-        functools.partial(sum_kernel, scale, narrow, cap, block),
+        functools.partial(sum_kernel, scale, narrow, cap, block, 2 if direct else workers),
         out_shape=stack,
         in_specs=[VMEM] * len(parts),
         out_specs=VMEM,
@@ -459,6 +462,9 @@
         name="total",
     )(*parts)
 
+    if direct:
+        along_y = swap(chunk, 1)
+        along_y, lhs_part = lax.optimization_barrier((along_y, lhs_part))
     entity_grad = pl.pallas_call(
         functools.partial(entity_kernel, direct, narrow),
         out_shape=jax.ShapeDtypeStruct((narrow, rows), F32),
@@ -472,10 +478,7 @@
 
     power_row = narrow + SOURCES * cap
     if direct:
-        base = jnp.concatenate([chunk, swap(chunk, 2)], axis=0)
-        base = jnp.concatenate(
-            [base, swap(base, 1), swap(base, 0, 2), swap(base, 1, 2)], axis=0
-        )
+        base = jnp.concatenate([chunk, along_y, swap(chunk, 0, 2), swap(chunk, 1, 2)], axis=0)
         base, entity_grad = lax.optimization_barrier((base, entity_grad))
         swapped = lax.ppermute(base, "rep", [(i, i ^ 1) for i in range(replicas)])
         relation_t = pl.pallas_call(

time: 56.6 us -> 53.1 us (0.938)
  waiting for transfers between devices: 18.2 us -> 12.8 us
  starting transfers between devices: 18.9 us -> 20.8 us
    ppermute x8 -> x9, waiting for transfers between devices: 16.4 us -> 11 us  [swap(): return lax.ppermute(array, ('dom', 'rep'), pairs)]
    ppermute x8 -> x9, starting transfers between devices: 9.73 us -> 11.6 us  [swap(): return lax.ppermute(array, ('dom', 'rep'), pairs)]
    unnamed x14 -> x10, local copies, waits for them, and re-layouts: 3.13 us -> 3.08 us
  transfers between devices with their start and end apart: 13 -> 14, of which waited for: 7 -> 9; matrix products, arithmetic and copies ran while one was open for 0% -> 0% of each run, Pallas kernels for 11% -> 12%
where the time goes in v8:
time: 53.1 us; the launch traced here: 52.8 us
  starting transfers between devices  20.8 us (39%)
  Pallas kernels  14.6 us (27%)
  waiting for transfers between devices  12.8 us (24%)
  local copies, waits for them, and re-layouts  3.08 us (6%)
  between operations  1.37 us (3%)
    ppermute x9, starting transfers between devices, swap(): return lax.ppermute(array, ('dom', 'rep'), pairs)  11.6 us
    ppermute x9, waiting for transfers between devices, swap(): return lax.ppermute(array, ('dom', 'rep'), pairs)  11 us
    all_to_all x1, starting transfers between devices, shards(): received = lax.all_to_all(served, 'dom', 0, 0, tiled=True)  5.84 us
    pallas_call x1, Pallas kernels, shards(): pl.pallas_call(functools.partial(gather_kernel, (replicas, nrel, pad_rel,...  4.64 us
    pallas_call x1, Pallas kernels, shards(): pl.pallas_call(functools.partial(main_kernel, cfg), out_shape=[jax.ShapeD...  4.44 us
    ppermute x3, starting transfers between devices, shards(): held.append(lax.ppermute(idx, 'rep', turned(replicas, hop)))  3.23 us
    unnamed x10, local copies, waits for them, and re-layouts  3.08 us
    pallas_call x1, Pallas kernels, shards(): pl.pallas_call(functools.partial(spread_kernel, workers, replicas, narrow...  1.85 us
  transfers between devices with their start and end apart: 14, of which 9 were waited for; matrix products, arithmetic and copies ran while one was open for 0% of the time, Pallas kernels for 12%

profile of v8, /device:TPU:0, one launch (start us, length us, event | category | flops | bytes accessed | tf_op | source)
XLA Modules:
  0.0 52.8 jit_solution(9566620609501161193)
XLA Ops:
  1.3 1.8 %prep.1 = (s32[8,512]{1,0:T(8,128)}, f32[8,2,400]{2,1,0:T(2,128)}) custom-call(s32[1,2,8]{2,1,0:T(2,128)} %bitcast.9, s32[1,1]{1,0:T(1,128)S(6)} %copy.10.count, bf16[400,256]{1,0:T(8,128)(2,1)} %bitcast.7, s32[1,1,512]{2,1,0:T(1,128)} %src.1, s32[1,1,512]{2,1,0:T(1,128)} %rel.1, s32[1,1,512]{2,1,0:T(1,128)} %dst.1, s32[1,1,2,384]{3,2,1,0:T(2,128)} %neg.1), custom_call_target="tpu_custom_call" | custom-call | tf_op jit(solution)/shard_map/prep/pallas_call | solution.py:351
  3.1 2.4 %collective-permute-start.2 = (s32[8,512]{1,0:T(8,128)}, s32[8,512]{1,0:T(8,128)S(1)}, u32[]{:S(2)}, u32[]{:S(2)}) collective-permute-start(s32[8,512]{1,0:T(8,128)} %get-tuple-element.16.refs_0_), channel_id=1, source_target_pairs={{0,3},{1,0},{2,1},{3,2},{4,7},{5,4},{6,5},{7,6},{8,11},{9,8},{10,9... | collective-permute-start | bytes 49160 | tf_op jit(solution)/shard_map/ppermute | solution.py:376
  5.5 0.6 %collective-permute-start.1 = (s32[8,512]{1,0:T(8,128)}, s32[8,512]{1,0:T(8,128)S(1)}, u32[]{:S(2)}, u32[]{:S(2)}) collective-permute-start(s32[8,512]{1,0:T(8,128)} %get-tuple-element.16.refs_0_), channel_id=1, source_target_pairs={{0,2},{1,3},{2,0},{3,1},{4,6},{5,7},{6,4},{7,5},{8,10},{9,11},{10,... | collective-permute-start | bytes 49160 | tf_op jit(solution)/shard_map/ppermute | solution.py:376
  6.2 0.2 collective-permute-start
  6.3 5.8 %all-to-all-start = ((f32[8,2,400]{2,1,0:T(2,128)}), f32[8,2,400]{2,1,0:T(2,128)S(1)}, u32[]{:S(2)}, u32[]{:S(2)}) async-start(f32[8,2,400]{2,1,0:T(2,128)} %get-tuple-element.20), calls=%async_computation | async-start | bytes 65536 | tf_op jit(solution)/shard_map/all_to_all | solution.py:377
  12.2 0.1 pad_add_fusion.1.place
  12.2 0.0 collective-permute-done.2.refs_3_
  12.2 0.0 collective-permute-done.1.refs_2_
  12.2 0.0 collective-permute-done.refs_1_
  12.3 0.0 copy-start
  12.3 0.9 %copy-done = bf16[256,400]{0,1:T(8,128)(2,1)S(1)} copy-done((bf16[256,400]{0,1:T(8,128)(2,1)S(1)}, bf16[256,400]{0,1:T(8,128)(2,1)}, u32[]{:S(2)}) %copy-start) | copy-done | bytes 204824
  13.2 0.0 copy-start.1
  13.2 0.7 %copy-done.1 = s32[8,512]{1,0:T(8,128)S(1)} copy-done((s32[8,512]{1,0:T(8,128)S(1)}, s32[8,512]{1,0:T(8,128)}, u32[]{:S(2)}) %copy-start.1) | copy-done | bytes 16408
  13.9 0.0 copy-start.4
  13.9 1.4 %copy-done.4 = f32[1000,400]{0,1:T(8,128)S(1)} copy-done((f32[1000,400]{0,1:T(8,128)S(1)}, f32[1000,400]{0,1:T(8,128)}, u32[]{:S(2)}) %copy-start.4) | copy-done | bytes 1600024
  15.3 0.0 copy-start.2
  15.3 4.6 %gather.1 = (bf16[400,2048]{1,0:T(8,128)(2,1)S(1)}, f32[104,2048]{1,0:T(8,128)S(1)}, f32[104,2048]{1,0:T(8,128)S(1)}) custom-call(s32[2]{0:T(128)S(1)} %pad_add_fusion.1.place, s32[8,512]{1,0:T(8,128)S(1)} %copy-done.1, s32[8,512]{1,0:T(8,128)S(1)} %collective-permute-done.refs_1_, s32[8,512]{1,0:T(8,128)S(1)} %collective-permute-done.1.refs_2_, ...), custom_call_target="tpu_custom_call" | custom-call | flops 3774873600 | bytes 6553600 | tf_op jit(solution)/shard_map/gather/pallas_call | solution.py:380
  20.0 0.0 all-to-all-done.refs_7_
  20.0 0.0 copy-done.2
  20.0 0.0 copy-start.3
  20.0 4.4 %edges.1 = (f32[100,256]{1,0:T(8,128)S(1)}, s16[2,112,128]{2,1,0:T(8,128)(2,1)S(1)}, s16[2,112,128]{2,1,0:T(8,128)(2,1)S(1)}, s16[2,112,128]{2,1,0:T(8,128)(2,1)S(1)}, s16[2,112,128]{2,1,0:T(8,128)(2,1)S(1)}) custom-call(s32[2]{0:T(128)S(1)} %pad_add_fusion.1.place, s32[8,512]{1,0:T(8,128)S(1)} %copy-done.2, s32[8,512]{1,0:T(8,128)S(1)} %collective-permute-done.refs_1_, ...), custom_call_target="tpu_custom_call" | custom-call | tf_op jit(solution)/shard_map/edges/pallas_call | solution.py:406
  24.5 2.1 %collective-permute-start.3 = (s16[2,112,128]{2,1,0:T(8,128)(2,1)S(1)}, s16[2,112,128]{2,1,0:T(8,128)(2,1)S(1)}, u32[]{:S(2)}, u32[]{:S(2)}) collective-permute-start(s16[2,112,128]{2,1,0:T(8,128)(2,1)S(1)} %get-tuple-element.22), channel_id=1, source_target_pairs={{0,4},{1,5},{2,6},{3,7},{4,0},{5,1},{6,2},{7,3},{8,12},{9,13},{10,... | collective-permute-start | bytes 172040 | tf_op jit(solution)/shard_map/ppermute | solution.py:433
  26.6 1.5 %collective-permute-start.4 = (s16[2,112,128]{2,1,0:T(8,128)(2,1)S(1)}, s16[2,112,128]{2,1,0:T(8,128)(2,1)S(1)}, u32[]{:S(2)}, u32[]{:S(2)}) collective-permute-start(s16[2,112,128]{2,1,0:T(8,128)(2,1)S(1)} %get-tuple-element.23), channel_id=1, source_target_pairs={{0,8},{1,9},{2,10},{3,11},{4,12},{5,13},{6,14},{7,15},{8,0},{9,1},... | collective-permute-start | bytes 172040 | tf_op jit(solution)/shard_map/ppermute | solution.py:433
  28.0 0.1 collective-permute-start.5
  28.1 1.1 %collective-permute-done.3.refs_1_ = s16[2,112,128]{2,1,0:T(8,128)(2,1)S(1)} collective-permute-done((s16[2,112,128]{2,1,0:T(8,128)(2,1)S(1)}, s16[2,112,128]{2,1,0:T(8,128)(2,1)S(1)}, u32[]{:S(2)}, u32[]{:S(2)}) %collective-permute-start.3) | collective-permute-done | bytes 57376 | tf_op jit(solution)/shard_map/ppermute | solution.py:433
  29.3 1.7 %collective-permute-done.4.refs_2_ = s16[2,112,128]{2,1,0:T(8,128)(2,1)S(1)} collective-permute-done((s16[2,112,128]{2,1,0:T(8,128)(2,1)S(1)}, s16[2,112,128]{2,1,0:T(8,128)(2,1)S(1)}, u32[]{:S(2)}, u32[]{:S(2)}) %collective-permute-start.4) | collective-permute-done | bytes 57376 | tf_op jit(solution)/shard_map/ppermute | solution.py:433
  31.0 2.1 %collective-permute-done.5.refs_3_ = s16[2,112,128]{2,1,0:T(8,128)(2,1)S(1)} collective-permute-done((s16[2,112,128]{2,1,0:T(8,128)(2,1)S(1)}, s16[2,112,128]{2,1,0:T(8,128)(2,1)S(1)}, u32[]{:S(2)}, u32[]{:S(2)}) %collective-permute-start.5) | collective-permute-done | bytes 57376 | tf_op jit(solution)/shard_map/ppermute | solution.py:433
  33.1 0.1 quad.1.refs_0_
  33.2 2.4 %collective-permute-start.8 = (s16[2,112,128]{2,1,0:T(8,128)(2,1)S(1)}, s16[2,112,128]{2,1,0:T(8,128)(2,1)S(1)}, u32[]{:S(2)}, u32[]{:S(2)}) collective-permute-start(s16[2,112,128]{2,1,0:T(8,128)(2,1)S(1)} %quad.1.refs_0_), channel_id=1, source_target_pairs={{0,24},{1,25},{2,26},{3,27},{4,28},{5,29},{6,30},{7,31},{8,16},{9,... | collective-permute-start | bytes 172040 | tf_op jit(solution)/shard_map/ppermute | solution.py:433
  35.7 0.6 %collective-permute-start.7 = (s16[2,112,128]{2,1,0:T(8,128)(2,1)S(1)}, s16[2,112,128]{2,1,0:T(8,128)(2,1)S(1)}, u32[]{:S(2)}, u32[]{:S(2)}) collective-permute-start(s16[2,112,128]{2,1,0:T(8,128)(2,1)S(1)} %quad.1.refs_0_), channel_id=1, source_target_pairs={{0,8},{1,9},{2,10},{3,11},{4,12},{5,13},{6,14},{7,15},{8,0},{9,1},... | collective-permute-start | bytes 172040 | tf_op jit(solution)/shard_map/ppermute | solution.py:433
  36.2 1.5 %collective-permute-start.6 = (s16[2,112,128]{2,1,0:T(8,128)(2,1)S(1)}, s16[2,112,128]{2,1,0:T(8,128)(2,1)S(1)}, u32[]{:S(2)}, u32[]{:S(2)}) collective-permute-start(s16[2,112,128]{2,1,0:T(8,128)(2,1)S(1)} %quad.1.refs_0_), channel_id=1, source_target_pairs={{0,16},{1,17},{2,18},{3,19},{4,20},{5,21},{6,22},{7,23},{8,24},{9,... | collective-permute-start | bytes 172040 | tf_op jit(solution)/shard_map/ppermute | solution.py:433
  37.7 1.9 %collective-permute-done.8.refs_3_ = s16[2,112,128]{2,1,0:T(8,128)(2,1)S(1)} collective-permute-done((s16[2,112,128]{2,1,0:T(8,128)(2,1)S(1)}, s16[2,112,128]{2,1,0:T(8,128)(2,1)S(1)}, u32[]{:S(2)}, u32[]{:S(2)}) %collective-permute-start.8) | collective-permute-done | bytes 57376 | tf_op jit(solution)/shard_map/ppermute | solution.py:433
  39.5 0.5 collective-permute-done.7.refs_2_
  40.1 1.2 %collective-permute-done.6.refs_1_ = s16[2,112,128]{2,1,0:T(8,128)(2,1)S(1)} collective-permute-done((s16[2,112,128]{2,1,0:T(8,128)(2,1)S(1)}, s16[2,112,128]{2,1,0:T(8,128)(2,1)S(1)}, u32[]{:S(2)}, u32[]{:S(2)}) %collective-permute-start.6) | collective-permute-done | bytes 57376 | tf_op jit(solution)/shard_map/ppermute | solution.py:433
  41.3 0.2 total.1
  41.5 1.1 %collective-permute-start.9 = (s16[4,112,128]{2,1,0:T(8,128)(2,1)S(1)}, s16[4,112,128]{2,1,0:T(8,128)(2,1)S(1)}, u32[]{:S(2)}, u32[]{:S(2)}) collective-permute-start(s16[4,112,128]{2,1,0:T(8,128)(2,1)S(1)} %total.1), channel_id=1, source_target_pairs={{0,4},{1,5},{2,6},{3,7},{4,0},{5,1},{6,2},{7,3},{8,12},{9,13},{10,... | collective-permute-start | bytes 344072 | tf_op jit(solution)/shard_map/ppermute | solution.py:433
  42.6 1.6 %collective-permute-start.11 = (s16[4,112,128]{2,1,0:T(8,128)(2,1)S(1)}, s16[4,112,128]{2,1,0:T(8,128)(2,1)S(1)}, u32[]{:S(2)}, u32[]{:S(2)}) collective-permute-start(s16[4,112,128]{2,1,0:T(8,128)(2,1)S(1)} %total.1), channel_id=1, source_target_pairs={{0,6},{1,7},{2,4},{3,5},{4,2},{5,3},{6,0},{7,1},{8,14},{9,15},{10,... | collective-permute-start | bytes 344072 | tf_op jit(solution)/shard_map/ppermute | solution.py:433
  44.2 0.8 %collective-permute-start.10 = (s16[4,112,128]{2,1,0:T(8,128)(2,1)S(1)}, s16[4,112,128]{2,1,0:T(8,128)(2,1)S(1)}, u32[]{:S(2)}, u32[]{:S(2)}) collective-permute-start(s16[4,112,128]{2,1,0:T(8,128)(2,1)S(1)} %total.1), channel_id=1, source_target_pairs={{0,2},{1,3},{2,0},{3,1},{4,6},{5,7},{6,4},{7,5},{8,10},{9,11},{10,... | collective-permute-start | bytes 344072 | tf_op jit(solution)/shard_map/ppermute | solution.py:433
  45.0 2.2 %collective-permute-done.9 = s16[4,112,128]{2,1,0:T(8,128)(2,1)S(1)} collective-permute-done((s16[4,112,128]{2,1,0:T(8,128)(2,1)S(1)}, s16[4,112,128]{2,1,0:T(8,128)(2,1)S(1)}, u32[]{:S(2)}, u32[]{:S(2)}) %collective-permute-start.9) | collective-permute-done | bytes 114720 | tf_op jit(solution)/shard_map/ppermute | solution.py:433
  47.3 0.0 copy-done.3
  47.3 1.6 %entity.1 = f32[100,256]{1,0:T(8,128)} custom-call(s32[2]{0:T(128)S(1)} %pad_add_fusion.1.place, s32[1,2,8]{2,1,0:T(2,128)S(1)} %bitcast.10, f32[100,256]{1,0:T(8,128)S(1)} %get-tuple-element.27.lhs, s16[2,112,128]{2,1,0:T(8,128)(2,1)S(1)} %quad.1.refs_0_, s16[2,112,128]{2,1,0:T(8,128)(2,1)S(1)} %collective-permute-done.6.refs_1_), custom_call_target="tpu_custom_call" | custom-call | flops 1000000000 | bytes 1000000 | tf_op jit(solution)/shard_map/entity/pallas_call | solution.py:468
  48.9 0.0 collective-permute-done.11
  48.9 0.1 collective-permute-done.10
  49.0 0.1 collective-permute-start.12
  49.1 1.8 %collective-permute-done.12.other = s16[16,112,128]{2,1,0:T(8,128)(2,1)S(1)} collective-permute-done((s16[16,112,128]{2,1,0:T(8,128)(2,1)S(1)}, s16[16,112,128]{2,1,0:T(8,128)(2,1)S(1)}, u32[]{:S(2)}, u32[]{:S(2)}) %collective-permute-start.12) | collective-permute-done | bytes 458784 | tf_op jit(solution)/shard_map/ppermute | solution.py:483
  50.9 1.8 %spread.1 = f32[400,1000]{1,0:T(8,128)} custom-call(s32[2]{0:T(128)S(1)} %pad_add_fusion.1.place, s16[16,112,128]{2,1,0:T(8,128)(2,1)S(1)} %pad_add_fusion.mine, s16[16,112,128]{2,1,0:T(8,128)(2,1)S(1)} %collective-permute-done.12.other), custom_call_target="tpu_custom_call" | custom-call | tf_op jit(solution)/shard_map/spread/pallas_call | solution.py:484
  (1 shorter events, 0.0 us)
Async XLA Ops:
  3.1 9.1 %collective-permute-start.2 = (s32[8,512]{1,0:T(8,128)}, s32[8,512]{1,0:T(8,128)S(1)}, u32[]{:S(2)}, u32[]{:S(2)}) collective-permute-start(s32[8,512]{1,0:T(8,128)} %get-tuple-element.16.refs_0_), channel_id=1, source_target_pairs={{0,3},{1,0},{2,1},{3,2},{4,7},{5,4},{6,5},{7,6},{8,11},{9,8},{10,9... | collective-permute-start | bytes 49160 | tf_op jit(solution)/shard_map/ppermute | solution.py:376
  5.5 6.7 %collective-permute-start.1 = (s32[8,512]{1,0:T(8,128)}, s32[8,512]{1,0:T(8,128)S(1)}, u32[]{:S(2)}, u32[]{:S(2)}) collective-permute-start(s32[8,512]{1,0:T(8,128)} %get-tuple-element.16.refs_0_), channel_id=1, source_target_pairs={{0,2},{1,3},{2,0},{3,1},{4,6},{5,7},{6,4},{7,5},{8,10},{9,11},{10,... | collective-permute-start | bytes 49160 | tf_op jit(solution)/shard_map/ppermute | solution.py:376
  6.2 6.1 %collective-permute-start = (s32[8,512]{1,0:T(8,128)}, s32[8,512]{1,0:T(8,128)S(1)}, u32[]{:S(2)}, u32[]{:S(2)}) collective-permute-start(s32[8,512]{1,0:T(8,128)} %get-tuple-element.16.refs_0_), channel_id=1, source_target_pairs={{0,1},{1,2},{2,3},{3,0},{4,5},{5,6},{6,7},{7,4},{8,9},{9,10},{10,1... | collective-permute-start | bytes 49160 | tf_op jit(solution)/shard_map/ppermute | solution.py:376
  6.3 13.7 %all-to-all-start = ((f32[8,2,400]{2,1,0:T(2,128)}), f32[8,2,400]{2,1,0:T(2,128)S(1)}, u32[]{:S(2)}, u32[]{:S(2)}) async-start(f32[8,2,400]{2,1,0:T(2,128)} %get-tuple-element.20), calls=%async_computation | async-start | bytes 65536 | tf_op jit(solution)/shard_map/all_to_all | solution.py:377
  12.3 0.9 %copy-start = (bf16[256,400]{0,1:T(8,128)(2,1)S(1)}, bf16[256,400]{0,1:T(8,128)(2,1)}, u32[]{:S(2)}) copy-start(bf16[256,400]{0,1:T(8,128)(2,1)} %param.8) | copy-start | bytes 614404
  13.2 0.7 %copy-start.1 = (s32[8,512]{1,0:T(8,128)S(1)}, s32[8,512]{1,0:T(8,128)}, u32[]{:S(2)}) copy-start(s32[8,512]{1,0:T(8,128)} %get-tuple-element.16.refs_0_) | copy-start | bytes 49156
  13.9 1.4 %copy-start.4 = (f32[1000,400]{0,1:T(8,128)S(1)}, f32[1000,400]{0,1:T(8,128)}, u32[]{:S(2)}) copy-start(f32[1000,400]{0,1:T(8,128)} %param.9) | copy-start | bytes 4800004
  15.3 4.7 %copy-start.2 = (s32[8,512]{1,0:T(8,128)S(1)}, s32[8,512]{1,0:T(8,128)}, u32[]{:S(2)}) copy-start(s32[8,512]{1,0:T(8,128)} %get-tuple-element.16.refs_0_) | copy-start | bytes 49156
  20.0 27.3 %copy-start.3 = (s32[1,8,2]{1,2,0:T(2,128)S(1)}, s32[1,8,2]{1,2,0:T(2,128)}, u32[]{:S(2)}) copy-start(s32[1,8,2]{1,2,0:T(2,128)} %param.10) | copy-start | bytes 196
  24.5 4.8 %collective-permute-start.3 = (s16[2,112,128]{2,1,0:T(8,128)(2,1)S(1)}, s16[2,112,128]{2,1,0:T(8,128)(2,1)S(1)}, u32[]{:S(2)}, u32[]{:S(2)}) collective-permute-start(s16[2,112,128]{2,1,0:T(8,128)(2,1)S(1)} %get-tuple-element.22), channel_id=1, source_target_pairs={{0,4},{1,5},{2,6},{3,7},{4,0},{5,1},{6,2},{7,3},{8,12},{9,13},{10,... | collective-permute-start | bytes 172040 | tf_op jit(solution)/shard_map/ppermute | solution.py:433
  26.6 4.4 %collective-permute-start.4 = (s16[2,112,128]{2,1,0:T(8,128)(2,1)S(1)}, s16[2,112,128]{2,1,0:T(8,128)(2,1)S(1)}, u32[]{:S(2)}, u32[]{:S(2)}) collective-permute-start(s16[2,112,128]{2,1,0:T(8,128)(2,1)S(1)} %get-tuple-element.23), channel_id=1, source_target_pairs={{0,8},{1,9},{2,10},{3,11},{4,12},{5,13},{6,14},{7,15},{8,0},{9,1},... | collective-permute-start | bytes 172040 | tf_op jit(solution)/shard_map/ppermute | solution.py:433
  28.0 5.1 %collective-permute-start.5 = (s16[2,112,128]{2,1,0:T(8,128)(2,1)S(1)}, s16[2,112,128]{2,1,0:T(8,128)(2,1)S(1)}, u32[]{:S(2)}, u32[]{:S(2)}) collective-permute-start(s16[2,112,128]{2,1,0:T(8,128)(2,1)S(1)} %get-tuple-element.24), channel_id=1, source_target_pairs={{0,12},{1,13},{2,14},{3,15},{4,8},{5,9},{6,10},{7,11},{8,4},{9,5},... | collective-permute-start | bytes 172040 | tf_op jit(solution)/shard_map/ppermute | solution.py:433
  33.2 6.3 %collective-permute-start.8 = (s16[2,112,128]{2,1,0:T(8,128)(2,1)S(1)}, s16[2,112,128]{2,1,0:T(8,128)(2,1)S(1)}, u32[]{:S(2)}, u32[]{:S(2)}) collective-permute-start(s16[2,112,128]{2,1,0:T(8,128)(2,1)S(1)} %quad.1.refs_0_), channel_id=1, source_target_pairs={{0,24},{1,25},{2,26},{3,27},{4,28},{5,29},{6,30},{7,31},{8,16},{9,... | collective-permute-start | bytes 172040 | tf_op jit(solution)/shard_map/ppermute | solution.py:433
  35.7 4.4 %collective-permute-start.7 = (s16[2,112,128]{2,1,0:T(8,128)(2,1)S(1)}, s16[2,112,128]{2,1,0:T(8,128)(2,1)S(1)}, u32[]{:S(2)}, u32[]{:S(2)}) collective-permute-start(s16[2,112,128]{2,1,0:T(8,128)(2,1)S(1)} %quad.1.refs_0_), channel_id=1, source_target_pairs={{0,8},{1,9},{2,10},{3,11},{4,12},{5,13},{6,14},{7,15},{8,0},{9,1},... | collective-permute-start | bytes 172040 | tf_op jit(solution)/shard_map/ppermute | solution.py:433
  36.2 5.1 %collective-permute-start.6 = (s16[2,112,128]{2,1,0:T(8,128)(2,1)S(1)}, s16[2,112,128]{2,1,0:T(8,128)(2,1)S(1)}, u32[]{:S(2)}, u32[]{:S(2)}) collective-permute-start(s16[2,112,128]{2,1,0:T(8,128)(2,1)S(1)} %quad.1.refs_0_), channel_id=1, source_target_pairs={{0,16},{1,17},{2,18},{3,19},{4,20},{5,21},{6,22},{7,23},{8,24},{9,... | collective-permute-start | bytes 172040 | tf_op jit(solution)/shard_map/ppermute | solution.py:433
  41.5 5.8 %collective-permute-start.9 = (s16[4,112,128]{2,1,0:T(8,128)(2,1)S(1)}, s16[4,112,128]{2,1,0:T(8,128)(2,1)S(1)}, u32[]{:S(2)}, u32[]{:S(2)}) collective-permute-start(s16[4,112,128]{2,1,0:T(8,128)(2,1)S(1)} %total.1), channel_id=1, source_target_pairs={{0,4},{1,5},{2,6},{3,7},{4,0},{5,1},{6,2},{7,3},{8,12},{9,13},{10,... | collective-permute-start | bytes 344072 | tf_op jit(solution)/shard_map/ppermute | solution.py:433
  42.6 6.3 %collective-permute-start.11 = (s16[4,112,128]{2,1,0:T(8,128)(2,1)S(1)}, s16[4,112,128]{2,1,0:T(8,128)(2,1)S(1)}, u32[]{:S(2)}, u32[]{:S(2)}) collective-permute-start(s16[4,112,128]{2,1,0:T(8,128)(2,1)S(1)} %total.1), channel_id=1, source_target_pairs={{0,6},{1,7},{2,4},{3,5},{4,2},{5,3},{6,0},{7,1},{8,14},{9,15},{10,... | collective-permute-start | bytes 344072 | tf_op jit(solution)/shard_map/ppermute | solution.py:433
  44.2 4.8 %collective-permute-start.10 = (s16[4,112,128]{2,1,0:T(8,128)(2,1)S(1)}, s16[4,112,128]{2,1,0:T(8,128)(2,1)S(1)}, u32[]{:S(2)}, u32[]{:S(2)}) collective-permute-start(s16[4,112,128]{2,1,0:T(8,128)(2,1)S(1)} %total.1), channel_id=1, source_target_pairs={{0,2},{1,3},{2,0},{3,1},{4,6},{5,7},{6,4},{7,5},{8,10},{9,11},{10,... | collective-permute-start | bytes 344072 | tf_op jit(solution)/shard_map/ppermute | solution.py:433
  49.0 1.9 %collective-permute-start.12 = (s16[16,112,128]{2,1,0:T(8,128)(2,1)S(1)}, s16[16,112,128]{2,1,0:T(8,128)(2,1)S(1)}, u32[]{:S(2)}, u32[]{:S(2)}) collective-permute-start(s16[16,112,128]{2,1,0:T(8,128)(2,1)S(1)} %pad_add_fusion.mine), channel_id=1, source_target_pairs={{0,1},{1,0},{2,3},{3,2},{4,5},{5,4},{6,7},{7,6},{8,9},{9,8},{10,11... | collective-permute-start | bytes 1376264 | tf_op jit(solution)/shard_map/ppermute | solution.py:483

commit v9 on v8

--- a/solution.py
+++ b/solution.py
@@ -12,6 +12,7 @@
 IDX_ROWS = 8
 LANES = 128
 SOURCES = 4
+LIVE_EDGES = 1536
 VMEM = pl.BlockSpec(memory_space=pltpu.VMEM)
 SMEM = pl.BlockSpec(memory_space=pltpu.SMEM)
 HBM = pl.BlockSpec(memory_space=pltpu.HBM)
@@ -109,23 +110,44 @@
         out_rows[w] = picked_rows[w * cap : (w + 1) * cap]
 
 
+def packed_edges(idx_refs, groups, out_idx):
+    edges, span = idx_refs[0].shape[1], out_idx.shape[1]
+    wide = max(span, edges)
+    place = iota((IDX_ROWS, wide), 1)
+    row = iota((IDX_ROWS, edges), 0)
+    block = iota((IDX_ROWS, edges), 1) // (edges // groups)
+    packed = jnp.where(iota((IDX_ROWS, wide), 0) < 3, -1, 0)
+    first = 0
+    for i, ref in enumerate(idx_refs):
+        count = jnp.max(ref[IDX_ROWS - 1 : IDX_ROWS, :].astype(F32)).astype(jnp.int32)
+        rows = jnp.where(row < 3, ref[...], jnp.where(row == 3, block + i * groups, 1))
+        if wide > edges:
+            rows = jnp.concatenate(
+                [rows, jnp.zeros((IDX_ROWS, wide - edges), jnp.int32)], axis=1
+            )
+        moved = pltpu.roll(rows, first, 1)
+        packed = jnp.where((place >= first) & (place < first + count), moved, packed)
+        first = first + count
+    out_idx[...] = packed[:, :span]
+
+
 def gather_kernel(cfg, place, *refs):
-    replicas, nrel, pad_rel, narrow, window = cfg
+    replicas, groups, nrel, pad_rel, narrow, window, step = cfg
     idx_refs, refs = refs[:replicas], refs[replicas:]
-    ent, relation, out_query, out_lhs, out_rel, rel_parts, lhs_s, rel_s = refs
-    edges = idx_refs[0].shape[1]
+    ent, relation, out_idx, out_query, out_lhs, out_rel, rel_parts, lhs_s, rel_s = refs
     dim, rows = ent.shape
     base = pl.multiple_of((place[1] * narrow) // 8 * 8, 8)
+    packed_edges(idx_refs, groups, out_idx)
     hi, lo = split2(relation[...])
     if pad_rel > nrel:
         rel_parts[...] = jnp.zeros(rel_parts.shape, BF16)
     rel_parts[:dim, :nrel] = hi
     rel_parts[dim:, :nrel] = lo
-    for i in range(replicas):
-        span = slice(i * edges, (i + 1) * edges)
-        src_l, rel_l = idx_refs[i][0:1, :], idx_refs[i][1:2, :]
-        lhs = dot(ent[...], ones_where(iota((rows, edges), 0) == src_l))
-        both = dot(rel_parts[...], ones_where(iota((pad_rel, edges), 0) == rel_l))
+    for start in range(0, out_idx.shape[1], step):
+        span = slice(start, start + step)
+        src_l, rel_l = out_idx[0:1, span], out_idx[1:2, span]
+        lhs = dot(ent[...], ones_where(iota((rows, step), 0) == src_l))
+        both = dot(rel_parts[...], ones_where(iota((pad_rel, step), 0) == rel_l))
         rel_rows = both[:dim] + both[dim:]
         lhs_s[...] = lhs
         rel_s[...] = rel_rows
@@ -137,13 +159,12 @@
 def main_kernel(cfg, place, *refs):
     (direct, workers, replicas, cap, groups, width, pad_rel, block, narrow, window, offsets) = cfg
     idx_refs, refs = refs[:replicas], refs[replicas:]
-    (query_v, lhs_v, rel_v, received), refs = refs[:4], refs[4:]
+    (packed, query_v, lhs_v, rel_v, received), refs = refs[:5], refs[5:]
     out_lhs, refs = refs[0], refs[1:]
     outs, refs = (refs[:SOURCES], refs[SOURCES:]) if direct else (refs[:1], refs[1:])
-    table_f, table_t, query_s, acc_rel, acc_lhs, acc_tab, wide_t, mixed = refs[:8]
-    codes_s, powers_s, tables_s = refs[8:]
+    table_f, table_t, query_s, wide_t, mixed, codes_s, powers_s, tables_s = refs
     edges = idx_refs[0].shape[1]
-    dim = query_v.shape[0]
+    dim, total = query_v.shape
     rows = out_lhs.shape[1]
     slots = workers * cap
     rep = place[1]
@@ -157,48 +178,41 @@
     table = table_f[...].astype(BF16)
     own_t = table_t[pl.ds(base, window), :].astype(BF16)
     own_t = jnp.concatenate([own_t] * 3, axis=1)
-    acc_rel[...] = jnp.zeros(acc_rel.shape, F32)
-    acc_lhs[...] = jnp.zeros(acc_lhs.shape, F32)
-    acc_tab[...] = jnp.zeros(acc_tab.shape, F32)
-
+
+    query = query_v[...]
+    scores = dot(table, query)
+    query_s[...] = query.astype(F32)
+    lanes = packed[...]
+    cols = jnp.transpose(lanes)
+    times = jnp.zeros((slots, total), F32)
     for i in range(replicas):
-        here = slice(i * edges, (i + 1) * edges)
-        lanes = idx_refs[i][...]
-        cols = jnp.transpose(lanes)
-        dst_l = lanes[2:3]
-        count = lanes[IDX_ROWS - 1 : IDX_ROWS]
-        query = query_v[:, here]
-        query_s[...] = query.astype(F32)
-        scores = dot(table, query)
-        live = jnp.where(iota((1, edges), 1) < count, 1.0, 0.0).astype(F32)
-        own = jnp.where(iota((slots, edges), 0) == dst_l, 1.0, 0.0).astype(F32)
-        seen = own * live
-        parts = []
+        shard = idx_refs[i][...]
+        position = iota((slots, edges), 1)
+        seen = (iota((slots, edges), 0) == shard[2:3]) & (position < shard[IDX_ROWS - 1 : IDX_ROWS])
+        seen = jnp.where(seen, 1.0, 0.0).astype(F32)
         for g in range(groups):
-            span = slice(g * per, (g + 1) * per)
-            s, o = scores[:, span], own[:, span]
-            neg = jnp.where(
-                iota((slots, width), 0) == lanes[3 + g : 4 + g, :width], 1.0, 0.0
-            ).astype(F32)
-            times = jnp.sum(seen[:, span], axis=1, keepdims=True)
-            times = times + jnp.sum(neg, axis=1, keepdims=True)
-            s = jnp.where(times > 0, s, F32(-1e30))
-            top = jnp.max(s, axis=0, keepdims=True)
-            expo = jnp.exp(s - top)
-            probs = expo / jnp.sum(expo * times, axis=0, keepdims=True)
-            other = probs.astype(BF16).astype(F32)
-            itself = (probs - 1.0).astype(BF16).astype(F32)
-            parts.append(((times - o) * other + o * itself) * live[:, span])
-        grads = jnp.concatenate(parts, axis=1)
-        stack = jnp.concatenate(split3(grads), axis=0)
-        stack_t = jnp.concatenate(split3(jnp.transpose(grads)), axis=1)
-
-        dquery = dot(own_t, stack)
-        acc_tab[...] += dot(query_s[pl.ds(base, window), :].astype(BF16), stack_t)
-        y = jnp.concatenate(split2(dquery * lhs_v[:, here]), axis=0)
-        acc_rel[...] += dot(y, ones_where(iota((edges, pad_rel), 1) == cols[:, 1:2]))
-        x = jnp.concatenate(split2(dquery * rel_v[:, here]), axis=0)
-        acc_lhs[...] += dot(x, ones_where(iota((edges, rows), 1) == cols[:, 0:1]))
+            neg = iota((slots, width), 0) == shard[3 + g : 4 + g, :width]
+            often = jnp.sum(jnp.where(neg, 1.0, 0.0).astype(F32), axis=1, keepdims=True)
+            often = often + jnp.sum(seen[:, g * per : (g + 1) * per], axis=1, keepdims=True)
+            times = jnp.where(lanes[3:4] == i * groups + g, often, times)
+    live = lanes[4:5].astype(F32)
+    own = jnp.where(iota((slots, total), 0) == lanes[2:3], 1.0, 0.0).astype(F32)
+    scores = jnp.where(times > 0, scores, F32(-1e30))
+    expo = jnp.exp(scores - jnp.max(scores, axis=0, keepdims=True))
+    norm = jnp.sum(expo * times, axis=0, keepdims=True)
+    probs = expo / jnp.where(live > 0, norm, 1.0)
+    other = probs.astype(BF16).astype(F32)
+    itself = (probs - 1.0).astype(BF16).astype(F32)
+    grads = ((times - own) * other + own * itself) * live
+    stack = jnp.concatenate(split3(grads), axis=0)
+    stack_t = jnp.concatenate(split3(jnp.transpose(grads)), axis=1)
+
+    dquery = dot(own_t, stack)
+    y = jnp.concatenate(split2(dquery * lhs_v[...]), axis=0)
+    acc_rel = dot(y, ones_where(iota((total, pad_rel), 1) == cols[:, 1:2]))
+    x = jnp.concatenate(split2(dquery * rel_v[...]), axis=0)
+    acc_lhs = dot(x, ones_where(iota((total, rows), 1) == cols[:, 0:1]))
+    acc_tab = dot(query_s[pl.ds(base, window), :].astype(BF16), stack_t)
 
     pick = functools.partial(shifted_rows, offset=offset, narrow=narrow, offsets=offsets)
     out_lhs[...] = pick(acc_lhs[:window] + acc_lhs[window:])
@@ -376,16 +390,19 @@
         held.append(lax.ppermute(idx, "rep", turned(replicas, hop)))
     received = lax.all_to_all(served, "dom", 0, 0, tiled=True)
 
-    total = replicas * edges
-    query, lhs_rows, rel_rows = pl.pallas_call(
-        functools.partial(gather_kernel, (replicas, nrel, pad_rel, narrow, window)),
+    total = min(replicas * edges, up(LIVE_EDGES, edges))
+    packed, query, lhs_rows, rel_rows = pl.pallas_call(
+        functools.partial(
+            gather_kernel, (replicas, groups, nrel, pad_rel, narrow, window, edges)
+        ),
         out_shape=(
+            jax.ShapeDtypeStruct((IDX_ROWS, total), jnp.int32),
             jax.ShapeDtypeStruct((dim, total), BF16),
             jax.ShapeDtypeStruct((window, total), F32),
             jax.ShapeDtypeStruct((window, total), F32),
         ),
         in_specs=[SMEM] + [VMEM] * (replicas + 2),
-        out_specs=(VMEM, VMEM, VMEM),
+        out_specs=[VMEM] * 4,
         scratch_shapes=[
             pltpu.VMEM((2 * dim, pad_rel), BF16),
             pltpu.VMEM((dim, edges), F32),
@@ -406,15 +423,12 @@
     lhs_part, *sent = pl.pallas_call(
         functools.partial(main_kernel, cfg),
         out_shape=[jax.ShapeDtypeStruct((narrow, rows), F32)] + sizes,
-        in_specs=[SMEM] + [VMEM] * (replicas + 4),
+        in_specs=[SMEM] + [VMEM] * (replicas + 5),
         out_specs=[VMEM] * (1 + len(sizes)),
         scratch_shapes=[
             pltpu.VMEM((slots, dim), F32),
             pltpu.VMEM((dim, slots), F32),
-            pltpu.VMEM((dim, edges), F32),
-            pltpu.VMEM((2 * window, pad_rel), F32),
-            pltpu.VMEM((2 * window, rows), F32),
-            pltpu.VMEM((window, 3 * slots), F32),
+            pltpu.VMEM((dim, total), F32),
             pltpu.VMEM((lanes, slots), F32),
             pltpu.VMEM((height, lanes), jnp.int32),
             pltpu.VMEM((narrow, pad_rel), jnp.int32),
@@ -423,7 +437,7 @@
         ],
         compiler_params=params(),
         name="edges",
-    )(place, *held, query, lhs_rows, rel_rows, received)
+    )(place, *held, packed, query, lhs_rows, rel_rows, received)
 
     def swap(array, dom_bits=0, rep_bits=0):
         pairs = []

time: 53.1 us -> 51.1 us (0.962)
  Pallas kernels: 14.6 us -> 12.6 us
    pallas_call x1, Pallas kernels: 4.44 us -> 3.17 us  [shards(): pl.pallas_call(functools.partial(main_kernel, cfg), out_shape=[jax.ShapeD...]
    pallas_call x1, Pallas kernels: 4.64 us -> 3.93 us  [shards(): pl.pallas_call(functools.partial(gather_kernel, (replicas, groups, nrel,...]
  transfers between devices with their start and end apart: 14 -> 14, of which waited for: 9 -> 9; matrix products, arithmetic and copies ran while one was open for 0% -> 0% of each run, Pallas kernels for 12% -> 11%
where the time goes in v9:
time: 51.1 us; the launch traced here: 50.8 us
  starting transfers between devices  20.8 us (41%)
  waiting for transfers between devices  12.8 us (25%)
  Pallas kernels  12.6 us (25%)
  local copies, waits for them, and re-layouts  3.08 us (6%)
  between operations  1.37 us (3%)
    ppermute x9, starting transfers between devices, swap(): return lax.ppermute(array, ('dom', 'rep'), pairs)  11.6 us
    ppermute x9, waiting for transfers between devices, swap(): return lax.ppermute(array, ('dom', 'rep'), pairs)  11 us
    all_to_all x1, starting transfers between devices, shards(): received = lax.all_to_all(served, 'dom', 0, 0, tiled=True)  5.84 us
    pallas_call x1, Pallas kernels, shards(): pl.pallas_call(functools.partial(gather_kernel, (replicas, groups, nrel,...  3.93 us
    ppermute x3, starting transfers between devices, shards(): held.append(lax.ppermute(idx, 'rep', turned(replicas, hop)))  3.23 us
    pallas_call x1, Pallas kernels, shards(): pl.pallas_call(functools.partial(main_kernel, cfg), out_shape=[jax.ShapeD...  3.17 us
    unnamed x10, local copies, waits for them, and re-layouts  3.08 us
    pallas_call x1, Pallas kernels, shards(): pl.pallas_call(functools.partial(spread_kernel, workers, replicas, narrow...  1.84 us
  transfers between devices with their start and end apart: 14, of which 9 were waited for; matrix products, arithmetic and copies ran while one was open for 0% of the time, Pallas kernels for 11%

profile of v9, /device:TPU:0, one launch (start us, length us, event | category | flops | bytes accessed | tf_op | source)
XLA Modules:
  0.0 50.8 jit_solution(13178120740661589963)
XLA Ops:
  1.3 1.8 %prep.1 = (s32[8,512]{1,0:T(8,128)}, f32[8,2,400]{2,1,0:T(2,128)}) custom-call(s32[1,2,8]{2,1,0:T(2,128)} %bitcast.9, s32[1,1]{1,0:T(1,128)S(6)} %copy.10.count, bf16[400,256]{1,0:T(8,128)(2,1)} %bitcast.7, s32[1,1,512]{2,1,0:T(1,128)} %src.1, s32[1,1,512]{2,1,0:T(1,128)} %rel.1, s32[1,1,512]{2,1,0:T(1,128)} %dst.1, s32[1,1,2,384]{3,2,1,0:T(2,128)} %neg.1), custom_call_target="tpu_custom_call" | custom-call | tf_op jit(solution)/shard_map/prep/pallas_call | solution.py:365
  3.1 2.4 %collective-permute-start.2 = (s32[8,512]{1,0:T(8,128)}, s32[8,512]{1,0:T(8,128)S(1)}, u32[]{:S(2)}, u32[]{:S(2)}) collective-permute-start(s32[8,512]{1,0:T(8,128)} %get-tuple-element.17.refs_0_), channel_id=1, source_target_pairs={{0,3},{1,0},{2,1},{3,2},{4,7},{5,4},{6,5},{7,6},{8,11},{9,8},{10,9... | collective-permute-start | bytes 49160 | tf_op jit(solution)/shard_map/ppermute | solution.py:390
  5.5 0.6 %collective-permute-start.1 = (s32[8,512]{1,0:T(8,128)}, s32[8,512]{1,0:T(8,128)S(1)}, u32[]{:S(2)}, u32[]{:S(2)}) collective-permute-start(s32[8,512]{1,0:T(8,128)} %get-tuple-element.17.refs_0_), channel_id=1, source_target_pairs={{0,2},{1,3},{2,0},{3,1},{4,6},{5,7},{6,4},{7,5},{8,10},{9,11},{10,... | collective-permute-start | bytes 49160 | tf_op jit(solution)/shard_map/ppermute | solution.py:390
  6.2 0.2 collective-permute-start
  6.3 5.8 %all-to-all-start = ((f32[8,2,400]{2,1,0:T(2,128)}), f32[8,2,400]{2,1,0:T(2,128)S(1)}, u32[]{:S(2)}, u32[]{:S(2)}) async-start(f32[8,2,400]{2,1,0:T(2,128)} %get-tuple-element.22), calls=%async_computation | async-start | bytes 65536 | tf_op jit(solution)/shard_map/all_to_all | solution.py:391
  12.2 0.1 pad_add_fusion.1.place
  12.2 0.0 collective-permute-done.2.refs_3_
  12.2 0.0 collective-permute-done.1.refs_2_
  12.2 0.0 collective-permute-done.refs_1_
  12.3 0.0 copy-start
  12.3 0.9 %copy-done = bf16[256,400]{0,1:T(8,128)(2,1)S(1)} copy-done((bf16[256,400]{0,1:T(8,128)(2,1)S(1)}, bf16[256,400]{0,1:T(8,128)(2,1)}, u32[]{:S(2)}) %copy-start) | copy-done | bytes 204824
  13.2 0.0 copy-start.1
  13.2 0.7 %copy-done.1 = s32[8,512]{1,0:T(8,128)S(1)} copy-done((s32[8,512]{1,0:T(8,128)S(1)}, s32[8,512]{1,0:T(8,128)}, u32[]{:S(2)}) %copy-start.1) | copy-done | bytes 16408
  13.9 0.0 copy-start.4
  13.9 1.4 %copy-done.4 = f32[1000,400]{0,1:T(8,128)S(1)} copy-done((f32[1000,400]{0,1:T(8,128)S(1)}, f32[1000,400]{0,1:T(8,128)}, u32[]{:S(2)}) %copy-start.4) | copy-done | bytes 1600024
  15.3 0.0 copy-start.2
  15.3 3.9 %gather.1 = (s32[8,1536]{1,0:T(8,128)S(1)}, bf16[400,1536]{1,0:T(8,128)(2,1)S(1)}, f32[104,1536]{1,0:T(8,128)S(1)}, f32[104,1536]{1,0:T(8,128)S(1)}) custom-call(s32[2]{0:T(128)S(1)} %pad_add_fusion.1.place, s32[8,512]{1,0:T(8,128)S(1)} %copy-done.1, s32[8,512]{1,0:T(8,128)S(1)} %collective-permute-done.refs_1_, ...), custom_call_target="tpu_custom_call" | custom-call | flops 2831155200 | bytes 4915200 | tf_op jit(solution)/shard_map/gather/pallas_call | solution.py:394
  19.3 0.0 all-to-all-done.refs_8_
  19.3 0.0 copy-done.2
  19.3 0.0 copy-start.3
  19.3 3.2 %edges.1 = (f32[100,256]{1,0:T(8,128)S(1)}, s16[2,112,128]{2,1,0:T(8,128)(2,1)S(1)}, s16[2,112,128]{2,1,0:T(8,128)(2,1)S(1)}, s16[2,112,128]{2,1,0:T(8,128)(2,1)S(1)}, s16[2,112,128]{2,1,0:T(8,128)(2,1)S(1)}) custom-call(s32[2]{0:T(128)S(1)} %pad_add_fusion.1.place, s32[8,512]{1,0:T(8,128)S(1)} %copy-done.2, s32[8,512]{1,0:T(8,128)S(1)} %collective-permute-done.refs_1_, ...), custom_call_target="tpu_custom_call" | custom-call | tf_op jit(solution)/shard_map/edges/pallas_call | solution.py:423
  22.5 2.1 %collective-permute-start.3 = (s16[2,112,128]{2,1,0:T(8,128)(2,1)S(1)}, s16[2,112,128]{2,1,0:T(8,128)(2,1)S(1)}, u32[]{:S(2)}, u32[]{:S(2)}) collective-permute-start(s16[2,112,128]{2,1,0:T(8,128)(2,1)S(1)} %get-tuple-element.24), channel_id=1, source_target_pairs={{0,4},{1,5},{2,6},{3,7},{4,0},{5,1},{6,2},{7,3},{8,12},{9,13},{10,... | collective-permute-start | bytes 172040 | tf_op jit(solution)/shard_map/ppermute | solution.py:447
  24.6 1.5 %collective-permute-start.4 = (s16[2,112,128]{2,1,0:T(8,128)(2,1)S(1)}, s16[2,112,128]{2,1,0:T(8,128)(2,1)S(1)}, u32[]{:S(2)}, u32[]{:S(2)}) collective-permute-start(s16[2,112,128]{2,1,0:T(8,128)(2,1)S(1)} %get-tuple-element.25), channel_id=1, source_target_pairs={{0,8},{1,9},{2,10},{3,11},{4,12},{5,13},{6,14},{7,15},{8,0},{9,1},... | collective-permute-start | bytes 172040 | tf_op jit(solution)/shard_map/ppermute | solution.py:447
  26.0 0.1 collective-permute-start.5
  26.1 1.1 %collective-permute-done.3.refs_1_ = s16[2,112,128]{2,1,0:T(8,128)(2,1)S(1)} collective-permute-done((s16[2,112,128]{2,1,0:T(8,128)(2,1)S(1)}, s16[2,112,128]{2,1,0:T(8,128)(2,1)S(1)}, u32[]{:S(2)}, u32[]{:S(2)}) %collective-permute-start.3) | collective-permute-done | bytes 57376 | tf_op jit(solution)/shard_map/ppermute | solution.py:447
  27.2 1.7 %collective-permute-done.4.refs_2_ = s16[2,112,128]{2,1,0:T(8,128)(2,1)S(1)} collective-permute-done((s16[2,112,128]{2,1,0:T(8,128)(2,1)S(1)}, s16[2,112,128]{2,1,0:T(8,128)(2,1)S(1)}, u32[]{:S(2)}, u32[]{:S(2)}) %collective-permute-start.4) | collective-permute-done | bytes 57376 | tf_op jit(solution)/shard_map/ppermute | solution.py:447
  29.0 2.1 %collective-permute-done.5.refs_3_ = s16[2,112,128]{2,1,0:T(8,128)(2,1)S(1)} collective-permute-done((s16[2,112,128]{2,1,0:T(8,128)(2,1)S(1)}, s16[2,112,128]{2,1,0:T(8,128)(2,1)S(1)}, u32[]{:S(2)}, u32[]{:S(2)}) %collective-permute-start.5) | collective-permute-done | bytes 57376 | tf_op jit(solution)/shard_map/ppermute | solution.py:447
  31.1 0.1 quad.1.refs_0_
  31.2 2.4 %collective-permute-start.8 = (s16[2,112,128]{2,1,0:T(8,128)(2,1)S(1)}, s16[2,112,128]{2,1,0:T(8,128)(2,1)S(1)}, u32[]{:S(2)}, u32[]{:S(2)}) collective-permute-start(s16[2,112,128]{2,1,0:T(8,128)(2,1)S(1)} %quad.1.refs_0_), channel_id=1, source_target_pairs={{0,24},{1,25},{2,26},{3,27},{4,28},{5,29},{6,30},{7,31},{8,16},{9,... | collective-permute-start | bytes 172040 | tf_op jit(solution)/shard_map/ppermute | solution.py:447
  33.6 0.6 %collective-permute-start.7 = (s16[2,112,128]{2,1,0:T(8,128)(2,1)S(1)}, s16[2,112,128]{2,1,0:T(8,128)(2,1)S(1)}, u32[]{:S(2)}, u32[]{:S(2)}) collective-permute-start(s16[2,112,128]{2,1,0:T(8,128)(2,1)S(1)} %quad.1.refs_0_), channel_id=1, source_target_pairs={{0,8},{1,9},{2,10},{3,11},{4,12},{5,13},{6,14},{7,15},{8,0},{9,1},... | collective-permute-start | bytes 172040 | tf_op jit(solution)/shard_map/ppermute | solution.py:447
  34.2 1.5 %collective-permute-start.6 = (s16[2,112,128]{2,1,0:T(8,128)(2,1)S(1)}, s16[2,112,128]{2,1,0:T(8,128)(2,1)S(1)}, u32[]{:S(2)}, u32[]{:S(2)}) collective-permute-start(s16[2,112,128]{2,1,0:T(8,128)(2,1)S(1)} %quad.1.refs_0_), channel_id=1, source_target_pairs={{0,16},{1,17},{2,18},{3,19},{4,20},{5,21},{6,22},{7,23},{8,24},{9,... | collective-permute-start | bytes 172040 | tf_op jit(solution)/shard_map/ppermute | solution.py:447
  35.7 1.9 %collective-permute-done.8.refs_3_ = s16[2,112,128]{2,1,0:T(8,128)(2,1)S(1)} collective-permute-done((s16[2,112,128]{2,1,0:T(8,128)(2,1)S(1)}, s16[2,112,128]{2,1,0:T(8,128)(2,1)S(1)}, u32[]{:S(2)}, u32[]{:S(2)}) %collective-permute-start.8) | collective-permute-done | bytes 57376 | tf_op jit(solution)/shard_map/ppermute | solution.py:447
  37.5 0.5 %collective-permute-done.7.refs_2_ = s16[2,112,128]{2,1,0:T(8,128)(2,1)S(1)} collective-permute-done((s16[2,112,128]{2,1,0:T(8,128)(2,1)S(1)}, s16[2,112,128]{2,1,0:T(8,128)(2,1)S(1)}, u32[]{:S(2)}, u32[]{:S(2)}) %collective-permute-start.7) | collective-permute-done | bytes 57376 | tf_op jit(solution)/shard_map/ppermute | solution.py:447
  38.1 1.2 %collective-permute-done.6.refs_1_ = s16[2,112,128]{2,1,0:T(8,128)(2,1)S(1)} collective-permute-done((s16[2,112,128]{2,1,0:T(8,128)(2,1)S(1)}, s16[2,112,128]{2,1,0:T(8,128)(2,1)S(1)}, u32[]{:S(2)}, u32[]{:S(2)}) %collective-permute-start.6) | collective-permute-done | bytes 57376 | tf_op jit(solution)/shard_map/ppermute | solution.py:447
  39.3 0.2 total.1
  39.5 1.1 %collective-permute-start.9 = (s16[4,112,128]{2,1,0:T(8,128)(2,1)S(1)}, s16[4,112,128]{2,1,0:T(8,128)(2,1)S(1)}, u32[]{:S(2)}, u32[]{:S(2)}) collective-permute-start(s16[4,112,128]{2,1,0:T(8,128)(2,1)S(1)} %total.1), channel_id=1, source_target_pairs={{0,4},{1,5},{2,6},{3,7},{4,0},{5,1},{6,2},{7,3},{8,12},{9,13},{10,... | collective-permute-start | bytes 344072 | tf_op jit(solution)/shard_map/ppermute | solution.py:447
  40.6 1.6 %collective-permute-start.11 = (s16[4,112,128]{2,1,0:T(8,128)(2,1)S(1)}, s16[4,112,128]{2,1,0:T(8,128)(2,1)S(1)}, u32[]{:S(2)}, u32[]{:S(2)}) collective-permute-start(s16[4,112,128]{2,1,0:T(8,128)(2,1)S(1)} %total.1), channel_id=1, source_target_pairs={{0,6},{1,7},{2,4},{3,5},{4,2},{5,3},{6,0},{7,1},{8,14},{9,15},{10,... | collective-permute-start | bytes 344072 | tf_op jit(solution)/shard_map/ppermute | solution.py:447
  42.2 0.8 %collective-permute-start.10 = (s16[4,112,128]{2,1,0:T(8,128)(2,1)S(1)}, s16[4,112,128]{2,1,0:T(8,128)(2,1)S(1)}, u32[]{:S(2)}, u32[]{:S(2)}) collective-permute-start(s16[4,112,128]{2,1,0:T(8,128)(2,1)S(1)} %total.1), channel_id=1, source_target_pairs={{0,2},{1,3},{2,0},{3,1},{4,6},{5,7},{6,4},{7,5},{8,10},{9,11},{10,... | collective-permute-start | bytes 344072 | tf_op jit(solution)/shard_map/ppermute | solution.py:447
  43.0 2.2 %collective-permute-done.9 = s16[4,112,128]{2,1,0:T(8,128)(2,1)S(1)} collective-permute-done((s16[4,112,128]{2,1,0:T(8,128)(2,1)S(1)}, s16[4,112,128]{2,1,0:T(8,128)(2,1)S(1)}, u32[]{:S(2)}, u32[]{:S(2)}) %collective-permute-start.9) | collective-permute-done | bytes 114720 | tf_op jit(solution)/shard_map/ppermute | solution.py:447
  45.3 0.0 copy-done.3
  45.3 1.6 %entity.1 = f32[100,256]{1,0:T(8,128)} custom-call(s32[2]{0:T(128)S(1)} %pad_add_fusion.1.place, s32[1,2,8]{2,1,0:T(2,128)S(1)} %bitcast.10, f32[100,256]{1,0:T(8,128)S(1)} %get-tuple-element.29.lhs, s16[2,112,128]{2,1,0:T(8,128)(2,1)S(1)} %quad.1.refs_0_, s16[2,112,128]{2,1,0:T(8,128)(2,1)S(1)} %collective-permute-done.6.refs_1_), custom_call_target="tpu_custom_call" | custom-call | flops 1000000000 | bytes 1000000 | tf_op jit(solution)/shard_map/entity/pallas_call | solution.py:482
  46.9 0.0 collective-permute-done.11
  46.9 0.1 collective-permute-done.10
  47.0 0.1 collective-permute-start.12
  47.1 1.8 %collective-permute-done.12.other = s16[16,112,128]{2,1,0:T(8,128)(2,1)S(1)} collective-permute-done((s16[16,112,128]{2,1,0:T(8,128)(2,1)S(1)}, s16[16,112,128]{2,1,0:T(8,128)(2,1)S(1)}, u32[]{:S(2)}, u32[]{:S(2)}) %collective-permute-start.12) | collective-permute-done | bytes 458784 | tf_op jit(solution)/shard_map/ppermute | solution.py:497
  48.9 1.8 %spread.1 = f32[400,1000]{1,0:T(8,128)} custom-call(s32[2]{0:T(128)S(1)} %pad_add_fusion.1.place, s16[16,112,128]{2,1,0:T(8,128)(2,1)S(1)} %pad_add_fusion.mine, s16[16,112,128]{2,1,0:T(8,128)(2,1)S(1)} %collective-permute-done.12.other), custom_call_target="tpu_custom_call" | custom-call | tf_op jit(solution)/shard_map/spread/pallas_call | solution.py:498
  (1 shorter events, 0.0 us)
Async XLA Ops:
  3.1 9.1 %collective-permute-start.2 = (s32[8,512]{1,0:T(8,128)}, s32[8,512]{1,0:T(8,128)S(1)}, u32[]{:S(2)}, u32[]{:S(2)}) collective-permute-start(s32[8,512]{1,0:T(8,128)} %get-tuple-element.17.refs_0_), channel_id=1, source_target_pairs={{0,3},{1,0},{2,1},{3,2},{4,7},{5,4},{6,5},{7,6},{8,11},{9,8},{10,9... | collective-permute-start | bytes 49160 | tf_op jit(solution)/shard_map/ppermute | solution.py:390
  5.5 6.7 %collective-permute-start.1 = (s32[8,512]{1,0:T(8,128)}, s32[8,512]{1,0:T(8,128)S(1)}, u32[]{:S(2)}, u32[]{:S(2)}) collective-permute-start(s32[8,512]{1,0:T(8,128)} %get-tuple-element.17.refs_0_), channel_id=1, source_target_pairs={{0,2},{1,3},{2,0},{3,1},{4,6},{5,7},{6,4},{7,5},{8,10},{9,11},{10,... | collective-permute-start | bytes 49160 | tf_op jit(solution)/shard_map/ppermute | solution.py:390
  6.2 6.1 %collective-permute-start = (s32[8,512]{1,0:T(8,128)}, s32[8,512]{1,0:T(8,128)S(1)}, u32[]{:S(2)}, u32[]{:S(2)}) collective-permute-start(s32[8,512]{1,0:T(8,128)} %get-tuple-element.17.refs_0_), channel_id=1, source_target_pairs={{0,1},{1,2},{2,3},{3,0},{4,5},{5,6},{6,7},{7,4},{8,9},{9,10},{10,1... | collective-permute-start | bytes 49160 | tf_op jit(solution)/shard_map/ppermute | solution.py:390
  6.3 12.9 %all-to-all-start = ((f32[8,2,400]{2,1,0:T(2,128)}), f32[8,2,400]{2,1,0:T(2,128)S(1)}, u32[]{:S(2)}, u32[]{:S(2)}) async-start(f32[8,2,400]{2,1,0:T(2,128)} %get-tuple-element.22), calls=%async_computation | async-start | bytes 65536 | tf_op jit(solution)/shard_map/all_to_all | solution.py:391
  12.3 0.9 %copy-start = (bf16[256,400]{0,1:T(8,128)(2,1)S(1)}, bf16[256,400]{0,1:T(8,128)(2,1)}, u32[]{:S(2)}) copy-start(bf16[256,400]{0,1:T(8,128)(2,1)} %param.8) | copy-start | bytes 614404
  13.2 0.7 %copy-start.1 = (s32[8,512]{1,0:T(8,128)S(1)}, s32[8,512]{1,0:T(8,128)}, u32[]{:S(2)}) copy-start(s32[8,512]{1,0:T(8,128)} %get-tuple-element.17.refs_0_) | copy-start | bytes 49156
  13.9 1.4 %copy-start.4 = (f32[1000,400]{0,1:T(8,128)S(1)}, f32[1000,400]{0,1:T(8,128)}, u32[]{:S(2)}) copy-start(f32[1000,400]{0,1:T(8,128)} %param.9) | copy-start | bytes 4800004
  15.3 3.9 %copy-start.2 = (s32[8,512]{1,0:T(8,128)S(1)}, s32[8,512]{1,0:T(8,128)}, u32[]{:S(2)}) copy-start(s32[8,512]{1,0:T(8,128)} %get-tuple-element.17.refs_0_) | copy-start | bytes 49156
  19.3 26.0 %copy-start.3 = (s32[1,8,2]{1,2,0:T(2,128)S(1)}, s32[1,8,2]{1,2,0:T(2,128)}, u32[]{:S(2)}) copy-start(s32[1,8,2]{1,2,0:T(2,128)} %param.10) | copy-start | bytes 196
  22.5 4.8 %collective-permute-start.3 = (s16[2,112,128]{2,1,0:T(8,128)(2,1)S(1)}, s16[2,112,128]{2,1,0:T(8,128)(2,1)S(1)}, u32[]{:S(2)}, u32[]{:S(2)}) collective-permute-start(s16[2,112,128]{2,1,0:T(8,128)(2,1)S(1)} %get-tuple-element.24), channel_id=1, source_target_pairs={{0,4},{1,5},{2,6},{3,7},{4,0},{5,1},{6,2},{7,3},{8,12},{9,13},{10,... | collective-permute-start | bytes 172040 | tf_op jit(solution)/shard_map/ppermute | solution.py:447
  24.6 4.4 %collective-permute-start.4 = (s16[2,112,128]{2,1,0:T(8,128)(2,1)S(1)}, s16[2,112,128]{2,1,0:T(8,128)(2,1)S(1)}, u32[]{:S(2)}, u32[]{:S(2)}) collective-permute-start(s16[2,112,128]{2,1,0:T(8,128)(2,1)S(1)} %get-tuple-element.25), channel_id=1, source_target_pairs={{0,8},{1,9},{2,10},{3,11},{4,12},{5,13},{6,14},{7,15},{8,0},{9,1},... | collective-permute-start | bytes 172040 | tf_op jit(solution)/shard_map/ppermute | solution.py:447
  26.0 5.1 %collective-permute-start.5 = (s16[2,112,128]{2,1,0:T(8,128)(2,1)S(1)}, s16[2,112,128]{2,1,0:T(8,128)(2,1)S(1)}, u32[]{:S(2)}, u32[]{:S(2)}) collective-permute-start(s16[2,112,128]{2,1,0:T(8,128)(2,1)S(1)} %get-tuple-element.26), channel_id=1, source_target_pairs={{0,12},{1,13},{2,14},{3,15},{4,8},{5,9},{6,10},{7,11},{8,4},{9,5},... | collective-permute-start | bytes 172040 | tf_op jit(solution)/shard_map/ppermute | solution.py:447
  31.2 6.3 %collective-permute-start.8 = (s16[2,112,128]{2,1,0:T(8,128)(2,1)S(1)}, s16[2,112,128]{2,1,0:T(8,128)(2,1)S(1)}, u32[]{:S(2)}, u32[]{:S(2)}) collective-permute-start(s16[2,112,128]{2,1,0:T(8,128)(2,1)S(1)} %quad.1.refs_0_), channel_id=1, source_target_pairs={{0,24},{1,25},{2,26},{3,27},{4,28},{5,29},{6,30},{7,31},{8,16},{9,... | collective-permute-start | bytes 172040 | tf_op jit(solution)/shard_map/ppermute | solution.py:447
  33.6 4.4 %collective-permute-start.7 = (s16[2,112,128]{2,1,0:T(8,128)(2,1)S(1)}, s16[2,112,128]{2,1,0:T(8,128)(2,1)S(1)}, u32[]{:S(2)}, u32[]{:S(2)}) collective-permute-start(s16[2,112,128]{2,1,0:T(8,128)(2,1)S(1)} %quad.1.refs_0_), channel_id=1, source_target_pairs={{0,8},{1,9},{2,10},{3,11},{4,12},{5,13},{6,14},{7,15},{8,0},{9,1},... | collective-permute-start | bytes 172040 | tf_op jit(solution)/shard_map/ppermute | solution.py:447
  34.2 5.1 %collective-permute-start.6 = (s16[2,112,128]{2,1,0:T(8,128)(2,1)S(1)}, s16[2,112,128]{2,1,0:T(8,128)(2,1)S(1)}, u32[]{:S(2)}, u32[]{:S(2)}) collective-permute-start(s16[2,112,128]{2,1,0:T(8,128)(2,1)S(1)} %quad.1.refs_0_), channel_id=1, source_target_pairs={{0,16},{1,17},{2,18},{3,19},{4,20},{5,21},{6,22},{7,23},{8,24},{9,... | collective-permute-start | bytes 172040 | tf_op jit(solution)/shard_map/ppermute | solution.py:447
  39.5 5.8 %collective-permute-start.9 = (s16[4,112,128]{2,1,0:T(8,128)(2,1)S(1)}, s16[4,112,128]{2,1,0:T(8,128)(2,1)S(1)}, u32[]{:S(2)}, u32[]{:S(2)}) collective-permute-start(s16[4,112,128]{2,1,0:T(8,128)(2,1)S(1)} %total.1), channel_id=1, source_target_pairs={{0,4},{1,5},{2,6},{3,7},{4,0},{5,1},{6,2},{7,3},{8,12},{9,13},{10,... | collective-permute-start | bytes 344072 | tf_op jit(solution)/shard_map/ppermute | solution.py:447
  40.6 6.3 %collective-permute-start.11 = (s16[4,112,128]{2,1,0:T(8,128)(2,1)S(1)}, s16[4,112,128]{2,1,0:T(8,128)(2,1)S(1)}, u32[]{:S(2)}, u32[]{:S(2)}) collective-permute-start(s16[4,112,128]{2,1,0:T(8,128)(2,1)S(1)} %total.1), channel_id=1, source_target_pairs={{0,6},{1,7},{2,4},{3,5},{4,2},{5,3},{6,0},{7,1},{8,14},{9,15},{10,... | collective-permute-start | bytes 344072 | tf_op jit(solution)/shard_map/ppermute | solution.py:447
  42.2 4.8 %collective-permute-start.10 = (s16[4,112,128]{2,1,0:T(8,128)(2,1)S(1)}, s16[4,112,128]{2,1,0:T(8,128)(2,1)S(1)}, u32[]{:S(2)}, u32[]{:S(2)}) collective-permute-start(s16[4,112,128]{2,1,0:T(8,128)(2,1)S(1)} %total.1), channel_id=1, source_target_pairs={{0,2},{1,3},{2,0},{3,1},{4,6},{5,7},{6,4},{7,5},{8,10},{9,11},{10,... | collective-permute-start | bytes 344072 | tf_op jit(solution)/shard_map/ppermute | solution.py:447
  47.0 1.9 %collective-permute-start.12 = (s16[16,112,128]{2,1,0:T(8,128)(2,1)S(1)}, s16[16,112,128]{2,1,0:T(8,128)(2,1)S(1)}, u32[]{:S(2)}, u32[]{:S(2)}) collective-permute-start(s16[16,112,128]{2,1,0:T(8,128)(2,1)S(1)} %pad_add_fusion.mine), channel_id=1, source_target_pairs={{0,1},{1,0},{2,3},{3,2},{4,5},{5,4},{6,7},{7,6},{8,9},{9,8},{10,11... | collective-permute-start | bytes 1376264 | tf_op jit(solution)/shard_map/ppermute | solution.py:497

commit v10 on v9

--- a/solution.py
+++ b/solution.py
@@ -134,10 +134,19 @@
 def gather_kernel(cfg, place, *refs):
     replicas, groups, nrel, pad_rel, narrow, window, step = cfg
     idx_refs, refs = refs[:replicas], refs[replicas:]
-    ent, relation, out_idx, out_query, out_lhs, out_rel, rel_parts, lhs_s, rel_s = refs
+    ent_h, relation_h, out_idx, out_query, out_lhs, out_rel = refs[:6]
+    ent, relation, rel_parts, lhs_s, rel_s, sems = refs[6:]
     dim, rows = ent.shape
     base = pl.multiple_of((place[1] * narrow) // 8 * 8, 8)
+    moves = [
+        pltpu.make_async_copy(relation_h, relation, sems.at[0]),
+        pltpu.make_async_copy(ent_h, ent, sems.at[1]),
+    ]
+    for move in moves:
+        move.start()
     packed_edges(idx_refs, groups, out_idx)
+    for move in moves:
+        move.wait()
     hi, lo = split2(relation[...])
     if pad_rel > nrel:
         rel_parts[...] = jnp.zeros(rel_parts.shape, BF16)
@@ -401,14 +410,17 @@
             jax.ShapeDtypeStruct((window, total), F32),
             jax.ShapeDtypeStruct((window, total), F32),
         ),
-        in_specs=[SMEM] + [VMEM] * (replicas + 2),
+        in_specs=[SMEM] + [VMEM] * replicas + [HBM] * 2,
         out_specs=[VMEM] * 4,
         scratch_shapes=[
+            pltpu.VMEM(ent_t.shape, BF16),
+            pltpu.VMEM(rel_t.shape, F32),
             pltpu.VMEM((2 * dim, pad_rel), BF16),
             pltpu.VMEM((dim, edges), F32),
             pltpu.VMEM((dim, edges), F32),
+            pltpu.SemaphoreType.DMA((2,)),
         ],
-        compiler_params=params(),
+        compiler_params=params(57),
         cost_estimate=cost(2 * total * dim * (2 * pad_rel + rows), 8 * total * dim),
         name="gather",
     )(place, *held, ent_t, rel_t)
@@ -449,6 +461,7 @@
     stack = jax.ShapeDtypeStruct((outs[0], height, lanes), jnp.int16)
     mixed = [pltpu.VMEM((height, lanes), jnp.int32)]
     if direct:
+        got = {n: swap(sent[n], n) for n in reversed(range(1, SOURCES))}
         summed = pl.pallas_call(
             functools.partial(quad_kernel, narrow, cap),
             out_shape=stack,
@@ -457,7 +470,7 @@
             scratch_shapes=mixed,
             compiler_params=params(),
             name="quad",
-        )(sent[0], *[swap(sent[n], n) for n in range(1, SOURCES)])
+        )(sent[0], *[got[n] for n in range(1, SOURCES)])
         recv = [summed, swap(summed, 4)]
         parts = recv + [swap(summed, 2), swap(summed, 6)]
         stack = jax.ShapeDtypeStruct((4, height, lanes), jnp.int16)
@@ -477,8 +490,10 @@
     )(*parts)
 
     if direct:
-        along_y = swap(chunk, 1)
-        along_y, lhs_part = lax.optimization_barrier((along_y, lhs_part))
+        base = jnp.concatenate(
+            [chunk, swap(chunk, 1), swap(chunk, 0, 2), swap(chunk, 1, 2)], axis=0
+        )
+        base, lhs_part = lax.optimization_barrier((base, lhs_part))
     entity_grad = pl.pallas_call(
         functools.partial(entity_kernel, direct, narrow),
         out_shape=jax.ShapeDtypeStruct((narrow, rows), F32),
@@ -492,9 +507,8 @@
 
     power_row = narrow + SOURCES * cap
     if direct:
-        base = jnp.concatenate([chunk, along_y, swap(chunk, 0, 2), swap(chunk, 1, 2)], axis=0)
-        base, entity_grad = lax.optimization_barrier((base, entity_grad))
         swapped = lax.ppermute(base, "rep", [(i, i ^ 1) for i in range(replicas)])
+        swapped, entity_grad = lax.optimization_barrier((swapped, entity_grad))
         relation_t = pl.pallas_call(
             functools.partial(spread_kernel, workers, replicas, narrow, power_row, block),
             out_shape=jax.ShapeDtypeStruct((dim, nrel), F32),

time: 51.1 us -> 58.8 us (1.15)
  local copies, waits for them, and re-layouts: 3.08 us -> 7 us
  Pallas kernels: 12.6 us -> 15.7 us
    unnamed x10 -> x26, local copies, waits for them, and re-layouts: 3.08 us -> 7 us
    pallas_call x1, Pallas kernels: 3.93 us -> 6.97 us  [shards(): pl.pallas_call(functools.partial(gather_kernel, (replicas, groups, nrel,...]
    ppermute x1, waiting for transfers between devices: 1.8 us -> 0.19 us  [shards(): swapped = lax.ppermute(base, 'rep', [(i, i ^ 1) for i in range(replicas)])]
    ppermute x9, waiting for transfers between devices: 11 us -> 12.4 us  [swap(): return lax.ppermute(array, ('dom', 'rep'), pairs)]
  transfers between devices with their start and end apart: 14 -> 14, of which waited for: 9 -> 10; matrix products, arithmetic and copies ran while one was open for 0% -> 1% of each run, Pallas kernels for 11% -> 15%
where the time goes in v10:
time: 58.8 us; the launch traced here: 58.2 us
  starting transfers between devices  20.8 us (35%)
  Pallas kernels  15.7 us (27%)
  waiting for transfers between devices  12.6 us (21%)
  local copies, waits for them, and re-layouts  7 us (12%)
  between operations  1.41 us (2%)
  other arithmetic  0.67 us (1%)
    ppermute x9, waiting for transfers between devices, swap(): return lax.ppermute(array, ('dom', 'rep'), pairs)  12.4 us
    ppermute x9, starting transfers between devices, swap(): return lax.ppermute(array, ('dom', 'rep'), pairs)  11.6 us
    unnamed x26, local copies, waits for them, and re-layouts  7 us
    pallas_call x1, Pallas kernels, shards(): pl.pallas_call(functools.partial(gather_kernel, (replicas, groups, nrel,...  6.97 us
    all_to_all x1, starting transfers between devices, shards(): received = lax.all_to_all(served, 'dom', 0, 0, tiled=True)  5.84 us
    ppermute x3, starting transfers between devices, shards(): held.append(lax.ppermute(idx, 'rep', turned(replicas, hop)))  3.23 us
    pallas_call x1, Pallas kernels, shards(): pl.pallas_call(functools.partial(main_kernel, cfg), out_shape=[jax.ShapeD...  3.19 us
    pallas_call x1, Pallas kernels, shards(): pl.pallas_call(functools.partial(spread_kernel, workers, replicas, narrow...  1.84 us
  transfers between devices with their start and end apart: 14, of which 10 were waited for; matrix products, arithmetic and copies ran while one was open for 1% of the time, Pallas kernels for 15%

profile of v10, /device:TPU:0, one launch (start us, length us, event | category | flops | bytes accessed | tf_op | source)
XLA Modules:
  0.0 58.2 jit_solution(157151089906218940)
XLA Ops:
  1.3 1.8 %prep.1 = (s32[8,512]{1,0:T(8,128)}, f32[8,2,400]{2,1,0:T(2,128)}) custom-call(s32[1,2,8]{2,1,0:T(2,128)} %bitcast.7, s32[1,1]{1,0:T(1,128)S(6)} %copy.10.count, bf16[400,256]{1,0:T(8,128)(2,1)} %bitcast.10, s32[1,1,512]{2,1,0:T(1,128)} %src.1, s32[1,1,512]{2,1,0:T(1,128)} %rel.1, s32[1,1,512]{2,1,0:T(1,128)} %dst.1, s32[1,1,2,384]{3,2,1,0:T(2,128)} %neg.1), custom_call_target="tpu_custom_call" | custom-call | tf_op jit(solution)/shard_map/prep/pallas_call | solution.py:374
  3.1 2.4 %collective-permute-start.2 = (s32[8,512]{1,0:T(8,128)}, s32[8,512]{1,0:T(8,128)S(1)}, u32[]{:S(2)}, u32[]{:S(2)}) collective-permute-start(s32[8,512]{1,0:T(8,128)} %get-tuple-element.17.refs_0_), channel_id=1, source_target_pairs={{0,3},{1,0},{2,1},{3,2},{4,7},{5,4},{6,5},{7,6},{8,11},{9,8},{10,9... | collective-permute-start | bytes 49160 | tf_op jit(solution)/shard_map/ppermute | solution.py:399
  5.5 0.6 %collective-permute-start.1 = (s32[8,512]{1,0:T(8,128)}, s32[8,512]{1,0:T(8,128)S(1)}, u32[]{:S(2)}, u32[]{:S(2)}) collective-permute-start(s32[8,512]{1,0:T(8,128)} %get-tuple-element.17.refs_0_), channel_id=1, source_target_pairs={{0,2},{1,3},{2,0},{3,1},{4,6},{5,7},{6,4},{7,5},{8,10},{9,11},{10,... | collective-permute-start | bytes 49160 | tf_op jit(solution)/shard_map/ppermute | solution.py:399
  6.2 0.2 collective-permute-start
  6.3 5.8 %all-to-all-start = ((f32[8,2,400]{2,1,0:T(2,128)}), f32[8,2,400]{2,1,0:T(2,128)S(1)}, u32[]{:S(2)}, u32[]{:S(2)}) async-start(f32[8,2,400]{2,1,0:T(2,128)} %get-tuple-element.22), calls=%async_computation | async-start | bytes 65536 | tf_op jit(solution)/shard_map/all_to_all | solution.py:400
  12.2 0.6 %pad_add_fusion.1.place = s32[2]{0:T(128)} fusion(s32[1]{0:T(128)} %bitcast.1, s32[1]{0:T(128)} %bitcast), kind=kLoop, calls=%fused_computation.1 | loop fusion | flops 2 | bytes 16 | tf_op jit(solution)/shard_map/stack | solution.py:372
  12.8 0.0 collective-permute-done.2.refs_3_
  12.8 0.0 copy-start.5
  12.8 0.0 collective-permute-done.1.refs_2_
  12.8 0.0 copy-start.7
  12.8 0.0 collective-permute-done.refs_1_
  12.8 0.0 copy-start.9
  12.8 0.6 copy-done.5
  13.4 0.0 copy-done.7
  13.4 0.0 copy-done.9
  13.4 0.0 copy-start.4
  13.4 0.0 copy-start.11
  13.4 7.0 %gather.1 = (s32[8,1536]{1,0:T(8,128)}, bf16[400,1536]{1,0:T(8,128)(2,1)}, f32[104,1536]{1,0:T(8,128)}, f32[104,1536]{1,0:T(8,128)}) custom-call(s32[2]{0:T(128)} %pad_add_fusion.1.place, s32[8,512]{1,0:T(8,128)} %get-tuple-element.17.refs_0_, s32[8,512]{1,0:T(8,128)} %copy-done.9, s32[8,512]{1,0:T(8,128)} %copy-done.7, s32[8,512]{1,0:T(8,128)} %copy-done.5, ...), custom_call_target="tpu_custom_call" | custom-call | flops 2831155200 | bytes 4915200 | tf_op jit(solution)/shard_map/gather/pallas_call | solution.py:403
  20.4 0.0 all-to-all-done.refs_8_
  20.4 0.0 copy-done.4
  20.4 0.0 copy-done.11
  20.5 0.0 copy-start
  20.5 1.3 %copy-done = bf16[400,1536]{1,0:T(8,128)(2,1)S(1)} copy-done((bf16[400,1536]{1,0:T(8,128)(2,1)S(1)}, bf16[400,1536]{1,0:T(8,128)(2,1)}, u32[]{:S(2)}) %copy-start) | copy-done | bytes 1228824
  21.7 0.0 copy-start.1
  21.7 1.1 %copy-done.1 = f32[104,1536]{1,0:T(8,128)S(1)} copy-done((f32[104,1536]{1,0:T(8,128)S(1)}, f32[104,1536]{1,0:T(8,128)}, u32[]{:S(2)}) %copy-start.1) | copy-done | bytes 639000
  22.8 0.0 copy-start.2
  22.8 1.1 %copy-done.2 = f32[104,1536]{1,0:T(8,128)S(1)} copy-done((f32[104,1536]{1,0:T(8,128)S(1)}, f32[104,1536]{1,0:T(8,128)}, u32[]{:S(2)}) %copy-start.2) | copy-done | bytes 639000
  23.9 0.0 copy-start.3
  23.9 0.8 %copy-done.3 = s32[8,1536]{1,0:T(8,128)S(1)} copy-done((s32[8,1536]{1,0:T(8,128)S(1)}, s32[8,1536]{1,0:T(8,128)}, u32[]{:S(2)}) %copy-start.3) | copy-done | bytes 49176
  24.7 0.0 copy-start.6
  24.7 0.7 %copy-done.6 = s32[8,512]{1,0:T(8,128)S(1)} copy-done((s32[8,512]{1,0:T(8,128)S(1)}, s32[8,512]{1,0:T(8,128)}, u32[]{:S(2)}) %copy-start.6) | copy-done | bytes 16408
  25.4 0.0 copy-start.8
  25.4 0.7 %copy-done.8 = s32[8,512]{1,0:T(8,128)S(1)} copy-done((s32[8,512]{1,0:T(8,128)S(1)}, s32[8,512]{1,0:T(8,128)}, u32[]{:S(2)}) %copy-start.8) | copy-done | bytes 16408
  26.1 0.0 copy-start.10
  26.1 0.7 %copy-done.10 = s32[8,512]{1,0:T(8,128)S(1)} copy-done((s32[8,512]{1,0:T(8,128)S(1)}, s32[8,512]{1,0:T(8,128)}, u32[]{:S(2)}) %copy-start.10) | copy-done | bytes 16408
  26.9 0.0 copy-start.12
  26.9 3.2 %edges.1 = (f32[100,256]{1,0:T(8,128)S(1)}, s16[2,112,128]{2,1,0:T(8,128)(2,1)S(1)}, s16[2,112,128]{2,1,0:T(8,128)(2,1)S(1)}, s16[2,112,128]{2,1,0:T(8,128)(2,1)S(1)}, s16[2,112,128]{2,1,0:T(8,128)(2,1)S(1)}) custom-call(s32[2]{0:T(128)S(1)} %copy-done.11, s32[8,512]{1,0:T(8,128)S(1)} %copy-done.4, s32[8,512]{1,0:T(8,128)S(1)} %copy-done.10, ...), custom_call_target="tpu_custom_call" | custom-call | tf_op jit(solution)/shard_map/edges/pallas_call | solution.py:435
  30.1 2.1 %collective-permute-start.3 = (s16[2,112,128]{2,1,0:T(8,128)(2,1)S(1)}, s16[2,112,128]{2,1,0:T(8,128)(2,1)S(1)}, u32[]{:S(2)}, u32[]{:S(2)}) collective-permute-start(s16[2,112,128]{2,1,0:T(8,128)(2,1)S(1)} %get-tuple-element.24), channel_id=1, source_target_pairs={{0,4},{1,5},{2,6},{3,7},{4,0},{5,1},{6,2},{7,3},{8,12},{9,13},{10,... | collective-permute-start | bytes 172040 | tf_op jit(solution)/shard_map/ppermute | solution.py:459
  32.1 1.5 %collective-permute-start.4 = (s16[2,112,128]{2,1,0:T(8,128)(2,1)S(1)}, s16[2,112,128]{2,1,0:T(8,128)(2,1)S(1)}, u32[]{:S(2)}, u32[]{:S(2)}) collective-permute-start(s16[2,112,128]{2,1,0:T(8,128)(2,1)S(1)} %get-tuple-element.25), channel_id=1, source_target_pairs={{0,8},{1,9},{2,10},{3,11},{4,12},{5,13},{6,14},{7,15},{8,0},{9,1},... | collective-permute-start | bytes 172040 | tf_op jit(solution)/shard_map/ppermute | solution.py:459
  33.6 0.1 collective-permute-start.5
  33.7 1.1 %collective-permute-done.3.refs_1_ = s16[2,112,128]{2,1,0:T(8,128)(2,1)S(1)} collective-permute-done((s16[2,112,128]{2,1,0:T(8,128)(2,1)S(1)}, s16[2,112,128]{2,1,0:T(8,128)(2,1)S(1)}, u32[]{:S(2)}, u32[]{:S(2)}) %collective-permute-start.3) | collective-permute-done | bytes 57376 | tf_op jit(solution)/shard_map/ppermute | solution.py:459
  34.8 1.7 %collective-permute-done.4.refs_2_ = s16[2,112,128]{2,1,0:T(8,128)(2,1)S(1)} collective-permute-done((s16[2,112,128]{2,1,0:T(8,128)(2,1)S(1)}, s16[2,112,128]{2,1,0:T(8,128)(2,1)S(1)}, u32[]{:S(2)}, u32[]{:S(2)}) %collective-permute-start.4) | collective-permute-done | bytes 57376 | tf_op jit(solution)/shard_map/ppermute | solution.py:459
  36.6 2.1 %collective-permute-done.5.refs_3_ = s16[2,112,128]{2,1,0:T(8,128)(2,1)S(1)} collective-permute-done((s16[2,112,128]{2,1,0:T(8,128)(2,1)S(1)}, s16[2,112,128]{2,1,0:T(8,128)(2,1)S(1)}, u32[]{:S(2)}, u32[]{:S(2)}) %collective-permute-start.5) | collective-permute-done | bytes 57376 | tf_op jit(solution)/shard_map/ppermute | solution.py:459
  38.7 0.1 quad.1.refs_0_
  38.8 2.4 %collective-permute-start.8 = (s16[2,112,128]{2,1,0:T(8,128)(2,1)S(1)}, s16[2,112,128]{2,1,0:T(8,128)(2,1)S(1)}, u32[]{:S(2)}, u32[]{:S(2)}) collective-permute-start(s16[2,112,128]{2,1,0:T(8,128)(2,1)S(1)} %quad.1.refs_0_), channel_id=1, source_target_pairs={{0,24},{1,25},{2,26},{3,27},{4,28},{5,29},{6,30},{7,31},{8,16},{9,... | collective-permute-start | bytes 172040 | tf_op jit(solution)/shard_map/ppermute | solution.py:459
  41.2 0.6 collective-permute-start.7
  41.8 1.5 %collective-permute-start.6 = (s16[2,112,128]{2,1,0:T(8,128)(2,1)S(1)}, s16[2,112,128]{2,1,0:T(8,128)(2,1)S(1)}, u32[]{:S(2)}, u32[]{:S(2)}) collective-permute-start(s16[2,112,128]{2,1,0:T(8,128)(2,1)S(1)} %quad.1.refs_0_), channel_id=1, source_target_pairs={{0,16},{1,17},{2,18},{3,19},{4,20},{5,21},{6,22},{7,23},{8,24},{9,... | collective-permute-start | bytes 172040 | tf_op jit(solution)/shard_map/ppermute | solution.py:459
  43.3 1.9 %collective-permute-done.8.refs_3_ = s16[2,112,128]{2,1,0:T(8,128)(2,1)S(1)} collective-permute-done((s16[2,112,128]{2,1,0:T(8,128)(2,1)S(1)}, s16[2,112,128]{2,1,0:T(8,128)(2,1)S(1)}, u32[]{:S(2)}, u32[]{:S(2)}) %collective-permute-start.8) | collective-permute-done | bytes 57376 | tf_op jit(solution)/shard_map/ppermute | solution.py:459
  45.1 0.5 collective-permute-done.7.refs_2_
  45.6 1.2 %collective-permute-done.6.refs_1_ = s16[2,112,128]{2,1,0:T(8,128)(2,1)S(1)} collective-permute-done((s16[2,112,128]{2,1,0:T(8,128)(2,1)S(1)}, s16[2,112,128]{2,1,0:T(8,128)(2,1)S(1)}, u32[]{:S(2)}, u32[]{:S(2)}) %collective-permute-start.6) | collective-permute-done | bytes 57376 | tf_op jit(solution)/shard_map/ppermute | solution.py:459
  46.9 0.2 total.1
  47.0 1.3 %collective-permute-start.11 = (s16[4,112,128]{2,1,0:T(8,128)(2,1)S(1)}, s16[4,112,128]{2,1,0:T(8,128)(2,1)S(1)}, u32[]{:S(2)}, u32[]{:S(2)}) collective-permute-start(s16[4,112,128]{2,1,0:T(8,128)(2,1)S(1)} %total.1), channel_id=1, source_target_pairs={{0,6},{1,7},{2,4},{3,5},{4,2},{5,3},{6,0},{7,1},{8,14},{9,15},{10,... | collective-permute-start | bytes 344072 | tf_op jit(solution)/shard_map/ppermute | solution.py:459
  48.3 1.3 %collective-permute-start.10 = (s16[4,112,128]{2,1,0:T(8,128)(2,1)S(1)}, s16[4,112,128]{2,1,0:T(8,128)(2,1)S(1)}, u32[]{:S(2)}, u32[]{:S(2)}) collective-permute-start(s16[4,112,128]{2,1,0:T(8,128)(2,1)S(1)} %total.1), channel_id=1, source_target_pairs={{0,2},{1,3},{2,0},{3,1},{4,6},{5,7},{6,4},{7,5},{8,10},{9,11},{10,... | collective-permute-start | bytes 344072 | tf_op jit(solution)/shard_map/ppermute | solution.py:459
  49.6 1.0 %collective-permute-start.9 = (s16[4,112,128]{2,1,0:T(8,128)(2,1)S(1)}, s16[4,112,128]{2,1,0:T(8,128)(2,1)S(1)}, u32[]{:S(2)}, u32[]{:S(2)}) collective-permute-start(s16[4,112,128]{2,1,0:T(8,128)(2,1)S(1)} %total.1), channel_id=1, source_target_pairs={{0,4},{1,5},{2,6},{3,7},{4,0},{5,1},{6,2},{7,3},{8,12},{9,13},{10,... | collective-permute-start | bytes 344072 | tf_op jit(solution)/shard_map/ppermute | solution.py:459
  50.6 2.3 %collective-permute-done.11 = s16[4,112,128]{2,1,0:T(8,128)(2,1)S(1)} collective-permute-done((s16[4,112,128]{2,1,0:T(8,128)(2,1)S(1)}, s16[4,112,128]{2,1,0:T(8,128)(2,1)S(1)}, u32[]{:S(2)}, u32[]{:S(2)}) %collective-permute-start.11) | collective-permute-done | bytes 114720 | tf_op jit(solution)/shard_map/ppermute | solution.py:459
  52.9 1.1 %collective-permute-done.10 = s16[4,112,128]{2,1,0:T(8,128)(2,1)S(1)} collective-permute-done((s16[4,112,128]{2,1,0:T(8,128)(2,1)S(1)}, s16[4,112,128]{2,1,0:T(8,128)(2,1)S(1)}, u32[]{:S(2)}, u32[]{:S(2)}) %collective-permute-start.10) | collective-permute-done | bytes 114720 | tf_op jit(solution)/shard_map/ppermute | solution.py:459
  54.0 0.4 collective-permute-done.9
  54.5 0.1 collective-permute-start.12
  54.5 0.0 copy-done.12
  54.6 1.6 %entity.1 = f32[100,256]{1,0:T(8,128)} custom-call(s32[2]{0:T(128)S(1)} %copy-done.11, s32[1,2,8]{2,1,0:T(2,128)S(1)} %bitcast.8, f32[100,256]{1,0:T(8,128)S(1)} %get-tuple-element.29.lhs, s16[2,112,128]{2,1,0:T(8,128)(2,1)S(1)} %quad.1.refs_0_, s16[2,112,128]{2,1,0:T(8,128)(2,1)S(1)} %collective-permute-done.6.refs_1_), custom_call_target="tpu_custom_call" | custom-call | flops 1000000000 | bytes 1000000 | tf_op jit(solution)/shard_map/entity/pallas_call | solution.py:497
  56.2 0.2 collective-permute-done.12.other
  56.3 1.8 %spread.1 = f32[400,1000]{1,0:T(8,128)} custom-call(s32[2]{0:T(128)S(1)} %copy-done.11, s16[16,112,128]{2,1,0:T(8,128)(2,1)S(1)} %pad_add_fusion.mine, s16[16,112,128]{2,1,0:T(8,128)(2,1)S(1)} %collective-permute-done.12.other), custom_call_target="tpu_custom_call" | custom-call | tf_op jit(solution)/shard_map/spread/pallas_call | solution.py:512
  (1 shorter events, 0.0 us)
Async XLA Ops:
  3.1 9.7 %collective-permute-start.2 = (s32[8,512]{1,0:T(8,128)}, s32[8,512]{1,0:T(8,128)S(1)}, u32[]{:S(2)}, u32[]{:S(2)}) collective-permute-start(s32[8,512]{1,0:T(8,128)} %get-tuple-element.17.refs_0_), channel_id=1, source_target_pairs={{0,3},{1,0},{2,1},{3,2},{4,7},{5,4},{6,5},{7,6},{8,11},{9,8},{10,9... | collective-permute-start | bytes 49160 | tf_op jit(solution)/shard_map/ppermute | solution.py:399
  5.5 7.3 %collective-permute-start.1 = (s32[8,512]{1,0:T(8,128)}, s32[8,512]{1,0:T(8,128)S(1)}, u32[]{:S(2)}, u32[]{:S(2)}) collective-permute-start(s32[8,512]{1,0:T(8,128)} %get-tuple-element.17.refs_0_), channel_id=1, source_target_pairs={{0,2},{1,3},{2,0},{3,1},{4,6},{5,7},{6,4},{7,5},{8,10},{9,11},{10,... | collective-permute-start | bytes 49160 | tf_op jit(solution)/shard_map/ppermute | solution.py:399
  6.2 6.7 %collective-permute-start = (s32[8,512]{1,0:T(8,128)}, s32[8,512]{1,0:T(8,128)S(1)}, u32[]{:S(2)}, u32[]{:S(2)}) collective-permute-start(s32[8,512]{1,0:T(8,128)} %get-tuple-element.17.refs_0_), channel_id=1, source_target_pairs={{0,1},{1,2},{2,3},{3,0},{4,5},{5,6},{6,7},{7,4},{8,9},{9,10},{10,1... | collective-permute-start | bytes 49160 | tf_op jit(solution)/shard_map/ppermute | solution.py:399
  6.3 14.1 %all-to-all-start = ((f32[8,2,400]{2,1,0:T(2,128)}), f32[8,2,400]{2,1,0:T(2,128)S(1)}, u32[]{:S(2)}, u32[]{:S(2)}) async-start(f32[8,2,400]{2,1,0:T(2,128)} %get-tuple-element.22), calls=%async_computation | async-start | bytes 65536 | tf_op jit(solution)/shard_map/all_to_all | solution.py:400
  12.8 0.6 %copy-start.5 = (s32[8,512]{1,0:T(8,128)}, s32[8,512]{1,0:T(8,128)S(1)}, u32[]{:S(2)}) copy-start(s32[8,512]{1,0:T(8,128)S(1)} %collective-permute-done.2.refs_3_) | copy-start | bytes 49156
  12.8 0.6 %copy-start.7 = (s32[8,512]{1,0:T(8,128)}, s32[8,512]{1,0:T(8,128)S(1)}, u32[]{:S(2)}) copy-start(s32[8,512]{1,0:T(8,128)S(1)} %collective-permute-done.1.refs_2_) | copy-start | bytes 49156
  12.8 0.6 %copy-start.9 = (s32[8,512]{1,0:T(8,128)}, s32[8,512]{1,0:T(8,128)S(1)}, u32[]{:S(2)}) copy-start(s32[8,512]{1,0:T(8,128)S(1)} %collective-permute-done.refs_1_) | copy-start | bytes 49156
  13.4 7.0 %copy-start.4 = (s32[8,512]{1,0:T(8,128)S(1)}, s32[8,512]{1,0:T(8,128)}, u32[]{:S(2)}) copy-start(s32[8,512]{1,0:T(8,128)} %get-tuple-element.17.refs_0_) | copy-start | bytes 49156
  13.4 7.0 %copy-start.11 = (s32[2]{0:T(128)S(1)}, s32[2]{0:T(128)}, u32[]{:S(2)}) copy-start(s32[2]{0:T(128)} %pad_add_fusion.1.place) | copy-start | bytes 28
  20.5 1.3 %copy-start = (bf16[400,1536]{1,0:T(8,128)(2,1)S(1)}, bf16[400,1536]{1,0:T(8,128)(2,1)}, u32[]{:S(2)}) copy-start(bf16[400,1536]{1,0:T(8,128)(2,1)} %get-tuple-element.19.refs_5_) | copy-start | bytes 3686404
  21.7 1.1 %copy-start.1 = (f32[104,1536]{1,0:T(8,128)S(1)}, f32[104,1536]{1,0:T(8,128)}, u32[]{:S(2)}) copy-start(f32[104,1536]{1,0:T(8,128)} %get-tuple-element.20.refs_6_) | copy-start | bytes 1916932
  22.8 1.1 %copy-start.2 = (f32[104,1536]{1,0:T(8,128)S(1)}, f32[104,1536]{1,0:T(8,128)}, u32[]{:S(2)}) copy-start(f32[104,1536]{1,0:T(8,128)} %get-tuple-element.21.refs_7_) | copy-start | bytes 1916932
  23.9 0.8 %copy-start.3 = (s32[8,1536]{1,0:T(8,128)S(1)}, s32[8,1536]{1,0:T(8,128)}, u32[]{:S(2)}) copy-start(s32[8,1536]{1,0:T(8,128)} %get-tuple-element.18.refs_4_) | copy-start | bytes 147460
  24.7 0.7 %copy-start.6 = (s32[8,512]{1,0:T(8,128)S(1)}, s32[8,512]{1,0:T(8,128)}, u32[]{:S(2)}) copy-start(s32[8,512]{1,0:T(8,128)} %copy-done.5) | copy-start | bytes 49156
  25.4 0.7 %copy-start.8 = (s32[8,512]{1,0:T(8,128)S(1)}, s32[8,512]{1,0:T(8,128)}, u32[]{:S(2)}) copy-start(s32[8,512]{1,0:T(8,128)} %copy-done.7) | copy-start | bytes 49156
  26.1 0.7 %copy-start.10 = (s32[8,512]{1,0:T(8,128)S(1)}, s32[8,512]{1,0:T(8,128)}, u32[]{:S(2)}) copy-start(s32[8,512]{1,0:T(8,128)} %copy-done.9) | copy-start | bytes 49156
  26.9 27.7 %copy-start.12 = (s32[1,8,2]{1,2,0:T(2,128)S(1)}, s32[1,8,2]{1,2,0:T(2,128)}, u32[]{:S(2)}) copy-start(s32[1,8,2]{1,2,0:T(2,128)} %param.10) | copy-start | bytes 196
  30.1 4.8 %collective-permute-start.3 = (s16[2,112,128]{2,1,0:T(8,128)(2,1)S(1)}, s16[2,112,128]{2,1,0:T(8,128)(2,1)S(1)}, u32[]{:S(2)}, u32[]{:S(2)}) collective-permute-start(s16[2,112,128]{2,1,0:T(8,128)(2,1)S(1)} %get-tuple-element.24), channel_id=1, source_target_pairs={{0,4},{1,5},{2,6},{3,7},{4,0},{5,1},{6,2},{7,3},{8,12},{9,13},{10,... | collective-permute-start | bytes 172040 | tf_op jit(solution)/shard_map/ppermute | solution.py:459
  32.1 4.4 %collective-permute-start.4 = (s16[2,112,128]{2,1,0:T(8,128)(2,1)S(1)}, s16[2,112,128]{2,1,0:T(8,128)(2,1)S(1)}, u32[]{:S(2)}, u32[]{:S(2)}) collective-permute-start(s16[2,112,128]{2,1,0:T(8,128)(2,1)S(1)} %get-tuple-element.25), channel_id=1, source_target_pairs={{0,8},{1,9},{2,10},{3,11},{4,12},{5,13},{6,14},{7,15},{8,0},{9,1},... | collective-permute-start | bytes 172040 | tf_op jit(solution)/shard_map/ppermute | solution.py:459
  33.6 5.1 %collective-permute-start.5 = (s16[2,112,128]{2,1,0:T(8,128)(2,1)S(1)}, s16[2,112,128]{2,1,0:T(8,128)(2,1)S(1)}, u32[]{:S(2)}, u32[]{:S(2)}) collective-permute-start(s16[2,112,128]{2,1,0:T(8,128)(2,1)S(1)} %get-tuple-element.26), channel_id=1, source_target_pairs={{0,12},{1,13},{2,14},{3,15},{4,8},{5,9},{6,10},{7,11},{8,4},{9,5},... | collective-permute-start | bytes 172040 | tf_op jit(solution)/shard_map/ppermute | solution.py:459
  38.8 6.3 %collective-permute-start.8 = (s16[2,112,128]{2,1,0:T(8,128)(2,1)S(1)}, s16[2,112,128]{2,1,0:T(8,128)(2,1)S(1)}, u32[]{:S(2)}, u32[]{:S(2)}) collective-permute-start(s16[2,112,128]{2,1,0:T(8,128)(2,1)S(1)} %quad.1.refs_0_), channel_id=1, source_target_pairs={{0,24},{1,25},{2,26},{3,27},{4,28},{5,29},{6,30},{7,31},{8,16},{9,... | collective-permute-start | bytes 172040 | tf_op jit(solution)/shard_map/ppermute | solution.py:459
  41.2 4.4 %collective-permute-start.7 = (s16[2,112,128]{2,1,0:T(8,128)(2,1)S(1)}, s16[2,112,128]{2,1,0:T(8,128)(2,1)S(1)}, u32[]{:S(2)}, u32[]{:S(2)}) collective-permute-start(s16[2,112,128]{2,1,0:T(8,128)(2,1)S(1)} %quad.1.refs_0_), channel_id=1, source_target_pairs={{0,8},{1,9},{2,10},{3,11},{4,12},{5,13},{6,14},{7,15},{8,0},{9,1},... | collective-permute-start | bytes 172040 | tf_op jit(solution)/shard_map/ppermute | solution.py:459
  41.8 5.1 %collective-permute-start.6 = (s16[2,112,128]{2,1,0:T(8,128)(2,1)S(1)}, s16[2,112,128]{2,1,0:T(8,128)(2,1)S(1)}, u32[]{:S(2)}, u32[]{:S(2)}) collective-permute-start(s16[2,112,128]{2,1,0:T(8,128)(2,1)S(1)} %quad.1.refs_0_), channel_id=1, source_target_pairs={{0,16},{1,17},{2,18},{3,19},{4,20},{5,21},{6,22},{7,23},{8,24},{9,... | collective-permute-start | bytes 172040 | tf_op jit(solution)/shard_map/ppermute | solution.py:459
  47.0 5.9 %collective-permute-start.11 = (s16[4,112,128]{2,1,0:T(8,128)(2,1)S(1)}, s16[4,112,128]{2,1,0:T(8,128)(2,1)S(1)}, u32[]{:S(2)}, u32[]{:S(2)}) collective-permute-start(s16[4,112,128]{2,1,0:T(8,128)(2,1)S(1)} %total.1), channel_id=1, source_target_pairs={{0,6},{1,7},{2,4},{3,5},{4,2},{5,3},{6,0},{7,1},{8,14},{9,15},{10,... | collective-permute-start | bytes 344072 | tf_op jit(solution)/shard_map/ppermute | solution.py:459
  48.3 5.7 %collective-permute-start.10 = (s16[4,112,128]{2,1,0:T(8,128)(2,1)S(1)}, s16[4,112,128]{2,1,0:T(8,128)(2,1)S(1)}, u32[]{:S(2)}, u32[]{:S(2)}) collective-permute-start(s16[4,112,128]{2,1,0:T(8,128)(2,1)S(1)} %total.1), channel_id=1, source_target_pairs={{0,2},{1,3},{2,0},{3,1},{4,6},{5,7},{6,4},{7,5},{8,10},{9,11},{10,... | collective-permute-start | bytes 344072 | tf_op jit(solution)/shard_map/ppermute | solution.py:459
  49.6 4.8 %collective-permute-start.9 = (s16[4,112,128]{2,1,0:T(8,128)(2,1)S(1)}, s16[4,112,128]{2,1,0:T(8,128)(2,1)S(1)}, u32[]{:S(2)}, u32[]{:S(2)}) collective-permute-start(s16[4,112,128]{2,1,0:T(8,128)(2,1)S(1)} %total.1), channel_id=1, source_target_pairs={{0,4},{1,5},{2,6},{3,7},{4,0},{5,1},{6,2},{7,3},{8,12},{9,13},{10,... | collective-permute-start | bytes 344072 | tf_op jit(solution)/shard_map/ppermute | solution.py:459
  54.5 1.9 %collective-permute-start.12 = (s16[16,112,128]{2,1,0:T(8,128)(2,1)S(1)}, s16[16,112,128]{2,1,0:T(8,128)(2,1)S(1)}, u32[]{:S(2)}, u32[]{:S(2)}) collective-permute-start(s16[16,112,128]{2,1,0:T(8,128)(2,1)S(1)} %pad_add_fusion.mine), channel_id=1, source_target_pairs={{0,1},{1,0},{2,3},{3,2},{4,5},{5,4},{6,7},{7,6},{8,9},{9,8},{10,11... | collective-permute-start | bytes 1376264 | tf_op jit(solution)/shard_map/ppermute | solution.py:510

commit v11 on v9

--- a/solution.py
+++ b/solution.py
@@ -161,7 +161,7 @@
     idx_refs, refs = refs[:replicas], refs[replicas:]
     (packed, query_v, lhs_v, rel_v, received), refs = refs[:5], refs[5:]
     out_lhs, refs = refs[0], refs[1:]
-    outs, refs = (refs[:SOURCES], refs[SOURCES:]) if direct else (refs[:1], refs[1:])
+    out, refs = refs[0], refs[1:]
     table_f, table_t, query_s, wide_t, mixed, codes_s, powers_s, tables_s = refs
     edges = idx_refs[0].shape[1]
     dim, total = query_v.shape
@@ -238,31 +238,23 @@
         target[...] = mixed[...].astype(jnp.int16)
 
     if direct:
-        for h in range(SOURCES):
+        for low in range(SOURCES):
             for top in range(2):
-                o = top * 4 + flipped(dom % 4, h)
-                write(outs[h].at[top], o, pl.ds(pl.multiple_of(o * block, block), block))
+                o = top * SOURCES + low
+                write(out.at[low, top], o, slice(o * block, (o + 1) * block))
     else:
         for o in range(workers):
-            write(outs[0].at[o], o, slice(o * block, (o + 1) * block))
-
-
-def flipped(index, mask):
-    out, bit = index * 0, 1
-    while bit < 4:
-        out = out + bit * lax.rem(index // bit + (mask // bit) % 2, 2)
-        bit *= 2
-    return out
+            write(out.at[o, 0], o, slice(o * block, (o + 1) * block))
 
 
 def quad_kernel(narrow, cap, *refs):
-    parts, out, mixed = refs[:-2], refs[-2], refs[-1]
+    parts, out, mixed = refs
     power = slice(narrow + SOURCES * cap, narrow + SOURCES * cap + 1)
     mixed[...] = jnp.zeros(mixed.shape, jnp.int32)
     for top in range(out.shape[0]):
         total = jnp.zeros((narrow, out.shape[2]), F32)
-        for n, part in enumerate(parts):
-            both = part[top].astype(jnp.int32)
+        for n in range(SOURCES):
+            both = parts[n, top].astype(jnp.int32)
             total += decode(both[:narrow], both[power])
             row = narrow + n * cap
             mixed[row : row + cap, :] = both[narrow : narrow + cap]
@@ -270,41 +262,38 @@
         out[top] = mixed[...].astype(jnp.int16)
 
 
-def sum_kernel(scale, narrow, cap, block, terms, *refs):
-    parts, out, mixed = refs[:-2], refs[-2], refs[-1]
-    depth = parts[0].shape[0]
+def sum_kernel(scale, narrow, cap, block, recv, out, mixed):
+    sources, depth = recv.shape[:2]
+    pairs = out.shape[0] // depth
     power = slice(narrow + SOURCES * cap, narrow + SOURCES * cap + 1)
     mixed[...] = jnp.zeros(mixed.shape, jnp.int32)
-    for first in range(0, len(parts), terms):
+    for first in range(pairs):
         for top in range(depth):
             total = jnp.zeros((narrow, block), F32)
-            for part in parts[first : first + terms]:
-                both = part[top].astype(jnp.int32)
+            for n in range(first, sources, pairs):
+                both = recv[n, top].astype(jnp.int32)
                 total += decode(both[:narrow, :block], both[power, :block])
             mixed[:narrow, :block], mixed[power, :block] = encode(total * F32(scale), 0)
-            out[first // terms * depth + top] = mixed[...].astype(jnp.int16)
-
-
-def entity_kernel(direct, narrow, place, serve, lhs, *refs):
-    recv, out, terms, onehot = refs[:-3], refs[-3], refs[-2], refs[-1]
+            out[first * depth + top] = mixed[...].astype(jnp.int16)
+
+
+def entity_kernel(direct, narrow, place, serve, lhs, recv, out, terms, onehot):
     cap, workers = serve.shape[1], serve.shape[2]
     rows = out.shape[1]
     lane = iota((1, rows), 1)
     for h in range(workers):
         if direct:
-            turn, hop = h % SOURCES, h // SOURCES
-            mine = place[0] // 4
-            both = recv[hop][mine].astype(jnp.int32)
-            worker = lax.rem(mine + hop, 2) * 4 + flipped(place[0] % 4, turn)
+            turn, low = h % SOURCES, lax.rem(place[0] // 2, 2)
+            both = recv[h // SOURCES * 2 + low, place[0] // SOURCES].astype(jnp.int32)
         else:
-            turn, both, worker = 0, recv[0][h].astype(jnp.int32), h
+            turn, both = 0, recv[h, 0].astype(jnp.int32)
         row = narrow + turn * cap
         both = both[row : row + cap]
         terms[h * cap : (h + 1) * cap, :] = jnp.where(
             iota(both.shape, 1) < narrow, decode(both, both[:, narrow : narrow + 1]), 0.0
         )
         for c in range(cap):
-            spot = jnp.where(lane == serve[0, c, worker], 1.0, 0.0).astype(F32)
+            spot = jnp.where(lane == serve[0, c, h], 1.0, 0.0).astype(F32)
             onehot[h * cap + c : h * cap + c + 1, :] = spot
     spots = onehot[...].astype(BF16)
     parts = jnp.concatenate(split3(jnp.transpose(terms[...])), axis=1)
@@ -319,10 +308,9 @@
     moves, start = [], 0
     for r in range(replicas):
         for o in range(workers):
-            over_low = lax.rem(dom // 2 + o // 2, 2)
             over_y = lax.rem(dom + o, 2)
             over_x = lax.rem(rep // 2 + r // 2, 2)
-            spot = (over_y + 2 * over_x) * 4 + over_low * 2 + o // 4
+            spot = (over_y + 2 * over_x) * 4 + o // 2 % 2 * 2 + o // 4
             both = jnp.where(
                 here == r % 2, mine[spot].astype(jnp.int32), other[spot].astype(jnp.int32)
             )
@@ -418,13 +406,15 @@
         tuple(offsets),
     )
     lanes = max(up(block, LANES), up(narrow, LANES))
-    outs = [2] * SOURCES if direct else [workers]
-    sizes = [jax.ShapeDtypeStruct((n, height, lanes), jnp.int16) for n in outs]
-    lhs_part, *sent = pl.pallas_call(
+    leading = (SOURCES, 2) if direct else (workers, 1)
+    lhs_part, sent = pl.pallas_call(
         functools.partial(main_kernel, cfg),
-        out_shape=[jax.ShapeDtypeStruct((narrow, rows), F32)] + sizes,
+        out_shape=(
+            jax.ShapeDtypeStruct((narrow, rows), F32),
+            jax.ShapeDtypeStruct(leading + (height, lanes), jnp.int16),
+        ),
         in_specs=[SMEM] + [VMEM] * (replicas + 5),
-        out_specs=[VMEM] * (1 + len(sizes)),
+        out_specs=(VMEM, VMEM),
         scratch_shapes=[
             pltpu.VMEM((slots, dim), F32),
             pltpu.VMEM((dim, slots), F32),
@@ -446,55 +436,56 @@
                 pairs.append((o * replicas + r, (o ^ dom_bits) * replicas + (r ^ rep_bits)))
         return lax.ppermute(array, ("dom", "rep"), pairs)
 
-    stack = jax.ShapeDtypeStruct((outs[0], height, lanes), jnp.int16)
     mixed = [pltpu.VMEM((height, lanes), jnp.int32)]
     if direct:
+        low_groups = [list(range(n, n + SOURCES)) for n in range(0, workers, SOURCES)]
+        got = lax.all_to_all(sent, "dom", 0, 0, axis_index_groups=low_groups, tiled=True)
         summed = pl.pallas_call(
             functools.partial(quad_kernel, narrow, cap),
-            out_shape=stack,
-            in_specs=[VMEM] * SOURCES,
+            out_shape=jax.ShapeDtypeStruct(leading[1:] + (height, lanes), jnp.int16),
+            in_specs=[VMEM],
             out_specs=VMEM,
             scratch_shapes=mixed,
             compiler_params=params(),
             name="quad",
-        )(sent[0], *[swap(sent[n], n) for n in range(1, SOURCES)])
-        recv = [summed, swap(summed, 4)]
-        parts = recv + [swap(summed, 2), swap(summed, 6)]
-        stack = jax.ShapeDtypeStruct((4, height, lanes), jnp.int16)
+        )(got)
+        columns = [list(range(n, workers, 2)) for n in range(2)]
+        recv = lax.all_gather(summed, "dom", axis_index_groups=columns)
+        stack = (4, height, lanes)
     else:
-        recv = [lax.all_to_all(sent[0], "dom", 0, 0, tiled=True)]
-        parts = [recv[0][w : w + 1] for w in range(workers)]
-        stack = jax.ShapeDtypeStruct((1, height, lanes), jnp.int16)
+        recv = lax.all_to_all(sent, "dom", 0, 0, tiled=True)
+        stack = (1, height, lanes)
     scale = 1.0 / (edges * workers * replicas)
     chunk = pl.pallas_call(
-        functools.partial(sum_kernel, scale, narrow, cap, block, 2 if direct else workers),
-        out_shape=stack,
-        in_specs=[VMEM] * len(parts),
+        functools.partial(sum_kernel, scale, narrow, cap, block),
+        out_shape=jax.ShapeDtypeStruct(stack, jnp.int16),
+        in_specs=[VMEM],
         out_specs=VMEM,
         scratch_shapes=mixed,
         compiler_params=params(),
         name="total",
-    )(*parts)
+    )(recv)
 
     if direct:
-        along_y = swap(chunk, 1)
-        along_y, lhs_part = lax.optimization_barrier((along_y, lhs_part))
+        base = jnp.concatenate(
+            [chunk, swap(chunk, 1), swap(chunk, 0, 2), swap(chunk, 1, 2)], axis=0
+        )
+        base, lhs_part = lax.optimization_barrier((base, lhs_part))
     entity_grad = pl.pallas_call(
         functools.partial(entity_kernel, direct, narrow),
         out_shape=jax.ShapeDtypeStruct((narrow, rows), F32),
-        in_specs=[SMEM] * 2 + [VMEM] * (1 + len(recv)),
+        in_specs=[SMEM] * 2 + [VMEM] * 2,
         out_specs=VMEM,
         scratch_shapes=[pltpu.VMEM((slots, lanes), F32), pltpu.VMEM((slots, rows), F32)],
         compiler_params=params(),
         cost_estimate=cost(10**9, 10**6),
         name="entity",
-    )(place, serve_t, lhs_part, *recv)
+    )(place, serve_t, lhs_part, recv)
 
     power_row = narrow + SOURCES * cap
     if direct:
-        base = jnp.concatenate([chunk, along_y, swap(chunk, 0, 2), swap(chunk, 1, 2)], axis=0)
-        base, entity_grad = lax.optimization_barrier((base, entity_grad))
         swapped = lax.ppermute(base, "rep", [(i, i ^ 1) for i in range(replicas)])
+        swapped, entity_grad = lax.optimization_barrier((swapped, entity_grad))
         relation_t = pl.pallas_call(
             functools.partial(spread_kernel, workers, replicas, narrow, power_row, block),
             out_shape=jax.ShapeDtypeStruct((dim, nrel), F32),

time: 51.1 us -> 58.3 us (1.14)
  blocking collectives: 0 us -> 24.3 us
  waiting for transfers between devices: 12.8 us -> 3.79 us
  starting transfers between devices: 20.8 us -> 12.7 us
    all_gather x0 -> x1, blocking collectives: none -> 13.8 us  [shards(): recv = lax.all_gather(summed, 'dom', axis_index_groups=columns)]
    all_to_all x0 -> x1, blocking collectives: none -> 10.5 us  [shards(): lax.all_to_all(sent, 'dom', 0, 0, axis_index_groups=low_groups, tiled=True)]
    ppermute x9 -> x3, starting transfers between devices: 11.6 us -> 3.55 us  [swap(): return lax.ppermute(array, ('dom', 'rep'), pairs)]
    ppermute x9 -> x3, waiting for transfers between devices: 11 us -> 3.58 us  [swap(): return lax.ppermute(array, ('dom', 'rep'), pairs)]
    ppermute x1, waiting for transfers between devices: 1.8 us -> 0.2 us  [shards(): swapped = lax.ppermute(base, 'rep', [(i, i ^ 1) for i in range(replicas)])]
  transfers between devices with their start and end apart: 14 -> 8, of which waited for: 9 -> 4; matrix products, arithmetic and copies ran while one was open for 0% -> 0% of each run, Pallas kernels for 11% -> 10%
where the time goes in v11:
time: 58.3 us; the launch traced here: 57.9 us
  blocking collectives  24.3 us (42%)
  starting transfers between devices  12.7 us (22%)
  Pallas kernels  12.6 us (22%)
  waiting for transfers between devices  3.79 us (7%)
  local copies, waits for them, and re-layouts  3.08 us (5%)
  between operations  1.37 us (2%)
    all_gather x1, blocking collectives, shards(): recv = lax.all_gather(summed, 'dom', axis_index_groups=columns)  13.8 us
    all_to_all x1, blocking collectives, shards(): lax.all_to_all(sent, 'dom', 0, 0, axis_index_groups=low_groups, tiled=True)  10.5 us
    all_to_all x1, starting transfers between devices, shards(): received = lax.all_to_all(served, 'dom', 0, 0, tiled=True)  5.84 us
    pallas_call x1, Pallas kernels, shards(): pl.pallas_call(functools.partial(gather_kernel, (replicas, groups, nrel,...  3.95 us
    ppermute x3, waiting for transfers between devices, swap(): return lax.ppermute(array, ('dom', 'rep'), pairs)  3.58 us
    ppermute x3, starting transfers between devices, swap(): return lax.ppermute(array, ('dom', 'rep'), pairs)  3.55 us
    ppermute x3, starting transfers between devices, shards(): held.append(lax.ppermute(idx, 'rep', turned(replicas, hop)))  3.23 us
    pallas_call x1, Pallas kernels, shards(): pl.pallas_call(functools.partial(main_kernel, cfg), out_shape=(jax.ShapeD...  3.16 us
  transfers between devices with their start and end apart: 8, of which 4 were waited for; matrix products, arithmetic and copies ran while one was open for 0% of the time, Pallas kernels for 10%

profile of v11, /device:TPU:0, one launch (start us, length us, event | category | flops | bytes accessed | tf_op | source)
XLA Modules:
  0.0 57.9 jit_solution(17291649397754893428)
XLA Ops:
  1.3 1.8 %prep.1 = (s32[8,512]{1,0:T(8,128)}, f32[8,2,400]{2,1,0:T(2,128)}) custom-call(s32[1,2,8]{2,1,0:T(2,128)} %bitcast.12, s32[1,1]{1,0:T(1,128)S(6)} %copy.10.count, bf16[400,256]{1,0:T(8,128)(2,1)} %bitcast.10, s32[1,1,512]{2,1,0:T(1,128)} %src.1, s32[1,1,512]{2,1,0:T(1,128)} %rel.1, s32[1,1,512]{2,1,0:T(1,128)} %dst.1, s32[1,1,2,384]{3,2,1,0:T(2,128)} %neg.1), custom_call_target="tpu_custom_call" | custom-call | tf_op jit(solution)/shard_map/prep/pallas_call | solution.py:353
  3.1 2.4 %collective-permute-start.2 = (s32[8,512]{1,0:T(8,128)}, s32[8,512]{1,0:T(8,128)S(1)}, u32[]{:S(2)}, u32[]{:S(2)}) collective-permute-start(s32[8,512]{1,0:T(8,128)} %get-tuple-element.14.refs_0_), channel_id=1, source_target_pairs={{0,3},{1,0},{2,1},{3,2},{4,7},{5,4},{6,5},{7,6},{8,11},{9,8},{10,9... | collective-permute-start | bytes 49160 | tf_op jit(solution)/shard_map/ppermute | solution.py:378
  5.5 0.6 %collective-permute-start.1 = (s32[8,512]{1,0:T(8,128)}, s32[8,512]{1,0:T(8,128)S(1)}, u32[]{:S(2)}, u32[]{:S(2)}) collective-permute-start(s32[8,512]{1,0:T(8,128)} %get-tuple-element.14.refs_0_), channel_id=1, source_target_pairs={{0,2},{1,3},{2,0},{3,1},{4,6},{5,7},{6,4},{7,5},{8,10},{9,11},{10,... | collective-permute-start | bytes 49160 | tf_op jit(solution)/shard_map/ppermute | solution.py:378
  6.2 0.2 collective-permute-start
  6.3 5.8 %all-to-all-start = ((f32[8,2,400]{2,1,0:T(2,128)}), f32[8,2,400]{2,1,0:T(2,128)S(1)}, u32[]{:S(2)}, u32[]{:S(2)}) async-start(f32[8,2,400]{2,1,0:T(2,128)} %get-tuple-element.19), calls=%async_computation | async-start | bytes 65536 | tf_op jit(solution)/shard_map/all_to_all | solution.py:379
  12.2 0.1 pad_add_fusion.1.place
  12.2 0.0 collective-permute-done.2.refs_3_
  12.2 0.0 collective-permute-done.1.refs_2_
  12.2 0.0 collective-permute-done.refs_1_
  12.3 0.0 copy-start
  12.3 0.9 %copy-done = bf16[256,400]{0,1:T(8,128)(2,1)S(1)} copy-done((bf16[256,400]{0,1:T(8,128)(2,1)S(1)}, bf16[256,400]{0,1:T(8,128)(2,1)}, u32[]{:S(2)}) %copy-start) | copy-done | bytes 204824
  13.2 0.0 copy-start.1
  13.2 0.7 %copy-done.1 = s32[8,512]{1,0:T(8,128)S(1)} copy-done((s32[8,512]{1,0:T(8,128)S(1)}, s32[8,512]{1,0:T(8,128)}, u32[]{:S(2)}) %copy-start.1) | copy-done | bytes 16408
  13.9 0.0 copy-start.4
  13.9 1.4 %copy-done.4 = f32[1000,400]{0,1:T(8,128)S(1)} copy-done((f32[1000,400]{0,1:T(8,128)S(1)}, f32[1000,400]{0,1:T(8,128)}, u32[]{:S(2)}) %copy-start.4) | copy-done | bytes 1600024
  15.3 0.0 copy-start.2
  15.3 4.0 %gather.1 = (s32[8,1536]{1,0:T(8,128)S(1)}, bf16[400,1536]{1,0:T(8,128)(2,1)S(1)}, f32[104,1536]{1,0:T(8,128)S(1)}, f32[104,1536]{1,0:T(8,128)S(1)}) custom-call(s32[2]{0:T(128)S(1)} %pad_add_fusion.1.place, s32[8,512]{1,0:T(8,128)S(1)} %copy-done.1, s32[8,512]{1,0:T(8,128)S(1)} %collective-permute-done.refs_1_, ...), custom_call_target="tpu_custom_call" | custom-call | flops 2831155200 | bytes 4915200 | tf_op jit(solution)/shard_map/gather/pallas_call | solution.py:382
  19.3 0.0 all-to-all-done.refs_8_
  19.3 0.0 copy-done.2
  19.3 3.2 %edges.1 = (f32[100,256]{1,0:T(8,128)S(1)}, s16[4,2,112,128]{3,2,1,0:T(8,128)(2,1)S(1)}) custom-call(s32[2]{0:T(128)S(1)} %pad_add_fusion.1.place, s32[8,512]{1,0:T(8,128)S(1)} %copy-done.2, s32[8,512]{1,0:T(8,128)S(1)} %collective-permute-done.refs_1_, s32[8,512]{1,0:T(8,128)S(1)} %collective-permute-done.1.refs_2_, ...), custom_call_target="tpu_custom_call" | custom-call | tf_op jit(solution)/shard_map/edges/pallas_call | solution.py:410
  22.5 0.0 copy-start.3
  22.5 10.5 %all_to_all.10.refs_0_ = s16[4,2,112,128]{3,2,1,0:T(8,128)(2,1)S(1)} all-to-all(s16[4,2,112,128]{3,2,1,0:T(8,128)(2,1)S(1)} %get-tuple-element.20), channel_id=1, replica_groups={{0,4,8,12},{16,20,24,28},{1,5,9,13},{17,21,25,29},{2,6,10,14},{18,22,26..., dimensions={0} | all-to-all | bytes 458752 | tf_op jit(solution)/shard_map/all_to_all | solution.py:442
  33.0 0.1 quad.1
  33.1 13.8 %all-gather = s16[8,112,128]{2,1,0:T(8,128)(2,1)S(1)} all-gather(s16[2,112,128]{2,1,0:T(8,128)(2,1)S(1)} %quad.1), channel_id=2, replica_groups={{0,8,16,24},{4,12,20,28},{1,9,17,25},{5,13,21,29},{2,10,18,26},{6,14,22..., dimensions={0}, use_global_device_ids=true | all-gather | bytes 286720 | tf_op jit(solution)/shard_map/all_gather | solution.py:453
  46.9 0.2 total.1
  47.0 1.0 %collective-permute-start.5 = (s16[4,112,128]{2,1,0:T(8,128)(2,1)S(1)}, s16[4,112,128]{2,1,0:T(8,128)(2,1)S(1)}, u32[]{:S(2)}, u32[]{:S(2)}) collective-permute-start(s16[4,112,128]{2,1,0:T(8,128)(2,1)S(1)} %total.1), channel_id=1, source_target_pairs={{0,6},{1,7},{2,4},{3,5},{4,2},{5,3},{6,0},{7,1},{8,14},{9,15},{10,... | collective-permute-start | bytes 344072 | tf_op jit(solution)/shard_map/ppermute | solution.py:437
  48.1 1.3 %collective-permute-start.4 = (s16[4,112,128]{2,1,0:T(8,128)(2,1)S(1)}, s16[4,112,128]{2,1,0:T(8,128)(2,1)S(1)}, u32[]{:S(2)}, u32[]{:S(2)}) collective-permute-start(s16[4,112,128]{2,1,0:T(8,128)(2,1)S(1)} %total.1), channel_id=1, source_target_pairs={{0,2},{1,3},{2,0},{3,1},{4,6},{5,7},{6,4},{7,5},{8,10},{9,11},{10,... | collective-permute-start | bytes 344072 | tf_op jit(solution)/shard_map/ppermute | solution.py:437
  49.4 1.2 %collective-permute-start.3 = (s16[4,112,128]{2,1,0:T(8,128)(2,1)S(1)}, s16[4,112,128]{2,1,0:T(8,128)(2,1)S(1)}, u32[]{:S(2)}, u32[]{:S(2)}) collective-permute-start(s16[4,112,128]{2,1,0:T(8,128)(2,1)S(1)} %total.1), channel_id=1, source_target_pairs={{0,4},{1,5},{2,6},{3,7},{4,0},{5,1},{6,2},{7,3},{8,12},{9,13},{10,... | collective-permute-start | bytes 344072 | tf_op jit(solution)/shard_map/ppermute | solution.py:437
  50.6 2.2 %collective-permute-done.5 = s16[4,112,128]{2,1,0:T(8,128)(2,1)S(1)} collective-permute-done((s16[4,112,128]{2,1,0:T(8,128)(2,1)S(1)}, s16[4,112,128]{2,1,0:T(8,128)(2,1)S(1)}, u32[]{:S(2)}, u32[]{:S(2)}) %collective-permute-start.5) | collective-permute-done | bytes 114720 | tf_op jit(solution)/shard_map/ppermute | solution.py:437
  52.8 0.6 collective-permute-done.4
  53.4 0.8 %collective-permute-done.3 = s16[4,112,128]{2,1,0:T(8,128)(2,1)S(1)} collective-permute-done((s16[4,112,128]{2,1,0:T(8,128)(2,1)S(1)}, s16[4,112,128]{2,1,0:T(8,128)(2,1)S(1)}, u32[]{:S(2)}, u32[]{:S(2)}) %collective-permute-start.3) | collective-permute-done | bytes 114720 | tf_op jit(solution)/shard_map/ppermute | solution.py:437
  54.2 0.1 collective-permute-start.6
  54.3 0.0 copy-done.3
  54.3 1.6 %entity.1 = f32[100,256]{1,0:T(8,128)} custom-call(s32[2]{0:T(128)S(1)} %pad_add_fusion.1.place, s32[1,2,8]{2,1,0:T(2,128)S(1)} %bitcast.13, f32[100,256]{1,0:T(8,128)S(1)} %get-tuple-element.23.lhs, s16[4,2,112,128]{3,2,1,0:T(8,128)(2,1)S(1)} %bitcast.9), custom_call_target="tpu_custom_call" | custom-call | flops 1000000000 | bytes 1000000 | tf_op jit(solution)/shard_map/entity/pallas_call | solution.py:474
  55.9 0.2 collective-permute-done.6.other
  56.1 1.8 %spread.1 = f32[400,1000]{1,0:T(8,128)} custom-call(s32[2]{0:T(128)S(1)} %pad_add_fusion.1.place, s16[16,112,128]{2,1,0:T(8,128)(2,1)S(1)} %pad_add_fusion.mine, s16[16,112,128]{2,1,0:T(8,128)(2,1)S(1)} %collective-permute-done.6.other), custom_call_target="tpu_custom_call" | custom-call | tf_op jit(solution)/shard_map/spread/pallas_call | solution.py:489
  (1 shorter events, 0.0 us)
Async XLA Ops:
  3.1 9.1 %collective-permute-start.2 = (s32[8,512]{1,0:T(8,128)}, s32[8,512]{1,0:T(8,128)S(1)}, u32[]{:S(2)}, u32[]{:S(2)}) collective-permute-start(s32[8,512]{1,0:T(8,128)} %get-tuple-element.14.refs_0_), channel_id=1, source_target_pairs={{0,3},{1,0},{2,1},{3,2},{4,7},{5,4},{6,5},{7,6},{8,11},{9,8},{10,9... | collective-permute-start | bytes 49160 | tf_op jit(solution)/shard_map/ppermute | solution.py:378
  5.5 6.7 %collective-permute-start.1 = (s32[8,512]{1,0:T(8,128)}, s32[8,512]{1,0:T(8,128)S(1)}, u32[]{:S(2)}, u32[]{:S(2)}) collective-permute-start(s32[8,512]{1,0:T(8,128)} %get-tuple-element.14.refs_0_), channel_id=1, source_target_pairs={{0,2},{1,3},{2,0},{3,1},{4,6},{5,7},{6,4},{7,5},{8,10},{9,11},{10,... | collective-permute-start | bytes 49160 | tf_op jit(solution)/shard_map/ppermute | solution.py:378
  6.2 6.1 %collective-permute-start = (s32[8,512]{1,0:T(8,128)}, s32[8,512]{1,0:T(8,128)S(1)}, u32[]{:S(2)}, u32[]{:S(2)}) collective-permute-start(s32[8,512]{1,0:T(8,128)} %get-tuple-element.14.refs_0_), channel_id=1, source_target_pairs={{0,1},{1,2},{2,3},{3,0},{4,5},{5,6},{6,7},{7,4},{8,9},{9,10},{10,1... | collective-permute-start | bytes 49160 | tf_op jit(solution)/shard_map/ppermute | solution.py:378
  6.3 13.0 %all-to-all-start = ((f32[8,2,400]{2,1,0:T(2,128)}), f32[8,2,400]{2,1,0:T(2,128)S(1)}, u32[]{:S(2)}, u32[]{:S(2)}) async-start(f32[8,2,400]{2,1,0:T(2,128)} %get-tuple-element.19), calls=%async_computation | async-start | bytes 65536 | tf_op jit(solution)/shard_map/all_to_all | solution.py:379
  12.3 0.9 %copy-start = (bf16[256,400]{0,1:T(8,128)(2,1)S(1)}, bf16[256,400]{0,1:T(8,128)(2,1)}, u32[]{:S(2)}) copy-start(bf16[256,400]{0,1:T(8,128)(2,1)} %param.8) | copy-start | bytes 614404
  13.2 0.7 %copy-start.1 = (s32[8,512]{1,0:T(8,128)S(1)}, s32[8,512]{1,0:T(8,128)}, u32[]{:S(2)}) copy-start(s32[8,512]{1,0:T(8,128)} %get-tuple-element.14.refs_0_) | copy-start | bytes 49156
  13.9 1.4 %copy-start.4 = (f32[1000,400]{0,1:T(8,128)S(1)}, f32[1000,400]{0,1:T(8,128)}, u32[]{:S(2)}) copy-start(f32[1000,400]{0,1:T(8,128)} %param.9) | copy-start | bytes 4800004
  15.3 4.0 %copy-start.2 = (s32[8,512]{1,0:T(8,128)S(1)}, s32[8,512]{1,0:T(8,128)}, u32[]{:S(2)}) copy-start(s32[8,512]{1,0:T(8,128)} %get-tuple-element.14.refs_0_) | copy-start | bytes 49156
  22.5 31.8 %copy-start.3 = (s32[1,8,2]{1,2,0:T(2,128)S(1)}, s32[1,8,2]{1,2,0:T(2,128)}, u32[]{:S(2)}) copy-start(s32[1,8,2]{1,2,0:T(2,128)} %param.10) | copy-start | bytes 196
  47.0 5.8 %collective-permute-start.5 = (s16[4,112,128]{2,1,0:T(8,128)(2,1)S(1)}, s16[4,112,128]{2,1,0:T(8,128)(2,1)S(1)}, u32[]{:S(2)}, u32[]{:S(2)}) collective-permute-start(s16[4,112,128]{2,1,0:T(8,128)(2,1)S(1)} %total.1), channel_id=1, source_target_pairs={{0,6},{1,7},{2,4},{3,5},{4,2},{5,3},{6,0},{7,1},{8,14},{9,15},{10,... | collective-permute-start | bytes 344072 | tf_op jit(solution)/shard_map/ppermute | solution.py:437
  48.1 5.3 %collective-permute-start.4 = (s16[4,112,128]{2,1,0:T(8,128)(2,1)S(1)}, s16[4,112,128]{2,1,0:T(8,128)(2,1)S(1)}, u32[]{:S(2)}, u32[]{:S(2)}) collective-permute-start(s16[4,112,128]{2,1,0:T(8,128)(2,1)S(1)} %total.1), channel_id=1, source_target_pairs={{0,2},{1,3},{2,0},{3,1},{4,6},{5,7},{6,4},{7,5},{8,10},{9,11},{10,... | collective-permute-start | bytes 344072 | tf_op jit(solution)/shard_map/ppermute | solution.py:437
  49.4 4.8 %collective-permute-start.3 = (s16[4,112,128]{2,1,0:T(8,128)(2,1)S(1)}, s16[4,112,128]{2,1,0:T(8,128)(2,1)S(1)}, u32[]{:S(2)}, u32[]{:S(2)}) collective-permute-start(s16[4,112,128]{2,1,0:T(8,128)(2,1)S(1)} %total.1), channel_id=1, source_target_pairs={{0,4},{1,5},{2,6},{3,7},{4,0},{5,1},{6,2},{7,3},{8,12},{9,13},{10,... | collective-permute-start | bytes 344072 | tf_op jit(solution)/shard_map/ppermute | solution.py:437
  54.2 1.9 %collective-permute-start.6 = (s16[16,112,128]{2,1,0:T(8,128)(2,1)S(1)}, s16[16,112,128]{2,1,0:T(8,128)(2,1)S(1)}, u32[]{:S(2)}, u32[]{:S(2)}) collective-permute-start(s16[16,112,128]{2,1,0:T(8,128)(2,1)S(1)} %pad_add_fusion.mine), channel_id=1, source_target_pairs={{0,1},{1,0},{2,3},{3,2},{4,5},{5,4},{6,7},{7,6},{8,9},{9,8},{10,11... | collective-permute-start | bytes 1376264 | tf_op jit(solution)/shard_map/ppermute | solution.py:487

commit v12 on v9

--- a/solution.py
+++ b/solution.py
@@ -312,28 +312,64 @@
     out[...] = lhs[...] + added[:narrow]
 
 
-def spread_kernel(workers, replicas, narrow, power_row, block, place, mine, other, out, whole, sems):
-    dim, nrel = out.shape
-    dom, rep = place[0], place[1]
-    here = lax.rem(rep, 2)
-    moves, start = [], 0
-    for r in range(replicas):
+def decoded(pieces, place, workers, power_row, o, over_x, rows):
+    dom = place[0]
+    over_low = lax.rem(dom // 2 + o // 2, 2)
+    over_y = lax.rem(dom + o, 2)
+    spot = (over_y + 2 * over_x) * 4 + over_low * 2 + o // 4
+    both = pieces[spot].astype(jnp.int32)
+    return decode(both[rows], both[power_row : power_row + 1])
+
+
+def spread_core(pieces, core, place, sizes, bands, out, sems):
+    workers, narrow, power_row, block, nrel = sizes
+    length = narrow // 8 * 8
+    extra = narrow - length
+    moves = []
+    for x in range(2):
+        over_x = lax.rem(place[1] // 2 + x, 2)
         for o in range(workers):
-            over_low = lax.rem(dom // 2 + o // 2, 2)
-            over_y = lax.rem(dom + o, 2)
-            over_x = lax.rem(rep // 2 + r // 2, 2)
-            spot = (over_y + 2 * over_x) * 4 + over_low * 2 + o // 4
-            both = jnp.where(
-                here == r % 2, mine[spot].astype(jnp.int32), other[spot].astype(jnp.int32)
-            )
-            value = decode(both[:narrow], both[power_row : power_row + 1])
+            value = decoded(pieces, place, workers, power_row, o, over_x, slice(0, narrow))
+            value = jnp.where(core == 0, value[:length], value[extra:])
             end = min((o + 1) * block, nrel)
-            whole[r * narrow : (r + 1) * narrow, o * block : end] = value[:, : end - o * block]
-        end = (r + 1) * narrow // 8 * 8 if r + 1 < replicas else dim
-        band = slice(start, end)
-        moves.append(pltpu.make_async_copy(whole.at[band], out.at[band], sems.at[r]))
-        moves[-1].start()
-        start = end
+            bands[x * length : (x + 1) * length, o * block : end] = value[:, : end - o * block]
+        first = pl.multiple_of(2 * narrow * x + (length + 8) * core, 8)
+        move = pltpu.make_async_copy(
+            bands.at[x * length : (x + 1) * length], out.at[pl.ds(first, length)], sems.at[x]
+        )
+        move.start()
+        moves.append(move)
+    return moves
+
+
+def spread_own_kernel(sizes, place, mine, out, bands, sems):
+    for move in spread_core(mine, lax.rem(place[1], 2), place, sizes, bands, out, sems):
+        move.wait()
+
+
+def spread_rest_kernel(sizes, place, mine, other, partial, out, bands, shared, sems):
+    workers, narrow, power_row, block, nrel = sizes
+    core = lax.rem(place[1], 2)
+    length = narrow // 8 * 8
+    extra = narrow - length
+    moves = spread_core(other, 1 - core, place, sizes, bands, out, sems)
+    for x in range(2):
+        over_x = lax.rem(place[1] // 2 + x, 2)
+        for o in range(workers):
+            parts = []
+            for which, rows in ((0, slice(length, narrow)), (1, slice(0, 8 - extra))):
+                ours = decoded(mine, place, workers, power_row, o, over_x, rows)
+                theirs = decoded(other, place, workers, power_row, o, over_x, rows)
+                parts.append(jnp.where(core == which, ours, theirs))
+            value = jnp.concatenate(parts, axis=0)
+            end = min((o + 1) * block, nrel)
+            shared[x * 8 : (x + 1) * 8, o * block : end] = value[:, : end - o * block]
+        first = 2 * narrow * x + length
+        move = pltpu.make_async_copy(
+            shared.at[x * 8 : (x + 1) * 8], out.at[first : first + 8], sems.at[2 + x]
+        )
+        move.start()
+        moves.append(move)
     for move in moves:
         move.wait()
 
@@ -352,7 +388,7 @@
     groups, width = neg_ids.shape[2], neg_ids.shape[3]
     slots = workers * cap
     narrow = dim // replicas
-    direct = workers == 8 and replicas == 4
+    direct = workers == 8 and replicas == 4 and narrow % 8 == 4
     block = up(-(-nrel // workers), LANES if direct else 8)
     pad_rel = up(max(nrel, workers * block), LANES)
     offsets = sorted({(narrow * r) % 8 for r in range(replicas)})
@@ -449,6 +485,7 @@
     stack = jax.ShapeDtypeStruct((outs[0], height, lanes), jnp.int16)
     mixed = [pltpu.VMEM((height, lanes), jnp.int32)]
     if direct:
+        got = {n: swap(sent[n], n) for n in reversed(range(1, SOURCES))}
         summed = pl.pallas_call(
             functools.partial(quad_kernel, narrow, cap),
             out_shape=stack,
@@ -457,7 +494,7 @@
             scratch_shapes=mixed,
             compiler_params=params(),
             name="quad",
-        )(sent[0], *[swap(sent[n], n) for n in range(1, SOURCES)])
+        )(sent[0], *[got[n] for n in range(1, SOURCES)])
         recv = [summed, swap(summed, 4)]
         parts = recv + [swap(summed, 2), swap(summed, 6)]
         stack = jax.ShapeDtypeStruct((4, height, lanes), jnp.int16)
@@ -477,8 +514,9 @@
     )(*parts)
 
     if direct:
-        along_y = swap(chunk, 1)
-        along_y, lhs_part = lax.optimization_barrier((along_y, lhs_part))
+        base = jnp.concatenate(
+            [chunk, swap(chunk, 1), swap(chunk, 0, 2), swap(chunk, 1, 2)], axis=0
+        )
     entity_grad = pl.pallas_call(
         functools.partial(entity_kernel, direct, narrow),
         out_shape=jax.ShapeDtypeStruct((narrow, rows), F32),
@@ -492,21 +530,31 @@
 
     power_row = narrow + SOURCES * cap
     if direct:
-        base = jnp.concatenate([chunk, along_y, swap(chunk, 0, 2), swap(chunk, 1, 2)], axis=0)
         base, entity_grad = lax.optimization_barrier((base, entity_grad))
         swapped = lax.ppermute(base, "rep", [(i, i ^ 1) for i in range(replicas)])
+        sizes = (workers, narrow, power_row, block, nrel)
+        result = jax.ShapeDtypeStruct((dim, nrel), F32)
+        bands = pltpu.VMEM((narrow // 8 * 16, nrel), F32)
+        own_half = pl.pallas_call(
+            functools.partial(spread_own_kernel, sizes),
+            out_shape=result,
+            in_specs=[SMEM, VMEM],
+            out_specs=HBM,
+            scratch_shapes=[bands, pltpu.SemaphoreType.DMA((2,))],
+            compiler_params=params(),
+            cost_estimate=cost(10**6, 4 * dim * nrel),
+            name="spread_own",
+        )(place, base)
         relation_t = pl.pallas_call(
-            functools.partial(spread_kernel, workers, replicas, narrow, power_row, block),
-            out_shape=jax.ShapeDtypeStruct((dim, nrel), F32),
-            in_specs=[SMEM] + [VMEM] * 2,
+            functools.partial(spread_rest_kernel, sizes),
+            out_shape=result,
+            in_specs=[SMEM, VMEM, VMEM, HBM],
             out_specs=HBM,
-            scratch_shapes=[
-                pltpu.VMEM((dim, nrel), F32),
-                pltpu.SemaphoreType.DMA((replicas,)),
-            ],
+            scratch_shapes=[bands, pltpu.VMEM((16, nrel), F32), pltpu.SemaphoreType.DMA((4,))],
+            input_output_aliases={3: 0},
             compiler_params=params(),
-            name="spread",
-        )(place, base, swapped)
+            name="spread_rest",
+        )(place, base, swapped, own_half)
     else:
         whole = lax.all_gather(chunk[0, :, :block], ("dom", "rep"), axis=0)
         whole = decode(whole[:, :narrow], whole[:, power_row : power_row + 1])

time: 51.1 us -> 50.7 us (level)
  waiting for transfers between devices: 12.8 us -> 11.1 us
  Pallas kernels: 12.6 us -> 13.9 us
    ppermute x1, waiting for transfers between devices: 1.8 us -> 0.25 us  [shards(): swapped = lax.ppermute(base, 'rep', [(i, i ^ 1) for i in range(replicas)])]
    pallas_call x1 -> x2, Pallas kernels: 1.84 us -> 3.12 us  [the longest x1 1.57 us: shards(): pl.pallas_call(functools.partial(spread_rest_kernel, sizes), out_shape=re...]
  transfers between devices with their start and end apart: 14 -> 14, of which waited for: 9 -> 10; matrix products, arithmetic and copies ran while one was open for 0% -> 0% of each run, Pallas kernels for 11% -> 14%
where the time goes in v12:
time: 50.7 us; the launch traced here: 50.3 us
  starting transfers between devices  20.8 us (41%)
  Pallas kernels  13.9 us (27%)
  waiting for transfers between devices  11.1 us (22%)
  local copies, waits for them, and re-layouts  3.08 us (6%)
  between operations  1.38 us (3%)
    ppermute x9, starting transfers between devices, swap(): return lax.ppermute(array, ('dom', 'rep'), pairs)  11.6 us
    ppermute x9, waiting for transfers between devices, swap(): return lax.ppermute(array, ('dom', 'rep'), pairs)  10.8 us
    all_to_all x1, starting transfers between devices, shards(): received = lax.all_to_all(served, 'dom', 0, 0, tiled=True)  5.84 us
    pallas_call x1, Pallas kernels, shards(): pl.pallas_call(functools.partial(gather_kernel, (replicas, groups, nrel,...  3.93 us
    ppermute x3, starting transfers between devices, shards(): held.append(lax.ppermute(idx, 'rep', turned(replicas, hop)))  3.23 us
    pallas_call x1, Pallas kernels, shards(): pl.pallas_call(functools.partial(main_kernel, cfg), out_shape=[jax.ShapeD...  3.17 us
    unnamed x10, local copies, waits for them, and re-layouts  3.08 us
    pallas_call x1, Pallas kernels, shards(): pl.pallas_call(prep_kernel, out_shape=(jax.ShapeDtypeStruct((IDX_ROWS, ed...  1.81 us
  transfers between devices with their start and end apart: 14, of which 10 were waited for; matrix products, arithmetic and copies ran while one was open for 0% of the time, Pallas kernels for 14%

profile of v12, /device:TPU:0, one launch (start us, length us, event | category | flops | bytes accessed | tf_op | source)
XLA Modules:
  0.0 50.3 jit_solution(11898741390730747283)
XLA Ops:
  1.3 1.8 %prep.1 = (s32[8,512]{1,0:T(8,128)}, f32[8,2,400]{2,1,0:T(2,128)}) custom-call(s32[1,2,8]{2,1,0:T(2,128)} %bitcast.9, s32[1,1]{1,0:T(1,128)S(6)} %copy.12.count, bf16[400,256]{1,0:T(8,128)(2,1)} %bitcast.7, s32[1,1,512]{2,1,0:T(1,128)} %src.1, s32[1,1,512]{2,1,0:T(1,128)} %rel.1, s32[1,1,512]{2,1,0:T(1,128)} %dst.1, s32[1,1,2,384]{3,2,1,0:T(2,128)} %neg.1), custom_call_target="tpu_custom_call" | custom-call | tf_op jit(solution)/shard_map/prep/pallas_call | solution.py:401
  3.1 2.4 %collective-permute-start.2 = (s32[8,512]{1,0:T(8,128)}, s32[8,512]{1,0:T(8,128)S(1)}, u32[]{:S(2)}, u32[]{:S(2)}) collective-permute-start(s32[8,512]{1,0:T(8,128)} %get-tuple-element.15.refs_0_), channel_id=1, source_target_pairs={{0,3},{1,0},{2,1},{3,2},{4,7},{5,4},{6,5},{7,6},{8,11},{9,8},{10,9... | collective-permute-start | bytes 49160 | tf_op jit(solution)/shard_map/ppermute | solution.py:426
  5.5 0.6 %collective-permute-start.1 = (s32[8,512]{1,0:T(8,128)}, s32[8,512]{1,0:T(8,128)S(1)}, u32[]{:S(2)}, u32[]{:S(2)}) collective-permute-start(s32[8,512]{1,0:T(8,128)} %get-tuple-element.15.refs_0_), channel_id=1, source_target_pairs={{0,2},{1,3},{2,0},{3,1},{4,6},{5,7},{6,4},{7,5},{8,10},{9,11},{10,... | collective-permute-start | bytes 49160 | tf_op jit(solution)/shard_map/ppermute | solution.py:426
  6.2 0.2 collective-permute-start
  6.3 5.8 %all-to-all-start = ((f32[8,2,400]{2,1,0:T(2,128)}), f32[8,2,400]{2,1,0:T(2,128)S(1)}, u32[]{:S(2)}, u32[]{:S(2)}) async-start(f32[8,2,400]{2,1,0:T(2,128)} %get-tuple-element.20), calls=%async_computation | async-start | bytes 65536 | tf_op jit(solution)/shard_map/all_to_all | solution.py:427
  12.2 0.1 pad_add_fusion.1.place
  12.2 0.0 collective-permute-done.2.refs_3_
  12.2 0.0 collective-permute-done.1.refs_2_
  12.2 0.0 collective-permute-done.refs_1_
  12.3 0.0 copy-start
  12.3 0.9 %copy-done = bf16[256,400]{0,1:T(8,128)(2,1)S(1)} copy-done((bf16[256,400]{0,1:T(8,128)(2,1)S(1)}, bf16[256,400]{0,1:T(8,128)(2,1)}, u32[]{:S(2)}) %copy-start) | copy-done | bytes 204824
  13.2 0.0 copy-start.1
  13.2 0.7 %copy-done.1 = s32[8,512]{1,0:T(8,128)S(1)} copy-done((s32[8,512]{1,0:T(8,128)S(1)}, s32[8,512]{1,0:T(8,128)}, u32[]{:S(2)}) %copy-start.1) | copy-done | bytes 16408
  13.9 0.0 copy-start.4
  13.9 1.4 %copy-done.4 = f32[1000,400]{0,1:T(8,128)S(1)} copy-done((f32[1000,400]{0,1:T(8,128)S(1)}, f32[1000,400]{0,1:T(8,128)}, u32[]{:S(2)}) %copy-start.4) | copy-done | bytes 1600024
  15.3 0.0 copy-start.2
  15.3 3.9 %gather.1 = (s32[8,1536]{1,0:T(8,128)S(1)}, bf16[400,1536]{1,0:T(8,128)(2,1)S(1)}, f32[104,1536]{1,0:T(8,128)S(1)}, f32[104,1536]{1,0:T(8,128)S(1)}) custom-call(s32[2]{0:T(128)S(1)} %pad_add_fusion.1.place, s32[8,512]{1,0:T(8,128)S(1)} %copy-done.1, s32[8,512]{1,0:T(8,128)S(1)} %collective-permute-done.refs_1_, ...), custom_call_target="tpu_custom_call" | custom-call | flops 2831155200 | bytes 4915200 | tf_op jit(solution)/shard_map/gather/pallas_call | solution.py:430
  19.3 0.0 all-to-all-done.refs_8_
  19.3 0.0 copy-done.2
  19.3 0.0 copy-start.3
  19.3 3.2 %edges.1 = (f32[100,256]{1,0:T(8,128)S(1)}, s16[2,112,128]{2,1,0:T(8,128)(2,1)S(1)}, s16[2,112,128]{2,1,0:T(8,128)(2,1)S(1)}, s16[2,112,128]{2,1,0:T(8,128)(2,1)S(1)}, s16[2,112,128]{2,1,0:T(8,128)(2,1)S(1)}) custom-call(s32[2]{0:T(128)S(1)} %pad_add_fusion.1.place, s32[8,512]{1,0:T(8,128)S(1)} %copy-done.2, s32[8,512]{1,0:T(8,128)S(1)} %collective-permute-done.refs_1_, ...), custom_call_target="tpu_custom_call" | custom-call | tf_op jit(solution)/shard_map/edges/pallas_call | solution.py:459
  22.5 2.1 %collective-permute-start.3 = (s16[2,112,128]{2,1,0:T(8,128)(2,1)S(1)}, s16[2,112,128]{2,1,0:T(8,128)(2,1)S(1)}, u32[]{:S(2)}, u32[]{:S(2)}) collective-permute-start(s16[2,112,128]{2,1,0:T(8,128)(2,1)S(1)} %get-tuple-element.22), channel_id=1, source_target_pairs={{0,4},{1,5},{2,6},{3,7},{4,0},{5,1},{6,2},{7,3},{8,12},{9,13},{10,... | collective-permute-start | bytes 172040 | tf_op jit(solution)/shard_map/ppermute | solution.py:483
  24.6 1.5 %collective-permute-start.4 = (s16[2,112,128]{2,1,0:T(8,128)(2,1)S(1)}, s16[2,112,128]{2,1,0:T(8,128)(2,1)S(1)}, u32[]{:S(2)}, u32[]{:S(2)}) collective-permute-start(s16[2,112,128]{2,1,0:T(8,128)(2,1)S(1)} %get-tuple-element.23), channel_id=1, source_target_pairs={{0,8},{1,9},{2,10},{3,11},{4,12},{5,13},{6,14},{7,15},{8,0},{9,1},... | collective-permute-start | bytes 172040 | tf_op jit(solution)/shard_map/ppermute | solution.py:483
  26.0 0.1 collective-permute-start.5
  26.1 1.1 %collective-permute-done.3.refs_1_ = s16[2,112,128]{2,1,0:T(8,128)(2,1)S(1)} collective-permute-done((s16[2,112,128]{2,1,0:T(8,128)(2,1)S(1)}, s16[2,112,128]{2,1,0:T(8,128)(2,1)S(1)}, u32[]{:S(2)}, u32[]{:S(2)}) %collective-permute-start.3) | collective-permute-done | bytes 57376 | tf_op jit(solution)/shard_map/ppermute | solution.py:483
  27.2 1.7 %collective-permute-done.4.refs_2_ = s16[2,112,128]{2,1,0:T(8,128)(2,1)S(1)} collective-permute-done((s16[2,112,128]{2,1,0:T(8,128)(2,1)S(1)}, s16[2,112,128]{2,1,0:T(8,128)(2,1)S(1)}, u32[]{:S(2)}, u32[]{:S(2)}) %collective-permute-start.4) | collective-permute-done | bytes 57376 | tf_op jit(solution)/shard_map/ppermute | solution.py:483
  29.0 2.1 %collective-permute-done.5.refs_3_ = s16[2,112,128]{2,1,0:T(8,128)(2,1)S(1)} collective-permute-done((s16[2,112,128]{2,1,0:T(8,128)(2,1)S(1)}, s16[2,112,128]{2,1,0:T(8,128)(2,1)S(1)}, u32[]{:S(2)}, u32[]{:S(2)}) %collective-permute-start.5) | collective-permute-done | bytes 57376 | tf_op jit(solution)/shard_map/ppermute | solution.py:483
  31.1 0.1 quad.1.refs_0_
  31.2 2.4 %collective-permute-start.8 = (s16[2,112,128]{2,1,0:T(8,128)(2,1)S(1)}, s16[2,112,128]{2,1,0:T(8,128)(2,1)S(1)}, u32[]{:S(2)}, u32[]{:S(2)}) collective-permute-start(s16[2,112,128]{2,1,0:T(8,128)(2,1)S(1)} %quad.1.refs_0_), channel_id=1, source_target_pairs={{0,24},{1,25},{2,26},{3,27},{4,28},{5,29},{6,30},{7,31},{8,16},{9,... | collective-permute-start | bytes 172040 | tf_op jit(solution)/shard_map/ppermute | solution.py:483
  33.6 0.6 %collective-permute-start.7 = (s16[2,112,128]{2,1,0:T(8,128)(2,1)S(1)}, s16[2,112,128]{2,1,0:T(8,128)(2,1)S(1)}, u32[]{:S(2)}, u32[]{:S(2)}) collective-permute-start(s16[2,112,128]{2,1,0:T(8,128)(2,1)S(1)} %quad.1.refs_0_), channel_id=1, source_target_pairs={{0,8},{1,9},{2,10},{3,11},{4,12},{5,13},{6,14},{7,15},{8,0},{9,1},... | collective-permute-start | bytes 172040 | tf_op jit(solution)/shard_map/ppermute | solution.py:483
  34.2 1.5 %collective-permute-start.6 = (s16[2,112,128]{2,1,0:T(8,128)(2,1)S(1)}, s16[2,112,128]{2,1,0:T(8,128)(2,1)S(1)}, u32[]{:S(2)}, u32[]{:S(2)}) collective-permute-start(s16[2,112,128]{2,1,0:T(8,128)(2,1)S(1)} %quad.1.refs_0_), channel_id=1, source_target_pairs={{0,16},{1,17},{2,18},{3,19},{4,20},{5,21},{6,22},{7,23},{8,24},{9,... | collective-permute-start | bytes 172040 | tf_op jit(solution)/shard_map/ppermute | solution.py:483
  35.7 1.9 %collective-permute-done.8.refs_3_ = s16[2,112,128]{2,1,0:T(8,128)(2,1)S(1)} collective-permute-done((s16[2,112,128]{2,1,0:T(8,128)(2,1)S(1)}, s16[2,112,128]{2,1,0:T(8,128)(2,1)S(1)}, u32[]{:S(2)}, u32[]{:S(2)}) %collective-permute-start.8) | collective-permute-done | bytes 57376 | tf_op jit(solution)/shard_map/ppermute | solution.py:483
  37.5 0.5 %collective-permute-done.7.refs_2_ = s16[2,112,128]{2,1,0:T(8,128)(2,1)S(1)} collective-permute-done((s16[2,112,128]{2,1,0:T(8,128)(2,1)S(1)}, s16[2,112,128]{2,1,0:T(8,128)(2,1)S(1)}, u32[]{:S(2)}, u32[]{:S(2)}) %collective-permute-start.7) | collective-permute-done | bytes 57376 | tf_op jit(solution)/shard_map/ppermute | solution.py:483
  38.1 1.2 %collective-permute-done.6.refs_1_ = s16[2,112,128]{2,1,0:T(8,128)(2,1)S(1)} collective-permute-done((s16[2,112,128]{2,1,0:T(8,128)(2,1)S(1)}, s16[2,112,128]{2,1,0:T(8,128)(2,1)S(1)}, u32[]{:S(2)}, u32[]{:S(2)}) %collective-permute-start.6) | collective-permute-done | bytes 57376 | tf_op jit(solution)/shard_map/ppermute | solution.py:483
  39.3 0.2 total.1
  39.5 1.3 %collective-permute-start.11 = (s16[4,112,128]{2,1,0:T(8,128)(2,1)S(1)}, s16[4,112,128]{2,1,0:T(8,128)(2,1)S(1)}, u32[]{:S(2)}, u32[]{:S(2)}) collective-permute-start(s16[4,112,128]{2,1,0:T(8,128)(2,1)S(1)} %total.1), channel_id=1, source_target_pairs={{0,6},{1,7},{2,4},{3,5},{4,2},{5,3},{6,0},{7,1},{8,14},{9,15},{10,... | collective-permute-start | bytes 344072 | tf_op jit(solution)/shard_map/ppermute | solution.py:483
  40.8 1.3 %collective-permute-start.10 = (s16[4,112,128]{2,1,0:T(8,128)(2,1)S(1)}, s16[4,112,128]{2,1,0:T(8,128)(2,1)S(1)}, u32[]{:S(2)}, u32[]{:S(2)}) collective-permute-start(s16[4,112,128]{2,1,0:T(8,128)(2,1)S(1)} %total.1), channel_id=1, source_target_pairs={{0,2},{1,3},{2,0},{3,1},{4,6},{5,7},{6,4},{7,5},{8,10},{9,11},{10,... | collective-permute-start | bytes 344072 | tf_op jit(solution)/shard_map/ppermute | solution.py:483
  42.1 1.0 %collective-permute-start.9 = (s16[4,112,128]{2,1,0:T(8,128)(2,1)S(1)}, s16[4,112,128]{2,1,0:T(8,128)(2,1)S(1)}, u32[]{:S(2)}, u32[]{:S(2)}) collective-permute-start(s16[4,112,128]{2,1,0:T(8,128)(2,1)S(1)} %total.1), channel_id=1, source_target_pairs={{0,4},{1,5},{2,6},{3,7},{4,0},{5,1},{6,2},{7,3},{8,12},{9,13},{10,... | collective-permute-start | bytes 344072 | tf_op jit(solution)/shard_map/ppermute | solution.py:483
  43.0 0.0 copy-done.3
  43.0 1.6 %entity.1 = f32[100,256]{1,0:T(8,128)} custom-call(s32[2]{0:T(128)S(1)} %pad_add_fusion.1.place, s32[1,2,8]{2,1,0:T(2,128)S(1)} %bitcast.10, f32[100,256]{1,0:T(8,128)S(1)} %get-tuple-element.25.lhs, s16[2,112,128]{2,1,0:T(8,128)(2,1)S(1)} %quad.1.refs_0_, s16[2,112,128]{2,1,0:T(8,128)(2,1)S(1)} %collective-permute-done.6.refs_1_), custom_call_target="tpu_custom_call" | custom-call | flops 1000000000 | bytes 1000000 | tf_op jit(solution)/shard_map/entity/pallas_call | solution.py:520
  44.6 0.7 %collective-permute-done.11 = s16[4,112,128]{2,1,0:T(8,128)(2,1)S(1)} collective-permute-done((s16[4,112,128]{2,1,0:T(8,128)(2,1)S(1)}, s16[4,112,128]{2,1,0:T(8,128)(2,1)S(1)}, u32[]{:S(2)}, u32[]{:S(2)}) %collective-permute-start.11) | collective-permute-done | bytes 114720 | tf_op jit(solution)/shard_map/ppermute | solution.py:483
  45.3 1.1 %collective-permute-done.10 = s16[4,112,128]{2,1,0:T(8,128)(2,1)S(1)} collective-permute-done((s16[4,112,128]{2,1,0:T(8,128)(2,1)S(1)}, s16[4,112,128]{2,1,0:T(8,128)(2,1)S(1)}, u32[]{:S(2)}, u32[]{:S(2)}) %collective-permute-start.10) | collective-permute-done | bytes 114720 | tf_op jit(solution)/shard_map/ppermute | solution.py:483
  46.5 0.4 collective-permute-done.9
  46.9 0.1 collective-permute-start.12
  47.0 1.5 %spread_own.1.partial = f32[400,1000]{1,0:T(8,128)} custom-call(s32[2]{0:T(128)S(1)} %pad_add_fusion.1.place, s16[16,112,128]{2,1,0:T(8,128)(2,1)S(1)} %pad_add_fusion.mine), custom_call_target="tpu_custom_call" | custom-call | flops 1000000 | bytes 1600000 | tf_op jit(solution)/shard_map/spread_own/pallas_call | solution.py:538
  48.5 0.2 collective-permute-done.12.other
  48.8 1.6 %spread_rest.1 = f32[400,1000]{1,0:T(8,128)} custom-call(s32[2]{0:T(128)S(1)} %pad_add_fusion.1.place, s16[16,112,128]{2,1,0:T(8,128)(2,1)S(1)} %pad_add_fusion.mine, s16[16,112,128]{2,1,0:T(8,128)(2,1)S(1)} %collective-permute-done.12.other, f32[400,1000]{1,0:T(8,128)} %spread_own.1.partial), custom_call_target="tpu_custom_call", output_to_operand_aliasing={{}: (3, {})} | custom-call | tf_op jit(solution)/shard_map/spread_rest/pallas_call | solution.py:548
  (1 shorter events, 0.0 us)
Async XLA Ops:
  3.1 9.1 %collective-permute-start.2 = (s32[8,512]{1,0:T(8,128)}, s32[8,512]{1,0:T(8,128)S(1)}, u32[]{:S(2)}, u32[]{:S(2)}) collective-permute-start(s32[8,512]{1,0:T(8,128)} %get-tuple-element.15.refs_0_), channel_id=1, source_target_pairs={{0,3},{1,0},{2,1},{3,2},{4,7},{5,4},{6,5},{7,6},{8,11},{9,8},{10,9... | collective-permute-start | bytes 49160 | tf_op jit(solution)/shard_map/ppermute | solution.py:426
  5.5 6.7 %collective-permute-start.1 = (s32[8,512]{1,0:T(8,128)}, s32[8,512]{1,0:T(8,128)S(1)}, u32[]{:S(2)}, u32[]{:S(2)}) collective-permute-start(s32[8,512]{1,0:T(8,128)} %get-tuple-element.15.refs_0_), channel_id=1, source_target_pairs={{0,2},{1,3},{2,0},{3,1},{4,6},{5,7},{6,4},{7,5},{8,10},{9,11},{10,... | collective-permute-start | bytes 49160 | tf_op jit(solution)/shard_map/ppermute | solution.py:426
  6.2 6.1 %collective-permute-start = (s32[8,512]{1,0:T(8,128)}, s32[8,512]{1,0:T(8,128)S(1)}, u32[]{:S(2)}, u32[]{:S(2)}) collective-permute-start(s32[8,512]{1,0:T(8,128)} %get-tuple-element.15.refs_0_), channel_id=1, source_target_pairs={{0,1},{1,2},{2,3},{3,0},{4,5},{5,6},{6,7},{7,4},{8,9},{9,10},{10,1... | collective-permute-start | bytes 49160 | tf_op jit(solution)/shard_map/ppermute | solution.py:426
  6.3 12.9 %all-to-all-start = ((f32[8,2,400]{2,1,0:T(2,128)}), f32[8,2,400]{2,1,0:T(2,128)S(1)}, u32[]{:S(2)}, u32[]{:S(2)}) async-start(f32[8,2,400]{2,1,0:T(2,128)} %get-tuple-element.20), calls=%async_computation | async-start | bytes 65536 | tf_op jit(solution)/shard_map/all_to_all | solution.py:427
  12.3 0.9 %copy-start = (bf16[256,400]{0,1:T(8,128)(2,1)S(1)}, bf16[256,400]{0,1:T(8,128)(2,1)}, u32[]{:S(2)}) copy-start(bf16[256,400]{0,1:T(8,128)(2,1)} %param.8) | copy-start | bytes 614404
  13.2 0.7 %copy-start.1 = (s32[8,512]{1,0:T(8,128)S(1)}, s32[8,512]{1,0:T(8,128)}, u32[]{:S(2)}) copy-start(s32[8,512]{1,0:T(8,128)} %get-tuple-element.15.refs_0_) | copy-start | bytes 49156
  13.9 1.4 %copy-start.4 = (f32[1000,400]{0,1:T(8,128)S(1)}, f32[1000,400]{0,1:T(8,128)}, u32[]{:S(2)}) copy-start(f32[1000,400]{0,1:T(8,128)} %param.9) | copy-start | bytes 4800004
  15.3 3.9 %copy-start.2 = (s32[8,512]{1,0:T(8,128)S(1)}, s32[8,512]{1,0:T(8,128)}, u32[]{:S(2)}) copy-start(s32[8,512]{1,0:T(8,128)} %get-tuple-element.15.refs_0_) | copy-start | bytes 49156
  19.3 23.7 %copy-start.3 = (s32[1,8,2]{1,2,0:T(2,128)S(1)}, s32[1,8,2]{1,2,0:T(2,128)}, u32[]{:S(2)}) copy-start(s32[1,8,2]{1,2,0:T(2,128)} %param.10) | copy-start | bytes 196
  22.5 4.8 %collective-permute-start.3 = (s16[2,112,128]{2,1,0:T(8,128)(2,1)S(1)}, s16[2,112,128]{2,1,0:T(8,128)(2,1)S(1)}, u32[]{:S(2)}, u32[]{:S(2)}) collective-permute-start(s16[2,112,128]{2,1,0:T(8,128)(2,1)S(1)} %get-tuple-element.22), channel_id=1, source_target_pairs={{0,4},{1,5},{2,6},{3,7},{4,0},{5,1},{6,2},{7,3},{8,12},{9,13},{10,... | collective-permute-start | bytes 172040 | tf_op jit(solution)/shard_map/ppermute | solution.py:483
  24.6 4.4 %collective-permute-start.4 = (s16[2,112,128]{2,1,0:T(8,128)(2,1)S(1)}, s16[2,112,128]{2,1,0:T(8,128)(2,1)S(1)}, u32[]{:S(2)}, u32[]{:S(2)}) collective-permute-start(s16[2,112,128]{2,1,0:T(8,128)(2,1)S(1)} %get-tuple-element.23), channel_id=1, source_target_pairs={{0,8},{1,9},{2,10},{3,11},{4,12},{5,13},{6,14},{7,15},{8,0},{9,1},... | collective-permute-start | bytes 172040 | tf_op jit(solution)/shard_map/ppermute | solution.py:483
  26.0 5.1 %collective-permute-start.5 = (s16[2,112,128]{2,1,0:T(8,128)(2,1)S(1)}, s16[2,112,128]{2,1,0:T(8,128)(2,1)S(1)}, u32[]{:S(2)}, u32[]{:S(2)}) collective-permute-start(s16[2,112,128]{2,1,0:T(8,128)(2,1)S(1)} %get-tuple-element.24), channel_id=1, source_target_pairs={{0,12},{1,13},{2,14},{3,15},{4,8},{5,9},{6,10},{7,11},{8,4},{9,5},... | collective-permute-start | bytes 172040 | tf_op jit(solution)/shard_map/ppermute | solution.py:483
  31.2 6.3 %collective-permute-start.8 = (s16[2,112,128]{2,1,0:T(8,128)(2,1)S(1)}, s16[2,112,128]{2,1,0:T(8,128)(2,1)S(1)}, u32[]{:S(2)}, u32[]{:S(2)}) collective-permute-start(s16[2,112,128]{2,1,0:T(8,128)(2,1)S(1)} %quad.1.refs_0_), channel_id=1, source_target_pairs={{0,24},{1,25},{2,26},{3,27},{4,28},{5,29},{6,30},{7,31},{8,16},{9,... | collective-permute-start | bytes 172040 | tf_op jit(solution)/shard_map/ppermute | solution.py:483
  33.6 4.4 %collective-permute-start.7 = (s16[2,112,128]{2,1,0:T(8,128)(2,1)S(1)}, s16[2,112,128]{2,1,0:T(8,128)(2,1)S(1)}, u32[]{:S(2)}, u32[]{:S(2)}) collective-permute-start(s16[2,112,128]{2,1,0:T(8,128)(2,1)S(1)} %quad.1.refs_0_), channel_id=1, source_target_pairs={{0,8},{1,9},{2,10},{3,11},{4,12},{5,13},{6,14},{7,15},{8,0},{9,1},... | collective-permute-start | bytes 172040 | tf_op jit(solution)/shard_map/ppermute | solution.py:483
  34.2 5.1 %collective-permute-start.6 = (s16[2,112,128]{2,1,0:T(8,128)(2,1)S(1)}, s16[2,112,128]{2,1,0:T(8,128)(2,1)S(1)}, u32[]{:S(2)}, u32[]{:S(2)}) collective-permute-start(s16[2,112,128]{2,1,0:T(8,128)(2,1)S(1)} %quad.1.refs_0_), channel_id=1, source_target_pairs={{0,16},{1,17},{2,18},{3,19},{4,20},{5,21},{6,22},{7,23},{8,24},{9,... | collective-permute-start | bytes 172040 | tf_op jit(solution)/shard_map/ppermute | solution.py:483
  39.5 5.9 %collective-permute-start.11 = (s16[4,112,128]{2,1,0:T(8,128)(2,1)S(1)}, s16[4,112,128]{2,1,0:T(8,128)(2,1)S(1)}, u32[]{:S(2)}, u32[]{:S(2)}) collective-permute-start(s16[4,112,128]{2,1,0:T(8,128)(2,1)S(1)} %total.1), channel_id=1, source_target_pairs={{0,6},{1,7},{2,4},{3,5},{4,2},{5,3},{6,0},{7,1},{8,14},{9,15},{10,... | collective-permute-start | bytes 344072 | tf_op jit(solution)/shard_map/ppermute | solution.py:483
  40.8 5.7 %collective-permute-start.10 = (s16[4,112,128]{2,1,0:T(8,128)(2,1)S(1)}, s16[4,112,128]{2,1,0:T(8,128)(2,1)S(1)}, u32[]{:S(2)}, u32[]{:S(2)}) collective-permute-start(s16[4,112,128]{2,1,0:T(8,128)(2,1)S(1)} %total.1), channel_id=1, source_target_pairs={{0,2},{1,3},{2,0},{3,1},{4,6},{5,7},{6,4},{7,5},{8,10},{9,11},{10,... | collective-permute-start | bytes 344072 | tf_op jit(solution)/shard_map/ppermute | solution.py:483
  42.1 4.8 %collective-permute-start.9 = (s16[4,112,128]{2,1,0:T(8,128)(2,1)S(1)}, s16[4,112,128]{2,1,0:T(8,128)(2,1)S(1)}, u32[]{:S(2)}, u32[]{:S(2)}) collective-permute-start(s16[4,112,128]{2,1,0:T(8,128)(2,1)S(1)} %total.1), channel_id=1, source_target_pairs={{0,4},{1,5},{2,6},{3,7},{4,0},{5,1},{6,2},{7,3},{8,12},{9,13},{10,... | collective-permute-start | bytes 344072 | tf_op jit(solution)/shard_map/ppermute | solution.py:483
  46.9 1.9 %collective-permute-start.12 = (s16[16,112,128]{2,1,0:T(8,128)(2,1)S(1)}, s16[16,112,128]{2,1,0:T(8,128)(2,1)S(1)}, u32[]{:S(2)}, u32[]{:S(2)}) collective-permute-start(s16[16,112,128]{2,1,0:T(8,128)(2,1)S(1)} %pad_add_fusion.mine), channel_id=1, source_target_pairs={{0,1},{1,0},{2,3},{3,2},{4,5},{5,4},{6,7},{7,6},{8,9},{9,8},{10,11... | collective-permute-start | bytes 1376264 | tf_op jit(solution)/shard_map/ppermute | solution.py:534

commit v13 on v12

--- a/solution.py
+++ b/solution.py
@@ -160,12 +160,11 @@
     (direct, workers, replicas, cap, groups, width, pad_rel, block, narrow, window, offsets) = cfg
     idx_refs, refs = refs[:replicas], refs[replicas:]
     (packed, query_v, lhs_v, rel_v, received), refs = refs[:5], refs[5:]
-    out_lhs, refs = refs[0], refs[1:]
-    outs, refs = (refs[:SOURCES], refs[SOURCES:]) if direct else (refs[:1], refs[1:])
-    table_f, table_t, query_s, wide_t, mixed, codes_s, powers_s, tables_s = refs
+    out_x, tables, refs = refs[0], refs[1], refs[2:]
+    out_y, refs = (refs[0], refs[1:]) if direct else (None, refs)
+    outs, (table_f, table_t, query_s, wide_t, mixed) = refs[:-5], refs[-5:]
     edges = idx_refs[0].shape[1]
     dim, total = query_v.shape
-    rows = out_lhs.shape[1]
     slots = workers * cap
     rep = place[1]
     per = edges // groups
@@ -208,43 +207,52 @@
     stack_t = jnp.concatenate(split3(jnp.transpose(grads)), axis=1)
 
     dquery = dot(own_t, stack)
-    y = jnp.concatenate(split2(dquery * lhs_v[...]), axis=0)
-    acc_rel = dot(y, ones_where(iota((total, pad_rel), 1) == cols[:, 1:2]))
-    x = jnp.concatenate(split2(dquery * rel_v[...]), axis=0)
-    acc_lhs = dot(x, ones_where(iota((total, rows), 1) == cols[:, 0:1]))
     acc_tab = dot(query_s[pl.ds(base, window), :].astype(BF16), stack_t)
-
-    pick = functools.partial(shifted_rows, offset=offset, narrow=narrow, offsets=offsets)
-    out_lhs[...] = pick(acc_lhs[:window] + acc_lhs[window:])
-    codes, powers = encode(pick(acc_rel[:window] + acc_rel[window:]), 0)
     wide_t[...] = jnp.zeros(wide_t.shape, F32)
-    wide_t[:narrow] = pick(
-        acc_tab[:, :slots] + acc_tab[:, slots : 2 * slots] + acc_tab[:, 2 * slots :]
+    wide_t[:narrow] = shifted_rows(
+        acc_tab[:, :slots] + acc_tab[:, slots : 2 * slots] + acc_tab[:, 2 * slots :],
+        offset,
+        narrow,
+        offsets,
     )
     table_codes, table_powers = encode(jnp.transpose(wide_t[...]), 1)
     spare = iota(table_codes.shape, 1) >= narrow
-    tables_s[...] = jnp.where(spare, table_powers, table_codes)
-    codes_s[...] = codes
-    powers_s[...] = powers
+    tables[...] = jnp.where(spare, table_powers, table_codes)
+    y = jnp.concatenate(split2(dquery * lhs_v[...]), axis=0)
+    out_x[...] = jnp.concatenate(split2(dquery * rel_v[...]), axis=0)
+    if direct:
+        out_y[...] = y
+        targets = [
+            (outs[h - 1].at[top], top * 4 + flipped(place[0] % 4, h))
+            for h in range(1, SOURCES)
+            for top in range(2)
+        ]
+    else:
+        targets = [(outs[0].at[o], o) for o in range(workers)]
+    write_blocks(y, cols, targets, tables, mixed, rep, block, narrow, cap, offsets)
+
+
+def write_blocks(y, cols, targets, tables, mixed, rep, block, narrow, cap, offsets):
+    window = y.shape[0] // 2
+    ids = jnp.concatenate([iota((1, block), 1) + o * block for _, o in targets], axis=1)
+    both = dot(y, ones_where(cols[:, 1:2] == ids))
+    part = shifted_rows(both[:window] + both[window:], (rep * narrow) % 8, narrow, offsets)
+    codes, powers = encode(part, 0)
+    power_row = narrow + SOURCES * cap
     mixed[...] = jnp.zeros(mixed.shape, jnp.int32)
-    power_row = narrow + SOURCES * cap
-    dom = place[0]
-
-    def write(target, o, lane):
-        mixed[:narrow, :block] = codes_s[:, lane]
+    for n, (ref, o) in enumerate(targets):
+        span = slice(n * block, (n + 1) * block)
+        mixed[:narrow, :block] = codes[:, span]
         for c in range(cap):
-            mixed[narrow + c : narrow + c + 1, :] = tables_s[pl.ds(o * cap + c, 1), :]
-        mixed[power_row : power_row + 1, :block] = powers_s[0:1, lane]
-        target[...] = mixed[...].astype(jnp.int16)
-
-    if direct:
-        for h in range(SOURCES):
-            for top in range(2):
-                o = top * 4 + flipped(dom % 4, h)
-                write(outs[h].at[top], o, pl.ds(pl.multiple_of(o * block, block), block))
-    else:
-        for o in range(workers):
-            write(outs[0].at[o], o, slice(o * block, (o + 1) * block))
+            mixed[narrow + c : narrow + c + 1, :] = tables[pl.ds(o * cap + c, 1), :]
+        mixed[power_row : power_row + 1, :block] = powers[:, span]
+        ref[...] = mixed[...].astype(jnp.int16)
+
+
+def own_kernel(block, narrow, cap, offsets, place, packed, y, tables, out, mixed):
+    cols = jnp.transpose(packed[...])
+    targets = [(out.at[top], top * 4 + place[0] % 4) for top in range(2)]
+    write_blocks(y[...], cols, targets, tables, mixed, place[1], block, narrow, cap, offsets)
 
 
 def flipped(index, mask):
@@ -281,11 +289,12 @@
             for part in parts[first : first + terms]:
                 both = part[top].astype(jnp.int32)
                 total += decode(both[:narrow, :block], both[power, :block])
-            mixed[:narrow, :block], mixed[power, :block] = encode(total * F32(scale), 0)
+            codes, powers = encode(total * F32(scale), 0)
+            mixed[:narrow, :block], mixed[narrow : narrow + 1, :block] = codes, powers
             out[first // terms * depth + top] = mixed[...].astype(jnp.int16)
 
 
-def entity_kernel(direct, narrow, place, serve, lhs, *refs):
+def entity_kernel(direct, narrow, offsets, place, serve, packed, x, *refs):
     recv, out, terms, onehot = refs[:-3], refs[-3], refs[-2], refs[-1]
     cap, workers = serve.shape[1], serve.shape[2]
     rows = out.shape[1]
@@ -309,7 +318,11 @@
     spots = onehot[...].astype(BF16)
     parts = jnp.concatenate(split3(jnp.transpose(terms[...])), axis=1)
     added = dot(parts, jnp.concatenate([spots] * 3, axis=0))
-    out[...] = lhs[...] + added[:narrow]
+    sources = jnp.transpose(packed[...])[:, 0:1]
+    both = dot(x[...], ones_where(iota((x.shape[1], rows), 1) == sources))
+    window = x.shape[0] // 2
+    both = both[:window] + both[window:]
+    out[...] = shifted_rows(both, (place[1] * narrow) % 8, narrow, offsets) + added[:narrow]
 
 
 def decoded(pieces, place, workers, power_row, o, over_x, rows):
@@ -454,23 +467,23 @@
         tuple(offsets),
     )
     lanes = max(up(block, LANES), up(narrow, LANES))
-    outs = [2] * SOURCES if direct else [workers]
-    sizes = [jax.ShapeDtypeStruct((n, height, lanes), jnp.int16) for n in outs]
-    lhs_part, *sent = pl.pallas_call(
+    pieces = jax.ShapeDtypeStruct((2 * window, total), BF16)
+    outs = [2] * (SOURCES - 1) if direct else [workers]
+    sizes = [pieces] if direct else []
+    sizes += [jax.ShapeDtypeStruct((n, height, lanes), jnp.int16) for n in outs]
+    mixed = [pltpu.VMEM((height, lanes), jnp.int32)]
+    x_parts, tables, *sent = pl.pallas_call(
         functools.partial(main_kernel, cfg),
-        out_shape=[jax.ShapeDtypeStruct((narrow, rows), F32)] + sizes,
+        out_shape=[pieces, jax.ShapeDtypeStruct((slots, lanes), jnp.int32)] + sizes,
         in_specs=[SMEM] + [VMEM] * (replicas + 5),
-        out_specs=[VMEM] * (1 + len(sizes)),
+        out_specs=[VMEM] * (2 + len(sizes)),
         scratch_shapes=[
             pltpu.VMEM((slots, dim), F32),
             pltpu.VMEM((dim, slots), F32),
             pltpu.VMEM((dim, total), F32),
             pltpu.VMEM((lanes, slots), F32),
-            pltpu.VMEM((height, lanes), jnp.int32),
-            pltpu.VMEM((narrow, pad_rel), jnp.int32),
-            pltpu.VMEM((1, pad_rel), jnp.int32),
-            pltpu.VMEM((slots, lanes), jnp.int32),
-        ],
+        ]
+        + mixed,
         compiler_params=params(),
         name="edges",
     )(place, *held, packed, query, lhs_rows, rel_rows, received)
@@ -483,9 +496,19 @@
         return lax.ppermute(array, ("dom", "rep"), pairs)
 
     stack = jax.ShapeDtypeStruct((outs[0], height, lanes), jnp.int16)
-    mixed = [pltpu.VMEM((height, lanes), jnp.int32)]
     if direct:
-        got = {n: swap(sent[n], n) for n in reversed(range(1, SOURCES))}
+        y_parts, *sent = sent
+        got = {n: swap(sent[n - 1], n) for n in reversed(range(1, SOURCES))}
+        kept = pl.pallas_call(
+            functools.partial(own_kernel, block, narrow, cap, offsets),
+            out_shape=stack,
+            in_specs=[SMEM] + [VMEM] * 3,
+            out_specs=VMEM,
+            scratch_shapes=mixed,
+            compiler_params=params(),
+            cost_estimate=cost(4 * window * total * 2 * block, 10**6),
+            name="own",
+        )(place, packed, y_parts, tables)
         summed = pl.pallas_call(
             functools.partial(quad_kernel, narrow, cap),
             out_shape=stack,
@@ -494,21 +517,21 @@
             scratch_shapes=mixed,
             compiler_params=params(),
             name="quad",
-        )(sent[0], *[got[n] for n in range(1, SOURCES)])
+        )(kept, *[got[n] for n in range(1, SOURCES)])
         recv = [summed, swap(summed, 4)]
         parts = recv + [swap(summed, 2), swap(summed, 6)]
-        stack = jax.ShapeDtypeStruct((4, height, lanes), jnp.int16)
+        stack = 4
     else:
         recv = [lax.all_to_all(sent[0], "dom", 0, 0, tiled=True)]
         parts = [recv[0][w : w + 1] for w in range(workers)]
-        stack = jax.ShapeDtypeStruct((1, height, lanes), jnp.int16)
+        stack = 1
     scale = 1.0 / (edges * workers * replicas)
     chunk = pl.pallas_call(
         functools.partial(sum_kernel, scale, narrow, cap, block, 2 if direct else workers),
-        out_shape=stack,
+        out_shape=jax.ShapeDtypeStruct((stack, up(narrow + 1, 8), lanes), jnp.int16),
         in_specs=[VMEM] * len(parts),
         out_specs=VMEM,
-        scratch_shapes=mixed,
+        scratch_shapes=[pltpu.VMEM((up(narrow + 1, 8), lanes), jnp.int32)],
         compiler_params=params(),
         name="total",
     )(*parts)
@@ -518,17 +541,17 @@
             [chunk, swap(chunk, 1), swap(chunk, 0, 2), swap(chunk, 1, 2)], axis=0
         )
     entity_grad = pl.pallas_call(
-        functools.partial(entity_kernel, direct, narrow),
+        functools.partial(entity_kernel, direct, narrow, offsets),
         out_shape=jax.ShapeDtypeStruct((narrow, rows), F32),
-        in_specs=[SMEM] * 2 + [VMEM] * (1 + len(recv)),
+        in_specs=[SMEM] * 2 + [VMEM] * (2 + len(recv)),
         out_specs=VMEM,
         scratch_shapes=[pltpu.VMEM((slots, lanes), F32), pltpu.VMEM((slots, rows), F32)],
         compiler_params=params(),
         cost_estimate=cost(10**9, 10**6),
         name="entity",
-    )(place, serve_t, lhs_part, *recv)
-
-    power_row = narrow + SOURCES * cap
+    )(place, serve_t, packed, x_parts, *recv)
+
+    power_row = narrow
     if direct:
         base, entity_grad = lax.optimization_barrier((base, entity_grad))
         swapped = lax.ppermute(base, "rep", [(i, i ^ 1) for i in range(replicas)])

time: 50.7 us -> 50 us (0.986)
  waiting for transfers between devices: 11.1 us -> 9.17 us
  Pallas kernels: 13.9 us -> 15.1 us
    ppermute x9, waiting for transfers between devices: 10.8 us -> 8.96 us  [swap(): return lax.ppermute(array, ('dom', 'rep'), pairs)]
    pallas_call x2 -> x3, Pallas kernels: 4.77 us -> 5.98 us  [the longest x1 2.59 us: shards(): pl.pallas_call(functools.partial(main_kernel, cfg), out_shape=[pieces, ja...]
  transfers between devices with their start and end apart: 14 -> 14, of which waited for: 10 -> 9; matrix products, arithmetic and copies ran while one was open for 0% -> 0% of each run, Pallas kernels for 14% -> 18%
where the time goes in v13:
time: 50 us; the launch traced here: 49.7 us
  starting transfers between devices  20.8 us (42%)
  Pallas kernels  15.1 us (30%)
  waiting for transfers between devices  9.17 us (18%)
  local copies, waits for them, and re-layouts  3.08 us (6%)
  between operations  1.39 us (3%)
    ppermute x9, starting transfers between devices, swap(): return lax.ppermute(array, ('dom', 'rep'), pairs)  11.6 us
    ppermute x9, waiting for transfers between devices, swap(): return lax.ppermute(array, ('dom', 'rep'), pairs)  8.96 us
    all_to_all x1, starting transfers between devices, shards(): received = lax.all_to_all(served, 'dom', 0, 0, tiled=True)  5.84 us
    pallas_call x1, Pallas kernels, shards(): pl.pallas_call(functools.partial(gather_kernel, (replicas, groups, nrel,...  3.95 us
    ppermute x3, starting transfers between devices, shards(): held.append(lax.ppermute(idx, 'rep', turned(replicas, hop)))  3.23 us
    unnamed x10, local copies, waits for them, and re-layouts  3.08 us
    pallas_call x1, Pallas kernels, shards(): pl.pallas_call(functools.partial(main_kernel, cfg), out_shape=[pieces, ja...  2.59 us
    pallas_call x1, Pallas kernels, shards(): pl.pallas_call(functools.partial(entity_kernel, direct, narrow, offsets),...  2.04 us
  transfers between devices with their start and end apart: 14, of which 9 were waited for; matrix products, arithmetic and copies ran while one was open for 0% of the time, Pallas kernels for 18%

profile of v13, /device:TPU:0, one launch (start us, length us, event | category | flops | bytes accessed | tf_op | source)
XLA Modules:
  0.0 49.7 jit_solution(7754434204435853678)
XLA Ops:
  1.3 1.8 %prep.1 = (s32[8,512]{1,0:T(8,128)}, f32[8,2,400]{2,1,0:T(2,128)}) custom-call(s32[1,2,8]{2,1,0:T(2,128)} %bitcast.9, s32[1,1]{1,0:T(1,128)S(6)} %copy.12.count, bf16[400,256]{1,0:T(8,128)(2,1)} %bitcast.7, s32[1,1,512]{2,1,0:T(1,128)} %src.1, s32[1,1,512]{2,1,0:T(1,128)} %rel.1, s32[1,1,512]{2,1,0:T(1,128)} %dst.1, s32[1,1,2,384]{3,2,1,0:T(2,128)} %neg.1), custom_call_target="tpu_custom_call" | custom-call | tf_op jit(solution)/shard_map/prep/pallas_call | solution.py:414
  3.1 2.4 %collective-permute-start.2 = (s32[8,512]{1,0:T(8,128)}, s32[8,512]{1,0:T(8,128)S(1)}, u32[]{:S(2)}, u32[]{:S(2)}) collective-permute-start(s32[8,512]{1,0:T(8,128)} %get-tuple-element.16.refs_0_), channel_id=1, source_target_pairs={{0,3},{1,0},{2,1},{3,2},{4,7},{5,4},{6,5},{7,6},{8,11},{9,8},{10,9... | collective-permute-start | bytes 49160 | tf_op jit(solution)/shard_map/ppermute | solution.py:439
  5.5 0.6 %collective-permute-start.1 = (s32[8,512]{1,0:T(8,128)}, s32[8,512]{1,0:T(8,128)S(1)}, u32[]{:S(2)}, u32[]{:S(2)}) collective-permute-start(s32[8,512]{1,0:T(8,128)} %get-tuple-element.16.refs_0_), channel_id=1, source_target_pairs={{0,2},{1,3},{2,0},{3,1},{4,6},{5,7},{6,4},{7,5},{8,10},{9,11},{10,... | collective-permute-start | bytes 49160 | tf_op jit(solution)/shard_map/ppermute | solution.py:439
  6.2 0.2 collective-permute-start
  6.3 5.8 %all-to-all-start = ((f32[8,2,400]{2,1,0:T(2,128)}), f32[8,2,400]{2,1,0:T(2,128)S(1)}, u32[]{:S(2)}, u32[]{:S(2)}) async-start(f32[8,2,400]{2,1,0:T(2,128)} %get-tuple-element.21), calls=%async_computation | async-start | bytes 65536 | tf_op jit(solution)/shard_map/all_to_all | solution.py:440
  12.2 0.1 pad_add_fusion.1.place
  12.2 0.0 collective-permute-done.2.refs_3_
  12.2 0.0 collective-permute-done.1.refs_2_
  12.2 0.0 collective-permute-done.refs_1_
  12.3 0.0 copy-start
  12.3 0.9 %copy-done = bf16[256,400]{0,1:T(8,128)(2,1)S(1)} copy-done((bf16[256,400]{0,1:T(8,128)(2,1)S(1)}, bf16[256,400]{0,1:T(8,128)(2,1)}, u32[]{:S(2)}) %copy-start) | copy-done | bytes 204824
  13.2 0.0 copy-start.1
  13.2 0.7 %copy-done.1 = s32[8,512]{1,0:T(8,128)S(1)} copy-done((s32[8,512]{1,0:T(8,128)S(1)}, s32[8,512]{1,0:T(8,128)}, u32[]{:S(2)}) %copy-start.1) | copy-done | bytes 16408
  13.9 0.0 copy-start.4
  13.9 1.4 %copy-done.4 = f32[1000,400]{0,1:T(8,128)S(1)} copy-done((f32[1000,400]{0,1:T(8,128)S(1)}, f32[1000,400]{0,1:T(8,128)}, u32[]{:S(2)}) %copy-start.4) | copy-done | bytes 1600024
  15.3 0.0 copy-start.2
  15.3 3.9 %gather.1 = (s32[8,1536]{1,0:T(8,128)S(1)}, bf16[400,1536]{1,0:T(8,128)(2,1)S(1)}, f32[104,1536]{1,0:T(8,128)S(1)}, f32[104,1536]{1,0:T(8,128)S(1)}) custom-call(s32[2]{0:T(128)S(1)} %pad_add_fusion.1.place, s32[8,512]{1,0:T(8,128)S(1)} %copy-done.1, s32[8,512]{1,0:T(8,128)S(1)} %collective-permute-done.refs_1_, ...), custom_call_target="tpu_custom_call" | custom-call | flops 2831155200 | bytes 4915200 | tf_op jit(solution)/shard_map/gather/pallas_call | solution.py:443
  19.3 0.0 all-to-all-done.refs_8_
  19.3 0.0 copy-done.2
  19.3 0.0 copy-start.3
  19.3 2.6 %edges.1 = (bf16[208,1536]{1,0:T(8,128)(2,1)S(1)}, s32[16,128]{1,0:T(8,128)S(1)}, bf16[208,1536]{1,0:T(8,128)(2,1)S(1)}, s16[2,112,128]{2,1,0:T(8,128)(2,1)S(1)}...) custom-call(s32[2]{0:T(128)S(1)} %pad_add_fusion.1.place, s32[8,512]{1,0:T(8,128)S(1)} %copy-done.2, ...), custom_call_target="tpu_custom_call" | custom-call | tf_op jit(solution)/shard_map/edges/pallas_call | solution.py:475
  21.9 2.1 %collective-permute-start.3 = (s16[2,112,128]{2,1,0:T(8,128)(2,1)S(1)}, s16[2,112,128]{2,1,0:T(8,128)(2,1)S(1)}, u32[]{:S(2)}, u32[]{:S(2)}) collective-permute-start(s16[2,112,128]{2,1,0:T(8,128)(2,1)S(1)} %get-tuple-element.24), channel_id=1, source_target_pairs={{0,4},{1,5},{2,6},{3,7},{4,0},{5,1},{6,2},{7,3},{8,12},{9,13},{10,... | collective-permute-start | bytes 172040 | tf_op jit(solution)/shard_map/ppermute | solution.py:496
  24.0 1.5 %collective-permute-start.4 = (s16[2,112,128]{2,1,0:T(8,128)(2,1)S(1)}, s16[2,112,128]{2,1,0:T(8,128)(2,1)S(1)}, u32[]{:S(2)}, u32[]{:S(2)}) collective-permute-start(s16[2,112,128]{2,1,0:T(8,128)(2,1)S(1)} %get-tuple-element.25), channel_id=1, source_target_pairs={{0,8},{1,9},{2,10},{3,11},{4,12},{5,13},{6,14},{7,15},{8,0},{9,1},... | collective-permute-start | bytes 172040 | tf_op jit(solution)/shard_map/ppermute | solution.py:496
  25.5 0.1 collective-permute-start.5
  25.6 1.3 %own.1.refs_0_ = s16[2,112,128]{2,1,0:T(8,128)(2,1)S(1)} custom-call(s32[2]{0:T(128)S(1)} %pad_add_fusion.1.place, s32[8,1536]{1,0:T(8,128)S(1)} %get-tuple-element.17.refs_4_.packed, bf16[208,1536]{1,0:T(8,128)(2,1)S(1)} %get-tuple-element.22.y, s32[16,128]{1,0:T(8,128)S(1)} %get-tuple-element.23.tables), custom_call_target="tpu_custom_call" | custom-call | flops 163577856 | bytes 1000000 | tf_op jit(solution)/shard_map/own/pallas_call | solution.py:502
  26.9 0.0 collective-permute-done.3.refs_1_
  26.9 1.5 %collective-permute-done.4.refs_2_ = s16[2,112,128]{2,1,0:T(8,128)(2,1)S(1)} collective-permute-done((s16[2,112,128]{2,1,0:T(8,128)(2,1)S(1)}, s16[2,112,128]{2,1,0:T(8,128)(2,1)S(1)}, u32[]{:S(2)}, u32[]{:S(2)}) %collective-permute-start.4) | collective-permute-done | bytes 57376 | tf_op jit(solution)/shard_map/ppermute | solution.py:496
  28.4 2.1 %collective-permute-done.5.refs_3_ = s16[2,112,128]{2,1,0:T(8,128)(2,1)S(1)} collective-permute-done((s16[2,112,128]{2,1,0:T(8,128)(2,1)S(1)}, s16[2,112,128]{2,1,0:T(8,128)(2,1)S(1)}, u32[]{:S(2)}, u32[]{:S(2)}) %collective-permute-start.5) | collective-permute-done | bytes 57376 | tf_op jit(solution)/shard_map/ppermute | solution.py:496
  30.6 0.1 quad.1.refs_0_
  30.7 2.4 %collective-permute-start.8 = (s16[2,112,128]{2,1,0:T(8,128)(2,1)S(1)}, s16[2,112,128]{2,1,0:T(8,128)(2,1)S(1)}, u32[]{:S(2)}, u32[]{:S(2)}) collective-permute-start(s16[2,112,128]{2,1,0:T(8,128)(2,1)S(1)} %quad.1.refs_0_), channel_id=1, source_target_pairs={{0,24},{1,25},{2,26},{3,27},{4,28},{5,29},{6,30},{7,31},{8,16},{9,... | collective-permute-start | bytes 172040 | tf_op jit(solution)/shard_map/ppermute | solution.py:496
  33.1 0.6 %collective-permute-start.7 = (s16[2,112,128]{2,1,0:T(8,128)(2,1)S(1)}, s16[2,112,128]{2,1,0:T(8,128)(2,1)S(1)}, u32[]{:S(2)}, u32[]{:S(2)}) collective-permute-start(s16[2,112,128]{2,1,0:T(8,128)(2,1)S(1)} %quad.1.refs_0_), channel_id=1, source_target_pairs={{0,8},{1,9},{2,10},{3,11},{4,12},{5,13},{6,14},{7,15},{8,0},{9,1},... | collective-permute-start | bytes 172040 | tf_op jit(solution)/shard_map/ppermute | solution.py:496
  33.7 1.5 %collective-permute-start.6 = (s16[2,112,128]{2,1,0:T(8,128)(2,1)S(1)}, s16[2,112,128]{2,1,0:T(8,128)(2,1)S(1)}, u32[]{:S(2)}, u32[]{:S(2)}) collective-permute-start(s16[2,112,128]{2,1,0:T(8,128)(2,1)S(1)} %quad.1.refs_0_), channel_id=1, source_target_pairs={{0,16},{1,17},{2,18},{3,19},{4,20},{5,21},{6,22},{7,23},{8,24},{9,... | collective-permute-start | bytes 172040 | tf_op jit(solution)/shard_map/ppermute | solution.py:496
  35.1 1.9 %collective-permute-done.8.refs_3_ = s16[2,112,128]{2,1,0:T(8,128)(2,1)S(1)} collective-permute-done((s16[2,112,128]{2,1,0:T(8,128)(2,1)S(1)}, s16[2,112,128]{2,1,0:T(8,128)(2,1)S(1)}, u32[]{:S(2)}, u32[]{:S(2)}) %collective-permute-start.8) | collective-permute-done | bytes 57376 | tf_op jit(solution)/shard_map/ppermute | solution.py:496
  37.0 0.5 %collective-permute-done.7.refs_2_ = s16[2,112,128]{2,1,0:T(8,128)(2,1)S(1)} collective-permute-done((s16[2,112,128]{2,1,0:T(8,128)(2,1)S(1)}, s16[2,112,128]{2,1,0:T(8,128)(2,1)S(1)}, u32[]{:S(2)}, u32[]{:S(2)}) %collective-permute-start.7) | collective-permute-done | bytes 57376 | tf_op jit(solution)/shard_map/ppermute | solution.py:496
  37.5 1.2 %collective-permute-done.6.refs_1_ = s16[2,112,128]{2,1,0:T(8,128)(2,1)S(1)} collective-permute-done((s16[2,112,128]{2,1,0:T(8,128)(2,1)S(1)}, s16[2,112,128]{2,1,0:T(8,128)(2,1)S(1)}, u32[]{:S(2)}, u32[]{:S(2)}) %collective-permute-start.6) | collective-permute-done | bytes 57376 | tf_op jit(solution)/shard_map/ppermute | solution.py:496
  38.7 0.2 total.1
  38.9 1.3 %collective-permute-start.11 = (s16[4,104,128]{2,1,0:T(8,128)(2,1)S(1)}, s16[4,104,128]{2,1,0:T(8,128)(2,1)S(1)}, u32[]{:S(2)}, u32[]{:S(2)}) collective-permute-start(s16[4,104,128]{2,1,0:T(8,128)(2,1)S(1)} %total.1), channel_id=1, source_target_pairs={{0,6},{1,7},{2,4},{3,5},{4,2},{5,3},{6,0},{7,1},{8,14},{9,15},{10,... | collective-permute-start | bytes 319496 | tf_op jit(solution)/shard_map/ppermute | solution.py:496
  40.2 1.3 %collective-permute-start.10 = (s16[4,104,128]{2,1,0:T(8,128)(2,1)S(1)}, s16[4,104,128]{2,1,0:T(8,128)(2,1)S(1)}, u32[]{:S(2)}, u32[]{:S(2)}) collective-permute-start(s16[4,104,128]{2,1,0:T(8,128)(2,1)S(1)} %total.1), channel_id=1, source_target_pairs={{0,2},{1,3},{2,0},{3,1},{4,6},{5,7},{6,4},{7,5},{8,10},{9,11},{10,... | collective-permute-start | bytes 319496 | tf_op jit(solution)/shard_map/ppermute | solution.py:496
  41.5 1.0 %collective-permute-start.9 = (s16[4,104,128]{2,1,0:T(8,128)(2,1)S(1)}, s16[4,104,128]{2,1,0:T(8,128)(2,1)S(1)}, u32[]{:S(2)}, u32[]{:S(2)}) collective-permute-start(s16[4,104,128]{2,1,0:T(8,128)(2,1)S(1)} %total.1), channel_id=1, source_target_pairs={{0,4},{1,5},{2,6},{3,7},{4,0},{5,1},{6,2},{7,3},{8,12},{9,13},{10,... | collective-permute-start | bytes 319496 | tf_op jit(solution)/shard_map/ppermute | solution.py:496
  42.5 0.0 copy-done.3
  42.5 2.0 %entity.1 = f32[100,256]{1,0:T(8,128)} custom-call(s32[2]{0:T(128)S(1)} %pad_add_fusion.1.place, s32[1,2,8]{2,1,0:T(2,128)S(1)} %bitcast.10, s32[8,1536]{1,0:T(8,128)S(1)} %get-tuple-element.17.refs_4_.packed, bf16[208,1536]{1,0:T(8,128)(2,1)S(1)} %get-tuple-element.27.x, s16[2,112,128]{2,1,0:T(8,128)(2,1)S(1)} %quad.1.refs_0_, ...), custom_call_target="tpu_custom_call" | custom-call | flops 1000000000 | bytes 1000000 | tf_op jit(solution)/shard_map/entity/pallas_call | solution.py:543
  44.5 0.2 collective-permute-done.11
  44.7 0.9 %collective-permute-done.10 = s16[4,104,128]{2,1,0:T(8,128)(2,1)S(1)} collective-permute-done((s16[4,104,128]{2,1,0:T(8,128)(2,1)S(1)}, s16[4,104,128]{2,1,0:T(8,128)(2,1)S(1)}, u32[]{:S(2)}, u32[]{:S(2)}) %collective-permute-start.10) | collective-permute-done | bytes 106528 | tf_op jit(solution)/shard_map/ppermute | solution.py:496
  45.6 0.6 %collective-permute-done.9 = s16[4,104,128]{2,1,0:T(8,128)(2,1)S(1)} collective-permute-done((s16[4,104,128]{2,1,0:T(8,128)(2,1)S(1)}, s16[4,104,128]{2,1,0:T(8,128)(2,1)S(1)}, u32[]{:S(2)}, u32[]{:S(2)}) %collective-permute-start.9) | collective-permute-done | bytes 106528 | tf_op jit(solution)/shard_map/ppermute | solution.py:496
  46.3 0.1 collective-permute-start.12
  46.3 1.5 %spread_own.1.partial = f32[400,1000]{1,0:T(8,128)} custom-call(s32[2]{0:T(128)S(1)} %pad_add_fusion.1.place, s16[16,104,128]{2,1,0:T(8,128)(2,1)S(1)} %pad_add_fusion.mine), custom_call_target="tpu_custom_call" | custom-call | flops 1000000 | bytes 1600000 | tf_op jit(solution)/shard_map/spread_own/pallas_call | solution.py:561
  47.9 0.2 collective-permute-done.12.other
  48.1 1.6 %spread_rest.1 = f32[400,1000]{1,0:T(8,128)} custom-call(s32[2]{0:T(128)S(1)} %pad_add_fusion.1.place, s16[16,104,128]{2,1,0:T(8,128)(2,1)S(1)} %pad_add_fusion.mine, s16[16,104,128]{2,1,0:T(8,128)(2,1)S(1)} %collective-permute-done.12.other, f32[400,1000]{1,0:T(8,128)} %spread_own.1.partial), custom_call_target="tpu_custom_call", output_to_operand_aliasing={{}: (3, {})} | custom-call | tf_op jit(solution)/shard_map/spread_rest/pallas_call | solution.py:571
  (1 shorter events, 0.0 us)
Async XLA Ops:
  3.1 9.1 %collective-permute-start.2 = (s32[8,512]{1,0:T(8,128)}, s32[8,512]{1,0:T(8,128)S(1)}, u32[]{:S(2)}, u32[]{:S(2)}) collective-permute-start(s32[8,512]{1,0:T(8,128)} %get-tuple-element.16.refs_0_), channel_id=1, source_target_pairs={{0,3},{1,0},{2,1},{3,2},{4,7},{5,4},{6,5},{7,6},{8,11},{9,8},{10,9... | collective-permute-start | bytes 49160 | tf_op jit(solution)/shard_map/ppermute | solution.py:439
  5.5 6.7 %collective-permute-start.1 = (s32[8,512]{1,0:T(8,128)}, s32[8,512]{1,0:T(8,128)S(1)}, u32[]{:S(2)}, u32[]{:S(2)}) collective-permute-start(s32[8,512]{1,0:T(8,128)} %get-tuple-element.16.refs_0_), channel_id=1, source_target_pairs={{0,2},{1,3},{2,0},{3,1},{4,6},{5,7},{6,4},{7,5},{8,10},{9,11},{10,... | collective-permute-start | bytes 49160 | tf_op jit(solution)/shard_map/ppermute | solution.py:439
  6.2 6.1 %collective-permute-start = (s32[8,512]{1,0:T(8,128)}, s32[8,512]{1,0:T(8,128)S(1)}, u32[]{:S(2)}, u32[]{:S(2)}) collective-permute-start(s32[8,512]{1,0:T(8,128)} %get-tuple-element.16.refs_0_), channel_id=1, source_target_pairs={{0,1},{1,2},{2,3},{3,0},{4,5},{5,6},{6,7},{7,4},{8,9},{9,10},{10,1... | collective-permute-start | bytes 49160 | tf_op jit(solution)/shard_map/ppermute | solution.py:439
  6.3 13.0 %all-to-all-start = ((f32[8,2,400]{2,1,0:T(2,128)}), f32[8,2,400]{2,1,0:T(2,128)S(1)}, u32[]{:S(2)}, u32[]{:S(2)}) async-start(f32[8,2,400]{2,1,0:T(2,128)} %get-tuple-element.21), calls=%async_computation | async-start | bytes 65536 | tf_op jit(solution)/shard_map/all_to_all | solution.py:440
  12.3 0.9 %copy-start = (bf16[256,400]{0,1:T(8,128)(2,1)S(1)}, bf16[256,400]{0,1:T(8,128)(2,1)}, u32[]{:S(2)}) copy-start(bf16[256,400]{0,1:T(8,128)(2,1)} %param.8) | copy-start | bytes 614404
  13.2 0.7 %copy-start.1 = (s32[8,512]{1,0:T(8,128)S(1)}, s32[8,512]{1,0:T(8,128)}, u32[]{:S(2)}) copy-start(s32[8,512]{1,0:T(8,128)} %get-tuple-element.16.refs_0_) | copy-start | bytes 49156
  13.9 1.4 %copy-start.4 = (f32[1000,400]{0,1:T(8,128)S(1)}, f32[1000,400]{0,1:T(8,128)}, u32[]{:S(2)}) copy-start(f32[1000,400]{0,1:T(8,128)} %param.9) | copy-start | bytes 4800004
  15.3 4.0 %copy-start.2 = (s32[8,512]{1,0:T(8,128)S(1)}, s32[8,512]{1,0:T(8,128)}, u32[]{:S(2)}) copy-start(s32[8,512]{1,0:T(8,128)} %get-tuple-element.16.refs_0_) | copy-start | bytes 49156
  19.3 23.2 %copy-start.3 = (s32[1,8,2]{1,2,0:T(2,128)S(1)}, s32[1,8,2]{1,2,0:T(2,128)}, u32[]{:S(2)}) copy-start(s32[1,8,2]{1,2,0:T(2,128)} %param.10) | copy-start | bytes 196
  21.9 5.0 %collective-permute-start.3 = (s16[2,112,128]{2,1,0:T(8,128)(2,1)S(1)}, s16[2,112,128]{2,1,0:T(8,128)(2,1)S(1)}, u32[]{:S(2)}, u32[]{:S(2)}) collective-permute-start(s16[2,112,128]{2,1,0:T(8,128)(2,1)S(1)} %get-tuple-element.24), channel_id=1, source_target_pairs={{0,4},{1,5},{2,6},{3,7},{4,0},{5,1},{6,2},{7,3},{8,12},{9,13},{10,... | collective-permute-start | bytes 172040 | tf_op jit(solution)/shard_map/ppermute | solution.py:496
  24.0 4.4 %collective-permute-start.4 = (s16[2,112,128]{2,1,0:T(8,128)(2,1)S(1)}, s16[2,112,128]{2,1,0:T(8,128)(2,1)S(1)}, u32[]{:S(2)}, u32[]{:S(2)}) collective-permute-start(s16[2,112,128]{2,1,0:T(8,128)(2,1)S(1)} %get-tuple-element.25), channel_id=1, source_target_pairs={{0,8},{1,9},{2,10},{3,11},{4,12},{5,13},{6,14},{7,15},{8,0},{9,1},... | collective-permute-start | bytes 172040 | tf_op jit(solution)/shard_map/ppermute | solution.py:496
  25.5 5.1 %collective-permute-start.5 = (s16[2,112,128]{2,1,0:T(8,128)(2,1)S(1)}, s16[2,112,128]{2,1,0:T(8,128)(2,1)S(1)}, u32[]{:S(2)}, u32[]{:S(2)}) collective-permute-start(s16[2,112,128]{2,1,0:T(8,128)(2,1)S(1)} %get-tuple-element.26), channel_id=1, source_target_pairs={{0,12},{1,13},{2,14},{3,15},{4,8},{5,9},{6,10},{7,11},{8,4},{9,5},... | collective-permute-start | bytes 172040 | tf_op jit(solution)/shard_map/ppermute | solution.py:496
  30.7 6.3 %collective-permute-start.8 = (s16[2,112,128]{2,1,0:T(8,128)(2,1)S(1)}, s16[2,112,128]{2,1,0:T(8,128)(2,1)S(1)}, u32[]{:S(2)}, u32[]{:S(2)}) collective-permute-start(s16[2,112,128]{2,1,0:T(8,128)(2,1)S(1)} %quad.1.refs_0_), channel_id=1, source_target_pairs={{0,24},{1,25},{2,26},{3,27},{4,28},{5,29},{6,30},{7,31},{8,16},{9,... | collective-permute-start | bytes 172040 | tf_op jit(solution)/shard_map/ppermute | solution.py:496
  33.1 4.4 %collective-permute-start.7 = (s16[2,112,128]{2,1,0:T(8,128)(2,1)S(1)}, s16[2,112,128]{2,1,0:T(8,128)(2,1)S(1)}, u32[]{:S(2)}, u32[]{:S(2)}) collective-permute-start(s16[2,112,128]{2,1,0:T(8,128)(2,1)S(1)} %quad.1.refs_0_), channel_id=1, source_target_pairs={{0,8},{1,9},{2,10},{3,11},{4,12},{5,13},{6,14},{7,15},{8,0},{9,1},... | collective-permute-start | bytes 172040 | tf_op jit(solution)/shard_map/ppermute | solution.py:496
  33.7 5.1 %collective-permute-start.6 = (s16[2,112,128]{2,1,0:T(8,128)(2,1)S(1)}, s16[2,112,128]{2,1,0:T(8,128)(2,1)S(1)}, u32[]{:S(2)}, u32[]{:S(2)}) collective-permute-start(s16[2,112,128]{2,1,0:T(8,128)(2,1)S(1)} %quad.1.refs_0_), channel_id=1, source_target_pairs={{0,16},{1,17},{2,18},{3,19},{4,20},{5,21},{6,22},{7,23},{8,24},{9,... | collective-permute-start | bytes 172040 | tf_op jit(solution)/shard_map/ppermute | solution.py:496
  38.9 5.8 %collective-permute-start.11 = (s16[4,104,128]{2,1,0:T(8,128)(2,1)S(1)}, s16[4,104,128]{2,1,0:T(8,128)(2,1)S(1)}, u32[]{:S(2)}, u32[]{:S(2)}) collective-permute-start(s16[4,104,128]{2,1,0:T(8,128)(2,1)S(1)} %total.1), channel_id=1, source_target_pairs={{0,6},{1,7},{2,4},{3,5},{4,2},{5,3},{6,0},{7,1},{8,14},{9,15},{10,... | collective-permute-start | bytes 319496 | tf_op jit(solution)/shard_map/ppermute | solution.py:496
  40.2 5.4 %collective-permute-start.10 = (s16[4,104,128]{2,1,0:T(8,128)(2,1)S(1)}, s16[4,104,128]{2,1,0:T(8,128)(2,1)S(1)}, u32[]{:S(2)}, u32[]{:S(2)}) collective-permute-start(s16[4,104,128]{2,1,0:T(8,128)(2,1)S(1)} %total.1), channel_id=1, source_target_pairs={{0,2},{1,3},{2,0},{3,1},{4,6},{5,7},{6,4},{7,5},{8,10},{9,11},{10,... | collective-permute-start | bytes 319496 | tf_op jit(solution)/shard_map/ppermute | solution.py:496
  41.5 4.7 %collective-permute-start.9 = (s16[4,104,128]{2,1,0:T(8,128)(2,1)S(1)}, s16[4,104,128]{2,1,0:T(8,128)(2,1)S(1)}, u32[]{:S(2)}, u32[]{:S(2)}) collective-permute-start(s16[4,104,128]{2,1,0:T(8,128)(2,1)S(1)} %total.1), channel_id=1, source_target_pairs={{0,4},{1,5},{2,6},{3,7},{4,0},{5,1},{6,2},{7,3},{8,12},{9,13},{10,... | collective-permute-start | bytes 319496 | tf_op jit(solution)/shard_map/ppermute | solution.py:496
  46.3 1.8 %collective-permute-start.12 = (s16[16,104,128]{2,1,0:T(8,128)(2,1)S(1)}, s16[16,104,128]{2,1,0:T(8,128)(2,1)S(1)}, u32[]{:S(2)}, u32[]{:S(2)}) collective-permute-start(s16[16,104,128]{2,1,0:T(8,128)(2,1)S(1)} %pad_add_fusion.mine), channel_id=1, source_target_pairs={{0,1},{1,0},{2,3},{3,2},{4,5},{5,4},{6,7},{7,6},{8,9},{9,8},{10,11... | collective-permute-start | bytes 1277960 | tf_op jit(solution)/shard_map/ppermute | solution.py:557

commit v14 on v13

--- a/solution.py
+++ b/solution.py
@@ -78,6 +78,13 @@
     out = x[offsets[0] : offsets[0] + narrow]
     for other in offsets[1:]:
         out = jnp.where(offset == other, x[other : other + narrow], out)
+    return out
+
+
+def window_rows(x, rep, starts, window):
+    out = x[starts[0] : starts[0] + window]
+    for n, start in enumerate(starts[1:], 1):
+        out = jnp.where(rep == n, x[start : start + window], out)
     return out
 
 
@@ -134,13 +141,14 @@
 def gather_kernel(cfg, place, *refs):
     replicas, groups, nrel, pad_rel, narrow, window, step = cfg
     idx_refs, refs = refs[:replicas], refs[replicas:]
-    ent, relation, out_idx, out_query, out_lhs, out_rel, rel_parts, lhs_s, rel_s = refs
+    ent, relation, out_idx, out_query, out_lhs, out_rel, rel_parts = refs
     dim, rows = ent.shape
-    base = pl.multiple_of((place[1] * narrow) // 8 * 8, 8)
+    starts = [narrow * r // 8 * 8 for r in range(replicas)]
     packed_edges(idx_refs, groups, out_idx)
     hi, lo = split2(relation[...])
     if pad_rel > nrel:
-        rel_parts[...] = jnp.zeros(rel_parts.shape, BF16)
+        edge = nrel // LANES * LANES
+        rel_parts[:, edge:] = jnp.zeros((2 * dim, pad_rel - edge), BF16)
     rel_parts[:dim, :nrel] = hi
     rel_parts[dim:, :nrel] = lo
     for start in range(0, out_idx.shape[1], step):
@@ -149,11 +157,9 @@
         lhs = dot(ent[...], ones_where(iota((rows, step), 0) == src_l))
         both = dot(rel_parts[...], ones_where(iota((pad_rel, step), 0) == rel_l))
         rel_rows = both[:dim] + both[dim:]
-        lhs_s[...] = lhs
-        rel_s[...] = rel_rows
         out_query[:, span] = (lhs * rel_rows).astype(BF16)
-        out_lhs[:, span] = lhs_s[pl.ds(base, window), :]
-        out_rel[:, span] = rel_s[pl.ds(base, window), :]
+        out_lhs[:, span] = window_rows(lhs, place[1], starts, window)
+        out_rel[:, span] = window_rows(rel_rows, place[1], starts, window)
 
 
 def main_kernel(cfg, place, *refs):
@@ -162,7 +168,7 @@
     (packed, query_v, lhs_v, rel_v, received), refs = refs[:5], refs[5:]
     out_x, tables, refs = refs[0], refs[1], refs[2:]
     out_y, refs = (refs[0], refs[1:]) if direct else (None, refs)
-    outs, (table_f, table_t, query_s, wide_t, mixed) = refs[:-5], refs[-5:]
+    outs, (table_f, table_t, wide_t, mixed) = refs[:-4], refs[-4:]
     edges = idx_refs[0].shape[1]
     dim, total = query_v.shape
     slots = workers * cap
@@ -180,7 +186,6 @@
 
     query = query_v[...]
     scores = dot(table, query)
-    query_s[...] = query.astype(F32)
     lanes = packed[...]
     cols = jnp.transpose(lanes)
     times = jnp.zeros((slots, total), F32)
@@ -207,7 +212,9 @@
     stack_t = jnp.concatenate(split3(jnp.transpose(grads)), axis=1)
 
     dquery = dot(own_t, stack)
-    acc_tab = dot(query_s[pl.ds(base, window), :].astype(BF16), stack_t)
+    acc_tab = window_rows(
+        dot(query, stack_t), rep, [narrow * r // 8 * 8 for r in range(replicas)], window
+    )
     wide_t[...] = jnp.zeros(wide_t.shape, F32)
     wide_t[:narrow] = shifted_rows(
         acc_tab[:, :slots] + acc_tab[:, slots : 2 * slots] + acc_tab[:, 2 * slots :],
@@ -278,9 +285,10 @@
         out[top] = mixed[...].astype(jnp.int16)
 
 
-def sum_kernel(scale, narrow, cap, block, terms, *refs):
+def sum_kernel(scale, narrow, cap, block, terms, place, *refs):
     parts, out, mixed = refs[:-2], refs[-2], refs[-1]
     depth = parts[0].shape[0]
+    lowered = mixed.shape[0] - narrow if terms == 2 else 0
     power = slice(narrow + SOURCES * cap, narrow + SOURCES * cap + 1)
     mixed[...] = jnp.zeros(mixed.shape, jnp.int32)
     for first in range(0, len(parts), terms):
@@ -290,7 +298,15 @@
                 both = part[top].astype(jnp.int32)
                 total += decode(both[:narrow, :block], both[power, :block])
             codes, powers = encode(total * F32(scale), 0)
-            mixed[:narrow, :block], mixed[narrow : narrow + 1, :block] = codes, powers
+            if lowered:
+                rest = jnp.broadcast_to(powers, (lowered, block))
+                mixed[:, :block] = jnp.where(
+                    lax.rem(place[1], 2) == 0,
+                    jnp.concatenate([codes, rest], axis=0),
+                    jnp.concatenate([rest, codes], axis=0),
+                )
+            else:
+                mixed[:narrow, :block], mixed[narrow : narrow + 1, :block] = codes, powers
             out[first // terms * depth + top] = mixed[...].astype(jnp.int16)
 
 
@@ -325,25 +341,23 @@
     out[...] = shifted_rows(both, (place[1] * narrow) % 8, narrow, offsets) + added[:narrow]
 
 
-def decoded(pieces, place, workers, power_row, o, over_x, rows):
+def found(pieces, place, o, over_x):
     dom = place[0]
     over_low = lax.rem(dom // 2 + o // 2, 2)
     over_y = lax.rem(dom + o, 2)
-    spot = (over_y + 2 * over_x) * 4 + over_low * 2 + o // 4
-    both = pieces[spot].astype(jnp.int32)
-    return decode(both[rows], both[power_row : power_row + 1])
+    return pieces[(over_y + 2 * over_x) * 4 + over_low * 2 + o // 4].astype(jnp.int32)
 
 
 def spread_core(pieces, core, place, sizes, bands, out, sems):
-    workers, narrow, power_row, block, nrel = sizes
+    workers, narrow, block, nrel = sizes
     length = narrow // 8 * 8
-    extra = narrow - length
     moves = []
     for x in range(2):
         over_x = lax.rem(place[1] // 2 + x, 2)
         for o in range(workers):
-            value = decoded(pieces, place, workers, power_row, o, over_x, slice(0, narrow))
-            value = jnp.where(core == 0, value[:length], value[extra:])
+            both = found(pieces, place, o, over_x)
+            codes = jnp.where(core == 0, both[:length], both[8:])
+            value = decode(codes, jnp.where(core == 0, both[narrow : narrow + 1], both[:1]))
             end = min((o + 1) * block, nrel)
             bands[x * length : (x + 1) * length, o * block : end] = value[:, : end - o * block]
         first = pl.multiple_of(2 * narrow * x + (length + 8) * core, 8)
@@ -361,20 +375,21 @@
 
 
 def spread_rest_kernel(sizes, place, mine, other, partial, out, bands, shared, sems):
-    workers, narrow, power_row, block, nrel = sizes
+    workers, narrow, block, nrel = sizes
     core = lax.rem(place[1], 2)
     length = narrow // 8 * 8
-    extra = narrow - length
     moves = spread_core(other, 1 - core, place, sizes, bands, out, sems)
     for x in range(2):
         over_x = lax.rem(place[1] // 2 + x, 2)
         for o in range(workers):
-            parts = []
-            for which, rows in ((0, slice(length, narrow)), (1, slice(0, 8 - extra))):
-                ours = decoded(mine, place, workers, power_row, o, over_x, rows)
-                theirs = decoded(other, place, workers, power_row, o, over_x, rows)
-                parts.append(jnp.where(core == which, ours, theirs))
-            value = jnp.concatenate(parts, axis=0)
+            ours, theirs = found(mine, place, o, over_x), found(other, place, o, over_x)
+            low = jnp.where(core == 0, ours[length:], theirs[length:])
+            high = jnp.where(core == 0, theirs[:8], ours[:8])
+            upper = iota(low.shape, 0) < narrow - length
+            split = narrow - length
+            value = jnp.where(
+                upper, decode(low, low[split : split + 1]), decode(high, high[:1])
+            )
             end = min((o + 1) * block, nrel)
             shared[x * 8 : (x + 1) * 8, o * block : end] = value[:, : end - o * block]
         first = 2 * narrow * x + length
@@ -454,8 +469,6 @@
         out_specs=[VMEM] * 4,
         scratch_shapes=[
             pltpu.VMEM((2 * dim, pad_rel), BF16),
-            pltpu.VMEM((dim, edges), F32),
-            pltpu.VMEM((dim, edges), F32),
         ],
         compiler_params=params(),
         cost_estimate=cost(2 * total * dim * (2 * pad_rel + rows), 8 * total * dim),
@@ -480,7 +493,6 @@
         scratch_shapes=[
             pltpu.VMEM((slots, dim), F32),
             pltpu.VMEM((dim, slots), F32),
-            pltpu.VMEM((dim, total), F32),
             pltpu.VMEM((lanes, slots), F32),
         ]
         + mixed,
@@ -529,12 +541,12 @@
     chunk = pl.pallas_call(
         functools.partial(sum_kernel, scale, narrow, cap, block, 2 if direct else workers),
         out_shape=jax.ShapeDtypeStruct((stack, up(narrow + 1, 8), lanes), jnp.int16),
-        in_specs=[VMEM] * len(parts),
+        in_specs=[SMEM] + [VMEM] * len(parts),
         out_specs=VMEM,
         scratch_shapes=[pltpu.VMEM((up(narrow + 1, 8), lanes), jnp.int32)],
         compiler_params=params(),
         name="total",
-    )(*parts)
+    )(place, *parts)
 
     if direct:
         base = jnp.concatenate(
@@ -551,11 +563,10 @@
         name="entity",
     )(place, serve_t, packed, x_parts, *recv)
 
-    power_row = narrow
     if direct:
         base, entity_grad = lax.optimization_barrier((base, entity_grad))
         swapped = lax.ppermute(base, "rep", [(i, i ^ 1) for i in range(replicas)])
-        sizes = (workers, narrow, power_row, block, nrel)
+        sizes = (workers, narrow, block, nrel)
         result = jax.ShapeDtypeStruct((dim, nrel), F32)
         bands = pltpu.VMEM((narrow // 8 * 16, nrel), F32)
         own_half = pl.pallas_call(
@@ -580,7 +591,7 @@
         )(place, base, swapped, own_half)
     else:
         whole = lax.all_gather(chunk[0, :, :block], ("dom", "rep"), axis=0)
-        whole = decode(whole[:, :narrow], whole[:, power_row : power_row + 1])
+        whole = decode(whole[:, :narrow], whole[:, narrow : narrow + 1])
         whole = whole.reshape(workers, replicas, narrow, block).transpose(1, 2, 0, 3)
         relation_t = whole.reshape(dim, workers * block)[:, :nrel]
     return (entity_grad.T, relation_t.T)

time: 50 us -> 50.7 us (1.014)
  Pallas kernels: 15.1 us -> 15.8 us
    pallas_call x1, Pallas kernels: 0.16 us -> 0.7 us  [shards(): pl.pallas_call(functools.partial(sum_kernel, scale, narrow, cap, block, 2...]
where the time goes in v14:
time: 50.7 us; the launch traced here: 50.3 us
  starting transfers between devices  20.8 us (41%)
  Pallas kernels  15.8 us (31%)
  waiting for transfers between devices  9.2 us (18%)
  local copies, waits for them, and re-layouts  3.08 us (6%)
  between operations  1.4 us (3%)
    ppermute x9, starting transfers between devices, swap(): return lax.ppermute(array, ('dom', 'rep'), pairs)  11.6 us
    ppermute x9, waiting for transfers between devices, swap(): return lax.ppermute(array, ('dom', 'rep'), pairs)  8.96 us
    all_to_all x1, starting transfers between devices, shards(): received = lax.all_to_all(served, 'dom', 0, 0, tiled=True)  5.84 us
    pallas_call x1, Pallas kernels, shards(): pl.pallas_call(functools.partial(gather_kernel, (replicas, groups, nrel,...  3.94 us
    ppermute x3, starting transfers between devices, shards(): held.append(lax.ppermute(idx, 'rep', turned(replicas, hop)))  3.23 us
    unnamed x10, local copies, waits for them, and re-layouts  3.08 us
    pallas_call x1, Pallas kernels, shards(): pl.pallas_call(functools.partial(main_kernel, cfg), out_shape=[pieces, ja...  2.74 us
    pallas_call x1, Pallas kernels, shards(): pl.pallas_call(functools.partial(entity_kernel, direct, narrow, offsets),...  2.04 us
  transfers between devices with their start and end apart: 14, of which 9 were waited for; matrix products, arithmetic and copies ran while one was open for 0% of the time, Pallas kernels for 18%

profile of v14, /device:TPU:0, one launch (start us, length us, event | category | flops | bytes accessed | tf_op | source)
XLA Modules:
  0.0 50.3 jit_solution(9736374660767394130)
XLA Ops:
  1.3 1.8 %prep.1 = (s32[8,512]{1,0:T(8,128)}, f32[8,2,400]{2,1,0:T(2,128)}) custom-call(s32[1,2,8]{2,1,0:T(2,128)} %bitcast.9, s32[1,1]{1,0:T(1,128)S(6)} %copy.12.count, bf16[400,256]{1,0:T(8,128)(2,1)} %bitcast.7, s32[1,1,512]{2,1,0:T(1,128)} %src.1, s32[1,1,512]{2,1,0:T(1,128)} %rel.1, s32[1,1,512]{2,1,0:T(1,128)} %dst.1, s32[1,1,2,384]{3,2,1,0:T(2,128)} %neg.1), custom_call_target="tpu_custom_call" | custom-call | tf_op jit(solution)/shard_map/prep/pallas_call | solution.py:429
  3.1 2.4 %collective-permute-start.2 = (s32[8,512]{1,0:T(8,128)}, s32[8,512]{1,0:T(8,128)S(1)}, u32[]{:S(2)}, u32[]{:S(2)}) collective-permute-start(s32[8,512]{1,0:T(8,128)} %get-tuple-element.16.refs_0_), channel_id=1, source_target_pairs={{0,3},{1,0},{2,1},{3,2},{4,7},{5,4},{6,5},{7,6},{8,11},{9,8},{10,9... | collective-permute-start | bytes 49160 | tf_op jit(solution)/shard_map/ppermute | solution.py:454
  5.5 0.6 %collective-permute-start.1 = (s32[8,512]{1,0:T(8,128)}, s32[8,512]{1,0:T(8,128)S(1)}, u32[]{:S(2)}, u32[]{:S(2)}) collective-permute-start(s32[8,512]{1,0:T(8,128)} %get-tuple-element.16.refs_0_), channel_id=1, source_target_pairs={{0,2},{1,3},{2,0},{3,1},{4,6},{5,7},{6,4},{7,5},{8,10},{9,11},{10,... | collective-permute-start | bytes 49160 | tf_op jit(solution)/shard_map/ppermute | solution.py:454
  6.2 0.2 collective-permute-start
  6.3 5.8 %all-to-all-start = ((f32[8,2,400]{2,1,0:T(2,128)}), f32[8,2,400]{2,1,0:T(2,128)S(1)}, u32[]{:S(2)}, u32[]{:S(2)}) async-start(f32[8,2,400]{2,1,0:T(2,128)} %get-tuple-element.21), calls=%async_computation | async-start | bytes 65536 | tf_op jit(solution)/shard_map/all_to_all | solution.py:455
  12.2 0.1 pad_add_fusion.1.place
  12.2 0.0 collective-permute-done.2.refs_3_
  12.2 0.0 collective-permute-done.1.refs_2_
  12.2 0.0 collective-permute-done.refs_1_
  12.3 0.0 copy-start
  12.3 0.9 %copy-done = bf16[256,400]{0,1:T(8,128)(2,1)S(1)} copy-done((bf16[256,400]{0,1:T(8,128)(2,1)S(1)}, bf16[256,400]{0,1:T(8,128)(2,1)}, u32[]{:S(2)}) %copy-start) | copy-done | bytes 204824
  13.2 0.0 copy-start.1
  13.2 0.7 %copy-done.1 = s32[8,512]{1,0:T(8,128)S(1)} copy-done((s32[8,512]{1,0:T(8,128)S(1)}, s32[8,512]{1,0:T(8,128)}, u32[]{:S(2)}) %copy-start.1) | copy-done | bytes 16408
  13.9 0.0 copy-start.4
  13.9 1.4 %copy-done.4 = f32[1000,400]{0,1:T(8,128)S(1)} copy-done((f32[1000,400]{0,1:T(8,128)S(1)}, f32[1000,400]{0,1:T(8,128)}, u32[]{:S(2)}) %copy-start.4) | copy-done | bytes 1600024
  15.3 0.0 copy-start.2
  15.3 3.9 %gather.1 = (s32[8,1536]{1,0:T(8,128)S(1)}, bf16[400,1536]{1,0:T(8,128)(2,1)S(1)}, f32[104,1536]{1,0:T(8,128)S(1)}, f32[104,1536]{1,0:T(8,128)S(1)}) custom-call(s32[2]{0:T(128)S(1)} %pad_add_fusion.1.place, s32[8,512]{1,0:T(8,128)S(1)} %copy-done.1, s32[8,512]{1,0:T(8,128)S(1)} %collective-permute-done.refs_1_, ...), custom_call_target="tpu_custom_call" | custom-call | flops 2831155200 | bytes 4915200 | tf_op jit(solution)/shard_map/gather/pallas_call | solution.py:458
  19.3 0.0 all-to-all-done.refs_8_
  19.3 0.0 copy-done.2
  19.3 0.0 copy-start.3
  19.3 2.7 %edges.1 = (bf16[208,1536]{1,0:T(8,128)(2,1)S(1)}, s32[16,128]{1,0:T(8,128)S(1)}, bf16[208,1536]{1,0:T(8,128)(2,1)S(1)}, s16[2,112,128]{2,1,0:T(8,128)(2,1)S(1)}...) custom-call(s32[2]{0:T(128)S(1)} %pad_add_fusion.1.place, s32[8,512]{1,0:T(8,128)S(1)} %copy-done.2, ...), custom_call_target="tpu_custom_call" | custom-call | tf_op jit(solution)/shard_map/edges/pallas_call | solution.py:488
  22.1 2.1 %collective-permute-start.3 = (s16[2,112,128]{2,1,0:T(8,128)(2,1)S(1)}, s16[2,112,128]{2,1,0:T(8,128)(2,1)S(1)}, u32[]{:S(2)}, u32[]{:S(2)}) collective-permute-start(s16[2,112,128]{2,1,0:T(8,128)(2,1)S(1)} %get-tuple-element.24), channel_id=1, source_target_pairs={{0,4},{1,5},{2,6},{3,7},{4,0},{5,1},{6,2},{7,3},{8,12},{9,13},{10,... | collective-permute-start | bytes 172040 | tf_op jit(solution)/shard_map/ppermute | solution.py:508
  24.2 1.5 %collective-permute-start.4 = (s16[2,112,128]{2,1,0:T(8,128)(2,1)S(1)}, s16[2,112,128]{2,1,0:T(8,128)(2,1)S(1)}, u32[]{:S(2)}, u32[]{:S(2)}) collective-permute-start(s16[2,112,128]{2,1,0:T(8,128)(2,1)S(1)} %get-tuple-element.25), channel_id=1, source_target_pairs={{0,8},{1,9},{2,10},{3,11},{4,12},{5,13},{6,14},{7,15},{8,0},{9,1},... | collective-permute-start | bytes 172040 | tf_op jit(solution)/shard_map/ppermute | solution.py:508
  25.6 0.1 collective-permute-start.5
  25.7 1.3 %own.1.refs_0_ = s16[2,112,128]{2,1,0:T(8,128)(2,1)S(1)} custom-call(s32[2]{0:T(128)S(1)} %pad_add_fusion.1.place, s32[8,1536]{1,0:T(8,128)S(1)} %get-tuple-element.17.refs_4_.packed, bf16[208,1536]{1,0:T(8,128)(2,1)S(1)} %get-tuple-element.22.y, s32[16,128]{1,0:T(8,128)S(1)} %get-tuple-element.23.tables), custom_call_target="tpu_custom_call" | custom-call | flops 163577856 | bytes 1000000 | tf_op jit(solution)/shard_map/own/pallas_call | solution.py:514
  27.0 0.0 collective-permute-done.3.refs_1_
  27.1 1.5 %collective-permute-done.4.refs_2_ = s16[2,112,128]{2,1,0:T(8,128)(2,1)S(1)} collective-permute-done((s16[2,112,128]{2,1,0:T(8,128)(2,1)S(1)}, s16[2,112,128]{2,1,0:T(8,128)(2,1)S(1)}, u32[]{:S(2)}, u32[]{:S(2)}) %collective-permute-start.4) | collective-permute-done | bytes 57376 | tf_op jit(solution)/shard_map/ppermute | solution.py:508
  28.6 2.1 %collective-permute-done.5.refs_3_ = s16[2,112,128]{2,1,0:T(8,128)(2,1)S(1)} collective-permute-done((s16[2,112,128]{2,1,0:T(8,128)(2,1)S(1)}, s16[2,112,128]{2,1,0:T(8,128)(2,1)S(1)}, u32[]{:S(2)}, u32[]{:S(2)}) %collective-permute-start.5) | collective-permute-done | bytes 57376 | tf_op jit(solution)/shard_map/ppermute | solution.py:508
  30.7 0.1 quad.1.refs_0_
  30.8 2.4 %collective-permute-start.8 = (s16[2,112,128]{2,1,0:T(8,128)(2,1)S(1)}, s16[2,112,128]{2,1,0:T(8,128)(2,1)S(1)}, u32[]{:S(2)}, u32[]{:S(2)}) collective-permute-start(s16[2,112,128]{2,1,0:T(8,128)(2,1)S(1)} %quad.1.refs_0_), channel_id=1, source_target_pairs={{0,24},{1,25},{2,26},{3,27},{4,28},{5,29},{6,30},{7,31},{8,16},{9,... | collective-permute-start | bytes 172040 | tf_op jit(solution)/shard_map/ppermute | solution.py:508
  33.2 0.6 %collective-permute-start.7 = (s16[2,112,128]{2,1,0:T(8,128)(2,1)S(1)}, s16[2,112,128]{2,1,0:T(8,128)(2,1)S(1)}, u32[]{:S(2)}, u32[]{:S(2)}) collective-permute-start(s16[2,112,128]{2,1,0:T(8,128)(2,1)S(1)} %quad.1.refs_0_), channel_id=1, source_target_pairs={{0,8},{1,9},{2,10},{3,11},{4,12},{5,13},{6,14},{7,15},{8,0},{9,1},... | collective-permute-start | bytes 172040 | tf_op jit(solution)/shard_map/ppermute | solution.py:508
  33.8 1.5 %collective-permute-start.6 = (s16[2,112,128]{2,1,0:T(8,128)(2,1)S(1)}, s16[2,112,128]{2,1,0:T(8,128)(2,1)S(1)}, u32[]{:S(2)}, u32[]{:S(2)}) collective-permute-start(s16[2,112,128]{2,1,0:T(8,128)(2,1)S(1)} %quad.1.refs_0_), channel_id=1, source_target_pairs={{0,16},{1,17},{2,18},{3,19},{4,20},{5,21},{6,22},{7,23},{8,24},{9,... | collective-permute-start | bytes 172040 | tf_op jit(solution)/shard_map/ppermute | solution.py:508
  35.3 1.9 %collective-permute-done.8.refs_3_ = s16[2,112,128]{2,1,0:T(8,128)(2,1)S(1)} collective-permute-done((s16[2,112,128]{2,1,0:T(8,128)(2,1)S(1)}, s16[2,112,128]{2,1,0:T(8,128)(2,1)S(1)}, u32[]{:S(2)}, u32[]{:S(2)}) %collective-permute-start.8) | collective-permute-done | bytes 57376 | tf_op jit(solution)/shard_map/ppermute | solution.py:508
  37.1 0.5 %collective-permute-done.7.refs_2_ = s16[2,112,128]{2,1,0:T(8,128)(2,1)S(1)} collective-permute-done((s16[2,112,128]{2,1,0:T(8,128)(2,1)S(1)}, s16[2,112,128]{2,1,0:T(8,128)(2,1)S(1)}, u32[]{:S(2)}, u32[]{:S(2)}) %collective-permute-start.7) | collective-permute-done | bytes 57376 | tf_op jit(solution)/shard_map/ppermute | solution.py:508
  37.7 1.2 %collective-permute-done.6.refs_1_ = s16[2,112,128]{2,1,0:T(8,128)(2,1)S(1)} collective-permute-done((s16[2,112,128]{2,1,0:T(8,128)(2,1)S(1)}, s16[2,112,128]{2,1,0:T(8,128)(2,1)S(1)}, u32[]{:S(2)}, u32[]{:S(2)}) %collective-permute-start.6) | collective-permute-done | bytes 57376 | tf_op jit(solution)/shard_map/ppermute | solution.py:508
  38.9 0.7 %total.1 = s16[4,104,128]{2,1,0:T(8,128)(2,1)S(1)} custom-call(s32[2]{0:T(128)S(1)} %pad_add_fusion.1.place, s16[2,112,128]{2,1,0:T(8,128)(2,1)S(1)} %quad.1.refs_0_, s16[2,112,128]{2,1,0:T(8,128)(2,1)S(1)} %collective-permute-done.6.refs_1_, s16[2,112,128]{2,1,0:T(8,128)(2,1)S(1)} %collective-permute-done.7.refs_2_, ...), custom_call_target="tpu_custom_call" | custom-call | tf_op jit(solution)/shard_map/total/pallas_call | solution.py:541
  39.6 1.3 %collective-permute-start.11 = (s16[4,104,128]{2,1,0:T(8,128)(2,1)S(1)}, s16[4,104,128]{2,1,0:T(8,128)(2,1)S(1)}, u32[]{:S(2)}, u32[]{:S(2)}) collective-permute-start(s16[4,104,128]{2,1,0:T(8,128)(2,1)S(1)} %total.1), channel_id=1, source_target_pairs={{0,6},{1,7},{2,4},{3,5},{4,2},{5,3},{6,0},{7,1},{8,14},{9,15},{10,... | collective-permute-start | bytes 319496 | tf_op jit(solution)/shard_map/ppermute | solution.py:508
  40.9 1.3 %collective-permute-start.10 = (s16[4,104,128]{2,1,0:T(8,128)(2,1)S(1)}, s16[4,104,128]{2,1,0:T(8,128)(2,1)S(1)}, u32[]{:S(2)}, u32[]{:S(2)}) collective-permute-start(s16[4,104,128]{2,1,0:T(8,128)(2,1)S(1)} %total.1), channel_id=1, source_target_pairs={{0,2},{1,3},{2,0},{3,1},{4,6},{5,7},{6,4},{7,5},{8,10},{9,11},{10,... | collective-permute-start | bytes 319496 | tf_op jit(solution)/shard_map/ppermute | solution.py:508
  42.2 1.0 %collective-permute-start.9 = (s16[4,104,128]{2,1,0:T(8,128)(2,1)S(1)}, s16[4,104,128]{2,1,0:T(8,128)(2,1)S(1)}, u32[]{:S(2)}, u32[]{:S(2)}) collective-permute-start(s16[4,104,128]{2,1,0:T(8,128)(2,1)S(1)} %total.1), channel_id=1, source_target_pairs={{0,4},{1,5},{2,6},{3,7},{4,0},{5,1},{6,2},{7,3},{8,12},{9,13},{10,... | collective-permute-start | bytes 319496 | tf_op jit(solution)/shard_map/ppermute | solution.py:508
  43.2 0.0 copy-done.3
  43.2 2.0 %entity.1 = f32[100,256]{1,0:T(8,128)} custom-call(s32[2]{0:T(128)S(1)} %pad_add_fusion.1.place, s32[1,2,8]{2,1,0:T(2,128)S(1)} %bitcast.10, s32[8,1536]{1,0:T(8,128)S(1)} %get-tuple-element.17.refs_4_.packed, bf16[208,1536]{1,0:T(8,128)(2,1)S(1)} %get-tuple-element.27.x, s16[2,112,128]{2,1,0:T(8,128)(2,1)S(1)} %quad.1.refs_0_, ...), custom_call_target="tpu_custom_call" | custom-call | flops 1000000000 | bytes 1000000 | tf_op jit(solution)/shard_map/entity/pallas_call | solution.py:555
  45.2 0.2 collective-permute-done.11
  45.4 0.9 %collective-permute-done.10 = s16[4,104,128]{2,1,0:T(8,128)(2,1)S(1)} collective-permute-done((s16[4,104,128]{2,1,0:T(8,128)(2,1)S(1)}, s16[4,104,128]{2,1,0:T(8,128)(2,1)S(1)}, u32[]{:S(2)}, u32[]{:S(2)}) %collective-permute-start.10) | collective-permute-done | bytes 106528 | tf_op jit(solution)/shard_map/ppermute | solution.py:508
  46.3 0.6 %collective-permute-done.9 = s16[4,104,128]{2,1,0:T(8,128)(2,1)S(1)} collective-permute-done((s16[4,104,128]{2,1,0:T(8,128)(2,1)S(1)}, s16[4,104,128]{2,1,0:T(8,128)(2,1)S(1)}, u32[]{:S(2)}, u32[]{:S(2)}) %collective-permute-start.9) | collective-permute-done | bytes 106528 | tf_op jit(solution)/shard_map/ppermute | solution.py:508
  46.9 0.1 collective-permute-start.12
  47.0 1.5 %spread_own.1.partial = f32[400,1000]{1,0:T(8,128)} custom-call(s32[2]{0:T(128)S(1)} %pad_add_fusion.1.place, s16[16,104,128]{2,1,0:T(8,128)(2,1)S(1)} %pad_add_fusion.mine), custom_call_target="tpu_custom_call" | custom-call | flops 1000000 | bytes 1600000 | tf_op jit(solution)/shard_map/spread_own/pallas_call | solution.py:572
  48.6 0.2 collective-permute-done.12.other
  48.8 1.6 %spread_rest.1 = f32[400,1000]{1,0:T(8,128)} custom-call(s32[2]{0:T(128)S(1)} %pad_add_fusion.1.place, s16[16,104,128]{2,1,0:T(8,128)(2,1)S(1)} %pad_add_fusion.mine, s16[16,104,128]{2,1,0:T(8,128)(2,1)S(1)} %collective-permute-done.12.other, f32[400,1000]{1,0:T(8,128)} %spread_own.1.partial), custom_call_target="tpu_custom_call", output_to_operand_aliasing={{}: (3, {})} | custom-call | tf_op jit(solution)/shard_map/spread_rest/pallas_call | solution.py:582
  (1 shorter events, 0.0 us)
Async XLA Ops:
  3.1 9.1 %collective-permute-start.2 = (s32[8,512]{1,0:T(8,128)}, s32[8,512]{1,0:T(8,128)S(1)}, u32[]{:S(2)}, u32[]{:S(2)}) collective-permute-start(s32[8,512]{1,0:T(8,128)} %get-tuple-element.16.refs_0_), channel_id=1, source_target_pairs={{0,3},{1,0},{2,1},{3,2},{4,7},{5,4},{6,5},{7,6},{8,11},{9,8},{10,9... | collective-permute-start | bytes 49160 | tf_op jit(solution)/shard_map/ppermute | solution.py:454
  5.5 6.7 %collective-permute-start.1 = (s32[8,512]{1,0:T(8,128)}, s32[8,512]{1,0:T(8,128)S(1)}, u32[]{:S(2)}, u32[]{:S(2)}) collective-permute-start(s32[8,512]{1,0:T(8,128)} %get-tuple-element.16.refs_0_), channel_id=1, source_target_pairs={{0,2},{1,3},{2,0},{3,1},{4,6},{5,7},{6,4},{7,5},{8,10},{9,11},{10,... | collective-permute-start | bytes 49160 | tf_op jit(solution)/shard_map/ppermute | solution.py:454
  6.2 6.1 %collective-permute-start = (s32[8,512]{1,0:T(8,128)}, s32[8,512]{1,0:T(8,128)S(1)}, u32[]{:S(2)}, u32[]{:S(2)}) collective-permute-start(s32[8,512]{1,0:T(8,128)} %get-tuple-element.16.refs_0_), channel_id=1, source_target_pairs={{0,1},{1,2},{2,3},{3,0},{4,5},{5,6},{6,7},{7,4},{8,9},{9,10},{10,1... | collective-permute-start | bytes 49160 | tf_op jit(solution)/shard_map/ppermute | solution.py:454
  6.3 13.0 %all-to-all-start = ((f32[8,2,400]{2,1,0:T(2,128)}), f32[8,2,400]{2,1,0:T(2,128)S(1)}, u32[]{:S(2)}, u32[]{:S(2)}) async-start(f32[8,2,400]{2,1,0:T(2,128)} %get-tuple-element.21), calls=%async_computation | async-start | bytes 65536 | tf_op jit(solution)/shard_map/all_to_all | solution.py:455
  12.3 0.9 %copy-start = (bf16[256,400]{0,1:T(8,128)(2,1)S(1)}, bf16[256,400]{0,1:T(8,128)(2,1)}, u32[]{:S(2)}) copy-start(bf16[256,400]{0,1:T(8,128)(2,1)} %param.8) | copy-start | bytes 614404
  13.2 0.7 %copy-start.1 = (s32[8,512]{1,0:T(8,128)S(1)}, s32[8,512]{1,0:T(8,128)}, u32[]{:S(2)}) copy-start(s32[8,512]{1,0:T(8,128)} %get-tuple-element.16.refs_0_) | copy-start | bytes 49156
  13.9 1.4 %copy-start.4 = (f32[1000,400]{0,1:T(8,128)S(1)}, f32[1000,400]{0,1:T(8,128)}, u32[]{:S(2)}) copy-start(f32[1000,400]{0,1:T(8,128)} %param.9) | copy-start | bytes 4800004
  15.3 4.0 %copy-start.2 = (s32[8,512]{1,0:T(8,128)S(1)}, s32[8,512]{1,0:T(8,128)}, u32[]{:S(2)}) copy-start(s32[8,512]{1,0:T(8,128)} %get-tuple-element.16.refs_0_) | copy-start | bytes 49156
  19.3 23.9 %copy-start.3 = (s32[1,8,2]{1,2,0:T(2,128)S(1)}, s32[1,8,2]{1,2,0:T(2,128)}, u32[]{:S(2)}) copy-start(s32[1,8,2]{1,2,0:T(2,128)} %param.10) | copy-start | bytes 196
  22.1 5.0 %collective-permute-start.3 = (s16[2,112,128]{2,1,0:T(8,128)(2,1)S(1)}, s16[2,112,128]{2,1,0:T(8,128)(2,1)S(1)}, u32[]{:S(2)}, u32[]{:S(2)}) collective-permute-start(s16[2,112,128]{2,1,0:T(8,128)(2,1)S(1)} %get-tuple-element.24), channel_id=1, source_target_pairs={{0,4},{1,5},{2,6},{3,7},{4,0},{5,1},{6,2},{7,3},{8,12},{9,13},{10,... | collective-permute-start | bytes 172040 | tf_op jit(solution)/shard_map/ppermute | solution.py:508
  24.2 4.4 %collective-permute-start.4 = (s16[2,112,128]{2,1,0:T(8,128)(2,1)S(1)}, s16[2,112,128]{2,1,0:T(8,128)(2,1)S(1)}, u32[]{:S(2)}, u32[]{:S(2)}) collective-permute-start(s16[2,112,128]{2,1,0:T(8,128)(2,1)S(1)} %get-tuple-element.25), channel_id=1, source_target_pairs={{0,8},{1,9},{2,10},{3,11},{4,12},{5,13},{6,14},{7,15},{8,0},{9,1},... | collective-permute-start | bytes 172040 | tf_op jit(solution)/shard_map/ppermute | solution.py:508
  25.6 5.1 %collective-permute-start.5 = (s16[2,112,128]{2,1,0:T(8,128)(2,1)S(1)}, s16[2,112,128]{2,1,0:T(8,128)(2,1)S(1)}, u32[]{:S(2)}, u32[]{:S(2)}) collective-permute-start(s16[2,112,128]{2,1,0:T(8,128)(2,1)S(1)} %get-tuple-element.26), channel_id=1, source_target_pairs={{0,12},{1,13},{2,14},{3,15},{4,8},{5,9},{6,10},{7,11},{8,4},{9,5},... | collective-permute-start | bytes 172040 | tf_op jit(solution)/shard_map/ppermute | solution.py:508
  30.8 6.3 %collective-permute-start.8 = (s16[2,112,128]{2,1,0:T(8,128)(2,1)S(1)}, s16[2,112,128]{2,1,0:T(8,128)(2,1)S(1)}, u32[]{:S(2)}, u32[]{:S(2)}) collective-permute-start(s16[2,112,128]{2,1,0:T(8,128)(2,1)S(1)} %quad.1.refs_0_), channel_id=1, source_target_pairs={{0,24},{1,25},{2,26},{3,27},{4,28},{5,29},{6,30},{7,31},{8,16},{9,... | collective-permute-start | bytes 172040 | tf_op jit(solution)/shard_map/ppermute | solution.py:508
  33.2 4.4 %collective-permute-start.7 = (s16[2,112,128]{2,1,0:T(8,128)(2,1)S(1)}, s16[2,112,128]{2,1,0:T(8,128)(2,1)S(1)}, u32[]{:S(2)}, u32[]{:S(2)}) collective-permute-start(s16[2,112,128]{2,1,0:T(8,128)(2,1)S(1)} %quad.1.refs_0_), channel_id=1, source_target_pairs={{0,8},{1,9},{2,10},{3,11},{4,12},{5,13},{6,14},{7,15},{8,0},{9,1},... | collective-permute-start | bytes 172040 | tf_op jit(solution)/shard_map/ppermute | solution.py:508
  33.8 5.1 %collective-permute-start.6 = (s16[2,112,128]{2,1,0:T(8,128)(2,1)S(1)}, s16[2,112,128]{2,1,0:T(8,128)(2,1)S(1)}, u32[]{:S(2)}, u32[]{:S(2)}) collective-permute-start(s16[2,112,128]{2,1,0:T(8,128)(2,1)S(1)} %quad.1.refs_0_), channel_id=1, source_target_pairs={{0,16},{1,17},{2,18},{3,19},{4,20},{5,21},{6,22},{7,23},{8,24},{9,... | collective-permute-start | bytes 172040 | tf_op jit(solution)/shard_map/ppermute | solution.py:508
  39.6 5.8 %collective-permute-start.11 = (s16[4,104,128]{2,1,0:T(8,128)(2,1)S(1)}, s16[4,104,128]{2,1,0:T(8,128)(2,1)S(1)}, u32[]{:S(2)}, u32[]{:S(2)}) collective-permute-start(s16[4,104,128]{2,1,0:T(8,128)(2,1)S(1)} %total.1), channel_id=1, source_target_pairs={{0,6},{1,7},{2,4},{3,5},{4,2},{5,3},{6,0},{7,1},{8,14},{9,15},{10,... | collective-permute-start | bytes 319496 | tf_op jit(solution)/shard_map/ppermute | solution.py:508
  40.9 5.4 %collective-permute-start.10 = (s16[4,104,128]{2,1,0:T(8,128)(2,1)S(1)}, s16[4,104,128]{2,1,0:T(8,128)(2,1)S(1)}, u32[]{:S(2)}, u32[]{:S(2)}) collective-permute-start(s16[4,104,128]{2,1,0:T(8,128)(2,1)S(1)} %total.1), channel_id=1, source_target_pairs={{0,2},{1,3},{2,0},{3,1},{4,6},{5,7},{6,4},{7,5},{8,10},{9,11},{10,... | collective-permute-start | bytes 319496 | tf_op jit(solution)/shard_map/ppermute | solution.py:508
  42.2 4.7 %collective-permute-start.9 = (s16[4,104,128]{2,1,0:T(8,128)(2,1)S(1)}, s16[4,104,128]{2,1,0:T(8,128)(2,1)S(1)}, u32[]{:S(2)}, u32[]{:S(2)}) collective-permute-start(s16[4,104,128]{2,1,0:T(8,128)(2,1)S(1)} %total.1), channel_id=1, source_target_pairs={{0,4},{1,5},{2,6},{3,7},{4,0},{5,1},{6,2},{7,3},{8,12},{9,13},{10,... | collective-permute-start | bytes 319496 | tf_op jit(solution)/shard_map/ppermute | solution.py:508
  46.9 1.8 %collective-permute-start.12 = (s16[16,104,128]{2,1,0:T(8,128)(2,1)S(1)}, s16[16,104,128]{2,1,0:T(8,128)(2,1)S(1)}, u32[]{:S(2)}, u32[]{:S(2)}) collective-permute-start(s16[16,104,128]{2,1,0:T(8,128)(2,1)S(1)} %pad_add_fusion.mine), channel_id=1, source_target_pairs={{0,1},{1,0},{2,3},{3,2},{4,5},{5,4},{6,7},{7,6},{8,9},{9,8},{10,11... | collective-permute-start | bytes 1277960 | tf_op jit(solution)/shard_map/ppermute | solution.py:568

commit v15 on v14

--- a/solution.py
+++ b/solution.py
@@ -86,6 +86,10 @@
     for n, start in enumerate(starts[1:], 1):
         out = jnp.where(rep == n, x[start : start + window], out)
     return out
+
+
+def my_place():
+    return lax.axis_index("dom"), lax.axis_index("rep")
 
 
 def prep_kernel(serve, count, ent, src, rel, dst, neg, out_idx, out_rows, *refs):
@@ -138,7 +142,8 @@
     out_idx[...] = packed[:, :span]
 
 
-def gather_kernel(cfg, place, *refs):
+def gather_kernel(cfg, *refs):
+    place = my_place()
     replicas, groups, nrel, pad_rel, narrow, window, step = cfg
     idx_refs, refs = refs[:replicas], refs[replicas:]
     ent, relation, out_idx, out_query, out_lhs, out_rel, rel_parts = refs
@@ -162,13 +167,14 @@
         out_rel[:, span] = window_rows(rel_rows, place[1], starts, window)
 
 
-def main_kernel(cfg, place, *refs):
+def main_kernel(cfg, *refs):
+    place = my_place()
     (direct, workers, replicas, cap, groups, width, pad_rel, block, narrow, window, offsets) = cfg
     idx_refs, refs = refs[:replicas], refs[replicas:]
     (packed, query_v, lhs_v, rel_v, received), refs = refs[:5], refs[5:]
     out_x, tables, refs = refs[0], refs[1], refs[2:]
     out_y, refs = (refs[0], refs[1:]) if direct else (None, refs)
-    outs, (table_f, table_t, wide_t, mixed) = refs[:-4], refs[-4:]
+    outs, (table_f, table_t, query_s, wide_t, mixed) = refs[:-5], refs[-5:]
     edges = idx_refs[0].shape[1]
     dim, total = query_v.shape
     slots = workers * cap
@@ -186,6 +192,7 @@
 
     query = query_v[...]
     scores = dot(table, query)
+    query_s[...] = query.astype(F32)
     lanes = packed[...]
     cols = jnp.transpose(lanes)
     times = jnp.zeros((slots, total), F32)
@@ -212,9 +219,7 @@
     stack_t = jnp.concatenate(split3(jnp.transpose(grads)), axis=1)
 
     dquery = dot(own_t, stack)
-    acc_tab = window_rows(
-        dot(query, stack_t), rep, [narrow * r // 8 * 8 for r in range(replicas)], window
-    )
+    acc_tab = dot(query_s[pl.ds(base, window), :].astype(BF16), stack_t)
     wide_t[...] = jnp.zeros(wide_t.shape, F32)
     wide_t[:narrow] = shifted_rows(
         acc_tab[:, :slots] + acc_tab[:, slots : 2 * slots] + acc_tab[:, 2 * slots :],
@@ -256,7 +261,8 @@
         ref[...] = mixed[...].astype(jnp.int16)
 
 
-def own_kernel(block, narrow, cap, offsets, place, packed, y, tables, out, mixed):
+def own_kernel(block, narrow, cap, offsets, packed, y, tables, out, mixed):
+    place = my_place()
     cols = jnp.transpose(packed[...])
     targets = [(out.at[top], top * 4 + place[0] % 4) for top in range(2)]
     write_blocks(y[...], cols, targets, tables, mixed, place[1], block, narrow, cap, offsets)
@@ -285,7 +291,8 @@
         out[top] = mixed[...].astype(jnp.int16)
 
 
-def sum_kernel(scale, narrow, cap, block, terms, place, *refs):
+def sum_kernel(scale, narrow, cap, block, terms, *refs):
+    place = my_place()
     parts, out, mixed = refs[:-2], refs[-2], refs[-1]
     depth = parts[0].shape[0]
     lowered = mixed.shape[0] - narrow if terms == 2 else 0
@@ -310,7 +317,8 @@
             out[first // terms * depth + top] = mixed[...].astype(jnp.int16)
 
 
-def entity_kernel(direct, narrow, offsets, place, serve, packed, x, *refs):
+def entity_kernel(direct, narrow, offsets, serve, packed, x, *refs):
+    place = my_place()
     recv, out, terms, onehot = refs[:-3], refs[-3], refs[-2], refs[-1]
     cap, workers = serve.shape[1], serve.shape[2]
     rows = out.shape[1]
@@ -369,12 +377,14 @@
     return moves
 
 
-def spread_own_kernel(sizes, place, mine, out, bands, sems):
+def spread_own_kernel(sizes, mine, out, bands, sems):
+    place = my_place()
     for move in spread_core(mine, lax.rem(place[1], 2), place, sizes, bands, out, sems):
         move.wait()
 
 
-def spread_rest_kernel(sizes, place, mine, other, partial, out, bands, shared, sems):
+def spread_rest_kernel(sizes, mine, other, partial, out, bands, shared, sems):
+    place = my_place()
     workers, narrow, block, nrel = sizes
     core = lax.rem(place[1], 2)
     length = narrow // 8 * 8
@@ -424,7 +434,6 @@
     height = up(narrow + SOURCES * cap + 1, 16)
     ent_t, rel_t = entities.T, relation.T
     serve_t = jnp.transpose(serve_ids, (0, 2, 1))
-    place = jnp.stack([lax.axis_index("dom"), lax.axis_index("rep")]).astype(jnp.int32)
 
     idx, served = pl.pallas_call(
         prep_kernel,
@@ -465,7 +474,7 @@
             jax.ShapeDtypeStruct((window, total), F32),
             jax.ShapeDtypeStruct((window, total), F32),
         ),
-        in_specs=[SMEM] + [VMEM] * (replicas + 2),
+        in_specs=[VMEM] * (replicas + 2),
         out_specs=[VMEM] * 4,
         scratch_shapes=[
             pltpu.VMEM((2 * dim, pad_rel), BF16),
@@ -473,7 +482,7 @@
         compiler_params=params(),
         cost_estimate=cost(2 * total * dim * (2 * pad_rel + rows), 8 * total * dim),
         name="gather",
-    )(place, *held, ent_t, rel_t)
+    )(*held, ent_t, rel_t)
 
     cfg = (
         direct, workers, replicas, cap, groups, width, pad_rel, block, narrow, window,
@@ -488,17 +497,18 @@
     x_parts, tables, *sent = pl.pallas_call(
         functools.partial(main_kernel, cfg),
         out_shape=[pieces, jax.ShapeDtypeStruct((slots, lanes), jnp.int32)] + sizes,
-        in_specs=[SMEM] + [VMEM] * (replicas + 5),
+        in_specs=[VMEM] * (replicas + 5),
         out_specs=[VMEM] * (2 + len(sizes)),
         scratch_shapes=[
             pltpu.VMEM((slots, dim), F32),
             pltpu.VMEM((dim, slots), F32),
+            pltpu.VMEM((dim, total), F32),
             pltpu.VMEM((lanes, slots), F32),
         ]
         + mixed,
         compiler_params=params(),
         name="edges",
-    )(place, *held, packed, query, lhs_rows, rel_rows, received)
+    )(*held, packed, query, lhs_rows, rel_rows, received)
 
     def swap(array, dom_bits=0, rep_bits=0):
         pairs = []
@@ -514,13 +524,13 @@
         kept = pl.pallas_call(
             functools.partial(own_kernel, block, narrow, cap, offsets),
             out_shape=stack,
-            in_specs=[SMEM] + [VMEM] * 3,
+            in_specs=[VMEM] * 3,
             out_specs=VMEM,
             scratch_shapes=mixed,
             compiler_params=params(),
             cost_estimate=cost(4 * window * total * 2 * block, 10**6),
             name="own",
-        )(place, packed, y_parts, tables)
+        )(packed, y_parts, tables)
         summed = pl.pallas_call(
             functools.partial(quad_kernel, narrow, cap),
             out_shape=stack,
@@ -541,12 +551,12 @@
     chunk = pl.pallas_call(
         functools.partial(sum_kernel, scale, narrow, cap, block, 2 if direct else workers),
         out_shape=jax.ShapeDtypeStruct((stack, up(narrow + 1, 8), lanes), jnp.int16),
-        in_specs=[SMEM] + [VMEM] * len(parts),
+        in_specs=[VMEM] * len(parts),
         out_specs=VMEM,
         scratch_shapes=[pltpu.VMEM((up(narrow + 1, 8), lanes), jnp.int32)],
         compiler_params=params(),
         name="total",
-    )(place, *parts)
+    )(*parts)
 
     if direct:
         base = jnp.concatenate(
@@ -555,13 +565,13 @@
     entity_grad = pl.pallas_call(
         functools.partial(entity_kernel, direct, narrow, offsets),
         out_shape=jax.ShapeDtypeStruct((narrow, rows), F32),
-        in_specs=[SMEM] * 2 + [VMEM] * (2 + len(recv)),
+        in_specs=[SMEM] + [VMEM] * (2 + len(recv)),
         out_specs=VMEM,
         scratch_shapes=[pltpu.VMEM((slots, lanes), F32), pltpu.VMEM((slots, rows), F32)],
         compiler_params=params(),
         cost_estimate=cost(10**9, 10**6),
         name="entity",
-    )(place, serve_t, packed, x_parts, *recv)
+    )(serve_t, packed, x_parts, *recv)
 
     if direct:
         base, entity_grad = lax.optimization_barrier((base, entity_grad))
@@ -572,23 +582,23 @@
         own_half = pl.pallas_call(
             functools.partial(spread_own_kernel, sizes),
             out_shape=result,
-            in_specs=[SMEM, VMEM],
+            in_specs=[VMEM],
             out_specs=HBM,
             scratch_shapes=[bands, pltpu.SemaphoreType.DMA((2,))],
             compiler_params=params(),
             cost_estimate=cost(10**6, 4 * dim * nrel),
             name="spread_own",
-        )(place, base)
+        )(base)
         relation_t = pl.pallas_call(
             functools.partial(spread_rest_kernel, sizes),
             out_shape=result,
-            in_specs=[SMEM, VMEM, VMEM, HBM],
+            in_specs=[VMEM, VMEM, HBM],
             out_specs=HBM,
             scratch_shapes=[bands, pltpu.VMEM((16, nrel), F32), pltpu.SemaphoreType.DMA((4,))],
-            input_output_aliases={3: 0},
+            input_output_aliases={2: 0},
             compiler_params=params(),
             name="spread_rest",
-        )(place, base, swapped, own_half)
+        )(base, swapped, own_half)
     else:
         whole = lax.all_gather(chunk[0, :, :block], ("dom", "rep"), axis=0)
         whole = decode(whole[:, :narrow], whole[:, narrow : narrow + 1])

time: 50.7 us -> 48.3 us (0.953)
  Pallas kernels: 15.8 us -> 12.4 us
  waiting for transfers between devices: 9.2 us -> 10.3 us
    pallas_call x1, Pallas kernels: 2.74 us -> 2.06 us  [shards(): pl.pallas_call(functools.partial(main_kernel, cfg), out_shape=[pieces, ja...]
    pallas_call x1, Pallas kernels: 1.55 us -> 0.99 us  [shards(): pl.pallas_call(functools.partial(spread_rest_kernel, sizes), out_shape=re...]
    pallas_call x1, Pallas kernels: 3.94 us -> 3.39 us  [shards(): pl.pallas_call(functools.partial(gather_kernel, (replicas, groups, nrel,...]
    pallas_call x1, Pallas kernels: 1.34 us -> 0.8 us  [shards(): pl.pallas_call(functools.partial(own_kernel, block, narrow, cap, offsets)...]
    pallas_call x1, Pallas kernels: 0.7 us -> 0.17 us  [shards(): pl.pallas_call(functools.partial(sum_kernel, scale, narrow, cap, block, 2...]
    ppermute x1, waiting for transfers between devices: 0.22 us -> 0.76 us  [shards(): swapped = lax.ppermute(base, 'rep', [(i, i ^ 1) for i in range(replicas)])]
    pallas_call x1, Pallas kernels: 1.52 us -> 0.99 us  [shards(): pl.pallas_call(functools.partial(spread_own_kernel, sizes), out_shape=res...]
  transfers between devices with their start and end apart: 14 -> 14, of which waited for: 9 -> 11; matrix products, arithmetic and copies ran while one was open for 0% -> 0% of each run, Pallas kernels for 18% -> 15%
where the time goes in v15:
time: 48.3 us; the launch traced here: 47.9 us
  starting transfers between devices  20.7 us (43%)
  Pallas kernels  12.4 us (26%)
  waiting for transfers between devices  10.3 us (21%)
  local copies, waits for them, and re-layouts  3.08 us (6%)
  between operations  1.38 us (3%)
    ppermute x9, starting transfers between devices, swap(): return lax.ppermute(array, ('dom', 'rep'), pairs)  11.6 us
    ppermute x9, waiting for transfers between devices, swap(): return lax.ppermute(array, ('dom', 'rep'), pairs)  9.27 us
    all_to_all x1, starting transfers between devices, shards(): received = lax.all_to_all(served, 'dom', 0, 0, tiled=True)  5.84 us
    pallas_call x1, Pallas kernels, shards(): pl.pallas_call(functools.partial(gather_kernel, (replicas, groups, nrel,...  3.39 us
    ppermute x3, starting transfers between devices, shards(): held.append(lax.ppermute(idx, 'rep', turned(replicas, hop)))  3.23 us
    unnamed x10, local copies, waits for them, and re-layouts  3.08 us
    pallas_call x1, Pallas kernels, shards(): pl.pallas_call(functools.partial(entity_kernel, direct, narrow, offsets),...  2.07 us
    pallas_call x1, Pallas kernels, shards(): pl.pallas_call(functools.partial(main_kernel, cfg), out_shape=[pieces, ja...  2.06 us
  transfers between devices with their start and end apart: 14, of which 11 were waited for; matrix products, arithmetic and copies ran while one was open for 0% of the time, Pallas kernels for 15%

profile of v15, /device:TPU:0, one launch (start us, length us, event | category | flops | bytes accessed | tf_op | source)
XLA Modules:
  0.0 47.9 jit_solution(11940590259462802189)
XLA Ops:
  1.3 1.8 %prep.1 = (s32[8,512]{1,0:T(8,128)}, f32[8,2,400]{2,1,0:T(2,128)}) custom-call(s32[1,2,8]{2,1,0:T(2,128)} %bitcast.7, s32[1,1]{1,0:T(1,128)S(6)} %copy.12.count, bf16[400,256]{1,0:T(8,128)(2,1)} %bitcast.5, s32[1,1,512]{2,1,0:T(1,128)} %src.1, s32[1,1,512]{2,1,0:T(1,128)} %rel.1, s32[1,1,512]{2,1,0:T(1,128)} %dst.1, s32[1,1,2,384]{3,2,1,0:T(2,128)} %neg.1), custom_call_target="tpu_custom_call" | custom-call | tf_op jit(solution)/shard_map/prep/pallas_call | solution.py:438
  3.1 2.4 %collective-permute-start.2 = (s32[8,512]{1,0:T(8,128)}, s32[8,512]{1,0:T(8,128)S(1)}, u32[]{:S(2)}, u32[]{:S(2)}) collective-permute-start(s32[8,512]{1,0:T(8,128)} %get-tuple-element.16.refs_0_), channel_id=1, source_target_pairs={{0,3},{1,0},{2,1},{3,2},{4,7},{5,4},{6,5},{7,6},{8,11},{9,8},{10,9... | collective-permute-start | bytes 49160 | tf_op jit(solution)/shard_map/ppermute | solution.py:463
  5.5 0.6 %collective-permute-start.1 = (s32[8,512]{1,0:T(8,128)}, s32[8,512]{1,0:T(8,128)S(1)}, u32[]{:S(2)}, u32[]{:S(2)}) collective-permute-start(s32[8,512]{1,0:T(8,128)} %get-tuple-element.16.refs_0_), channel_id=1, source_target_pairs={{0,2},{1,3},{2,0},{3,1},{4,6},{5,7},{6,4},{7,5},{8,10},{9,11},{10,... | collective-permute-start | bytes 49160 | tf_op jit(solution)/shard_map/ppermute | solution.py:463
  6.2 0.2 collective-permute-start
  6.3 5.8 %all-to-all-start = ((f32[8,2,400]{2,1,0:T(2,128)}), f32[8,2,400]{2,1,0:T(2,128)S(1)}, u32[]{:S(2)}, u32[]{:S(2)}) async-start(f32[8,2,400]{2,1,0:T(2,128)} %get-tuple-element.21), calls=%async_computation | async-start | bytes 65536 | tf_op jit(solution)/shard_map/all_to_all | solution.py:464
  12.2 0.0 collective-permute-done.2.refs_3_
  12.2 0.0 collective-permute-done.1.refs_2_
  12.2 0.0 collective-permute-done.refs_1_
  12.2 0.0 copy-start
  12.2 0.9 %copy-done = bf16[256,400]{0,1:T(8,128)(2,1)S(1)} copy-done((bf16[256,400]{0,1:T(8,128)(2,1)S(1)}, bf16[256,400]{0,1:T(8,128)(2,1)}, u32[]{:S(2)}) %copy-start) | copy-done | bytes 204824
  13.1 0.0 copy-start.1
  13.1 0.7 %copy-done.1 = s32[8,512]{1,0:T(8,128)S(1)} copy-done((s32[8,512]{1,0:T(8,128)S(1)}, s32[8,512]{1,0:T(8,128)}, u32[]{:S(2)}) %copy-start.1) | copy-done | bytes 16408
  13.8 0.0 copy-start.4
  13.8 1.4 %copy-done.4 = f32[1000,400]{0,1:T(8,128)S(1)} copy-done((f32[1000,400]{0,1:T(8,128)S(1)}, f32[1000,400]{0,1:T(8,128)}, u32[]{:S(2)}) %copy-start.4) | copy-done | bytes 1600024
  15.3 0.0 copy-start.2
  15.3 3.4 %gather.1 = (s32[8,1536]{1,0:T(8,128)S(1)}, bf16[400,1536]{1,0:T(8,128)(2,1)S(1)}, f32[104,1536]{1,0:T(8,128)S(1)}, f32[104,1536]{1,0:T(8,128)S(1)}) custom-call(s32[8,512]{1,0:T(8,128)S(1)} %copy-done.1, s32[8,512]{1,0:T(8,128)S(1)} %collective-permute-done.refs_1_, s32[8,512]{1,0:T(8,128)S(1)} %collective-permute-done.1.refs_2_, ...), custom_call_target="tpu_custom_call" | custom-call | flops 2831155200 | bytes 4915200 | tf_op jit(solution)/shard_map/gather/pallas_call | solution.py:467
  18.7 0.3 all-to-all-done.refs_8_
  19.0 0.0 copy-done.2
  19.0 0.0 copy-start.3
  19.0 2.1 %edges.1 = (bf16[208,1536]{1,0:T(8,128)(2,1)S(1)}, s32[16,128]{1,0:T(8,128)S(1)}, bf16[208,1536]{1,0:T(8,128)(2,1)S(1)}, s16[2,112,128]{2,1,0:T(8,128)(2,1)S(1)}...) custom-call(s32[8,512]{1,0:T(8,128)S(1)} %copy-done.2, s32[8,512]{1,0:T(8,128)S(1)} %collective-permute-done.refs_1_, ...), custom_call_target="tpu_custom_call" | custom-call | tf_op jit(solution)/shard_map/edges/pallas_call | solution.py:497
  21.1 1.8 %collective-permute-start.3 = (s16[2,112,128]{2,1,0:T(8,128)(2,1)S(1)}, s16[2,112,128]{2,1,0:T(8,128)(2,1)S(1)}, u32[]{:S(2)}, u32[]{:S(2)}) collective-permute-start(s16[2,112,128]{2,1,0:T(8,128)(2,1)S(1)} %get-tuple-element.24), channel_id=1, source_target_pairs={{0,4},{1,5},{2,6},{3,7},{4,0},{5,1},{6,2},{7,3},{8,12},{9,13},{10,... | collective-permute-start | bytes 172040 | tf_op jit(solution)/shard_map/ppermute | solution.py:518
  22.9 1.5 %collective-permute-start.4 = (s16[2,112,128]{2,1,0:T(8,128)(2,1)S(1)}, s16[2,112,128]{2,1,0:T(8,128)(2,1)S(1)}, u32[]{:S(2)}, u32[]{:S(2)}) collective-permute-start(s16[2,112,128]{2,1,0:T(8,128)(2,1)S(1)} %get-tuple-element.25), channel_id=1, source_target_pairs={{0,8},{1,9},{2,10},{3,11},{4,12},{5,13},{6,14},{7,15},{8,0},{9,1},... | collective-permute-start | bytes 172040 | tf_op jit(solution)/shard_map/ppermute | solution.py:518
  24.3 0.3 collective-permute-start.5
  24.6 0.8 %own.1.refs_0_ = s16[2,112,128]{2,1,0:T(8,128)(2,1)S(1)} custom-call(s32[8,1536]{1,0:T(8,128)S(1)} %get-tuple-element.17.refs_4_.packed, bf16[208,1536]{1,0:T(8,128)(2,1)S(1)} %get-tuple-element.22.y, s32[16,128]{1,0:T(8,128)S(1)} %get-tuple-element.23.tables), custom_call_target="tpu_custom_call" | custom-call | flops 163577856 | bytes 1000000 | tf_op jit(solution)/shard_map/own/pallas_call | solution.py:524
  25.4 0.3 collective-permute-done.3.refs_1_
  25.7 1.5 %collective-permute-done.4.refs_2_ = s16[2,112,128]{2,1,0:T(8,128)(2,1)S(1)} collective-permute-done((s16[2,112,128]{2,1,0:T(8,128)(2,1)S(1)}, s16[2,112,128]{2,1,0:T(8,128)(2,1)S(1)}, u32[]{:S(2)}, u32[]{:S(2)}) %collective-permute-start.4) | collective-permute-done | bytes 57376 | tf_op jit(solution)/shard_map/ppermute | solution.py:518
  27.3 2.1 %collective-permute-done.5.refs_3_ = s16[2,112,128]{2,1,0:T(8,128)(2,1)S(1)} collective-permute-done((s16[2,112,128]{2,1,0:T(8,128)(2,1)S(1)}, s16[2,112,128]{2,1,0:T(8,128)(2,1)S(1)}, u32[]{:S(2)}, u32[]{:S(2)}) %collective-permute-start.5) | collective-permute-done | bytes 57376 | tf_op jit(solution)/shard_map/ppermute | solution.py:518
  29.4 0.1 quad.1.refs_0_
  29.5 2.4 %collective-permute-start.8 = (s16[2,112,128]{2,1,0:T(8,128)(2,1)S(1)}, s16[2,112,128]{2,1,0:T(8,128)(2,1)S(1)}, u32[]{:S(2)}, u32[]{:S(2)}) collective-permute-start(s16[2,112,128]{2,1,0:T(8,128)(2,1)S(1)} %quad.1.refs_0_), channel_id=1, source_target_pairs={{0,24},{1,25},{2,26},{3,27},{4,28},{5,29},{6,30},{7,31},{8,16},{9,... | collective-permute-start | bytes 172040 | tf_op jit(solution)/shard_map/ppermute | solution.py:518
  32.0 0.6 %collective-permute-start.7 = (s16[2,112,128]{2,1,0:T(8,128)(2,1)S(1)}, s16[2,112,128]{2,1,0:T(8,128)(2,1)S(1)}, u32[]{:S(2)}, u32[]{:S(2)}) collective-permute-start(s16[2,112,128]{2,1,0:T(8,128)(2,1)S(1)} %quad.1.refs_0_), channel_id=1, source_target_pairs={{0,8},{1,9},{2,10},{3,11},{4,12},{5,13},{6,14},{7,15},{8,0},{9,1},... | collective-permute-start | bytes 172040 | tf_op jit(solution)/shard_map/ppermute | solution.py:518
  32.5 1.5 %collective-permute-start.6 = (s16[2,112,128]{2,1,0:T(8,128)(2,1)S(1)}, s16[2,112,128]{2,1,0:T(8,128)(2,1)S(1)}, u32[]{:S(2)}, u32[]{:S(2)}) collective-permute-start(s16[2,112,128]{2,1,0:T(8,128)(2,1)S(1)} %quad.1.refs_0_), channel_id=1, source_target_pairs={{0,16},{1,17},{2,18},{3,19},{4,20},{5,21},{6,22},{7,23},{8,24},{9,... | collective-permute-start | bytes 172040 | tf_op jit(solution)/shard_map/ppermute | solution.py:518
  34.0 1.9 %collective-permute-done.8.refs_3_ = s16[2,112,128]{2,1,0:T(8,128)(2,1)S(1)} collective-permute-done((s16[2,112,128]{2,1,0:T(8,128)(2,1)S(1)}, s16[2,112,128]{2,1,0:T(8,128)(2,1)S(1)}, u32[]{:S(2)}, u32[]{:S(2)}) %collective-permute-start.8) | collective-permute-done | bytes 57376 | tf_op jit(solution)/shard_map/ppermute | solution.py:518
  35.8 0.5 %collective-permute-done.7.refs_2_ = s16[2,112,128]{2,1,0:T(8,128)(2,1)S(1)} collective-permute-done((s16[2,112,128]{2,1,0:T(8,128)(2,1)S(1)}, s16[2,112,128]{2,1,0:T(8,128)(2,1)S(1)}, u32[]{:S(2)}, u32[]{:S(2)}) %collective-permute-start.7) | collective-permute-done | bytes 57376 | tf_op jit(solution)/shard_map/ppermute | solution.py:518
  36.4 1.2 %collective-permute-done.6.refs_1_ = s16[2,112,128]{2,1,0:T(8,128)(2,1)S(1)} collective-permute-done((s16[2,112,128]{2,1,0:T(8,128)(2,1)S(1)}, s16[2,112,128]{2,1,0:T(8,128)(2,1)S(1)}, u32[]{:S(2)}, u32[]{:S(2)}) %collective-permute-start.6) | collective-permute-done | bytes 57376 | tf_op jit(solution)/shard_map/ppermute | solution.py:518
  37.6 0.2 total.1
  37.8 1.3 %collective-permute-start.11 = (s16[4,104,128]{2,1,0:T(8,128)(2,1)S(1)}, s16[4,104,128]{2,1,0:T(8,128)(2,1)S(1)}, u32[]{:S(2)}, u32[]{:S(2)}) collective-permute-start(s16[4,104,128]{2,1,0:T(8,128)(2,1)S(1)} %total.1), channel_id=1, source_target_pairs={{0,6},{1,7},{2,4},{3,5},{4,2},{5,3},{6,0},{7,1},{8,14},{9,15},{10,... | collective-permute-start | bytes 319496 | tf_op jit(solution)/shard_map/ppermute | solution.py:518
  39.1 1.3 %collective-permute-start.10 = (s16[4,104,128]{2,1,0:T(8,128)(2,1)S(1)}, s16[4,104,128]{2,1,0:T(8,128)(2,1)S(1)}, u32[]{:S(2)}, u32[]{:S(2)}) collective-permute-start(s16[4,104,128]{2,1,0:T(8,128)(2,1)S(1)} %total.1), channel_id=1, source_target_pairs={{0,2},{1,3},{2,0},{3,1},{4,6},{5,7},{6,4},{7,5},{8,10},{9,11},{10,... | collective-permute-start | bytes 319496 | tf_op jit(solution)/shard_map/ppermute | solution.py:518
  40.4 1.0 %collective-permute-start.9 = (s16[4,104,128]{2,1,0:T(8,128)(2,1)S(1)}, s16[4,104,128]{2,1,0:T(8,128)(2,1)S(1)}, u32[]{:S(2)}, u32[]{:S(2)}) collective-permute-start(s16[4,104,128]{2,1,0:T(8,128)(2,1)S(1)} %total.1), channel_id=1, source_target_pairs={{0,4},{1,5},{2,6},{3,7},{4,0},{5,1},{6,2},{7,3},{8,12},{9,13},{10,... | collective-permute-start | bytes 319496 | tf_op jit(solution)/shard_map/ppermute | solution.py:518
  41.3 0.0 copy-done.3
  41.3 2.1 %entity.1 = f32[100,256]{1,0:T(8,128)} custom-call(s32[1,2,8]{2,1,0:T(2,128)S(1)} %bitcast.8, s32[8,1536]{1,0:T(8,128)S(1)} %get-tuple-element.17.refs_4_.packed, bf16[208,1536]{1,0:T(8,128)(2,1)S(1)} %get-tuple-element.27.x, s16[2,112,128]{2,1,0:T(8,128)(2,1)S(1)} %quad.1.refs_0_, s16[2,112,128]{2,1,0:T(8,128)(2,1)S(1)} %collective-permute-done.6.refs_1_), custom_call_target="tpu_custom_call" | custom-call | flops 1000000000 | bytes 1000000 | tf_op jit(solution)/shard_map/entity/pallas_call | solution.py:565
  43.4 0.2 collective-permute-done.11
  43.5 0.9 %collective-permute-done.10 = s16[4,104,128]{2,1,0:T(8,128)(2,1)S(1)} collective-permute-done((s16[4,104,128]{2,1,0:T(8,128)(2,1)S(1)}, s16[4,104,128]{2,1,0:T(8,128)(2,1)S(1)}, u32[]{:S(2)}, u32[]{:S(2)}) %collective-permute-start.10) | collective-permute-done | bytes 106528 | tf_op jit(solution)/shard_map/ppermute | solution.py:518
  44.4 0.6 %collective-permute-done.9 = s16[4,104,128]{2,1,0:T(8,128)(2,1)S(1)} collective-permute-done((s16[4,104,128]{2,1,0:T(8,128)(2,1)S(1)}, s16[4,104,128]{2,1,0:T(8,128)(2,1)S(1)}, u32[]{:S(2)}, u32[]{:S(2)}) %collective-permute-start.9) | collective-permute-done | bytes 106528 | tf_op jit(solution)/shard_map/ppermute | solution.py:518
  45.1 0.1 collective-permute-start.12
  45.2 1.0 %spread_own.1.partial = f32[400,1000]{1,0:T(8,128)} custom-call(s16[16,104,128]{2,1,0:T(8,128)(2,1)S(1)} %pad_add_fusion.mine), custom_call_target="tpu_custom_call" | custom-call | flops 1000000 | bytes 1600000 | tf_op jit(solution)/shard_map/spread_own/pallas_call | solution.py:582
  46.2 0.8 %collective-permute-done.12.other = s16[16,104,128]{2,1,0:T(8,128)(2,1)S(1)} collective-permute-done((s16[16,104,128]{2,1,0:T(8,128)(2,1)S(1)}, s16[16,104,128]{2,1,0:T(8,128)(2,1)S(1)}, u32[]{:S(2)}, u32[]{:S(2)}) %collective-permute-start.12) | collective-permute-done | bytes 426016 | tf_op jit(solution)/shard_map/ppermute | solution.py:578
  46.9 1.0 %spread_rest.1 = f32[400,1000]{1,0:T(8,128)} custom-call(s16[16,104,128]{2,1,0:T(8,128)(2,1)S(1)} %pad_add_fusion.mine, s16[16,104,128]{2,1,0:T(8,128)(2,1)S(1)} %collective-permute-done.12.other, f32[400,1000]{1,0:T(8,128)} %spread_own.1.partial), custom_call_target="tpu_custom_call", output_to_operand_aliasing={{}: (2, {})} | custom-call | tf_op jit(solution)/shard_map/spread_rest/pallas_call | solution.py:592
  (1 shorter events, 0.0 us)
Async XLA Ops:
  3.1 9.1 %collective-permute-start.2 = (s32[8,512]{1,0:T(8,128)}, s32[8,512]{1,0:T(8,128)S(1)}, u32[]{:S(2)}, u32[]{:S(2)}) collective-permute-start(s32[8,512]{1,0:T(8,128)} %get-tuple-element.16.refs_0_), channel_id=1, source_target_pairs={{0,3},{1,0},{2,1},{3,2},{4,7},{5,4},{6,5},{7,6},{8,11},{9,8},{10,9... | collective-permute-start | bytes 49160 | tf_op jit(solution)/shard_map/ppermute | solution.py:463
  5.5 6.7 %collective-permute-start.1 = (s32[8,512]{1,0:T(8,128)}, s32[8,512]{1,0:T(8,128)S(1)}, u32[]{:S(2)}, u32[]{:S(2)}) collective-permute-start(s32[8,512]{1,0:T(8,128)} %get-tuple-element.16.refs_0_), channel_id=1, source_target_pairs={{0,2},{1,3},{2,0},{3,1},{4,6},{5,7},{6,4},{7,5},{8,10},{9,11},{10,... | collective-permute-start | bytes 49160 | tf_op jit(solution)/shard_map/ppermute | solution.py:463
  6.2 6.0 %collective-permute-start = (s32[8,512]{1,0:T(8,128)}, s32[8,512]{1,0:T(8,128)S(1)}, u32[]{:S(2)}, u32[]{:S(2)}) collective-permute-start(s32[8,512]{1,0:T(8,128)} %get-tuple-element.16.refs_0_), channel_id=1, source_target_pairs={{0,1},{1,2},{2,3},{3,0},{4,5},{5,6},{6,7},{7,4},{8,9},{9,10},{10,1... | collective-permute-start | bytes 49160 | tf_op jit(solution)/shard_map/ppermute | solution.py:463
  6.3 12.7 %all-to-all-start = ((f32[8,2,400]{2,1,0:T(2,128)}), f32[8,2,400]{2,1,0:T(2,128)S(1)}, u32[]{:S(2)}, u32[]{:S(2)}) async-start(f32[8,2,400]{2,1,0:T(2,128)} %get-tuple-element.21), calls=%async_computation | async-start | bytes 65536 | tf_op jit(solution)/shard_map/all_to_all | solution.py:464
  12.2 0.9 %copy-start = (bf16[256,400]{0,1:T(8,128)(2,1)S(1)}, bf16[256,400]{0,1:T(8,128)(2,1)}, u32[]{:S(2)}) copy-start(bf16[256,400]{0,1:T(8,128)(2,1)} %param.8) | copy-start | bytes 614404
  13.1 0.7 %copy-start.1 = (s32[8,512]{1,0:T(8,128)S(1)}, s32[8,512]{1,0:T(8,128)}, u32[]{:S(2)}) copy-start(s32[8,512]{1,0:T(8,128)} %get-tuple-element.16.refs_0_) | copy-start | bytes 49156
  13.8 1.4 %copy-start.4 = (f32[1000,400]{0,1:T(8,128)S(1)}, f32[1000,400]{0,1:T(8,128)}, u32[]{:S(2)}) copy-start(f32[1000,400]{0,1:T(8,128)} %param.9) | copy-start | bytes 4800004
  15.3 3.7 %copy-start.2 = (s32[8,512]{1,0:T(8,128)S(1)}, s32[8,512]{1,0:T(8,128)}, u32[]{:S(2)}) copy-start(s32[8,512]{1,0:T(8,128)} %get-tuple-element.16.refs_0_) | copy-start | bytes 49156
  19.0 22.3 %copy-start.3 = (s32[1,8,2]{1,2,0:T(2,128)S(1)}, s32[1,8,2]{1,2,0:T(2,128)}, u32[]{:S(2)}) copy-start(s32[1,8,2]{1,2,0:T(2,128)} %param.10) | copy-start | bytes 196
  21.1 4.7 %collective-permute-start.3 = (s16[2,112,128]{2,1,0:T(8,128)(2,1)S(1)}, s16[2,112,128]{2,1,0:T(8,128)(2,1)S(1)}, u32[]{:S(2)}, u32[]{:S(2)}) collective-permute-start(s16[2,112,128]{2,1,0:T(8,128)(2,1)S(1)} %get-tuple-element.24), channel_id=1, source_target_pairs={{0,4},{1,5},{2,6},{3,7},{4,0},{5,1},{6,2},{7,3},{8,12},{9,13},{10,... | collective-permute-start | bytes 172040 | tf_op jit(solution)/shard_map/ppermute | solution.py:518
  22.9 4.4 %collective-permute-start.4 = (s16[2,112,128]{2,1,0:T(8,128)(2,1)S(1)}, s16[2,112,128]{2,1,0:T(8,128)(2,1)S(1)}, u32[]{:S(2)}, u32[]{:S(2)}) collective-permute-start(s16[2,112,128]{2,1,0:T(8,128)(2,1)S(1)} %get-tuple-element.25), channel_id=1, source_target_pairs={{0,8},{1,9},{2,10},{3,11},{4,12},{5,13},{6,14},{7,15},{8,0},{9,1},... | collective-permute-start | bytes 172040 | tf_op jit(solution)/shard_map/ppermute | solution.py:518
  24.3 5.1 %collective-permute-start.5 = (s16[2,112,128]{2,1,0:T(8,128)(2,1)S(1)}, s16[2,112,128]{2,1,0:T(8,128)(2,1)S(1)}, u32[]{:S(2)}, u32[]{:S(2)}) collective-permute-start(s16[2,112,128]{2,1,0:T(8,128)(2,1)S(1)} %get-tuple-element.26), channel_id=1, source_target_pairs={{0,12},{1,13},{2,14},{3,15},{4,8},{5,9},{6,10},{7,11},{8,4},{9,5},... | collective-permute-start | bytes 172040 | tf_op jit(solution)/shard_map/ppermute | solution.py:518
  29.5 6.3 %collective-permute-start.8 = (s16[2,112,128]{2,1,0:T(8,128)(2,1)S(1)}, s16[2,112,128]{2,1,0:T(8,128)(2,1)S(1)}, u32[]{:S(2)}, u32[]{:S(2)}) collective-permute-start(s16[2,112,128]{2,1,0:T(8,128)(2,1)S(1)} %quad.1.refs_0_), channel_id=1, source_target_pairs={{0,24},{1,25},{2,26},{3,27},{4,28},{5,29},{6,30},{7,31},{8,16},{9,... | collective-permute-start | bytes 172040 | tf_op jit(solution)/shard_map/ppermute | solution.py:518
  32.0 4.4 %collective-permute-start.7 = (s16[2,112,128]{2,1,0:T(8,128)(2,1)S(1)}, s16[2,112,128]{2,1,0:T(8,128)(2,1)S(1)}, u32[]{:S(2)}, u32[]{:S(2)}) collective-permute-start(s16[2,112,128]{2,1,0:T(8,128)(2,1)S(1)} %quad.1.refs_0_), channel_id=1, source_target_pairs={{0,8},{1,9},{2,10},{3,11},{4,12},{5,13},{6,14},{7,15},{8,0},{9,1},... | collective-permute-start | bytes 172040 | tf_op jit(solution)/shard_map/ppermute | solution.py:518
  32.5 5.1 %collective-permute-start.6 = (s16[2,112,128]{2,1,0:T(8,128)(2,1)S(1)}, s16[2,112,128]{2,1,0:T(8,128)(2,1)S(1)}, u32[]{:S(2)}, u32[]{:S(2)}) collective-permute-start(s16[2,112,128]{2,1,0:T(8,128)(2,1)S(1)} %quad.1.refs_0_), channel_id=1, source_target_pairs={{0,16},{1,17},{2,18},{3,19},{4,20},{5,21},{6,22},{7,23},{8,24},{9,... | collective-permute-start | bytes 172040 | tf_op jit(solution)/shard_map/ppermute | solution.py:518
  37.8 5.8 %collective-permute-start.11 = (s16[4,104,128]{2,1,0:T(8,128)(2,1)S(1)}, s16[4,104,128]{2,1,0:T(8,128)(2,1)S(1)}, u32[]{:S(2)}, u32[]{:S(2)}) collective-permute-start(s16[4,104,128]{2,1,0:T(8,128)(2,1)S(1)} %total.1), channel_id=1, source_target_pairs={{0,6},{1,7},{2,4},{3,5},{4,2},{5,3},{6,0},{7,1},{8,14},{9,15},{10,... | collective-permute-start | bytes 319496 | tf_op jit(solution)/shard_map/ppermute | solution.py:518
  39.1 5.4 %collective-permute-start.10 = (s16[4,104,128]{2,1,0:T(8,128)(2,1)S(1)}, s16[4,104,128]{2,1,0:T(8,128)(2,1)S(1)}, u32[]{:S(2)}, u32[]{:S(2)}) collective-permute-start(s16[4,104,128]{2,1,0:T(8,128)(2,1)S(1)} %total.1), channel_id=1, source_target_pairs={{0,2},{1,3},{2,0},{3,1},{4,6},{5,7},{6,4},{7,5},{8,10},{9,11},{10,... | collective-permute-start | bytes 319496 | tf_op jit(solution)/shard_map/ppermute | solution.py:518
  40.4 4.7 %collective-permute-start.9 = (s16[4,104,128]{2,1,0:T(8,128)(2,1)S(1)}, s16[4,104,128]{2,1,0:T(8,128)(2,1)S(1)}, u32[]{:S(2)}, u32[]{:S(2)}) collective-permute-start(s16[4,104,128]{2,1,0:T(8,128)(2,1)S(1)} %total.1), channel_id=1, source_target_pairs={{0,4},{1,5},{2,6},{3,7},{4,0},{5,1},{6,2},{7,3},{8,12},{9,13},{10,... | collective-permute-start | bytes 319496 | tf_op jit(solution)/shard_map/ppermute | solution.py:518
  45.1 1.8 %collective-permute-start.12 = (s16[16,104,128]{2,1,0:T(8,128)(2,1)S(1)}, s16[16,104,128]{2,1,0:T(8,128)(2,1)S(1)}, u32[]{:S(2)}, u32[]{:S(2)}) collective-permute-start(s16[16,104,128]{2,1,0:T(8,128)(2,1)S(1)} %pad_add_fusion.mine), channel_id=1, source_target_pairs={{0,1},{1,0},{2,3},{3,2},{4,5},{5,4},{6,7},{7,6},{8,9},{9,8},{10,11... | collective-permute-start | bytes 1277960 | tf_op jit(solution)/shard_map/ppermute | solution.py:578

commit v16 on v15

--- a/solution.py
+++ b/solution.py
@@ -540,8 +540,9 @@
             compiler_params=params(),
             name="quad",
         )(kept, *[got[n] for n in range(1, SOURCES)])
+        near = swap(summed, 2)
         recv = [summed, swap(summed, 4)]
-        parts = recv + [swap(summed, 2), swap(summed, 6)]
+        parts = recv + [near, swap(summed, 6)]
         stack = 4
     else:
         recv = [lax.all_to_all(sent[0], "dom", 0, 0, tiled=True)]

time: 48.3 us -> 48.3 us (level)
  no operation moved by 1% of the time
where the time goes in v16:
time: 48.3 us; the launch traced here: 47.9 us
  starting transfers between devices  20.7 us (43%)
  Pallas kernels  12.4 us (26%)
  waiting for transfers between devices  10.3 us (21%)
  local copies, waits for them, and re-layouts  3.08 us (6%)
  between operations  1.38 us (3%)
    ppermute x9, starting transfers between devices, swap(): return lax.ppermute(array, ('dom', 'rep'), pairs)  11.6 us
    ppermute x9, waiting for transfers between devices, swap(): return lax.ppermute(array, ('dom', 'rep'), pairs)  9.27 us
    all_to_all x1, starting transfers between devices, shards(): received = lax.all_to_all(served, 'dom', 0, 0, tiled=True)  5.84 us
    pallas_call x1, Pallas kernels, shards(): pl.pallas_call(functools.partial(gather_kernel, (replicas, groups, nrel,...  3.39 us
    ppermute x3, starting transfers between devices, shards(): held.append(lax.ppermute(idx, 'rep', turned(replicas, hop)))  3.23 us
    unnamed x10, local copies, waits for them, and re-layouts  3.08 us
    pallas_call x1, Pallas kernels, shards(): pl.pallas_call(functools.partial(entity_kernel, direct, narrow, offsets),...  2.07 us
    pallas_call x1, Pallas kernels, shards(): pl.pallas_call(functools.partial(main_kernel, cfg), out_shape=[pieces, ja...  2.06 us
  transfers between devices with their start and end apart: 14, of which 11 were waited for; matrix products, arithmetic and copies ran while one was open for 0% of the time, Pallas kernels for 15%

profile of v16, /device:TPU:0, one launch (start us, length us, event | category | flops | bytes accessed | tf_op | source)
XLA Modules:
  0.0 47.9 jit_solution(11940590259462802189)
XLA Ops:
  1.3 1.8 %prep.1 = (s32[8,512]{1,0:T(8,128)}, f32[8,2,400]{2,1,0:T(2,128)}) custom-call(s32[1,2,8]{2,1,0:T(2,128)} %bitcast.7, s32[1,1]{1,0:T(1,128)S(6)} %copy.12.count, bf16[400,256]{1,0:T(8,128)(2,1)} %bitcast.5, s32[1,1,512]{2,1,0:T(1,128)} %src.1, s32[1,1,512]{2,1,0:T(1,128)} %rel.1, s32[1,1,512]{2,1,0:T(1,128)} %dst.1, s32[1,1,2,384]{3,2,1,0:T(2,128)} %neg.1), custom_call_target="tpu_custom_call" | custom-call | tf_op jit(solution)/shard_map/prep/pallas_call | solution.py:438
  3.1 2.4 %collective-permute-start.2 = (s32[8,512]{1,0:T(8,128)}, s32[8,512]{1,0:T(8,128)S(1)}, u32[]{:S(2)}, u32[]{:S(2)}) collective-permute-start(s32[8,512]{1,0:T(8,128)} %get-tuple-element.16.refs_0_), channel_id=1, source_target_pairs={{0,3},{1,0},{2,1},{3,2},{4,7},{5,4},{6,5},{7,6},{8,11},{9,8},{10,9... | collective-permute-start | bytes 49160 | tf_op jit(solution)/shard_map/ppermute | solution.py:463
  5.5 0.6 %collective-permute-start.1 = (s32[8,512]{1,0:T(8,128)}, s32[8,512]{1,0:T(8,128)S(1)}, u32[]{:S(2)}, u32[]{:S(2)}) collective-permute-start(s32[8,512]{1,0:T(8,128)} %get-tuple-element.16.refs_0_), channel_id=1, source_target_pairs={{0,2},{1,3},{2,0},{3,1},{4,6},{5,7},{6,4},{7,5},{8,10},{9,11},{10,... | collective-permute-start | bytes 49160 | tf_op jit(solution)/shard_map/ppermute | solution.py:463
  6.2 0.2 collective-permute-start
  6.3 5.8 %all-to-all-start = ((f32[8,2,400]{2,1,0:T(2,128)}), f32[8,2,400]{2,1,0:T(2,128)S(1)}, u32[]{:S(2)}, u32[]{:S(2)}) async-start(f32[8,2,400]{2,1,0:T(2,128)} %get-tuple-element.21), calls=%async_computation | async-start | bytes 65536 | tf_op jit(solution)/shard_map/all_to_all | solution.py:464
  12.2 0.0 collective-permute-done.2.refs_3_
  12.2 0.0 collective-permute-done.1.refs_2_
  12.2 0.0 collective-permute-done.refs_1_
  12.2 0.0 copy-start
  12.2 0.9 %copy-done = bf16[256,400]{0,1:T(8,128)(2,1)S(1)} copy-done((bf16[256,400]{0,1:T(8,128)(2,1)S(1)}, bf16[256,400]{0,1:T(8,128)(2,1)}, u32[]{:S(2)}) %copy-start) | copy-done | bytes 204824
  13.1 0.0 copy-start.1
  13.1 0.7 %copy-done.1 = s32[8,512]{1,0:T(8,128)S(1)} copy-done((s32[8,512]{1,0:T(8,128)S(1)}, s32[8,512]{1,0:T(8,128)}, u32[]{:S(2)}) %copy-start.1) | copy-done | bytes 16408
  13.8 0.0 copy-start.4
  13.8 1.4 %copy-done.4 = f32[1000,400]{0,1:T(8,128)S(1)} copy-done((f32[1000,400]{0,1:T(8,128)S(1)}, f32[1000,400]{0,1:T(8,128)}, u32[]{:S(2)}) %copy-start.4) | copy-done | bytes 1600024
  15.3 0.0 copy-start.2
  15.3 3.4 %gather.1 = (s32[8,1536]{1,0:T(8,128)S(1)}, bf16[400,1536]{1,0:T(8,128)(2,1)S(1)}, f32[104,1536]{1,0:T(8,128)S(1)}, f32[104,1536]{1,0:T(8,128)S(1)}) custom-call(s32[8,512]{1,0:T(8,128)S(1)} %copy-done.1, s32[8,512]{1,0:T(8,128)S(1)} %collective-permute-done.refs_1_, s32[8,512]{1,0:T(8,128)S(1)} %collective-permute-done.1.refs_2_, ...), custom_call_target="tpu_custom_call" | custom-call | flops 2831155200 | bytes 4915200 | tf_op jit(solution)/shard_map/gather/pallas_call | solution.py:467
  18.7 0.3 all-to-all-done.refs_8_
  19.0 0.0 copy-done.2
  19.0 0.0 copy-start.3
  19.0 2.1 %edges.1 = (bf16[208,1536]{1,0:T(8,128)(2,1)S(1)}, s32[16,128]{1,0:T(8,128)S(1)}, bf16[208,1536]{1,0:T(8,128)(2,1)S(1)}, s16[2,112,128]{2,1,0:T(8,128)(2,1)S(1)}...) custom-call(s32[8,512]{1,0:T(8,128)S(1)} %copy-done.2, s32[8,512]{1,0:T(8,128)S(1)} %collective-permute-done.refs_1_, ...), custom_call_target="tpu_custom_call" | custom-call | tf_op jit(solution)/shard_map/edges/pallas_call | solution.py:497
  21.1 1.8 %collective-permute-start.3 = (s16[2,112,128]{2,1,0:T(8,128)(2,1)S(1)}, s16[2,112,128]{2,1,0:T(8,128)(2,1)S(1)}, u32[]{:S(2)}, u32[]{:S(2)}) collective-permute-start(s16[2,112,128]{2,1,0:T(8,128)(2,1)S(1)} %get-tuple-element.24), channel_id=1, source_target_pairs={{0,4},{1,5},{2,6},{3,7},{4,0},{5,1},{6,2},{7,3},{8,12},{9,13},{10,... | collective-permute-start | bytes 172040 | tf_op jit(solution)/shard_map/ppermute | solution.py:518
  22.9 1.5 %collective-permute-start.4 = (s16[2,112,128]{2,1,0:T(8,128)(2,1)S(1)}, s16[2,112,128]{2,1,0:T(8,128)(2,1)S(1)}, u32[]{:S(2)}, u32[]{:S(2)}) collective-permute-start(s16[2,112,128]{2,1,0:T(8,128)(2,1)S(1)} %get-tuple-element.25), channel_id=1, source_target_pairs={{0,8},{1,9},{2,10},{3,11},{4,12},{5,13},{6,14},{7,15},{8,0},{9,1},... | collective-permute-start | bytes 172040 | tf_op jit(solution)/shard_map/ppermute | solution.py:518
  24.3 0.3 collective-permute-start.5
  24.6 0.8 %own.1.refs_0_ = s16[2,112,128]{2,1,0:T(8,128)(2,1)S(1)} custom-call(s32[8,1536]{1,0:T(8,128)S(1)} %get-tuple-element.17.refs_4_.packed, bf16[208,1536]{1,0:T(8,128)(2,1)S(1)} %get-tuple-element.22.y, s32[16,128]{1,0:T(8,128)S(1)} %get-tuple-element.23.tables), custom_call_target="tpu_custom_call" | custom-call | flops 163577856 | bytes 1000000 | tf_op jit(solution)/shard_map/own/pallas_call | solution.py:524
  25.4 0.3 collective-permute-done.3.refs_1_
  25.7 1.5 %collective-permute-done.4.refs_2_ = s16[2,112,128]{2,1,0:T(8,128)(2,1)S(1)} collective-permute-done((s16[2,112,128]{2,1,0:T(8,128)(2,1)S(1)}, s16[2,112,128]{2,1,0:T(8,128)(2,1)S(1)}, u32[]{:S(2)}, u32[]{:S(2)}) %collective-permute-start.4) | collective-permute-done | bytes 57376 | tf_op jit(solution)/shard_map/ppermute | solution.py:518
  27.3 2.1 %collective-permute-done.5.refs_3_ = s16[2,112,128]{2,1,0:T(8,128)(2,1)S(1)} collective-permute-done((s16[2,112,128]{2,1,0:T(8,128)(2,1)S(1)}, s16[2,112,128]{2,1,0:T(8,128)(2,1)S(1)}, u32[]{:S(2)}, u32[]{:S(2)}) %collective-permute-start.5) | collective-permute-done | bytes 57376 | tf_op jit(solution)/shard_map/ppermute | solution.py:518
  29.4 0.1 quad.1.refs_0_
  29.5 2.4 %collective-permute-start.8 = (s16[2,112,128]{2,1,0:T(8,128)(2,1)S(1)}, s16[2,112,128]{2,1,0:T(8,128)(2,1)S(1)}, u32[]{:S(2)}, u32[]{:S(2)}) collective-permute-start(s16[2,112,128]{2,1,0:T(8,128)(2,1)S(1)} %quad.1.refs_0_), channel_id=1, source_target_pairs={{0,24},{1,25},{2,26},{3,27},{4,28},{5,29},{6,30},{7,31},{8,16},{9,... | collective-permute-start | bytes 172040 | tf_op jit(solution)/shard_map/ppermute | solution.py:518
  32.0 0.6 %collective-permute-start.7 = (s16[2,112,128]{2,1,0:T(8,128)(2,1)S(1)}, s16[2,112,128]{2,1,0:T(8,128)(2,1)S(1)}, u32[]{:S(2)}, u32[]{:S(2)}) collective-permute-start(s16[2,112,128]{2,1,0:T(8,128)(2,1)S(1)} %quad.1.refs_0_), channel_id=1, source_target_pairs={{0,8},{1,9},{2,10},{3,11},{4,12},{5,13},{6,14},{7,15},{8,0},{9,1},... | collective-permute-start | bytes 172040 | tf_op jit(solution)/shard_map/ppermute | solution.py:518
  32.5 1.5 %collective-permute-start.6 = (s16[2,112,128]{2,1,0:T(8,128)(2,1)S(1)}, s16[2,112,128]{2,1,0:T(8,128)(2,1)S(1)}, u32[]{:S(2)}, u32[]{:S(2)}) collective-permute-start(s16[2,112,128]{2,1,0:T(8,128)(2,1)S(1)} %quad.1.refs_0_), channel_id=1, source_target_pairs={{0,16},{1,17},{2,18},{3,19},{4,20},{5,21},{6,22},{7,23},{8,24},{9,... | collective-permute-start | bytes 172040 | tf_op jit(solution)/shard_map/ppermute | solution.py:518
  34.0 1.9 %collective-permute-done.8.refs_3_ = s16[2,112,128]{2,1,0:T(8,128)(2,1)S(1)} collective-permute-done((s16[2,112,128]{2,1,0:T(8,128)(2,1)S(1)}, s16[2,112,128]{2,1,0:T(8,128)(2,1)S(1)}, u32[]{:S(2)}, u32[]{:S(2)}) %collective-permute-start.8) | collective-permute-done | bytes 57376 | tf_op jit(solution)/shard_map/ppermute | solution.py:518
  35.8 0.5 %collective-permute-done.7.refs_2_ = s16[2,112,128]{2,1,0:T(8,128)(2,1)S(1)} collective-permute-done((s16[2,112,128]{2,1,0:T(8,128)(2,1)S(1)}, s16[2,112,128]{2,1,0:T(8,128)(2,1)S(1)}, u32[]{:S(2)}, u32[]{:S(2)}) %collective-permute-start.7) | collective-permute-done | bytes 57376 | tf_op jit(solution)/shard_map/ppermute | solution.py:518
  36.4 1.2 %collective-permute-done.6.refs_1_ = s16[2,112,128]{2,1,0:T(8,128)(2,1)S(1)} collective-permute-done((s16[2,112,128]{2,1,0:T(8,128)(2,1)S(1)}, s16[2,112,128]{2,1,0:T(8,128)(2,1)S(1)}, u32[]{:S(2)}, u32[]{:S(2)}) %collective-permute-start.6) | collective-permute-done | bytes 57376 | tf_op jit(solution)/shard_map/ppermute | solution.py:518
  37.6 0.2 total.1
  37.8 1.3 %collective-permute-start.11 = (s16[4,104,128]{2,1,0:T(8,128)(2,1)S(1)}, s16[4,104,128]{2,1,0:T(8,128)(2,1)S(1)}, u32[]{:S(2)}, u32[]{:S(2)}) collective-permute-start(s16[4,104,128]{2,1,0:T(8,128)(2,1)S(1)} %total.1), channel_id=1, source_target_pairs={{0,6},{1,7},{2,4},{3,5},{4,2},{5,3},{6,0},{7,1},{8,14},{9,15},{10,... | collective-permute-start | bytes 319496 | tf_op jit(solution)/shard_map/ppermute | solution.py:518
  39.1 1.3 %collective-permute-start.10 = (s16[4,104,128]{2,1,0:T(8,128)(2,1)S(1)}, s16[4,104,128]{2,1,0:T(8,128)(2,1)S(1)}, u32[]{:S(2)}, u32[]{:S(2)}) collective-permute-start(s16[4,104,128]{2,1,0:T(8,128)(2,1)S(1)} %total.1), channel_id=1, source_target_pairs={{0,2},{1,3},{2,0},{3,1},{4,6},{5,7},{6,4},{7,5},{8,10},{9,11},{10,... | collective-permute-start | bytes 319496 | tf_op jit(solution)/shard_map/ppermute | solution.py:518
  40.4 1.0 %collective-permute-start.9 = (s16[4,104,128]{2,1,0:T(8,128)(2,1)S(1)}, s16[4,104,128]{2,1,0:T(8,128)(2,1)S(1)}, u32[]{:S(2)}, u32[]{:S(2)}) collective-permute-start(s16[4,104,128]{2,1,0:T(8,128)(2,1)S(1)} %total.1), channel_id=1, source_target_pairs={{0,4},{1,5},{2,6},{3,7},{4,0},{5,1},{6,2},{7,3},{8,12},{9,13},{10,... | collective-permute-start | bytes 319496 | tf_op jit(solution)/shard_map/ppermute | solution.py:518
  41.3 0.0 copy-done.3
  41.3 2.1 %entity.1 = f32[100,256]{1,0:T(8,128)} custom-call(s32[1,2,8]{2,1,0:T(2,128)S(1)} %bitcast.8, s32[8,1536]{1,0:T(8,128)S(1)} %get-tuple-element.17.refs_4_.packed, bf16[208,1536]{1,0:T(8,128)(2,1)S(1)} %get-tuple-element.27.x, s16[2,112,128]{2,1,0:T(8,128)(2,1)S(1)} %quad.1.refs_0_, s16[2,112,128]{2,1,0:T(8,128)(2,1)S(1)} %collective-permute-done.6.refs_1_), custom_call_target="tpu_custom_call" | custom-call | flops 1000000000 | bytes 1000000 | tf_op jit(solution)/shard_map/entity/pallas_call | solution.py:566
  43.4 0.2 collective-permute-done.11
  43.5 0.9 %collective-permute-done.10 = s16[4,104,128]{2,1,0:T(8,128)(2,1)S(1)} collective-permute-done((s16[4,104,128]{2,1,0:T(8,128)(2,1)S(1)}, s16[4,104,128]{2,1,0:T(8,128)(2,1)S(1)}, u32[]{:S(2)}, u32[]{:S(2)}) %collective-permute-start.10) | collective-permute-done | bytes 106528 | tf_op jit(solution)/shard_map/ppermute | solution.py:518
  44.4 0.6 %collective-permute-done.9 = s16[4,104,128]{2,1,0:T(8,128)(2,1)S(1)} collective-permute-done((s16[4,104,128]{2,1,0:T(8,128)(2,1)S(1)}, s16[4,104,128]{2,1,0:T(8,128)(2,1)S(1)}, u32[]{:S(2)}, u32[]{:S(2)}) %collective-permute-start.9) | collective-permute-done | bytes 106528 | tf_op jit(solution)/shard_map/ppermute | solution.py:518
  45.1 0.1 collective-permute-start.12
  45.2 1.0 %spread_own.1.partial = f32[400,1000]{1,0:T(8,128)} custom-call(s16[16,104,128]{2,1,0:T(8,128)(2,1)S(1)} %pad_add_fusion.mine), custom_call_target="tpu_custom_call" | custom-call | flops 1000000 | bytes 1600000 | tf_op jit(solution)/shard_map/spread_own/pallas_call | solution.py:583
  46.2 0.8 %collective-permute-done.12.other = s16[16,104,128]{2,1,0:T(8,128)(2,1)S(1)} collective-permute-done((s16[16,104,128]{2,1,0:T(8,128)(2,1)S(1)}, s16[16,104,128]{2,1,0:T(8,128)(2,1)S(1)}, u32[]{:S(2)}, u32[]{:S(2)}) %collective-permute-start.12) | collective-permute-done | bytes 426016 | tf_op jit(solution)/shard_map/ppermute | solution.py:579
  46.9 1.0 %spread_rest.1 = f32[400,1000]{1,0:T(8,128)} custom-call(s16[16,104,128]{2,1,0:T(8,128)(2,1)S(1)} %pad_add_fusion.mine, s16[16,104,128]{2,1,0:T(8,128)(2,1)S(1)} %collective-permute-done.12.other, f32[400,1000]{1,0:T(8,128)} %spread_own.1.partial), custom_call_target="tpu_custom_call", output_to_operand_aliasing={{}: (2, {})} | custom-call | tf_op jit(solution)/shard_map/spread_rest/pallas_call | solution.py:593
  (1 shorter events, 0.0 us)
Async XLA Ops:
  3.1 9.1 %collective-permute-start.2 = (s32[8,512]{1,0:T(8,128)}, s32[8,512]{1,0:T(8,128)S(1)}, u32[]{:S(2)}, u32[]{:S(2)}) collective-permute-start(s32[8,512]{1,0:T(8,128)} %get-tuple-element.16.refs_0_), channel_id=1, source_target_pairs={{0,3},{1,0},{2,1},{3,2},{4,7},{5,4},{6,5},{7,6},{8,11},{9,8},{10,9... | collective-permute-start | bytes 49160 | tf_op jit(solution)/shard_map/ppermute | solution.py:463
  5.5 6.7 %collective-permute-start.1 = (s32[8,512]{1,0:T(8,128)}, s32[8,512]{1,0:T(8,128)S(1)}, u32[]{:S(2)}, u32[]{:S(2)}) collective-permute-start(s32[8,512]{1,0:T(8,128)} %get-tuple-element.16.refs_0_), channel_id=1, source_target_pairs={{0,2},{1,3},{2,0},{3,1},{4,6},{5,7},{6,4},{7,5},{8,10},{9,11},{10,... | collective-permute-start | bytes 49160 | tf_op jit(solution)/shard_map/ppermute | solution.py:463
  6.2 6.0 %collective-permute-start = (s32[8,512]{1,0:T(8,128)}, s32[8,512]{1,0:T(8,128)S(1)}, u32[]{:S(2)}, u32[]{:S(2)}) collective-permute-start(s32[8,512]{1,0:T(8,128)} %get-tuple-element.16.refs_0_), channel_id=1, source_target_pairs={{0,1},{1,2},{2,3},{3,0},{4,5},{5,6},{6,7},{7,4},{8,9},{9,10},{10,1... | collective-permute-start | bytes 49160 | tf_op jit(solution)/shard_map/ppermute | solution.py:463
  6.3 12.7 %all-to-all-start = ((f32[8,2,400]{2,1,0:T(2,128)}), f32[8,2,400]{2,1,0:T(2,128)S(1)}, u32[]{:S(2)}, u32[]{:S(2)}) async-start(f32[8,2,400]{2,1,0:T(2,128)} %get-tuple-element.21), calls=%async_computation | async-start | bytes 65536 | tf_op jit(solution)/shard_map/all_to_all | solution.py:464
  12.2 0.9 %copy-start = (bf16[256,400]{0,1:T(8,128)(2,1)S(1)}, bf16[256,400]{0,1:T(8,128)(2,1)}, u32[]{:S(2)}) copy-start(bf16[256,400]{0,1:T(8,128)(2,1)} %param.8) | copy-start | bytes 614404
  13.1 0.7 %copy-start.1 = (s32[8,512]{1,0:T(8,128)S(1)}, s32[8,512]{1,0:T(8,128)}, u32[]{:S(2)}) copy-start(s32[8,512]{1,0:T(8,128)} %get-tuple-element.16.refs_0_) | copy-start | bytes 49156
  13.8 1.4 %copy-start.4 = (f32[1000,400]{0,1:T(8,128)S(1)}, f32[1000,400]{0,1:T(8,128)}, u32[]{:S(2)}) copy-start(f32[1000,400]{0,1:T(8,128)} %param.9) | copy-start | bytes 4800004
  15.3 3.7 %copy-start.2 = (s32[8,512]{1,0:T(8,128)S(1)}, s32[8,512]{1,0:T(8,128)}, u32[]{:S(2)}) copy-start(s32[8,512]{1,0:T(8,128)} %get-tuple-element.16.refs_0_) | copy-start | bytes 49156
  19.0 22.3 %copy-start.3 = (s32[1,8,2]{1,2,0:T(2,128)S(1)}, s32[1,8,2]{1,2,0:T(2,128)}, u32[]{:S(2)}) copy-start(s32[1,8,2]{1,2,0:T(2,128)} %param.10) | copy-start | bytes 196
  21.1 4.7 %collective-permute-start.3 = (s16[2,112,128]{2,1,0:T(8,128)(2,1)S(1)}, s16[2,112,128]{2,1,0:T(8,128)(2,1)S(1)}, u32[]{:S(2)}, u32[]{:S(2)}) collective-permute-start(s16[2,112,128]{2,1,0:T(8,128)(2,1)S(1)} %get-tuple-element.24), channel_id=1, source_target_pairs={{0,4},{1,5},{2,6},{3,7},{4,0},{5,1},{6,2},{7,3},{8,12},{9,13},{10,... | collective-permute-start | bytes 172040 | tf_op jit(solution)/shard_map/ppermute | solution.py:518
  22.9 4.4 %collective-permute-start.4 = (s16[2,112,128]{2,1,0:T(8,128)(2,1)S(1)}, s16[2,112,128]{2,1,0:T(8,128)(2,1)S(1)}, u32[]{:S(2)}, u32[]{:S(2)}) collective-permute-start(s16[2,112,128]{2,1,0:T(8,128)(2,1)S(1)} %get-tuple-element.25), channel_id=1, source_target_pairs={{0,8},{1,9},{2,10},{3,11},{4,12},{5,13},{6,14},{7,15},{8,0},{9,1},... | collective-permute-start | bytes 172040 | tf_op jit(solution)/shard_map/ppermute | solution.py:518
  24.3 5.1 %collective-permute-start.5 = (s16[2,112,128]{2,1,0:T(8,128)(2,1)S(1)}, s16[2,112,128]{2,1,0:T(8,128)(2,1)S(1)}, u32[]{:S(2)}, u32[]{:S(2)}) collective-permute-start(s16[2,112,128]{2,1,0:T(8,128)(2,1)S(1)} %get-tuple-element.26), channel_id=1, source_target_pairs={{0,12},{1,13},{2,14},{3,15},{4,8},{5,9},{6,10},{7,11},{8,4},{9,5},... | collective-permute-start | bytes 172040 | tf_op jit(solution)/shard_map/ppermute | solution.py:518
  29.5 6.3 %collective-permute-start.8 = (s16[2,112,128]{2,1,0:T(8,128)(2,1)S(1)}, s16[2,112,128]{2,1,0:T(8,128)(2,1)S(1)}, u32[]{:S(2)}, u32[]{:S(2)}) collective-permute-start(s16[2,112,128]{2,1,0:T(8,128)(2,1)S(1)} %quad.1.refs_0_), channel_id=1, source_target_pairs={{0,24},{1,25},{2,26},{3,27},{4,28},{5,29},{6,30},{7,31},{8,16},{9,... | collective-permute-start | bytes 172040 | tf_op jit(solution)/shard_map/ppermute | solution.py:518
  32.0 4.4 %collective-permute-start.7 = (s16[2,112,128]{2,1,0:T(8,128)(2,1)S(1)}, s16[2,112,128]{2,1,0:T(8,128)(2,1)S(1)}, u32[]{:S(2)}, u32[]{:S(2)}) collective-permute-start(s16[2,112,128]{2,1,0:T(8,128)(2,1)S(1)} %quad.1.refs_0_), channel_id=1, source_target_pairs={{0,8},{1,9},{2,10},{3,11},{4,12},{5,13},{6,14},{7,15},{8,0},{9,1},... | collective-permute-start | bytes 172040 | tf_op jit(solution)/shard_map/ppermute | solution.py:518
  32.5 5.1 %collective-permute-start.6 = (s16[2,112,128]{2,1,0:T(8,128)(2,1)S(1)}, s16[2,112,128]{2,1,0:T(8,128)(2,1)S(1)}, u32[]{:S(2)}, u32[]{:S(2)}) collective-permute-start(s16[2,112,128]{2,1,0:T(8,128)(2,1)S(1)} %quad.1.refs_0_), channel_id=1, source_target_pairs={{0,16},{1,17},{2,18},{3,19},{4,20},{5,21},{6,22},{7,23},{8,24},{9,... | collective-permute-start | bytes 172040 | tf_op jit(solution)/shard_map/ppermute | solution.py:518
  37.8 5.8 %collective-permute-start.11 = (s16[4,104,128]{2,1,0:T(8,128)(2,1)S(1)}, s16[4,104,128]{2,1,0:T(8,128)(2,1)S(1)}, u32[]{:S(2)}, u32[]{:S(2)}) collective-permute-start(s16[4,104,128]{2,1,0:T(8,128)(2,1)S(1)} %total.1), channel_id=1, source_target_pairs={{0,6},{1,7},{2,4},{3,5},{4,2},{5,3},{6,0},{7,1},{8,14},{9,15},{10,... | collective-permute-start | bytes 319496 | tf_op jit(solution)/shard_map/ppermute | solution.py:518
  39.1 5.4 %collective-permute-start.10 = (s16[4,104,128]{2,1,0:T(8,128)(2,1)S(1)}, s16[4,104,128]{2,1,0:T(8,128)(2,1)S(1)}, u32[]{:S(2)}, u32[]{:S(2)}) collective-permute-start(s16[4,104,128]{2,1,0:T(8,128)(2,1)S(1)} %total.1), channel_id=1, source_target_pairs={{0,2},{1,3},{2,0},{3,1},{4,6},{5,7},{6,4},{7,5},{8,10},{9,11},{10,... | collective-permute-start | bytes 319496 | tf_op jit(solution)/shard_map/ppermute | solution.py:518
  40.4 4.7 %collective-permute-start.9 = (s16[4,104,128]{2,1,0:T(8,128)(2,1)S(1)}, s16[4,104,128]{2,1,0:T(8,128)(2,1)S(1)}, u32[]{:S(2)}, u32[]{:S(2)}) collective-permute-start(s16[4,104,128]{2,1,0:T(8,128)(2,1)S(1)} %total.1), channel_id=1, source_target_pairs={{0,4},{1,5},{2,6},{3,7},{4,0},{5,1},{6,2},{7,3},{8,12},{9,13},{10,... | collective-permute-start | bytes 319496 | tf_op jit(solution)/shard_map/ppermute | solution.py:518
  45.1 1.8 %collective-permute-start.12 = (s16[16,104,128]{2,1,0:T(8,128)(2,1)S(1)}, s16[16,104,128]{2,1,0:T(8,128)(2,1)S(1)}, u32[]{:S(2)}, u32[]{:S(2)}) collective-permute-start(s16[16,104,128]{2,1,0:T(8,128)(2,1)S(1)} %pad_add_fusion.mine), channel_id=1, source_target_pairs={{0,1},{1,0},{2,3},{3,2},{4,5},{5,4},{6,7},{7,6},{8,9},{9,8},{10,11... | collective-permute-start | bytes 1277960 | tf_op jit(solution)/shard_map/ppermute | solution.py:579

commit v17 on v15

--- a/solution.py
+++ b/solution.py
@@ -559,9 +559,8 @@
     )(*parts)
 
     if direct:
-        base = jnp.concatenate(
-            [chunk, swap(chunk, 1), swap(chunk, 0, 2), swap(chunk, 1, 2)], axis=0
-        )
+        sibling = swap(chunk, 0, 1)
+        rest = jnp.concatenate([swap(chunk, 1), swap(chunk, 0, 2), swap(chunk, 1, 2)], axis=0)
     entity_grad = pl.pallas_call(
         functools.partial(entity_kernel, direct, narrow, offsets),
         out_shape=jax.ShapeDtypeStruct((narrow, rows), F32),
@@ -574,8 +573,9 @@
     )(serve_t, packed, x_parts, *recv)
 
     if direct:
-        base, entity_grad = lax.optimization_barrier((base, entity_grad))
-        swapped = lax.ppermute(base, "rep", [(i, i ^ 1) for i in range(replicas)])
+        rest, entity_grad = lax.optimization_barrier((rest, entity_grad))
+        base = jnp.concatenate([chunk, rest], axis=0)
+        swapped = jnp.concatenate([sibling, swap(rest, 0, 1)], axis=0)
         sizes = (workers, narrow, block, nrel)
         result = jax.ShapeDtypeStruct((dim, nrel), F32)
         bands = pltpu.VMEM((narrow // 8 * 16, nrel), F32)

time: 48.3 us -> 48.3 us (level)
  starting transfers between devices: 20.7 us -> 21.2 us
  waiting for transfers between devices: 10.3 us -> 9.81 us
    ppermute x1 -> x0, waiting for transfers between devices: 0.76 us -> none  [shards(): swapped = lax.ppermute(base, 'rep', [(i, i ^ 1) for i in range(replicas)])]
    ppermute x9 -> x11, starting transfers between devices: 11.6 us -> 12.1 us  [swap(): return lax.ppermute(array, ('dom', 'rep'), pairs)]
    ppermute x9 -> x11, waiting for transfers between devices: 9.27 us -> 9.49 us  [swap(): return lax.ppermute(array, ('dom', 'rep'), pairs)]
  transfers between devices with their start and end apart: 14 -> 15, of which waited for: 11 -> 11; matrix products, arithmetic and copies ran while one was open for 0% -> 0% of each run, Pallas kernels for 15% -> 15%
where the time goes in v17:
time: 48.3 us; the launch traced here: 48 us
  starting transfers between devices  21.2 us (44%)
  Pallas kernels  12.4 us (26%)
  waiting for transfers between devices  9.81 us (20%)
  local copies, waits for them, and re-layouts  3.08 us (6%)
  between operations  1.39 us (3%)
    ppermute x11, starting transfers between devices, swap(): return lax.ppermute(array, ('dom', 'rep'), pairs)  12.1 us
    ppermute x11, waiting for transfers between devices, swap(): return lax.ppermute(array, ('dom', 'rep'), pairs)  9.49 us
    all_to_all x1, starting transfers between devices, shards(): received = lax.all_to_all(served, 'dom', 0, 0, tiled=True)  5.84 us
    pallas_call x1, Pallas kernels, shards(): pl.pallas_call(functools.partial(gather_kernel, (replicas, groups, nrel,...  3.38 us
    ppermute x3, starting transfers between devices, shards(): held.append(lax.ppermute(idx, 'rep', turned(replicas, hop)))  3.23 us
    unnamed x10, local copies, waits for them, and re-layouts  3.08 us
    pallas_call x1, Pallas kernels, shards(): pl.pallas_call(functools.partial(entity_kernel, direct, narrow, offsets),...  2.07 us
    pallas_call x1, Pallas kernels, shards(): pl.pallas_call(functools.partial(main_kernel, cfg), out_shape=[pieces, ja...  2.05 us
  transfers between devices with their start and end apart: 15, of which 11 were waited for; matrix products, arithmetic and copies ran while one was open for 0% of the time, Pallas kernels for 15%

profile of v17, /device:TPU:0, one launch (start us, length us, event | category | flops | bytes accessed | tf_op | source)
XLA Modules:
  0.0 48.0 jit_solution(15884520825728057349)
XLA Ops:
  1.3 1.8 %prep.1 = (s32[8,512]{1,0:T(8,128)}, f32[8,2,400]{2,1,0:T(2,128)}) custom-call(s32[1,2,8]{2,1,0:T(2,128)} %bitcast.7, s32[1,1]{1,0:T(1,128)S(6)} %copy.12.count, bf16[400,256]{1,0:T(8,128)(2,1)} %bitcast.5, s32[1,1,512]{2,1,0:T(1,128)} %src.1, s32[1,1,512]{2,1,0:T(1,128)} %rel.1, s32[1,1,512]{2,1,0:T(1,128)} %dst.1, s32[1,1,2,384]{3,2,1,0:T(2,128)} %neg.1), custom_call_target="tpu_custom_call" | custom-call | tf_op jit(solution)/shard_map/prep/pallas_call | solution.py:438
  3.1 2.4 %collective-permute-start.2 = (s32[8,512]{1,0:T(8,128)}, s32[8,512]{1,0:T(8,128)S(1)}, u32[]{:S(2)}, u32[]{:S(2)}) collective-permute-start(s32[8,512]{1,0:T(8,128)} %get-tuple-element.16.refs_0_), channel_id=1, source_target_pairs={{0,3},{1,0},{2,1},{3,2},{4,7},{5,4},{6,5},{7,6},{8,11},{9,8},{10,9... | collective-permute-start | bytes 49160 | tf_op jit(solution)/shard_map/ppermute | solution.py:463
  5.5 0.6 %collective-permute-start.1 = (s32[8,512]{1,0:T(8,128)}, s32[8,512]{1,0:T(8,128)S(1)}, u32[]{:S(2)}, u32[]{:S(2)}) collective-permute-start(s32[8,512]{1,0:T(8,128)} %get-tuple-element.16.refs_0_), channel_id=1, source_target_pairs={{0,2},{1,3},{2,0},{3,1},{4,6},{5,7},{6,4},{7,5},{8,10},{9,11},{10,... | collective-permute-start | bytes 49160 | tf_op jit(solution)/shard_map/ppermute | solution.py:463
  6.2 0.2 collective-permute-start
  6.3 5.8 %all-to-all-start = ((f32[8,2,400]{2,1,0:T(2,128)}), f32[8,2,400]{2,1,0:T(2,128)S(1)}, u32[]{:S(2)}, u32[]{:S(2)}) async-start(f32[8,2,400]{2,1,0:T(2,128)} %get-tuple-element.21), calls=%async_computation | async-start | bytes 65536 | tf_op jit(solution)/shard_map/all_to_all | solution.py:464
  12.2 0.0 collective-permute-done.2.refs_3_
  12.2 0.0 collective-permute-done.1.refs_2_
  12.2 0.0 collective-permute-done.refs_1_
  12.2 0.0 copy-start
  12.2 0.9 %copy-done = bf16[256,400]{0,1:T(8,128)(2,1)S(1)} copy-done((bf16[256,400]{0,1:T(8,128)(2,1)S(1)}, bf16[256,400]{0,1:T(8,128)(2,1)}, u32[]{:S(2)}) %copy-start) | copy-done | bytes 204824
  13.1 0.0 copy-start.1
  13.1 0.7 %copy-done.1 = s32[8,512]{1,0:T(8,128)S(1)} copy-done((s32[8,512]{1,0:T(8,128)S(1)}, s32[8,512]{1,0:T(8,128)}, u32[]{:S(2)}) %copy-start.1) | copy-done | bytes 16408
  13.8 0.0 copy-start.4
  13.8 1.4 %copy-done.4 = f32[1000,400]{0,1:T(8,128)S(1)} copy-done((f32[1000,400]{0,1:T(8,128)S(1)}, f32[1000,400]{0,1:T(8,128)}, u32[]{:S(2)}) %copy-start.4) | copy-done | bytes 1600024
  15.3 0.0 copy-start.2
  15.3 3.4 %gather.1 = (s32[8,1536]{1,0:T(8,128)S(1)}, bf16[400,1536]{1,0:T(8,128)(2,1)S(1)}, f32[104,1536]{1,0:T(8,128)S(1)}, f32[104,1536]{1,0:T(8,128)S(1)}) custom-call(s32[8,512]{1,0:T(8,128)S(1)} %copy-done.1, s32[8,512]{1,0:T(8,128)S(1)} %collective-permute-done.refs_1_, s32[8,512]{1,0:T(8,128)S(1)} %collective-permute-done.1.refs_2_, ...), custom_call_target="tpu_custom_call" | custom-call | flops 2831155200 | bytes 4915200 | tf_op jit(solution)/shard_map/gather/pallas_call | solution.py:467
  18.7 0.3 all-to-all-done.refs_8_
  19.0 0.0 copy-done.2
  19.0 0.0 copy-start.3
  19.0 2.0 %edges.1 = (bf16[208,1536]{1,0:T(8,128)(2,1)S(1)}, s32[16,128]{1,0:T(8,128)S(1)}, bf16[208,1536]{1,0:T(8,128)(2,1)S(1)}, s16[2,112,128]{2,1,0:T(8,128)(2,1)S(1)}...) custom-call(s32[8,512]{1,0:T(8,128)S(1)} %copy-done.2, s32[8,512]{1,0:T(8,128)S(1)} %collective-permute-done.refs_1_, ...), custom_call_target="tpu_custom_call" | custom-call | tf_op jit(solution)/shard_map/edges/pallas_call | solution.py:497
  21.0 1.8 %collective-permute-start.3 = (s16[2,112,128]{2,1,0:T(8,128)(2,1)S(1)}, s16[2,112,128]{2,1,0:T(8,128)(2,1)S(1)}, u32[]{:S(2)}, u32[]{:S(2)}) collective-permute-start(s16[2,112,128]{2,1,0:T(8,128)(2,1)S(1)} %get-tuple-element.24), channel_id=1, source_target_pairs={{0,4},{1,5},{2,6},{3,7},{4,0},{5,1},{6,2},{7,3},{8,12},{9,13},{10,... | collective-permute-start | bytes 172040 | tf_op jit(solution)/shard_map/ppermute | solution.py:518
  22.8 1.5 %collective-permute-start.4 = (s16[2,112,128]{2,1,0:T(8,128)(2,1)S(1)}, s16[2,112,128]{2,1,0:T(8,128)(2,1)S(1)}, u32[]{:S(2)}, u32[]{:S(2)}) collective-permute-start(s16[2,112,128]{2,1,0:T(8,128)(2,1)S(1)} %get-tuple-element.25), channel_id=1, source_target_pairs={{0,8},{1,9},{2,10},{3,11},{4,12},{5,13},{6,14},{7,15},{8,0},{9,1},... | collective-permute-start | bytes 172040 | tf_op jit(solution)/shard_map/ppermute | solution.py:518
  24.3 0.3 collective-permute-start.5
  24.6 0.8 %own.1.refs_0_ = s16[2,112,128]{2,1,0:T(8,128)(2,1)S(1)} custom-call(s32[8,1536]{1,0:T(8,128)S(1)} %get-tuple-element.17.refs_4_.packed, bf16[208,1536]{1,0:T(8,128)(2,1)S(1)} %get-tuple-element.22.y, s32[16,128]{1,0:T(8,128)S(1)} %get-tuple-element.23.tables), custom_call_target="tpu_custom_call" | custom-call | flops 163577856 | bytes 1000000 | tf_op jit(solution)/shard_map/own/pallas_call | solution.py:524
  25.4 0.3 collective-permute-done.3.refs_1_
  25.7 1.5 %collective-permute-done.4.refs_2_ = s16[2,112,128]{2,1,0:T(8,128)(2,1)S(1)} collective-permute-done((s16[2,112,128]{2,1,0:T(8,128)(2,1)S(1)}, s16[2,112,128]{2,1,0:T(8,128)(2,1)S(1)}, u32[]{:S(2)}, u32[]{:S(2)}) %collective-permute-start.4) | collective-permute-done | bytes 57376 | tf_op jit(solution)/shard_map/ppermute | solution.py:518
  27.2 2.1 %collective-permute-done.5.refs_3_ = s16[2,112,128]{2,1,0:T(8,128)(2,1)S(1)} collective-permute-done((s16[2,112,128]{2,1,0:T(8,128)(2,1)S(1)}, s16[2,112,128]{2,1,0:T(8,128)(2,1)S(1)}, u32[]{:S(2)}, u32[]{:S(2)}) %collective-permute-start.5) | collective-permute-done | bytes 57376 | tf_op jit(solution)/shard_map/ppermute | solution.py:518
  29.4 0.1 quad.1.refs_0_
  29.5 2.4 %collective-permute-start.8 = (s16[2,112,128]{2,1,0:T(8,128)(2,1)S(1)}, s16[2,112,128]{2,1,0:T(8,128)(2,1)S(1)}, u32[]{:S(2)}, u32[]{:S(2)}) collective-permute-start(s16[2,112,128]{2,1,0:T(8,128)(2,1)S(1)} %quad.1.refs_0_), channel_id=1, source_target_pairs={{0,24},{1,25},{2,26},{3,27},{4,28},{5,29},{6,30},{7,31},{8,16},{9,... | collective-permute-start | bytes 172040 | tf_op jit(solution)/shard_map/ppermute | solution.py:518
  31.9 0.6 %collective-permute-start.7 = (s16[2,112,128]{2,1,0:T(8,128)(2,1)S(1)}, s16[2,112,128]{2,1,0:T(8,128)(2,1)S(1)}, u32[]{:S(2)}, u32[]{:S(2)}) collective-permute-start(s16[2,112,128]{2,1,0:T(8,128)(2,1)S(1)} %quad.1.refs_0_), channel_id=1, source_target_pairs={{0,8},{1,9},{2,10},{3,11},{4,12},{5,13},{6,14},{7,15},{8,0},{9,1},... | collective-permute-start | bytes 172040 | tf_op jit(solution)/shard_map/ppermute | solution.py:518
  32.5 1.5 %collective-permute-start.6 = (s16[2,112,128]{2,1,0:T(8,128)(2,1)S(1)}, s16[2,112,128]{2,1,0:T(8,128)(2,1)S(1)}, u32[]{:S(2)}, u32[]{:S(2)}) collective-permute-start(s16[2,112,128]{2,1,0:T(8,128)(2,1)S(1)} %quad.1.refs_0_), channel_id=1, source_target_pairs={{0,16},{1,17},{2,18},{3,19},{4,20},{5,21},{6,22},{7,23},{8,24},{9,... | collective-permute-start | bytes 172040 | tf_op jit(solution)/shard_map/ppermute | solution.py:518
  34.0 1.9 %collective-permute-done.8.refs_3_ = s16[2,112,128]{2,1,0:T(8,128)(2,1)S(1)} collective-permute-done((s16[2,112,128]{2,1,0:T(8,128)(2,1)S(1)}, s16[2,112,128]{2,1,0:T(8,128)(2,1)S(1)}, u32[]{:S(2)}, u32[]{:S(2)}) %collective-permute-start.8) | collective-permute-done | bytes 57376 | tf_op jit(solution)/shard_map/ppermute | solution.py:518
  35.8 0.5 %collective-permute-done.7.refs_2_ = s16[2,112,128]{2,1,0:T(8,128)(2,1)S(1)} collective-permute-done((s16[2,112,128]{2,1,0:T(8,128)(2,1)S(1)}, s16[2,112,128]{2,1,0:T(8,128)(2,1)S(1)}, u32[]{:S(2)}, u32[]{:S(2)}) %collective-permute-start.7) | collective-permute-done | bytes 57376 | tf_op jit(solution)/shard_map/ppermute | solution.py:518
  36.3 1.2 %collective-permute-done.6.refs_1_ = s16[2,112,128]{2,1,0:T(8,128)(2,1)S(1)} collective-permute-done((s16[2,112,128]{2,1,0:T(8,128)(2,1)S(1)}, s16[2,112,128]{2,1,0:T(8,128)(2,1)S(1)}, u32[]{:S(2)}, u32[]{:S(2)}) %collective-permute-start.6) | collective-permute-done | bytes 57376 | tf_op jit(solution)/shard_map/ppermute | solution.py:518
  37.6 0.2 total.1
  37.7 1.3 %collective-permute-start.11 = (s16[4,104,128]{2,1,0:T(8,128)(2,1)S(1)}, s16[4,104,128]{2,1,0:T(8,128)(2,1)S(1)}, u32[]{:S(2)}, u32[]{:S(2)}) collective-permute-start(s16[4,104,128]{2,1,0:T(8,128)(2,1)S(1)} %total.1), channel_id=1, source_target_pairs={{0,6},{1,7},{2,4},{3,5},{4,2},{5,3},{6,0},{7,1},{8,14},{9,15},{10,... | collective-permute-start | bytes 319496 | tf_op jit(solution)/shard_map/ppermute | solution.py:518
  39.0 1.3 %collective-permute-start.10 = (s16[4,104,128]{2,1,0:T(8,128)(2,1)S(1)}, s16[4,104,128]{2,1,0:T(8,128)(2,1)S(1)}, u32[]{:S(2)}, u32[]{:S(2)}) collective-permute-start(s16[4,104,128]{2,1,0:T(8,128)(2,1)S(1)} %total.1), channel_id=1, source_target_pairs={{0,2},{1,3},{2,0},{3,1},{4,6},{5,7},{6,4},{7,5},{8,10},{9,11},{10,... | collective-permute-start | bytes 319496 | tf_op jit(solution)/shard_map/ppermute | solution.py:518
  40.3 1.0 %collective-permute-start.9 = (s16[4,104,128]{2,1,0:T(8,128)(2,1)S(1)}, s16[4,104,128]{2,1,0:T(8,128)(2,1)S(1)}, u32[]{:S(2)}, u32[]{:S(2)}) collective-permute-start(s16[4,104,128]{2,1,0:T(8,128)(2,1)S(1)} %total.1), channel_id=1, source_target_pairs={{0,4},{1,5},{2,6},{3,7},{4,0},{5,1},{6,2},{7,3},{8,12},{9,13},{10,... | collective-permute-start | bytes 319496 | tf_op jit(solution)/shard_map/ppermute | solution.py:518
  41.3 0.0 copy-done.3
  41.3 2.1 %entity.1 = f32[100,256]{1,0:T(8,128)} custom-call(s32[1,2,8]{2,1,0:T(2,128)S(1)} %bitcast.8, s32[8,1536]{1,0:T(8,128)S(1)} %get-tuple-element.17.refs_4_.packed, bf16[208,1536]{1,0:T(8,128)(2,1)S(1)} %get-tuple-element.27.x, s16[2,112,128]{2,1,0:T(8,128)(2,1)S(1)} %quad.1.refs_0_, s16[2,112,128]{2,1,0:T(8,128)(2,1)S(1)} %collective-permute-done.6.refs_1_), custom_call_target="tpu_custom_call" | custom-call | flops 1000000000 | bytes 1000000 | tf_op jit(solution)/shard_map/entity/pallas_call | solution.py:564
  43.4 0.1 collective-permute-done.11
  43.5 0.9 %collective-permute-done.10 = s16[4,104,128]{2,1,0:T(8,128)(2,1)S(1)} collective-permute-done((s16[4,104,128]{2,1,0:T(8,128)(2,1)S(1)}, s16[4,104,128]{2,1,0:T(8,128)(2,1)S(1)}, u32[]{:S(2)}, u32[]{:S(2)}) %collective-permute-start.10) | collective-permute-done | bytes 106528 | tf_op jit(solution)/shard_map/ppermute | solution.py:518
  44.4 0.6 %collective-permute-done.9 = s16[4,104,128]{2,1,0:T(8,128)(2,1)S(1)} collective-permute-done((s16[4,104,128]{2,1,0:T(8,128)(2,1)S(1)}, s16[4,104,128]{2,1,0:T(8,128)(2,1)S(1)}, u32[]{:S(2)}, u32[]{:S(2)}) %collective-permute-start.9) | collective-permute-done | bytes 106528 | tf_op jit(solution)/shard_map/ppermute | solution.py:518
  45.1 0.1 collective-permute-start.13
  45.2 0.5 %collective-permute-start.12 = (s16[4,104,128]{2,1,0:T(8,128)(2,1)S(1)}, s16[4,104,128]{2,1,0:T(8,128)(2,1)S(1)}, u32[]{:S(2)}, u32[]{:S(2)}) collective-permute-start(s16[4,104,128]{2,1,0:T(8,128)(2,1)S(1)} %total.1), channel_id=1, source_target_pairs={{0,1},{1,0},{2,3},{3,2},{4,5},{5,4},{6,7},{7,6},{8,9},{9,8},{10,11... | collective-permute-start | bytes 319496 | tf_op jit(solution)/shard_map/ppermute | solution.py:518
  45.7 1.0 %spread_own.1.partial = f32[400,1000]{1,0:T(8,128)} custom-call(s16[16,104,128]{2,1,0:T(8,128)(2,1)S(1)} %pad_add_fusion.mine), custom_call_target="tpu_custom_call" | custom-call | flops 1000000 | bytes 1600000 | tf_op jit(solution)/shard_map/spread_own/pallas_call | solution.py:582
  46.7 0.2 collective-permute-done.12
  46.9 0.0 collective-permute-done.13
  47.0 1.0 %spread_rest.1 = f32[400,1000]{1,0:T(8,128)} custom-call(s16[16,104,128]{2,1,0:T(8,128)(2,1)S(1)} %pad_add_fusion.mine, s16[16,104,128]{2,1,0:T(8,128)(2,1)S(1)} %pad_add_fusion.1.other, f32[400,1000]{1,0:T(8,128)} %spread_own.1.partial), custom_call_target="tpu_custom_call", output_to_operand_aliasing={{}: (2, {})} | custom-call | tf_op jit(solution)/shard_map/spread_rest/pallas_call | solution.py:592
  (3 shorter events, 0.1 us)
Async XLA Ops:
  3.1 9.1 %collective-permute-start.2 = (s32[8,512]{1,0:T(8,128)}, s32[8,512]{1,0:T(8,128)S(1)}, u32[]{:S(2)}, u32[]{:S(2)}) collective-permute-start(s32[8,512]{1,0:T(8,128)} %get-tuple-element.16.refs_0_), channel_id=1, source_target_pairs={{0,3},{1,0},{2,1},{3,2},{4,7},{5,4},{6,5},{7,6},{8,11},{9,8},{10,9... | collective-permute-start | bytes 49160 | tf_op jit(solution)/shard_map/ppermute | solution.py:463
  5.5 6.7 %collective-permute-start.1 = (s32[8,512]{1,0:T(8,128)}, s32[8,512]{1,0:T(8,128)S(1)}, u32[]{:S(2)}, u32[]{:S(2)}) collective-permute-start(s32[8,512]{1,0:T(8,128)} %get-tuple-element.16.refs_0_), channel_id=1, source_target_pairs={{0,2},{1,3},{2,0},{3,1},{4,6},{5,7},{6,4},{7,5},{8,10},{9,11},{10,... | collective-permute-start | bytes 49160 | tf_op jit(solution)/shard_map/ppermute | solution.py:463
  6.2 6.0 %collective-permute-start = (s32[8,512]{1,0:T(8,128)}, s32[8,512]{1,0:T(8,128)S(1)}, u32[]{:S(2)}, u32[]{:S(2)}) collective-permute-start(s32[8,512]{1,0:T(8,128)} %get-tuple-element.16.refs_0_), channel_id=1, source_target_pairs={{0,1},{1,2},{2,3},{3,0},{4,5},{5,6},{6,7},{7,4},{8,9},{9,10},{10,1... | collective-permute-start | bytes 49160 | tf_op jit(solution)/shard_map/ppermute | solution.py:463
  6.3 12.7 %all-to-all-start = ((f32[8,2,400]{2,1,0:T(2,128)}), f32[8,2,400]{2,1,0:T(2,128)S(1)}, u32[]{:S(2)}, u32[]{:S(2)}) async-start(f32[8,2,400]{2,1,0:T(2,128)} %get-tuple-element.21), calls=%async_computation | async-start | bytes 65536 | tf_op jit(solution)/shard_map/all_to_all | solution.py:464
  12.2 0.9 %copy-start = (bf16[256,400]{0,1:T(8,128)(2,1)S(1)}, bf16[256,400]{0,1:T(8,128)(2,1)}, u32[]{:S(2)}) copy-start(bf16[256,400]{0,1:T(8,128)(2,1)} %param.8) | copy-start | bytes 614404
  13.1 0.7 %copy-start.1 = (s32[8,512]{1,0:T(8,128)S(1)}, s32[8,512]{1,0:T(8,128)}, u32[]{:S(2)}) copy-start(s32[8,512]{1,0:T(8,128)} %get-tuple-element.16.refs_0_) | copy-start | bytes 49156
  13.8 1.4 %copy-start.4 = (f32[1000,400]{0,1:T(8,128)S(1)}, f32[1000,400]{0,1:T(8,128)}, u32[]{:S(2)}) copy-start(f32[1000,400]{0,1:T(8,128)} %param.9) | copy-start | bytes 4800004
  15.3 3.7 %copy-start.2 = (s32[8,512]{1,0:T(8,128)S(1)}, s32[8,512]{1,0:T(8,128)}, u32[]{:S(2)}) copy-start(s32[8,512]{1,0:T(8,128)} %get-tuple-element.16.refs_0_) | copy-start | bytes 49156
  19.0 22.3 %copy-start.3 = (s32[1,8,2]{1,2,0:T(2,128)S(1)}, s32[1,8,2]{1,2,0:T(2,128)}, u32[]{:S(2)}) copy-start(s32[1,8,2]{1,2,0:T(2,128)} %param.10) | copy-start | bytes 196
  21.0 4.7 %collective-permute-start.3 = (s16[2,112,128]{2,1,0:T(8,128)(2,1)S(1)}, s16[2,112,128]{2,1,0:T(8,128)(2,1)S(1)}, u32[]{:S(2)}, u32[]{:S(2)}) collective-permute-start(s16[2,112,128]{2,1,0:T(8,128)(2,1)S(1)} %get-tuple-element.24), channel_id=1, source_target_pairs={{0,4},{1,5},{2,6},{3,7},{4,0},{5,1},{6,2},{7,3},{8,12},{9,13},{10,... | collective-permute-start | bytes 172040 | tf_op jit(solution)/shard_map/ppermute | solution.py:518
  22.8 4.4 %collective-permute-start.4 = (s16[2,112,128]{2,1,0:T(8,128)(2,1)S(1)}, s16[2,112,128]{2,1,0:T(8,128)(2,1)S(1)}, u32[]{:S(2)}, u32[]{:S(2)}) collective-permute-start(s16[2,112,128]{2,1,0:T(8,128)(2,1)S(1)} %get-tuple-element.25), channel_id=1, source_target_pairs={{0,8},{1,9},{2,10},{3,11},{4,12},{5,13},{6,14},{7,15},{8,0},{9,1},... | collective-permute-start | bytes 172040 | tf_op jit(solution)/shard_map/ppermute | solution.py:518
  24.3 5.1 %collective-permute-start.5 = (s16[2,112,128]{2,1,0:T(8,128)(2,1)S(1)}, s16[2,112,128]{2,1,0:T(8,128)(2,1)S(1)}, u32[]{:S(2)}, u32[]{:S(2)}) collective-permute-start(s16[2,112,128]{2,1,0:T(8,128)(2,1)S(1)} %get-tuple-element.26), channel_id=1, source_target_pairs={{0,12},{1,13},{2,14},{3,15},{4,8},{5,9},{6,10},{7,11},{8,4},{9,5},... | collective-permute-start | bytes 172040 | tf_op jit(solution)/shard_map/ppermute | solution.py:518
  29.5 6.3 %collective-permute-start.8 = (s16[2,112,128]{2,1,0:T(8,128)(2,1)S(1)}, s16[2,112,128]{2,1,0:T(8,128)(2,1)S(1)}, u32[]{:S(2)}, u32[]{:S(2)}) collective-permute-start(s16[2,112,128]{2,1,0:T(8,128)(2,1)S(1)} %quad.1.refs_0_), channel_id=1, source_target_pairs={{0,24},{1,25},{2,26},{3,27},{4,28},{5,29},{6,30},{7,31},{8,16},{9,... | collective-permute-start | bytes 172040 | tf_op jit(solution)/shard_map/ppermute | solution.py:518
  31.9 4.4 %collective-permute-start.7 = (s16[2,112,128]{2,1,0:T(8,128)(2,1)S(1)}, s16[2,112,128]{2,1,0:T(8,128)(2,1)S(1)}, u32[]{:S(2)}, u32[]{:S(2)}) collective-permute-start(s16[2,112,128]{2,1,0:T(8,128)(2,1)S(1)} %quad.1.refs_0_), channel_id=1, source_target_pairs={{0,8},{1,9},{2,10},{3,11},{4,12},{5,13},{6,14},{7,15},{8,0},{9,1},... | collective-permute-start | bytes 172040 | tf_op jit(solution)/shard_map/ppermute | solution.py:518
  32.5 5.1 %collective-permute-start.6 = (s16[2,112,128]{2,1,0:T(8,128)(2,1)S(1)}, s16[2,112,128]{2,1,0:T(8,128)(2,1)S(1)}, u32[]{:S(2)}, u32[]{:S(2)}) collective-permute-start(s16[2,112,128]{2,1,0:T(8,128)(2,1)S(1)} %quad.1.refs_0_), channel_id=1, source_target_pairs={{0,16},{1,17},{2,18},{3,19},{4,20},{5,21},{6,22},{7,23},{8,24},{9,... | collective-permute-start | bytes 172040 | tf_op jit(solution)/shard_map/ppermute | solution.py:518
  37.7 5.8 %collective-permute-start.11 = (s16[4,104,128]{2,1,0:T(8,128)(2,1)S(1)}, s16[4,104,128]{2,1,0:T(8,128)(2,1)S(1)}, u32[]{:S(2)}, u32[]{:S(2)}) collective-permute-start(s16[4,104,128]{2,1,0:T(8,128)(2,1)S(1)} %total.1), channel_id=1, source_target_pairs={{0,6},{1,7},{2,4},{3,5},{4,2},{5,3},{6,0},{7,1},{8,14},{9,15},{10,... | collective-permute-start | bytes 319496 | tf_op jit(solution)/shard_map/ppermute | solution.py:518
  39.0 5.4 %collective-permute-start.10 = (s16[4,104,128]{2,1,0:T(8,128)(2,1)S(1)}, s16[4,104,128]{2,1,0:T(8,128)(2,1)S(1)}, u32[]{:S(2)}, u32[]{:S(2)}) collective-permute-start(s16[4,104,128]{2,1,0:T(8,128)(2,1)S(1)} %total.1), channel_id=1, source_target_pairs={{0,2},{1,3},{2,0},{3,1},{4,6},{5,7},{6,4},{7,5},{8,10},{9,11},{10,... | collective-permute-start | bytes 319496 | tf_op jit(solution)/shard_map/ppermute | solution.py:518
  40.3 4.7 %collective-permute-start.9 = (s16[4,104,128]{2,1,0:T(8,128)(2,1)S(1)}, s16[4,104,128]{2,1,0:T(8,128)(2,1)S(1)}, u32[]{:S(2)}, u32[]{:S(2)}) collective-permute-start(s16[4,104,128]{2,1,0:T(8,128)(2,1)S(1)} %total.1), channel_id=1, source_target_pairs={{0,4},{1,5},{2,6},{3,7},{4,0},{5,1},{6,2},{7,3},{8,12},{9,13},{10,... | collective-permute-start | bytes 319496 | tf_op jit(solution)/shard_map/ppermute | solution.py:518
  45.1 1.8 %collective-permute-start.13 = (s16[12,104,128]{2,1,0:T(8,128)(2,1)S(1)}, s16[12,104,128]{2,1,0:T(8,128)(2,1)S(1)}, u32[]{:S(2)}, u32[]{:S(2)}) collective-permute-start(s16[12,104,128]{2,1,0:T(8,128)(2,1)S(1)} %pad_add_fusion.2), channel_id=1, source_target_pairs={{0,1},{1,0},{2,3},{3,2},{4,5},{5,4},{6,7},{7,6},{8,9},{9,8},{10,11... | collective-permute-start | bytes 958472 | tf_op jit(solution)/shard_map/ppermute | solution.py:518
  45.2 1.8 %collective-permute-start.12 = (s16[4,104,128]{2,1,0:T(8,128)(2,1)S(1)}, s16[4,104,128]{2,1,0:T(8,128)(2,1)S(1)}, u32[]{:S(2)}, u32[]{:S(2)}) collective-permute-start(s16[4,104,128]{2,1,0:T(8,128)(2,1)S(1)} %total.1), channel_id=1, source_target_pairs={{0,1},{1,0},{2,3},{3,2},{4,5},{5,4},{6,7},{7,6},{8,9},{9,8},{10,11... | collective-permute-start | bytes 319496 | tf_op jit(solution)/shard_map/ppermute | solution.py:518

commit v18 on v17

--- a/solution.py
+++ b/solution.py
@@ -458,10 +458,10 @@
         name="prep",
     )(serve_t, edge_count, ent_t, edge_src, edge_rel, edge_dst, neg_ids)
 
+    received = lax.all_to_all(served, "dom", 0, 0, tiled=True)
     held = [idx]
     for hop in range(1, replicas):
         held.append(lax.ppermute(idx, "rep", turned(replicas, hop)))
-    received = lax.all_to_all(served, "dom", 0, 0, tiled=True)
 
     total = min(replicas * edges, up(LIVE_EDGES, edges))
     packed, query, lhs_rows, rel_rows = pl.pallas_call(

time: 48.3 us -> 48.3 us (level)
  no operation moved by 1% of the time
where the time goes in v18:
time: 48.3 us; the launch traced here: 48 us
  starting transfers between devices  21.2 us (44%)
  Pallas kernels  12.4 us (26%)
  waiting for transfers between devices  9.81 us (20%)
  local copies, waits for them, and re-layouts  3.08 us (6%)
  between operations  1.39 us (3%)
    ppermute x11, starting transfers between devices, swap(): return lax.ppermute(array, ('dom', 'rep'), pairs)  12.1 us
    ppermute x11, waiting for transfers between devices, swap(): return lax.ppermute(array, ('dom', 'rep'), pairs)  9.49 us
    all_to_all x1, starting transfers between devices, shards(): received = lax.all_to_all(served, 'dom', 0, 0, tiled=True)  5.84 us
    pallas_call x1, Pallas kernels, shards(): pl.pallas_call(functools.partial(gather_kernel, (replicas, groups, nrel,...  3.38 us
    ppermute x3, starting transfers between devices, shards(): held.append(lax.ppermute(idx, 'rep', turned(replicas, hop)))  3.23 us
    unnamed x10, local copies, waits for them, and re-layouts  3.08 us
    pallas_call x1, Pallas kernels, shards(): pl.pallas_call(functools.partial(entity_kernel, direct, narrow, offsets),...  2.07 us
    pallas_call x1, Pallas kernels, shards(): pl.pallas_call(functools.partial(main_kernel, cfg), out_shape=[pieces, ja...  2.05 us
  transfers between devices with their start and end apart: 15, of which 11 were waited for; matrix products, arithmetic and copies ran while one was open for 0% of the time, Pallas kernels for 15%

profile of v18, /device:TPU:0, one launch (start us, length us, event | category | flops | bytes accessed | tf_op | source)
XLA Modules:
  0.0 48.0 jit_solution(15884520825728057349)
XLA Ops:
  1.3 1.8 %prep.1 = (s32[8,512]{1,0:T(8,128)}, f32[8,2,400]{2,1,0:T(2,128)}) custom-call(s32[1,2,8]{2,1,0:T(2,128)} %bitcast.7, s32[1,1]{1,0:T(1,128)S(6)} %copy.12.count, bf16[400,256]{1,0:T(8,128)(2,1)} %bitcast.5, s32[1,1,512]{2,1,0:T(1,128)} %src.1, s32[1,1,512]{2,1,0:T(1,128)} %rel.1, s32[1,1,512]{2,1,0:T(1,128)} %dst.1, s32[1,1,2,384]{3,2,1,0:T(2,128)} %neg.1), custom_call_target="tpu_custom_call" | custom-call | tf_op jit(solution)/shard_map/prep/pallas_call | solution.py:438
  3.1 2.4 %collective-permute-start.2 = (s32[8,512]{1,0:T(8,128)}, s32[8,512]{1,0:T(8,128)S(1)}, u32[]{:S(2)}, u32[]{:S(2)}) collective-permute-start(s32[8,512]{1,0:T(8,128)} %get-tuple-element.16.refs_0_), channel_id=1, source_target_pairs={{0,3},{1,0},{2,1},{3,2},{4,7},{5,4},{6,5},{7,6},{8,11},{9,8},{10,9... | collective-permute-start | bytes 49160 | tf_op jit(solution)/shard_map/ppermute | solution.py:464
  5.5 0.6 %collective-permute-start.1 = (s32[8,512]{1,0:T(8,128)}, s32[8,512]{1,0:T(8,128)S(1)}, u32[]{:S(2)}, u32[]{:S(2)}) collective-permute-start(s32[8,512]{1,0:T(8,128)} %get-tuple-element.16.refs_0_), channel_id=1, source_target_pairs={{0,2},{1,3},{2,0},{3,1},{4,6},{5,7},{6,4},{7,5},{8,10},{9,11},{10,... | collective-permute-start | bytes 49160 | tf_op jit(solution)/shard_map/ppermute | solution.py:464
  6.2 0.2 collective-permute-start
  6.3 5.8 %all-to-all-start = ((f32[8,2,400]{2,1,0:T(2,128)}), f32[8,2,400]{2,1,0:T(2,128)S(1)}, u32[]{:S(2)}, u32[]{:S(2)}) async-start(f32[8,2,400]{2,1,0:T(2,128)} %get-tuple-element.21), calls=%async_computation | async-start | bytes 65536 | tf_op jit(solution)/shard_map/all_to_all | solution.py:461
  12.2 0.0 collective-permute-done.2.refs_3_
  12.2 0.0 collective-permute-done.1.refs_2_
  12.2 0.0 collective-permute-done.refs_1_
  12.2 0.0 copy-start
  12.2 0.9 %copy-done = bf16[256,400]{0,1:T(8,128)(2,1)S(1)} copy-done((bf16[256,400]{0,1:T(8,128)(2,1)S(1)}, bf16[256,400]{0,1:T(8,128)(2,1)}, u32[]{:S(2)}) %copy-start) | copy-done | bytes 204824
  13.1 0.0 copy-start.1
  13.1 0.7 %copy-done.1 = s32[8,512]{1,0:T(8,128)S(1)} copy-done((s32[8,512]{1,0:T(8,128)S(1)}, s32[8,512]{1,0:T(8,128)}, u32[]{:S(2)}) %copy-start.1) | copy-done | bytes 16408
  13.8 0.0 copy-start.4
  13.8 1.4 %copy-done.4 = f32[1000,400]{0,1:T(8,128)S(1)} copy-done((f32[1000,400]{0,1:T(8,128)S(1)}, f32[1000,400]{0,1:T(8,128)}, u32[]{:S(2)}) %copy-start.4) | copy-done | bytes 1600024
  15.3 0.0 copy-start.2
  15.3 3.4 %gather.1 = (s32[8,1536]{1,0:T(8,128)S(1)}, bf16[400,1536]{1,0:T(8,128)(2,1)S(1)}, f32[104,1536]{1,0:T(8,128)S(1)}, f32[104,1536]{1,0:T(8,128)S(1)}) custom-call(s32[8,512]{1,0:T(8,128)S(1)} %copy-done.1, s32[8,512]{1,0:T(8,128)S(1)} %collective-permute-done.refs_1_, s32[8,512]{1,0:T(8,128)S(1)} %collective-permute-done.1.refs_2_, ...), custom_call_target="tpu_custom_call" | custom-call | flops 2831155200 | bytes 4915200 | tf_op jit(solution)/shard_map/gather/pallas_call | solution.py:467
  18.7 0.3 all-to-all-done.refs_8_
  19.0 0.0 copy-done.2
  19.0 0.0 copy-start.3
  19.0 2.0 %edges.1 = (bf16[208,1536]{1,0:T(8,128)(2,1)S(1)}, s32[16,128]{1,0:T(8,128)S(1)}, bf16[208,1536]{1,0:T(8,128)(2,1)S(1)}, s16[2,112,128]{2,1,0:T(8,128)(2,1)S(1)}...) custom-call(s32[8,512]{1,0:T(8,128)S(1)} %copy-done.2, s32[8,512]{1,0:T(8,128)S(1)} %collective-permute-done.refs_1_, ...), custom_call_target="tpu_custom_call" | custom-call | tf_op jit(solution)/shard_map/edges/pallas_call | solution.py:497
  21.0 1.8 %collective-permute-start.3 = (s16[2,112,128]{2,1,0:T(8,128)(2,1)S(1)}, s16[2,112,128]{2,1,0:T(8,128)(2,1)S(1)}, u32[]{:S(2)}, u32[]{:S(2)}) collective-permute-start(s16[2,112,128]{2,1,0:T(8,128)(2,1)S(1)} %get-tuple-element.24), channel_id=1, source_target_pairs={{0,4},{1,5},{2,6},{3,7},{4,0},{5,1},{6,2},{7,3},{8,12},{9,13},{10,... | collective-permute-start | bytes 172040 | tf_op jit(solution)/shard_map/ppermute | solution.py:518
  22.8 1.5 %collective-permute-start.4 = (s16[2,112,128]{2,1,0:T(8,128)(2,1)S(1)}, s16[2,112,128]{2,1,0:T(8,128)(2,1)S(1)}, u32[]{:S(2)}, u32[]{:S(2)}) collective-permute-start(s16[2,112,128]{2,1,0:T(8,128)(2,1)S(1)} %get-tuple-element.25), channel_id=1, source_target_pairs={{0,8},{1,9},{2,10},{3,11},{4,12},{5,13},{6,14},{7,15},{8,0},{9,1},... | collective-permute-start | bytes 172040 | tf_op jit(solution)/shard_map/ppermute | solution.py:518
  24.3 0.3 collective-permute-start.5
  24.6 0.8 %own.1.refs_0_ = s16[2,112,128]{2,1,0:T(8,128)(2,1)S(1)} custom-call(s32[8,1536]{1,0:T(8,128)S(1)} %get-tuple-element.17.refs_4_.packed, bf16[208,1536]{1,0:T(8,128)(2,1)S(1)} %get-tuple-element.22.y, s32[16,128]{1,0:T(8,128)S(1)} %get-tuple-element.23.tables), custom_call_target="tpu_custom_call" | custom-call | flops 163577856 | bytes 1000000 | tf_op jit(solution)/shard_map/own/pallas_call | solution.py:524
  25.4 0.3 collective-permute-done.3.refs_1_
  25.7 1.5 %collective-permute-done.4.refs_2_ = s16[2,112,128]{2,1,0:T(8,128)(2,1)S(1)} collective-permute-done((s16[2,112,128]{2,1,0:T(8,128)(2,1)S(1)}, s16[2,112,128]{2,1,0:T(8,128)(2,1)S(1)}, u32[]{:S(2)}, u32[]{:S(2)}) %collective-permute-start.4) | collective-permute-done | bytes 57376 | tf_op jit(solution)/shard_map/ppermute | solution.py:518
  27.2 2.1 %collective-permute-done.5.refs_3_ = s16[2,112,128]{2,1,0:T(8,128)(2,1)S(1)} collective-permute-done((s16[2,112,128]{2,1,0:T(8,128)(2,1)S(1)}, s16[2,112,128]{2,1,0:T(8,128)(2,1)S(1)}, u32[]{:S(2)}, u32[]{:S(2)}) %collective-permute-start.5) | collective-permute-done | bytes 57376 | tf_op jit(solution)/shard_map/ppermute | solution.py:518
  29.4 0.1 quad.1.refs_0_
  29.5 2.4 %collective-permute-start.8 = (s16[2,112,128]{2,1,0:T(8,128)(2,1)S(1)}, s16[2,112,128]{2,1,0:T(8,128)(2,1)S(1)}, u32[]{:S(2)}, u32[]{:S(2)}) collective-permute-start(s16[2,112,128]{2,1,0:T(8,128)(2,1)S(1)} %quad.1.refs_0_), channel_id=1, source_target_pairs={{0,24},{1,25},{2,26},{3,27},{4,28},{5,29},{6,30},{7,31},{8,16},{9,... | collective-permute-start | bytes 172040 | tf_op jit(solution)/shard_map/ppermute | solution.py:518
  31.9 0.6 %collective-permute-start.7 = (s16[2,112,128]{2,1,0:T(8,128)(2,1)S(1)}, s16[2,112,128]{2,1,0:T(8,128)(2,1)S(1)}, u32[]{:S(2)}, u32[]{:S(2)}) collective-permute-start(s16[2,112,128]{2,1,0:T(8,128)(2,1)S(1)} %quad.1.refs_0_), channel_id=1, source_target_pairs={{0,8},{1,9},{2,10},{3,11},{4,12},{5,13},{6,14},{7,15},{8,0},{9,1},... | collective-permute-start | bytes 172040 | tf_op jit(solution)/shard_map/ppermute | solution.py:518
  32.5 1.5 %collective-permute-start.6 = (s16[2,112,128]{2,1,0:T(8,128)(2,1)S(1)}, s16[2,112,128]{2,1,0:T(8,128)(2,1)S(1)}, u32[]{:S(2)}, u32[]{:S(2)}) collective-permute-start(s16[2,112,128]{2,1,0:T(8,128)(2,1)S(1)} %quad.1.refs_0_), channel_id=1, source_target_pairs={{0,16},{1,17},{2,18},{3,19},{4,20},{5,21},{6,22},{7,23},{8,24},{9,... | collective-permute-start | bytes 172040 | tf_op jit(solution)/shard_map/ppermute | solution.py:518
  34.0 1.9 %collective-permute-done.8.refs_3_ = s16[2,112,128]{2,1,0:T(8,128)(2,1)S(1)} collective-permute-done((s16[2,112,128]{2,1,0:T(8,128)(2,1)S(1)}, s16[2,112,128]{2,1,0:T(8,128)(2,1)S(1)}, u32[]{:S(2)}, u32[]{:S(2)}) %collective-permute-start.8) | collective-permute-done | bytes 57376 | tf_op jit(solution)/shard_map/ppermute | solution.py:518
  35.8 0.5 %collective-permute-done.7.refs_2_ = s16[2,112,128]{2,1,0:T(8,128)(2,1)S(1)} collective-permute-done((s16[2,112,128]{2,1,0:T(8,128)(2,1)S(1)}, s16[2,112,128]{2,1,0:T(8,128)(2,1)S(1)}, u32[]{:S(2)}, u32[]{:S(2)}) %collective-permute-start.7) | collective-permute-done | bytes 57376 | tf_op jit(solution)/shard_map/ppermute | solution.py:518
  36.3 1.2 %collective-permute-done.6.refs_1_ = s16[2,112,128]{2,1,0:T(8,128)(2,1)S(1)} collective-permute-done((s16[2,112,128]{2,1,0:T(8,128)(2,1)S(1)}, s16[2,112,128]{2,1,0:T(8,128)(2,1)S(1)}, u32[]{:S(2)}, u32[]{:S(2)}) %collective-permute-start.6) | collective-permute-done | bytes 57376 | tf_op jit(solution)/shard_map/ppermute | solution.py:518
  37.6 0.2 total.1
  37.7 1.3 %collective-permute-start.11 = (s16[4,104,128]{2,1,0:T(8,128)(2,1)S(1)}, s16[4,104,128]{2,1,0:T(8,128)(2,1)S(1)}, u32[]{:S(2)}, u32[]{:S(2)}) collective-permute-start(s16[4,104,128]{2,1,0:T(8,128)(2,1)S(1)} %total.1), channel_id=1, source_target_pairs={{0,6},{1,7},{2,4},{3,5},{4,2},{5,3},{6,0},{7,1},{8,14},{9,15},{10,... | collective-permute-start | bytes 319496 | tf_op jit(solution)/shard_map/ppermute | solution.py:518
  39.0 1.3 %collective-permute-start.10 = (s16[4,104,128]{2,1,0:T(8,128)(2,1)S(1)}, s16[4,104,128]{2,1,0:T(8,128)(2,1)S(1)}, u32[]{:S(2)}, u32[]{:S(2)}) collective-permute-start(s16[4,104,128]{2,1,0:T(8,128)(2,1)S(1)} %total.1), channel_id=1, source_target_pairs={{0,2},{1,3},{2,0},{3,1},{4,6},{5,7},{6,4},{7,5},{8,10},{9,11},{10,... | collective-permute-start | bytes 319496 | tf_op jit(solution)/shard_map/ppermute | solution.py:518
  40.3 1.0 %collective-permute-start.9 = (s16[4,104,128]{2,1,0:T(8,128)(2,1)S(1)}, s16[4,104,128]{2,1,0:T(8,128)(2,1)S(1)}, u32[]{:S(2)}, u32[]{:S(2)}) collective-permute-start(s16[4,104,128]{2,1,0:T(8,128)(2,1)S(1)} %total.1), channel_id=1, source_target_pairs={{0,4},{1,5},{2,6},{3,7},{4,0},{5,1},{6,2},{7,3},{8,12},{9,13},{10,... | collective-permute-start | bytes 319496 | tf_op jit(solution)/shard_map/ppermute | solution.py:518
  41.3 0.0 copy-done.3
  41.3 2.1 %entity.1 = f32[100,256]{1,0:T(8,128)} custom-call(s32[1,2,8]{2,1,0:T(2,128)S(1)} %bitcast.8, s32[8,1536]{1,0:T(8,128)S(1)} %get-tuple-element.17.refs_4_.packed, bf16[208,1536]{1,0:T(8,128)(2,1)S(1)} %get-tuple-element.27.x, s16[2,112,128]{2,1,0:T(8,128)(2,1)S(1)} %quad.1.refs_0_, s16[2,112,128]{2,1,0:T(8,128)(2,1)S(1)} %collective-permute-done.6.refs_1_), custom_call_target="tpu_custom_call" | custom-call | flops 1000000000 | bytes 1000000 | tf_op jit(solution)/shard_map/entity/pallas_call | solution.py:564
  43.4 0.1 collective-permute-done.11
  43.5 0.9 %collective-permute-done.10 = s16[4,104,128]{2,1,0:T(8,128)(2,1)S(1)} collective-permute-done((s16[4,104,128]{2,1,0:T(8,128)(2,1)S(1)}, s16[4,104,128]{2,1,0:T(8,128)(2,1)S(1)}, u32[]{:S(2)}, u32[]{:S(2)}) %collective-permute-start.10) | collective-permute-done | bytes 106528 | tf_op jit(solution)/shard_map/ppermute | solution.py:518
  44.4 0.6 %collective-permute-done.9 = s16[4,104,128]{2,1,0:T(8,128)(2,1)S(1)} collective-permute-done((s16[4,104,128]{2,1,0:T(8,128)(2,1)S(1)}, s16[4,104,128]{2,1,0:T(8,128)(2,1)S(1)}, u32[]{:S(2)}, u32[]{:S(2)}) %collective-permute-start.9) | collective-permute-done | bytes 106528 | tf_op jit(solution)/shard_map/ppermute | solution.py:518
  45.1 0.1 collective-permute-start.13
  45.2 0.5 %collective-permute-start.12 = (s16[4,104,128]{2,1,0:T(8,128)(2,1)S(1)}, s16[4,104,128]{2,1,0:T(8,128)(2,1)S(1)}, u32[]{:S(2)}, u32[]{:S(2)}) collective-permute-start(s16[4,104,128]{2,1,0:T(8,128)(2,1)S(1)} %total.1), channel_id=1, source_target_pairs={{0,1},{1,0},{2,3},{3,2},{4,5},{5,4},{6,7},{7,6},{8,9},{9,8},{10,11... | collective-permute-start | bytes 319496 | tf_op jit(solution)/shard_map/ppermute | solution.py:518
  45.7 1.0 %spread_own.1.partial = f32[400,1000]{1,0:T(8,128)} custom-call(s16[16,104,128]{2,1,0:T(8,128)(2,1)S(1)} %pad_add_fusion.mine), custom_call_target="tpu_custom_call" | custom-call | flops 1000000 | bytes 1600000 | tf_op jit(solution)/shard_map/spread_own/pallas_call | solution.py:582
  46.7 0.2 collective-permute-done.12
  46.9 0.0 collective-permute-done.13
  47.0 1.0 %spread_rest.1 = f32[400,1000]{1,0:T(8,128)} custom-call(s16[16,104,128]{2,1,0:T(8,128)(2,1)S(1)} %pad_add_fusion.mine, s16[16,104,128]{2,1,0:T(8,128)(2,1)S(1)} %pad_add_fusion.1.other, f32[400,1000]{1,0:T(8,128)} %spread_own.1.partial), custom_call_target="tpu_custom_call", output_to_operand_aliasing={{}: (2, {})} | custom-call | tf_op jit(solution)/shard_map/spread_rest/pallas_call | solution.py:592
  (3 shorter events, 0.1 us)
Async XLA Ops:
  3.1 9.1 %collective-permute-start.2 = (s32[8,512]{1,0:T(8,128)}, s32[8,512]{1,0:T(8,128)S(1)}, u32[]{:S(2)}, u32[]{:S(2)}) collective-permute-start(s32[8,512]{1,0:T(8,128)} %get-tuple-element.16.refs_0_), channel_id=1, source_target_pairs={{0,3},{1,0},{2,1},{3,2},{4,7},{5,4},{6,5},{7,6},{8,11},{9,8},{10,9... | collective-permute-start | bytes 49160 | tf_op jit(solution)/shard_map/ppermute | solution.py:464
  5.5 6.7 %collective-permute-start.1 = (s32[8,512]{1,0:T(8,128)}, s32[8,512]{1,0:T(8,128)S(1)}, u32[]{:S(2)}, u32[]{:S(2)}) collective-permute-start(s32[8,512]{1,0:T(8,128)} %get-tuple-element.16.refs_0_), channel_id=1, source_target_pairs={{0,2},{1,3},{2,0},{3,1},{4,6},{5,7},{6,4},{7,5},{8,10},{9,11},{10,... | collective-permute-start | bytes 49160 | tf_op jit(solution)/shard_map/ppermute | solution.py:464
  6.2 6.0 %collective-permute-start = (s32[8,512]{1,0:T(8,128)}, s32[8,512]{1,0:T(8,128)S(1)}, u32[]{:S(2)}, u32[]{:S(2)}) collective-permute-start(s32[8,512]{1,0:T(8,128)} %get-tuple-element.16.refs_0_), channel_id=1, source_target_pairs={{0,1},{1,2},{2,3},{3,0},{4,5},{5,6},{6,7},{7,4},{8,9},{9,10},{10,1... | collective-permute-start | bytes 49160 | tf_op jit(solution)/shard_map/ppermute | solution.py:464
  6.3 12.7 %all-to-all-start = ((f32[8,2,400]{2,1,0:T(2,128)}), f32[8,2,400]{2,1,0:T(2,128)S(1)}, u32[]{:S(2)}, u32[]{:S(2)}) async-start(f32[8,2,400]{2,1,0:T(2,128)} %get-tuple-element.21), calls=%async_computation | async-start | bytes 65536 | tf_op jit(solution)/shard_map/all_to_all | solution.py:461
  12.2 0.9 %copy-start = (bf16[256,400]{0,1:T(8,128)(2,1)S(1)}, bf16[256,400]{0,1:T(8,128)(2,1)}, u32[]{:S(2)}) copy-start(bf16[256,400]{0,1:T(8,128)(2,1)} %param.8) | copy-start | bytes 614404
  13.1 0.7 %copy-start.1 = (s32[8,512]{1,0:T(8,128)S(1)}, s32[8,512]{1,0:T(8,128)}, u32[]{:S(2)}) copy-start(s32[8,512]{1,0:T(8,128)} %get-tuple-element.16.refs_0_) | copy-start | bytes 49156
  13.8 1.4 %copy-start.4 = (f32[1000,400]{0,1:T(8,128)S(1)}, f32[1000,400]{0,1:T(8,128)}, u32[]{:S(2)}) copy-start(f32[1000,400]{0,1:T(8,128)} %param.9) | copy-start | bytes 4800004
  15.3 3.7 %copy-start.2 = (s32[8,512]{1,0:T(8,128)S(1)}, s32[8,512]{1,0:T(8,128)}, u32[]{:S(2)}) copy-start(s32[8,512]{1,0:T(8,128)} %get-tuple-element.16.refs_0_) | copy-start | bytes 49156
  19.0 22.3 %copy-start.3 = (s32[1,8,2]{1,2,0:T(2,128)S(1)}, s32[1,8,2]{1,2,0:T(2,128)}, u32[]{:S(2)}) copy-start(s32[1,8,2]{1,2,0:T(2,128)} %param.10) | copy-start | bytes 196
  21.0 4.7 %collective-permute-start.3 = (s16[2,112,128]{2,1,0:T(8,128)(2,1)S(1)}, s16[2,112,128]{2,1,0:T(8,128)(2,1)S(1)}, u32[]{:S(2)}, u32[]{:S(2)}) collective-permute-start(s16[2,112,128]{2,1,0:T(8,128)(2,1)S(1)} %get-tuple-element.24), channel_id=1, source_target_pairs={{0,4},{1,5},{2,6},{3,7},{4,0},{5,1},{6,2},{7,3},{8,12},{9,13},{10,... | collective-permute-start | bytes 172040 | tf_op jit(solution)/shard_map/ppermute | solution.py:518
  22.8 4.4 %collective-permute-start.4 = (s16[2,112,128]{2,1,0:T(8,128)(2,1)S(1)}, s16[2,112,128]{2,1,0:T(8,128)(2,1)S(1)}, u32[]{:S(2)}, u32[]{:S(2)}) collective-permute-start(s16[2,112,128]{2,1,0:T(8,128)(2,1)S(1)} %get-tuple-element.25), channel_id=1, source_target_pairs={{0,8},{1,9},{2,10},{3,11},{4,12},{5,13},{6,14},{7,15},{8,0},{9,1},... | collective-permute-start | bytes 172040 | tf_op jit(solution)/shard_map/ppermute | solution.py:518
  24.3 5.1 %collective-permute-start.5 = (s16[2,112,128]{2,1,0:T(8,128)(2,1)S(1)}, s16[2,112,128]{2,1,0:T(8,128)(2,1)S(1)}, u32[]{:S(2)}, u32[]{:S(2)}) collective-permute-start(s16[2,112,128]{2,1,0:T(8,128)(2,1)S(1)} %get-tuple-element.26), channel_id=1, source_target_pairs={{0,12},{1,13},{2,14},{3,15},{4,8},{5,9},{6,10},{7,11},{8,4},{9,5},... | collective-permute-start | bytes 172040 | tf_op jit(solution)/shard_map/ppermute | solution.py:518
  29.5 6.3 %collective-permute-start.8 = (s16[2,112,128]{2,1,0:T(8,128)(2,1)S(1)}, s16[2,112,128]{2,1,0:T(8,128)(2,1)S(1)}, u32[]{:S(2)}, u32[]{:S(2)}) collective-permute-start(s16[2,112,128]{2,1,0:T(8,128)(2,1)S(1)} %quad.1.refs_0_), channel_id=1, source_target_pairs={{0,24},{1,25},{2,26},{3,27},{4,28},{5,29},{6,30},{7,31},{8,16},{9,... | collective-permute-start | bytes 172040 | tf_op jit(solution)/shard_map/ppermute | solution.py:518
  31.9 4.4 %collective-permute-start.7 = (s16[2,112,128]{2,1,0:T(8,128)(2,1)S(1)}, s16[2,112,128]{2,1,0:T(8,128)(2,1)S(1)}, u32[]{:S(2)}, u32[]{:S(2)}) collective-permute-start(s16[2,112,128]{2,1,0:T(8,128)(2,1)S(1)} %quad.1.refs_0_), channel_id=1, source_target_pairs={{0,8},{1,9},{2,10},{3,11},{4,12},{5,13},{6,14},{7,15},{8,0},{9,1},... | collective-permute-start | bytes 172040 | tf_op jit(solution)/shard_map/ppermute | solution.py:518
  32.5 5.1 %collective-permute-start.6 = (s16[2,112,128]{2,1,0:T(8,128)(2,1)S(1)}, s16[2,112,128]{2,1,0:T(8,128)(2,1)S(1)}, u32[]{:S(2)}, u32[]{:S(2)}) collective-permute-start(s16[2,112,128]{2,1,0:T(8,128)(2,1)S(1)} %quad.1.refs_0_), channel_id=1, source_target_pairs={{0,16},{1,17},{2,18},{3,19},{4,20},{5,21},{6,22},{7,23},{8,24},{9,... | collective-permute-start | bytes 172040 | tf_op jit(solution)/shard_map/ppermute | solution.py:518
  37.7 5.8 %collective-permute-start.11 = (s16[4,104,128]{2,1,0:T(8,128)(2,1)S(1)}, s16[4,104,128]{2,1,0:T(8,128)(2,1)S(1)}, u32[]{:S(2)}, u32[]{:S(2)}) collective-permute-start(s16[4,104,128]{2,1,0:T(8,128)(2,1)S(1)} %total.1), channel_id=1, source_target_pairs={{0,6},{1,7},{2,4},{3,5},{4,2},{5,3},{6,0},{7,1},{8,14},{9,15},{10,... | collective-permute-start | bytes 319496 | tf_op jit(solution)/shard_map/ppermute | solution.py:518
  39.0 5.4 %collective-permute-start.10 = (s16[4,104,128]{2,1,0:T(8,128)(2,1)S(1)}, s16[4,104,128]{2,1,0:T(8,128)(2,1)S(1)}, u32[]{:S(2)}, u32[]{:S(2)}) collective-permute-start(s16[4,104,128]{2,1,0:T(8,128)(2,1)S(1)} %total.1), channel_id=1, source_target_pairs={{0,2},{1,3},{2,0},{3,1},{4,6},{5,7},{6,4},{7,5},{8,10},{9,11},{10,... | collective-permute-start | bytes 319496 | tf_op jit(solution)/shard_map/ppermute | solution.py:518
  40.3 4.7 %collective-permute-start.9 = (s16[4,104,128]{2,1,0:T(8,128)(2,1)S(1)}, s16[4,104,128]{2,1,0:T(8,128)(2,1)S(1)}, u32[]{:S(2)}, u32[]{:S(2)}) collective-permute-start(s16[4,104,128]{2,1,0:T(8,128)(2,1)S(1)} %total.1), channel_id=1, source_target_pairs={{0,4},{1,5},{2,6},{3,7},{4,0},{5,1},{6,2},{7,3},{8,12},{9,13},{10,... | collective-permute-start | bytes 319496 | tf_op jit(solution)/shard_map/ppermute | solution.py:518
  45.1 1.8 %collective-permute-start.13 = (s16[12,104,128]{2,1,0:T(8,128)(2,1)S(1)}, s16[12,104,128]{2,1,0:T(8,128)(2,1)S(1)}, u32[]{:S(2)}, u32[]{:S(2)}) collective-permute-start(s16[12,104,128]{2,1,0:T(8,128)(2,1)S(1)} %pad_add_fusion.2), channel_id=1, source_target_pairs={{0,1},{1,0},{2,3},{3,2},{4,5},{5,4},{6,7},{7,6},{8,9},{9,8},{10,11... | collective-permute-start | bytes 958472 | tf_op jit(solution)/shard_map/ppermute | solution.py:518
  45.2 1.8 %collective-permute-start.12 = (s16[4,104,128]{2,1,0:T(8,128)(2,1)S(1)}, s16[4,104,128]{2,1,0:T(8,128)(2,1)S(1)}, u32[]{:S(2)}, u32[]{:S(2)}) collective-permute-start(s16[4,104,128]{2,1,0:T(8,128)(2,1)S(1)} %total.1), channel_id=1, source_target_pairs={{0,1},{1,0},{2,3},{3,2},{4,5},{5,4},{6,7},{7,6},{8,9},{9,8},{10,11... | collective-permute-start | bytes 319496 | tf_op jit(solution)/shard_map/ppermute | solution.py:518
